TPU v7x, 512 devices: a whole 4x8x8 slice. The times are simulated.
512 devices in a mesh: seg: 8 (over z_hi, core), op: 64 (over x, z_lo, y).
Axes of the slice: x: 4, y: 8, z: 8 (z_hi: 4, z_lo: 2; z = z_hi * 2 + z_lo), core: 2. Of those that a mesh axis runs over, the one named last changes fastest.
Arguments:
- site_tensor: bfloat16 [8, 3, 4096, 128], P('seg'), may hold values from -0.375 to 0.375
- term_ops: bfloat16 [64, 4096, 128], P('op'), may hold values from -6 to 6
- env_rows: bfloat16 [4096, 128], P('op'), may hold values from -6 to 6
- term_shift: int32 [64], P('op'), may hold values from -1 to 1
- keep_weight: float32 [64, 3], P('op'), may hold values from 0.6 to 1.4
- env_weight: float32 [64, 3], P('op'), may hold values from -0.4375 to 0.4375
Outputs:
- bond_env: bfloat16 [8, 4096, 128], P('seg', 'op')
Inputs may be any that keep to these rules, and one draw needn't show every extreme that they name: term_shift[t] is the sector change of term t.
All inputs are finite; a program needn't handle non-finite values.
Results may differ from a plain program's by a relative error of at most 0.025.
Values may be sent and summed in bfloat16 or wider, within the bound.
No kernel may reach another device: no remote copies, remote signals or barrier semaphores. Data moves between devices by JAX's collectives and lax.ppermute only.
A program may use at most 64 MiB of HBM per device.

v0:
```python
import jax
import jax.numpy as jnp
from jax import lax
from jax.sharding import PartitionSpec as P


def passed_along(block, axis, distance):
    devices = range(lax.axis_size(axis))
    route = [(i - distance, i) for i in devices if i - distance in devices]
    return lax.ppermute(block, axis, route)


def take_window(blocks, start_at, length_of):
    return lax.dynamic_slice_in_dim(blocks, start_at, length_of, 0)


def left_product(own_blocks, image_one):
    return jnp.einsum("rik,rim->rkm", own_blocks, image_one, preferred_element_type=jnp.float32)


def update_group(
    site_blocks,
    padded_site,
    in_ops,
    in_env,
    term_shift,
    keep_weight,
    env_weight,
    first_row,
    group_size,
):
    states = site_blocks.shape[0]
    ops_window = lax.dynamic_slice_in_dim(in_ops, first_row, group_size + 2, 1)
    env_window = take_window(in_env, first_row, group_size + 2)

    def images_of(ops_one, term_move):
        image_list = []
        for state in range(states):
            right_blocks = take_window(
                padded_site[state], first_row + term_move + state + 2, group_size + 2
            )
            image_list.append(
                jnp.einsum(
                    "lij,ljm->lim", ops_one, right_blocks, preferred_element_type=jnp.float32
                ).astype(jnp.bfloat16)
            )
        return jnp.stack(image_list)

    images = jax.vmap(images_of)(ops_window, term_shift)
    terms_here = ops_window.shape[0]
    block_size = site_blocks.shape[-1]
    next_ops = jnp.zeros((terms_here, group_size, block_size, block_size), jnp.float32)
    next_env = jnp.zeros((group_size, block_size, block_size), jnp.float32)
    for state in range(states):
        own_blocks = take_window(site_blocks[state], first_row, group_size)
        half_env = jnp.einsum(
            "rij,rjm->rim",
            env_window[2 - state : 2 - state + group_size],
            own_blocks,
            preferred_element_type=jnp.float32,
        ).astype(jnp.bfloat16)
        next_env = next_env + left_product(own_blocks, half_env)
        own_terms = jax.vmap(
            lambda image_one: left_product(
                own_blocks, image_one[state, 2 - state : 2 - state + group_size]
            )
        )(images)
        next_ops = next_ops + keep_weight[:, state][:, None, None, None] * own_terms
        partner = state - term_shift
        usable = (partner >= 0) & (partner <= 2)
        picked = jax.vmap(
            lambda image_one, partner_one: lax.dynamic_index_in_dim(
                image_one, partner_one, 0, keepdims=False
            )
        )(images, jnp.clip(partner, 0, 2))
        cross_terms = jax.vmap(
            lambda image_one: left_product(
                own_blocks, image_one[2 - state : 2 - state + group_size]
            )
        )(picked)
        factors = jnp.where(usable, env_weight[:, state], 0.0)
        next_env = next_env + jnp.sum(factors[:, None, None, None] * cross_terms, axis=0)
    return (next_ops.astype(jnp.bfloat16), next_env.astype(jnp.bfloat16))


def body(site_tensor, term_ops, env_rows, term_shift, keep_weight, env_weight):
    site_flat = site_tensor[0]
    block_size = site_flat.shape[-1]
    sectors = site_flat.shape[1] // block_size
    states = site_flat.shape[0]
    site_blocks = site_flat.reshape(states, sectors, block_size, block_size)
    padded_site = jnp.pad(site_blocks, ((0, 0), (4, 4), (0, 0), (0, 0)))
    terms_here = term_ops.shape[0]
    sector_ids = jnp.arange(sectors, dtype=jnp.int32)
    target = sector_ids[None, :] + term_shift[:, None]
    inside = (target >= 0) & (target < sectors)
    start_ops = jnp.where(
        inside[:, :, None, None],
        term_ops.reshape(terms_here, sectors, block_size, block_size),
        jnp.zeros((), jnp.bfloat16),
    )
    in_ops = jnp.pad(start_ops, ((0, 0), (2, 0), (0, 0), (0, 0)))
    rows_here = env_rows.shape[0]
    start_env = lax.dynamic_update_slice_in_dim(
        jnp.zeros((sectors * block_size, block_size), jnp.bfloat16),
        env_rows,
        lax.axis_index("op") * rows_here,
        0,
    )
    in_env = jnp.pad(start_env.reshape(sectors, block_size, block_size), ((2, 0), (0, 0), (0, 0)))
    group_size = 4
    group_count = sectors // group_size
    position = lax.axis_index("seg")
    step_count = lax.axis_size("seg") + group_count - 1
    out_env = jnp.zeros((sectors, block_size, block_size), jnp.bfloat16)

    def advance(step_index, ops_now, env_now, out_now):
        turn_index = step_index - position
        active = (turn_index >= 0) & (turn_index < group_count)
        first_row = jnp.clip(turn_index, 0, group_count - 1) * group_size

        def compute_group(first_one):
            return update_group(
                site_blocks,
                padded_site,
                ops_now,
                env_now,
                term_shift,
                keep_weight,
                env_weight,
                first_one,
                group_size,
            )

        def skip_group(first_one):
            return (
                jnp.zeros((terms_here, group_size, block_size, block_size), jnp.bfloat16),
                jnp.zeros((group_size, block_size, block_size), jnp.bfloat16),
            )

        new_ops, new_env = lax.cond(active, compute_group, skip_group, first_row)
        old_piece = take_window(out_now, first_row, group_size)
        out_now = lax.dynamic_update_slice_in_dim(
            out_now, jnp.where(active, new_env, old_piece), first_row, 0
        )
        return (new_ops, new_env, out_now)

    def loop_body(step_index, state_now):
        ops_now, env_now, out_now = state_now
        new_ops, new_env, out_now = advance(step_index, ops_now, env_now, out_now)
        got_ops, got_env = passed_along((new_ops, new_env), "seg", 1)
        turn_index = step_index + 1 - position
        usable = (turn_index >= 0) & (turn_index < group_count) & (position > 0)
        spot = jnp.clip(turn_index, 0, group_count - 1) * group_size + 2
        old_ops = lax.dynamic_slice_in_dim(ops_now, spot, group_size, 1)
        old_env = take_window(env_now, spot, group_size)
        ops_now = lax.dynamic_update_slice_in_dim(
            ops_now, jnp.where(usable, got_ops, old_ops), spot, 1
        )
        env_now = lax.dynamic_update_slice_in_dim(
            env_now, jnp.where(usable, got_env, old_env), spot, 0
        )
        return (ops_now, env_now, out_now)

    ops_last, env_last, out_env = lax.fori_loop(
        0, step_count - 1, loop_body, (in_ops, in_env, out_env)
    )
    unused_ops, unused_env, out_env = advance(step_count - 1, ops_last, env_last, out_env)
    summed = lax.psum_scatter(
        out_env.reshape(sectors * block_size, block_size).astype(jnp.float32),
        "op",
        scatter_dimension=0,
        tiled=True,
    )
    return summed.astype(jnp.bfloat16)[None]


def solution(mesh):
    placed = (
        P("seg", None, None, None),
        P("op", None, None),
        P("op", None),
        P("op"),
        P("op", None),
        P("op", None),
    )
    return jax.shard_map(
        body, mesh=mesh, in_specs=placed, out_specs=P("seg", "op", None), check_vma=False
    )
```

profile of v0, /device:TPU:128, one launch (start us, length us, event | category | flops | bytes accessed | tf_op | source)
XLA Modules:
  0.0 750.4 jit_solution(15990551577566002646)
XLA Ops:
  6.5 3.5 copy.8
  10.1 4.4 pad.20
  19.2 376.4 %while.31 = (s32[]{:T(128)}, bf16[1,34,128,128]{3,2,1,0:T(8,128)(2,1)}, bf16[34,128,128]{2,1,0:T(8,128)(2,1)}, bf16[32,128,128]{2,1,0:T(8,128)(2,1)}, s32[]{:T(1...) while((s32[]{:T(128)}, ...), condition=%wide.region_3.4_spmd, body=%wide.region_0.3_spmd.sunk | while | flops 279085088 | bytes 40830188 | solution.py:165
  22.5 7.4 collective-permute-start
  36.1 2.7 collective-permute-start.1
  38.8 6.5 collective-permute-start
  47.0 20.9 %collective-permute-done.1 = bf16[4,128,128]{2,1,0:T(8,128)(2,1)S(1)} collective-permute-done((bf16[4,128,128]{2,1,0:T(8,128)(2,1)}, bf16[4,128,128]{2,1,0:T(8,128)(2,1)S(1)}, u32[]{:S(2)}, u32[]{:S(2)}) %collective-permute-start.1) | collective-permute-done | bytes 131104 | tf_op jit(solution)/shard_map/while/body/eval_jaxpr/ppermute | solution.py:10
  71.4 17.0 %conditional.4 = (bf16[1,4,128,128]{3,2,1,0:T(8,128)(2,1)}, bf16[4,128,128]{2,1,0:T(8,128)(2,1)}) conditional(s32[]{:T(128)} %convert_element_type.118, () %tuple.138, (f32[1,3]{1,0:T(1,128)S(1)}, bf16[3,32,128,128]{2,3,1,0:T(8,128)(2,1)S(1)}, s32[]{:T(128)}, bf16[1,34,128,128]{3,2,1,0:T(8,128)(2,1)}, bf16[3,40,128,128]{3,2,1,0:T(8,128)(2,1)}, ...), branch_computations={%region_1.1_spmd, %region_2.2_spmd} | conditional | flops 278888448 | bytes 38601412 | solution.py:141
  72.0 2.7 fusion.120
  99.3 17.0 %conditional.4 = (bf16[1,4,128,128]{3,2,1,0:T(8,128)(2,1)}, bf16[4,128,128]{2,1,0:T(8,128)(2,1)}) conditional(s32[]{:T(128)} %convert_element_type.118, () %tuple.138, (f32[1,3]{1,0:T(1,128)S(1)}, bf16[3,32,128,128]{2,3,1,0:T(8,128)(2,1)S(1)}, s32[]{:T(128)}, bf16[1,34,128,128]{3,2,1,0:T(8,128)(2,1)}, bf16[3,40,128,128]{3,2,1,0:T(8,128)(2,1)}, ...), branch_computations={%region_1.1_spmd, %region_2.2_spmd} | conditional | flops 278888448 | bytes 38601412 | solution.py:141
  100.0 2.7 fusion.120
  127.3 17.0 %conditional.4 = (bf16[1,4,128,128]{3,2,1,0:T(8,128)(2,1)}, bf16[4,128,128]{2,1,0:T(8,128)(2,1)}) conditional(s32[]{:T(128)} %convert_element_type.118, () %tuple.138, (f32[1,3]{1,0:T(1,128)S(1)}, bf16[3,32,128,128]{2,3,1,0:T(8,128)(2,1)S(1)}, s32[]{:T(128)}, bf16[1,34,128,128]{3,2,1,0:T(8,128)(2,1)}, bf16[3,40,128,128]{3,2,1,0:T(8,128)(2,1)}, ...), branch_computations={%region_1.1_spmd, %region_2.2_spmd} | conditional | flops 278888448 | bytes 38601412 | solution.py:141
  127.9 2.7 fusion.120
  155.2 17.0 %conditional.4 = (bf16[1,4,128,128]{3,2,1,0:T(8,128)(2,1)}, bf16[4,128,128]{2,1,0:T(8,128)(2,1)}) conditional(s32[]{:T(128)} %convert_element_type.118, () %tuple.138, (f32[1,3]{1,0:T(1,128)S(1)}, bf16[3,32,128,128]{2,3,1,0:T(8,128)(2,1)S(1)}, s32[]{:T(128)}, bf16[1,34,128,128]{3,2,1,0:T(8,128)(2,1)}, bf16[3,40,128,128]{3,2,1,0:T(8,128)(2,1)}, ...), branch_computations={%region_1.1_spmd, %region_2.2_spmd} | conditional | flops 278888448 | bytes 38601412 | solution.py:141
  174.2 4.1 collective-permute-start
  183.2 17.0 %conditional.4 = (bf16[1,4,128,128]{3,2,1,0:T(8,128)(2,1)}, bf16[4,128,128]{2,1,0:T(8,128)(2,1)}) conditional(s32[]{:T(128)} %convert_element_type.118, () %tuple.138, (f32[1,3]{1,0:T(1,128)S(1)}, bf16[3,32,128,128]{2,3,1,0:T(8,128)(2,1)S(1)}, s32[]{:T(128)}, bf16[1,34,128,128]{3,2,1,0:T(8,128)(2,1)}, bf16[3,40,128,128]{3,2,1,0:T(8,128)(2,1)}, ...), branch_computations={%region_1.1_spmd, %region_2.2_spmd} | conditional | flops 278888448 | bytes 38601412 | solution.py:141
  183.9 2.7 fusion.120
  202.2 5.3 collective-permute-start
  212.4 17.0 %conditional.4 = (bf16[1,4,128,128]{3,2,1,0:T(8,128)(2,1)}, bf16[4,128,128]{2,1,0:T(8,128)(2,1)}) conditional(s32[]{:T(128)} %convert_element_type.118, () %tuple.138, (f32[1,3]{1,0:T(1,128)S(1)}, bf16[3,32,128,128]{2,3,1,0:T(8,128)(2,1)S(1)}, s32[]{:T(128)}, bf16[1,34,128,128]{3,2,1,0:T(8,128)(2,1)}, bf16[3,40,128,128]{3,2,1,0:T(8,128)(2,1)}, ...), branch_computations={%region_1.1_spmd, %region_2.2_spmd} | conditional | flops 278888448 | bytes 38601412 | solution.py:141
  231.4 5.3 collective-permute-start
  241.6 17.0 %conditional.4 = (bf16[1,4,128,128]{3,2,1,0:T(8,128)(2,1)}, bf16[4,128,128]{2,1,0:T(8,128)(2,1)}) conditional(s32[]{:T(128)} %convert_element_type.118, () %tuple.138, (f32[1,3]{1,0:T(1,128)S(1)}, bf16[3,32,128,128]{2,3,1,0:T(8,128)(2,1)S(1)}, s32[]{:T(128)}, bf16[1,34,128,128]{3,2,1,0:T(8,128)(2,1)}, bf16[3,40,128,128]{3,2,1,0:T(8,128)(2,1)}, ...), branch_computations={%region_1.1_spmd, %region_2.2_spmd} | conditional | flops 278888448 | bytes 38601412 | solution.py:141
  260.5 5.3 collective-permute-start
  270.7 17.0 %conditional.4 = (bf16[1,4,128,128]{3,2,1,0:T(8,128)(2,1)}, bf16[4,128,128]{2,1,0:T(8,128)(2,1)}) conditional(s32[]{:T(128)} %convert_element_type.118, () %tuple.138, (f32[1,3]{1,0:T(1,128)S(1)}, bf16[3,32,128,128]{2,3,1,0:T(8,128)(2,1)S(1)}, s32[]{:T(128)}, bf16[1,34,128,128]{3,2,1,0:T(8,128)(2,1)}, bf16[3,40,128,128]{3,2,1,0:T(8,128)(2,1)}, ...), branch_computations={%region_1.1_spmd, %region_2.2_spmd} | conditional | flops 278888448 | bytes 38601412 | solution.py:141
  271.4 2.7 fusion.120
  289.7 5.3 collective-permute-start
  301.2 17.6 %collective-permute-start.1 = (bf16[4,128,128]{2,1,0:T(8,128)(2,1)}, bf16[4,128,128]{2,1,0:T(8,128)(2,1)S(1)}, u32[]{:S(2)}, u32[]{:S(2)}) collective-permute-start(bf16[4,128,128]{2,1,0:T(8,128)(2,1)} %get-tuple-element.582), channel_id=1, source_target_pairs={{0,64},{64,128},{128,192},{192,256},{256,320},{320,384},{384,448},... | collective-permute-start | bytes 393224 | tf_op jit(solution)/shard_map/while/body/eval_jaxpr/ppermute | solution.py:10
  318.8 5.3 collective-permute-start
  332.3 21.0 %collective-permute-start = (bf16[1,4,128,128]{3,2,1,0:T(8,128)(2,1)}, bf16[1,4,128,128]{3,2,1,0:T(8,128)(2,1)S(1)}, u32[]{:S(2)}, u32[]{:S(2)}) collective-permute-start(bf16[1,4,128,128]{3,2,1,0:T(8,128)(2,1)} %get-tuple-element.581), channel_id=1, source_target_pairs={{0,64},{64,128},{128,192},{192,256},{256,320},{320,384},{384,448},... | collective-permute-start | bytes 393224 | tf_op jit(solution)/shard_map/while/body/eval_jaxpr/ppermute | solution.py:10
  361.4 5.3 collective-permute-start
  372.9 12.5 %collective-permute-start.1 = (bf16[4,128,128]{2,1,0:T(8,128)(2,1)}, bf16[4,128,128]{2,1,0:T(8,128)(2,1)S(1)}, u32[]{:S(2)}, u32[]{:S(2)}) collective-permute-start(bf16[4,128,128]{2,1,0:T(8,128)(2,1)} %get-tuple-element.582), channel_id=1, source_target_pairs={{0,64},{64,128},{128,192},{192,256},{256,320},{320,384},{384,448},... | collective-permute-start | bytes 393224 | tf_op jit(solution)/shard_map/while/body/eval_jaxpr/ppermute | solution.py:10
  385.4 5.3 collective-permute-start
  400.0 342.3 %reduce-scatter.2.cloned.1.call-done = f32[64,128]{1,0:T(8,128)} async-done(((f32[4096,128]{1,0:T(8,128)}), f32[64,128]{1,0:T(8,128)}) %reduce-scatter.2.cloned.1.call-update) | async-done | bytes 32784 | tf_op jit(solution)/shard_map/reduce_scatter | solution.py:169
  (342 shorter events, 213.1 us)
Async XLA Ops:
  6.5 735.7 %reduce-scatter.2.cloned.1.call-start = ((), (), s32[]{:S(2)}) async-start(), calls=%async_computation.1 | async-start | bytes 2129920 | tf_op jit(solution)/shard_map/reduce_scatter | solution.py:169
  10.0 4.6 copy-start.11
  20.6 11.0 %collective-permute-start.1 = (bf16[4,128,128]{2,1,0:T(8,128)(2,1)}, bf16[4,128,128]{2,1,0:T(8,128)(2,1)S(1)}, u32[]{:S(2)}, u32[]{:S(2)}) collective-permute-start(bf16[4,128,128]{2,1,0:T(8,128)(2,1)} %get-tuple-element.582), channel_id=1, source_target_pairs={{0,64},{64,128},{128,192},{192,256},{256,320},{320,384},{384,448},... | collective-permute-start | bytes 393224 | tf_op jit(solution)/shard_map/while/body/eval_jaxpr/ppermute | solution.py:10
  22.5 10.7 %collective-permute-start = (bf16[1,4,128,128]{3,2,1,0:T(8,128)(2,1)}, bf16[1,4,128,128]{3,2,1,0:T(8,128)(2,1)S(1)}, u32[]{:S(2)}, u32[]{:S(2)}) collective-permute-start(bf16[1,4,128,128]{3,2,1,0:T(8,128)(2,1)} %get-tuple-element.581), channel_id=1, source_target_pairs={{0,64},{64,128},{128,192},{192,256},{256,320},{320,384},{384,448},... | collective-permute-start | bytes 393224 | tf_op jit(solution)/shard_map/while/body/eval_jaxpr/ppermute | solution.py:10
  36.1 31.8 %collective-permute-start.1 = (bf16[4,128,128]{2,1,0:T(8,128)(2,1)}, bf16[4,128,128]{2,1,0:T(8,128)(2,1)S(1)}, u32[]{:S(2)}, u32[]{:S(2)}) collective-permute-start(bf16[4,128,128]{2,1,0:T(8,128)(2,1)} %get-tuple-element.582), channel_id=1, source_target_pairs={{0,64},{64,128},{128,192},{192,256},{256,320},{320,384},{384,448},... | collective-permute-start | bytes 393224 | tf_op jit(solution)/shard_map/while/body/eval_jaxpr/ppermute | solution.py:10
  38.8 30.9 %collective-permute-start = (bf16[1,4,128,128]{3,2,1,0:T(8,128)(2,1)}, bf16[1,4,128,128]{3,2,1,0:T(8,128)(2,1)S(1)}, u32[]{:S(2)}, u32[]{:S(2)}) collective-permute-start(bf16[1,4,128,128]{3,2,1,0:T(8,128)(2,1)} %get-tuple-element.581), channel_id=1, source_target_pairs={{0,64},{64,128},{128,192},{192,256},{256,320},{320,384},{384,448},... | collective-permute-start | bytes 393224 | tf_op jit(solution)/shard_map/while/body/eval_jaxpr/ppermute | solution.py:10
  88.4 7.4 collective-permute-start.1
  90.3 7.4 collective-permute-start
  107.0 3.0 copy-start.6
  116.4 7.4 collective-permute-start.1
  118.3 7.4 collective-permute-start
  135.0 3.0 copy-start.6
  144.3 7.4 collective-permute-start.1
  146.2 7.4 collective-permute-start
  172.3 7.8 %collective-permute-start.1 = (bf16[4,128,128]{2,1,0:T(8,128)(2,1)}, bf16[4,128,128]{2,1,0:T(8,128)(2,1)S(1)}, u32[]{:S(2)}, u32[]{:S(2)}) collective-permute-start(bf16[4,128,128]{2,1,0:T(8,128)(2,1)} %get-tuple-element.582), channel_id=1, source_target_pairs={{0,64},{64,128},{128,192},{192,256},{256,320},{320,384},{384,448},... | collective-permute-start | bytes 393224 | tf_op jit(solution)/shard_map/while/body/eval_jaxpr/ppermute | solution.py:10
  174.2 7.4 collective-permute-start
  200.3 8.9 %collective-permute-start.1 = (bf16[4,128,128]{2,1,0:T(8,128)(2,1)}, bf16[4,128,128]{2,1,0:T(8,128)(2,1)S(1)}, u32[]{:S(2)}, u32[]{:S(2)}) collective-permute-start(bf16[4,128,128]{2,1,0:T(8,128)(2,1)} %get-tuple-element.582), channel_id=1, source_target_pairs={{0,64},{64,128},{128,192},{192,256},{256,320},{320,384},{384,448},... | collective-permute-start | bytes 393224 | tf_op jit(solution)/shard_map/while/body/eval_jaxpr/ppermute | solution.py:10
  202.2 8.6 %collective-permute-start = (bf16[1,4,128,128]{3,2,1,0:T(8,128)(2,1)}, bf16[1,4,128,128]{3,2,1,0:T(8,128)(2,1)S(1)}, u32[]{:S(2)}, u32[]{:S(2)}) collective-permute-start(bf16[1,4,128,128]{3,2,1,0:T(8,128)(2,1)} %get-tuple-element.581), channel_id=1, source_target_pairs={{0,64},{64,128},{128,192},{192,256},{256,320},{320,384},{384,448},... | collective-permute-start | bytes 393224 | tf_op jit(solution)/shard_map/while/body/eval_jaxpr/ppermute | solution.py:10
  229.5 8.9 %collective-permute-start.1 = (bf16[4,128,128]{2,1,0:T(8,128)(2,1)}, bf16[4,128,128]{2,1,0:T(8,128)(2,1)S(1)}, u32[]{:S(2)}, u32[]{:S(2)}) collective-permute-start(bf16[4,128,128]{2,1,0:T(8,128)(2,1)} %get-tuple-element.582), channel_id=1, source_target_pairs={{0,64},{64,128},{128,192},{192,256},{256,320},{320,384},{384,448},... | collective-permute-start | bytes 393224 | tf_op jit(solution)/shard_map/while/body/eval_jaxpr/ppermute | solution.py:10
  231.4 8.6 %collective-permute-start = (bf16[1,4,128,128]{3,2,1,0:T(8,128)(2,1)}, bf16[1,4,128,128]{3,2,1,0:T(8,128)(2,1)S(1)}, u32[]{:S(2)}, u32[]{:S(2)}) collective-permute-start(bf16[1,4,128,128]{3,2,1,0:T(8,128)(2,1)} %get-tuple-element.581), channel_id=1, source_target_pairs={{0,64},{64,128},{128,192},{192,256},{256,320},{320,384},{384,448},... | collective-permute-start | bytes 393224 | tf_op jit(solution)/shard_map/while/body/eval_jaxpr/ppermute | solution.py:10
  258.6 8.9 %collective-permute-start.1 = (bf16[4,128,128]{2,1,0:T(8,128)(2,1)}, bf16[4,128,128]{2,1,0:T(8,128)(2,1)S(1)}, u32[]{:S(2)}, u32[]{:S(2)}) collective-permute-start(bf16[4,128,128]{2,1,0:T(8,128)(2,1)} %get-tuple-element.582), channel_id=1, source_target_pairs={{0,64},{64,128},{128,192},{192,256},{256,320},{320,384},{384,448},... | collective-permute-start | bytes 393224 | tf_op jit(solution)/shard_map/while/body/eval_jaxpr/ppermute | solution.py:10
  260.5 8.6 %collective-permute-start = (bf16[1,4,128,128]{3,2,1,0:T(8,128)(2,1)}, bf16[1,4,128,128]{3,2,1,0:T(8,128)(2,1)S(1)}, u32[]{:S(2)}, u32[]{:S(2)}) collective-permute-start(bf16[1,4,128,128]{3,2,1,0:T(8,128)(2,1)} %get-tuple-element.581), channel_id=1, source_target_pairs={{0,64},{64,128},{128,192},{192,256},{256,320},{320,384},{384,448},... | collective-permute-start | bytes 393224 | tf_op jit(solution)/shard_map/while/body/eval_jaxpr/ppermute | solution.py:10
  287.8 8.9 %collective-permute-start.1 = (bf16[4,128,128]{2,1,0:T(8,128)(2,1)}, bf16[4,128,128]{2,1,0:T(8,128)(2,1)S(1)}, u32[]{:S(2)}, u32[]{:S(2)}) collective-permute-start(bf16[4,128,128]{2,1,0:T(8,128)(2,1)} %get-tuple-element.582), channel_id=1, source_target_pairs={{0,64},{64,128},{128,192},{192,256},{256,320},{320,384},{384,448},... | collective-permute-start | bytes 393224 | tf_op jit(solution)/shard_map/while/body/eval_jaxpr/ppermute | solution.py:10
  289.7 8.6 %collective-permute-start = (bf16[1,4,128,128]{3,2,1,0:T(8,128)(2,1)}, bf16[1,4,128,128]{3,2,1,0:T(8,128)(2,1)S(1)}, u32[]{:S(2)}, u32[]{:S(2)}) collective-permute-start(bf16[1,4,128,128]{3,2,1,0:T(8,128)(2,1)} %get-tuple-element.581), channel_id=1, source_target_pairs={{0,64},{64,128},{128,192},{192,256},{256,320},{320,384},{384,448},... | collective-permute-start | bytes 393224 | tf_op jit(solution)/shard_map/while/body/eval_jaxpr/ppermute | solution.py:10
  301.2 24.6 %collective-permute-start.1 = (bf16[4,128,128]{2,1,0:T(8,128)(2,1)}, bf16[4,128,128]{2,1,0:T(8,128)(2,1)S(1)}, u32[]{:S(2)}, u32[]{:S(2)}) collective-permute-start(bf16[4,128,128]{2,1,0:T(8,128)(2,1)} %get-tuple-element.582), channel_id=1, source_target_pairs={{0,64},{64,128},{128,192},{192,256},{256,320},{320,384},{384,448},... | collective-permute-start | bytes 393224 | tf_op jit(solution)/shard_map/while/body/eval_jaxpr/ppermute | solution.py:10
  318.8 8.5 %collective-permute-start = (bf16[1,4,128,128]{3,2,1,0:T(8,128)(2,1)}, bf16[1,4,128,128]{3,2,1,0:T(8,128)(2,1)S(1)}, u32[]{:S(2)}, u32[]{:S(2)}) collective-permute-start(bf16[1,4,128,128]{3,2,1,0:T(8,128)(2,1)} %get-tuple-element.581), channel_id=1, source_target_pairs={{0,64},{64,128},{128,192},{192,256},{256,320},{320,384},{384,448},... | collective-permute-start | bytes 393224 | tf_op jit(solution)/shard_map/while/body/eval_jaxpr/ppermute | solution.py:10
  330.3 24.6 %collective-permute-start.1 = (bf16[4,128,128]{2,1,0:T(8,128)(2,1)}, bf16[4,128,128]{2,1,0:T(8,128)(2,1)S(1)}, u32[]{:S(2)}, u32[]{:S(2)}) collective-permute-start(bf16[4,128,128]{2,1,0:T(8,128)(2,1)} %get-tuple-element.582), channel_id=1, source_target_pairs={{0,64},{64,128},{128,192},{192,256},{256,320},{320,384},{384,448},... | collective-permute-start | bytes 393224 | tf_op jit(solution)/shard_map/while/body/eval_jaxpr/ppermute | solution.py:10
  332.3 24.3 %collective-permute-start = (bf16[1,4,128,128]{3,2,1,0:T(8,128)(2,1)}, bf16[1,4,128,128]{3,2,1,0:T(8,128)(2,1)S(1)}, u32[]{:S(2)}, u32[]{:S(2)}) collective-permute-start(bf16[1,4,128,128]{3,2,1,0:T(8,128)(2,1)} %get-tuple-element.581), channel_id=1, source_target_pairs={{0,64},{64,128},{128,192},{192,256},{256,320},{320,384},{384,448},... | collective-permute-start | bytes 393224 | tf_op jit(solution)/shard_map/while/body/eval_jaxpr/ppermute | solution.py:10
  359.5 8.9 %collective-permute-start.1 = (bf16[4,128,128]{2,1,0:T(8,128)(2,1)}, bf16[4,128,128]{2,1,0:T(8,128)(2,1)S(1)}, u32[]{:S(2)}, u32[]{:S(2)}) collective-permute-start(bf16[4,128,128]{2,1,0:T(8,128)(2,1)} %get-tuple-element.582), channel_id=1, source_target_pairs={{0,64},{64,128},{128,192},{192,256},{256,320},{320,384},{384,448},... | collective-permute-start | bytes 393224 | tf_op jit(solution)/shard_map/while/body/eval_jaxpr/ppermute | solution.py:10
  361.4 8.6 %collective-permute-start = (bf16[1,4,128,128]{3,2,1,0:T(8,128)(2,1)}, bf16[1,4,128,128]{3,2,1,0:T(8,128)(2,1)S(1)}, u32[]{:S(2)}, u32[]{:S(2)}) collective-permute-start(bf16[1,4,128,128]{3,2,1,0:T(8,128)(2,1)} %get-tuple-element.581), channel_id=1, source_target_pairs={{0,64},{64,128},{128,192},{192,256},{256,320},{320,384},{384,448},... | collective-permute-start | bytes 393224 | tf_op jit(solution)/shard_map/while/body/eval_jaxpr/ppermute | solution.py:10
  372.9 19.5 %collective-permute-start.1 = (bf16[4,128,128]{2,1,0:T(8,128)(2,1)}, bf16[4,128,128]{2,1,0:T(8,128)(2,1)S(1)}, u32[]{:S(2)}, u32[]{:S(2)}) collective-permute-start(bf16[4,128,128]{2,1,0:T(8,128)(2,1)} %get-tuple-element.582), channel_id=1, source_target_pairs={{0,64},{64,128},{128,192},{192,256},{256,320},{320,384},{384,448},... | collective-permute-start | bytes 393224 | tf_op jit(solution)/shard_map/while/body/eval_jaxpr/ppermute | solution.py:10
  385.4 8.6 %collective-permute-start = (bf16[1,4,128,128]{3,2,1,0:T(8,128)(2,1)}, bf16[1,4,128,128]{3,2,1,0:T(8,128)(2,1)S(1)}, u32[]{:S(2)}, u32[]{:S(2)}) collective-permute-start(bf16[1,4,128,128]{3,2,1,0:T(8,128)(2,1)} %get-tuple-element.581), channel_id=1, source_target_pairs={{0,64},{64,128},{128,192},{192,256},{256,320},{320,384},{384,448},... | collective-permute-start | bytes 393224 | tf_op jit(solution)/shard_map/while/body/eval_jaxpr/ppermute | solution.py:10
  (33 other events, 71.6 us)
Sparse Core Ops, SparseCore 0:
  400.1 342.0 reduce-scatter.1
where the time goes:
time: 753 us; the launch traced here: 750 us
  waiting for transfers between devices  370 us (49%)
  starting transfers between devices  136 us (18%)
  other arithmetic  80.8 us (11%)
  local copies, waits for them, and re-layouts  63 us (8%)
  matrix products  49 us (7%)
  loops' own time  37.7 us (5%)
  between operations  14.1 us (2%)
    reduce_scatter x1, waiting for transfers between devices, body(): lax.psum_scatter(out_env.reshape(sectors * block_size, block_size).astype...  342 us
    ppermute x28, starting transfers between devices, passed_along(): return lax.ppermute(block, axis, route)  136 us
    dot_general x72, matrix products, left_product(): jnp.einsum('rik,rim->rkm', own_blocks, image_one, preferred_element_type=...  39 us
    another operation x15, loops' own time, advance(): new_ops, new_env = lax.cond(active, compute_group, skip_group, first_row)  36.9 us
    ppermute x28, waiting for transfers between devices, passed_along(): return lax.ppermute(block, axis, route)  27.7 us
    dynamic_update_slice x15, other arithmetic, advance(): lax.dynamic_update_slice_in_dim(out_now, jnp.where(active, new_env, old_p...  24.5 us
    dynamic_update_slice x14, other arithmetic, loop_body(): lax.dynamic_update_slice_in_dim(env_now, jnp.where(usable, got_env, old_e...  22.4 us
    dynamic_update_slice x14, other arithmetic, loop_body(): lax.dynamic_update_slice_in_dim(ops_now, jnp.where(usable, got_ops, old_o...  22.4 us
  transfers between devices with their start and end apart: 29, of which 9 were waited for; matrix products, arithmetic and copies ran while one was open for 6% of the time, Pallas kernels for 0%

commit v1 on v0

v1 whole, which is shorter than its diff:
```python
import functools

import jax
import jax.numpy as jnp
from jax import lax
from jax.experimental import pallas as pl
from jax.experimental.pallas import tpu as pltpu
from jax.sharding import Mesh, PartitionSpec as P

BLOCK = 128
OWN = 4
WINDOW = OWN + 2
STATES = 3
AXES = ("zhi", "core", "x", "zlo", "y")
BF16 = jnp.bfloat16
F32 = jnp.float32


def device_number(zhi, core, x, zlo, y):
    return (((zhi * 2 + core) * 4 + x) * 2 + zlo) * 8 + y


def all_places():
    return [
        (zhi, core, x, zlo, y)
        for zhi in range(4)
        for core in range(2)
        for x in range(4)
        for zlo in range(2)
        for y in range(8)
    ]


def to_slices():
    return [
        (device_number(*place), device_number(place[4] // 2, place[4] % 2, place[2], place[3], place[0] * 2 + place[1]))
        for place in all_places()
    ]


def rows_to_slices(back, halo=False):
    pairs = []
    for zhi, core, x, zlo, y in all_places():
        if not back and (zhi or core):
            continue
        if halo and (y < 4 or 2 * x + zlo == 7):
            continue
        outer = device_number(zhi, core, x, zlo, y)
        inner = device_number(zhi, core, y // 2, y % 2, 2 * x + zlo + (1 if halo else 0))
        pairs.append((inner, outer) if back else (outer, inner))
    return pairs


def site_piece(site_blocks, slice_at, half):
    sectors = site_blocks.shape[1]
    first = OWN * slice_at - 1 + 3 * half
    taken = lax.dynamic_slice_in_dim(site_blocks, jnp.clip(first, 0, sectors - 3), 3, 1)
    zero = jnp.zeros_like(taken[:, :1])
    low = jnp.concatenate([zero, taken[:, :2]], 1)
    high = jnp.concatenate([taken[:, 1:], zero], 1)
    return jnp.where(first < 0, low, jnp.where(first > sectors - 3, high, taken))


def ops_piece(ops_blocks, shift, slice_at):
    sectors = ops_blocks.shape[0]
    first = OWN * slice_at - 2
    taken = lax.dynamic_slice_in_dim(ops_blocks, jnp.maximum(first, 0), WINDOW, 0)
    low = jnp.concatenate([jnp.zeros_like(taken[:2]), taken[:OWN]], 0)
    taken = jnp.where(first < 0, low, taken)
    target = first + jnp.arange(WINDOW, dtype=jnp.int32) + shift
    inside = (target >= 0) & (target < sectors)
    return jnp.where(inside[:, None, None], taken, jnp.zeros((), BF16))


def phase_kernel(sites, steps, n_in, sources, targets, with_ops, *refs):
    whole, part, mine, other = refs[:4]
    ins = refs[4 : 4 + n_in]
    outs = refs[4 + n_in : -2]
    site_at, sems = refs[-2:]
    core = whole[0]
    shift = whole[1]

    def copies(slot, site, source):
        return [
            pltpu.make_async_copy(
                source.at[(site // 2) * 2 + half],
                site_at.at[slot, :, pl.ds(3 * half, 3)],
                sems.at[slot, half],
            )
            for half in range(2)
        ]

    for slot, site in enumerate(sites):
        @pl.when(core == site % 2)
        def _():
            for copy in copies(slot, site, mine):
                copy.start()

        @pl.when(core != site % 2)
        def _():
            for copy in copies(slot, site, other):
                copy.start()

    done_sites = set()
    state = {}

    def get(site, sector):
        if (site, sector) in state:
            return state[site, sector]
        where, index = sources[site, sector]
        return ins[where][index]

    for site, first in steps:
        slot = sites.index(site)
        if site not in done_sites:
            done_sites.add(site)
            for copy in copies(slot, site, mine):
                copy.wait()
        for sector in (first, first + 1):
            total = None
            for s in range(STATES):
                block = get(site, sector - s)
                ops, env = block[:, :BLOCK], block[:, BLOCK:]
                left = site_at[slot, s, sector + 1]
                cross = site_at[slot, jnp.clip(s - shift, 0, 2), sector + 1]
                half_env = jnp.dot(env, left, preferred_element_type=F32)
                if with_ops(site):
                    right = site_at[slot, s, sector + 1 + shift]
                    both = jnp.dot(ops, jnp.concatenate([right, cross], 1), preferred_element_type=F32)
                    image = jnp.concatenate(
                        [part[s] * both[:, :BLOCK], half_env + part[3 + s] * both[:, BLOCK:]], 1
                    )
                else:
                    image = half_env + part[3 + s] * jnp.dot(ops, cross, preferred_element_type=F32)
                product = lax.dot_general(
                    left, image.astype(BF16), (((0,), (0,)), ((), ())), preferred_element_type=F32
                )
                total = product if total is None else total + product
            total = total.astype(BF16)
            state[site + 1, sector] = total
            for which, index in targets[site + 1, sector]:
                outs[which][index] = total


def run_phase(sites, steps, ins, sources, outs, targets, with_ops, whole, part, mine, other):
    blocks = 2 * len(steps) * (15 if with_ops(sites[0]) else 9)
    return pl.pallas_call(
        functools.partial(phase_kernel, sites, steps, len(ins), sources, targets, with_ops),
        out_shape=[jax.ShapeDtypeStruct(shape, BF16) for shape in outs],
        in_specs=[pl.BlockSpec(memory_space=pltpu.SMEM)] * 2
        + [pl.BlockSpec(memory_space=pl.ANY)] * 2
        + [pl.BlockSpec(memory_space=pltpu.VMEM)] * len(ins),
        out_specs=[pl.BlockSpec(memory_space=pltpu.VMEM)] * len(outs),
        scratch_shapes=[
            pltpu.VMEM((len(sites), STATES, WINDOW, BLOCK, BLOCK), BF16),
            pltpu.SemaphoreType.DMA((len(sites), 2)),
        ],
        compiler_params=pltpu.CompilerParams(vmem_limit_bytes=32 * 1024 * 1024),
        cost_estimate=pl.CostEstimate(flops=blocks * 2 * BLOCK**3, bytes_accessed=4 << 20, transcendentals=0),
    )(whole, part, mine, other, *ins)


def body(site_tensor, term_ops, env_rows, term_shift, keep_weight, env_weight):
    sectors = site_tensor.shape[2] // BLOCK
    core = lax.axis_index("core")
    seg = lax.axis_index("zhi") * 2 + core
    at_x, at_zlo, at_y = (lax.axis_index(name) for name in ("x", "zlo", "y"))

    site_blocks = site_tensor[0].reshape(STATES, sectors, BLOCK, BLOCK)
    mine = lax.all_gather(site_piece(site_blocks, at_y, at_zlo), ("zhi", "zlo"))
    other = lax.ppermute(mine, "core", [(0, 1), (1, 0)])

    own_ops = ops_piece(term_ops[0].reshape(sectors, BLOCK, BLOCK), term_shift[0], seg)
    ops_now = lax.ppermute(own_ops, AXES, to_slices())
    figures = jnp.concatenate([keep_weight[0], env_weight[0], term_shift.astype(F32), jnp.zeros((1,), F32)])
    figures = lax.ppermute(figures, AXES, to_slices())
    shift = figures[6].astype(jnp.int32)
    partner = jnp.arange(STATES, dtype=jnp.int32) - shift
    factors = jnp.where((partner >= 0) & (partner <= 2), figures[3:6], 0.0)
    part = jnp.concatenate([figures[:3], factors])
    whole = jnp.stack([core.astype(jnp.int32), shift])

    piece = lax.ppermute(env_rows, AXES, rows_to_slices(False))
    halo = lax.ppermute(env_rows, AXES, rows_to_slices(False, True))
    env_now = jnp.zeros((WINDOW * BLOCK, BLOCK), BF16)
    spot = at_x * BLOCK + at_zlo * (BLOCK // 2)
    env_now = lax.dynamic_update_slice_in_dim(env_now, halo, jnp.maximum(spot - 2 * BLOCK, 0), 0)
    env_now = lax.dynamic_update_slice_in_dim(env_now, piece, spot + 2 * BLOCK, 0)
    window = jnp.concatenate([ops_now, env_now.reshape(WINDOW, BLOCK, BLOCK)], 2)

    wide = (BLOCK, 2 * BLOCK)
    onward = [(i, i + 1) for i in range(7)]

    def always(site):
        return True

    def before_last(site):
        return site < 7

    targets = {}
    for sector in range(OWN):
        targets[1, sector] = [(0, sector)] + ([(2, (0, sector - 2))] if sector >= 2 else [])
    for sector in (2, 3):
        targets[2, sector] = [(1, sector - 2), (2, (1, sector - 2))]
    sources = {(0, sector): (0, sector + 2) for sector in range(-2, OWN)}
    full, upper, tails = run_phase(
        [0, 1],
        [(0, 2), (0, 0), (1, 2)],
        [window],
        sources,
        [(OWN,) + wide, (2,) + wide, (2, 2) + wide],
        targets,
        always,
        whole,
        part,
        mine,
        other,
    )
    bonds = [full[:, :, BLOCK:]]
    for site in (1, 3, 5):
        tails = lax.ppermute(tails, "y", onward)
        last = site == 5
        sources = {}
        for sector in (-2, -1):
            sources[site, sector] = (2, (0, sector + 2))
            sources[site + 1, sector] = (2, (1, sector + 2))
        for sector in range(OWN):
            sources[site, sector] = (0, sector)
        for sector in (2, 3):
            sources[site + 1, sector] = (1, sector - 2)
        targets = {}
        for sector in (0, 1):
            targets[site + 1, sector] = [(0, sector)]
        for sector in range(OWN):
            targets[site + 2, sector] = [(1, sector)] + ([(3, (0, sector - 2))] if sector >= 2 else [])
        for sector in (2, 3):
            targets[site + 3, sector] = [(2, sector - 2)] + ([] if last else [(3, (1, sector - 2))])
        old_upper = upper
        narrow = (BLOCK, BLOCK)
        lower, full, upper, tails = run_phase(
            [site, site + 1, site + 2],
            [(site, 0), (site + 1, 2), (site + 1, 0), (site + 2, 2)],
            [full, upper, tails],
            sources,
            [(2,) + wide, (OWN,) + wide, (2,) + (narrow if last else wide), (1 if last else 2, 2) + wide],
            targets,
            before_last,
            whole,
            part,
            mine,
            other,
        )
        bonds += [lower[:, :, BLOCK:], old_upper[:, :, BLOCK:], full[:, :, BLOCK:]]
    tails = lax.ppermute(tails, "y", onward)
    sources = {(7, sector): (1, (0, sector + 2)) for sector in (-2, -1)}
    sources.update({(7, sector): (0, sector) for sector in range(2)})
    (lower,) = run_phase(
        [7],
        [(7, 0)],
        [full, tails],
        sources,
        [(2, BLOCK, BLOCK)],
        {(8, sector): [(0, sector)] for sector in (0, 1)},
        before_last,
        whole,
        part,
        mine,
        other,
    )
    bonds += [lower, upper]

    partial = jnp.concatenate(bonds, 0).reshape(4, 2, 8, BLOCK // 2, BLOCK).transpose(1, 0, 2, 3, 4)
    over = lax.all_to_all(partial, "core", 0, 0)
    summed = over.astype(F32).sum(0).astype(BF16)
    summed = summed.transpose(1, 0, 2, 3)
    over = lax.all_to_all(summed, ("x", "zlo"), 0, 0)
    summed = over.astype(F32).sum(0).astype(BF16)
    over = lax.all_to_all(summed, "zhi", 0, 0)
    summed = over.astype(F32).sum(0).astype(BF16)
    return lax.ppermute(summed, AXES, rows_to_slices(True))[None]


def solution(mesh):
    parts = Mesh(mesh.devices.reshape(4, 2, 4, 2, 8), AXES)
    seg, op = ("zhi", "core"), ("x", "zlo", "y")
    placed = (P(seg, None, None, None), P(op, None, None), P(op, None), P(op), P(op, None), P(op, None))
    return jax.shard_map(body, mesh=parts, in_specs=placed, out_specs=P(seg, op, None), check_vma=False)
```

time: 753 us -> 202 us (0.27)
  the two profiles are of different devices: /device:TPU:128 before, /device:TPU:12 now
where the time goes in v1:
time: 202 us; the launch traced here: 201 us
  waiting for transfers between devices  82.1 us (41%)
  starting transfers between devices  41.1 us (20%)
  blocking collectives  39.8 us (20%)
  between operations  15 us (7%)
  Pallas kernels  13.8 us (7%)
  local copies, waits for them, and re-layouts  5.4 us (3%)
  other arithmetic  4.11 us (2%)
    all_gather x1, waiting for transfers between devices, body(): mine = lax.all_gather(site_piece(site_blocks, at_y, at_zlo), ('zhi', 'zlo'))  49.8 us
    all_to_all x1, blocking collectives, body(): over = lax.all_to_all(summed, 'zhi', 0, 0)  22.6 us
    ppermute x4, waiting for transfers between devices, body(): tails = lax.ppermute(tails, 'y', onward)  21.3 us
    ppermute x4, starting transfers between devices, body(): tails = lax.ppermute(tails, 'y', onward)  20.5 us
    pallas_call x5, Pallas kernels, run_phase(): pl.pallas_call(functools.partial(phase_kernel, sites, steps, len(ins), so...  13.8 us
    all_to_all x1, blocking collectives, body(): over = lax.all_to_all(summed, ('x', 'zlo'), 0, 0)  12.6 us
    ppermute x1, waiting for transfers between devices, body(): return lax.ppermute(summed, AXES, rows_to_slices(True))[None]  7.06 us
    ppermute x1, starting transfers between devices, body(): piece = lax.ppermute(env_rows, AXES, rows_to_slices(False))  6.74 us
  transfers between devices with their start and end apart: 11, of which 8 were waited for; matrix products, arithmetic and copies ran while one was open for 2% of the time, Pallas kernels for 0%

profile of v1, /device:TPU:12, one launch (start us, length us, event | category | flops | bytes accessed | tf_op | source)
XLA Modules:
  0.0 201.2 jit_solution(2752246103194455308)
XLA Ops:
  6.5 1.0 constant_dynamic-slice_fusion.2
  7.6 1.7 select_select_fusion
  9.3 49.8 %all-gather.3.cloned.1.call-done = bf16[24,3,128,128]{3,2,1,0:T(8,128)(2,1)} async-done(((bf16[3,3,128,128]{3,2,1,0:T(8,128)(2,1)}), bf16[24,3,128,128]{3,2,1,0:T(8,128)(2,1)}) %all-gather.3.cloned.1.call-update) | async-done | bytes 2359312 | tf_op jit(solution)/shard_map/all_gather | solution.py:170
  59.1 1.9 collective-permute-start.1
  61.0 6.7 %collective-permute-start.4 = (bf16[64,128]{1,0:T(8,128)(2,1)}, bf16[64,128]{1,0:T(8,128)(2,1)S(1)}, u32[]{:S(2)}, u32[]{:S(2)}) collective-permute-start(bf16[64,128]{1,0:T(8,128)(2,1)} %param.8), channel_id=1, source_target_pairs={{0,0},{1,8},{2,16},{3,24},{4,32},{5,40},{6,48},{7,56},{8,1},{9,9},... | collective-permute-start | bytes 49160 | tf_op jit(solution)/shard_map/ppermute | solution.py:183
  67.8 1.3 collective-permute-start.3
  69.7 0.8 pad_maximum_fusion.1
  70.5 1.9 collective-permute-start
  72.4 0.9 constant_dynamic-slice_fusion
  73.3 1.0 select_select_fusion.1
  74.4 3.6 %collective-permute-start.2 = (bf16[6,128,128]{2,1,0:T(8,128)(2,1)S(1)}, bf16[6,128,128]{2,1,0:T(8,128)(2,1)S(1)}, u32[]{:S(2)}, u32[]{:S(2)}) collective-permute-start(bf16[6,128,128]{2,1,0:T(8,128)(2,1)S(1)} %select_select_fusion.1), channel_id=1, source_target_pairs={{0,0},{1,64},{2,128},{3,192},{4,256},{5,320},{6,384},{7,448},{8,8}... | collective-permute-start | bytes 589832 | tf_op jit(solution)/shard_map/ppermute | solution.py:174
  80.4 3.3 %collective-permute-done.2 = bf16[6,128,128]{2,1,0:T(8,128)(2,1)S(1)} collective-permute-done((bf16[6,128,128]{2,1,0:T(8,128)(2,1)S(1)}, bf16[6,128,128]{2,1,0:T(8,128)(2,1)S(1)}, u32[]{:S(2)}, u32[]{:S(2)}) %collective-permute-start.2) | collective-permute-done | bytes 196640 | tf_op jit(solution)/shard_map/ppermute | solution.py:174
  83.7 1.7 copy-done
  85.4 2.6 %shard_map.64 = (bf16[4,128,256]{2,1,0:T(8,128)(2,1)S(1)}, bf16[2,128,256]{2,1,0:T(8,128)(2,1)S(1)}, bf16[2,2,128,256]{3,2,1,0:T(8,128)(2,1)S(1)}) custom-call(s32[2]{0:T(128)S(1)} %pad_add_fusion.refs_0_, f32[6]{0:T(128)S(1)} %pad_maximum_fusion.2.refs_1_, bf16[8,3,3,128,128]{4,3,2,1,0:T(8,128)(2,1)S(1)} %bitcast.17, ...), custom_call_target="tpu_custom_call" | custom-call | flops 377487360 | bytes 4194304 | tf_op jit(solution)/shard_map/pallas_call | solution.py:147
  88.0 10.7 %collective-permute-start.5 = (bf16[2,2,128,256]{3,2,1,0:T(8,128)(2,1)S(1)}, bf16[2,2,128,256]{3,2,1,0:T(8,128)(2,1)S(1)}, u32[]{:S(2)}, u32[]{:S(2)}) collective-permute-start(bf16[2,2,128,256]{3,2,1,0:T(8,128)(2,1)S(1)} %get-tuple-element.22), channel_id=1, source_target_pairs={{0,1},{1,2},{2,3},{3,4},{4,5},{5,6},{6,7},{8,9},{9,10},{10,11},{11... | collective-permute-start | bytes 786440 | tf_op jit(solution)/shard_map/ppermute | solution.py:221
  98.7 5.7 %collective-permute-done.5.refs_6_ = bf16[2,2,128,256]{3,2,1,0:T(8,128)(2,1)S(1)} collective-permute-done((bf16[2,2,128,256]{3,2,1,0:T(8,128)(2,1)S(1)}, bf16[2,2,128,256]{3,2,1,0:T(8,128)(2,1)S(1)}, u32[]{:S(2)}, u32[]{:S(2)}) %collective-permute-start.5) | collective-permute-done | bytes 262176 | tf_op jit(solution)/shard_map/ppermute | solution.py:221
  104.4 3.4 %shard_map.65 = (bf16[2,128,256]{2,1,0:T(8,128)(2,1)S(1)}, bf16[4,128,256]{2,1,0:T(8,128)(2,1)S(1)}, bf16[2,128,256]{2,1,0:T(8,128)(2,1)S(1)}, bf16[2,2,128,256]{3,2,1,0:T(8,128)(2,1)S(1)}) custom-call(s32[2]{0:T(128)S(1)} %pad_add_fusion.refs_0_, f32[6]{0:T(128)S(1)} %pad_maximum_fusion.2.refs_1_, bf16[8,3,3,128,128]{4,3,2,1,0:T(8,128)(2,1)S(1)} %bitcast.18, ...), custom_call_target="tpu_custom_call" | custom-call | flops 503316480 | bytes 4194304 | tf_op jit(solution)/shard_map/pallas_call | solution.py:147
  107.8 4.4 %collective-permute-start.6 = (bf16[2,2,128,256]{3,2,1,0:T(8,128)(2,1)S(1)}, bf16[2,2,128,256]{3,2,1,0:T(8,128)(2,1)S(1)}, u32[]{:S(2)}, u32[]{:S(2)}) collective-permute-start(bf16[2,2,128,256]{3,2,1,0:T(8,128)(2,1)S(1)} %get-tuple-element.26), channel_id=1, source_target_pairs={{0,1},{1,2},{2,3},{3,4},{4,5},{5,6},{6,7},{8,9},{9,10},{10,11},{11... | collective-permute-start | bytes 786440 | tf_op jit(solution)/shard_map/ppermute | solution.py:221
  112.2 4.8 %collective-permute-done.6.refs_6_ = bf16[2,2,128,256]{3,2,1,0:T(8,128)(2,1)S(1)} collective-permute-done((bf16[2,2,128,256]{3,2,1,0:T(8,128)(2,1)S(1)}, bf16[2,2,128,256]{3,2,1,0:T(8,128)(2,1)S(1)}, u32[]{:S(2)}, u32[]{:S(2)}) %collective-permute-start.6) | collective-permute-done | bytes 262176 | tf_op jit(solution)/shard_map/ppermute | solution.py:221
  117.0 3.4 %shard_map.66 = (bf16[2,128,256]{2,1,0:T(8,128)(2,1)S(1)}, bf16[4,128,256]{2,1,0:T(8,128)(2,1)S(1)}, bf16[2,128,256]{2,1,0:T(8,128)(2,1)S(1)}, bf16[2,2,128,256]{3,2,1,0:T(8,128)(2,1)S(1)}) custom-call(s32[2]{0:T(128)S(1)} %pad_add_fusion.refs_0_, f32[6]{0:T(128)S(1)} %pad_maximum_fusion.2.refs_1_, bf16[8,3,3,128,128]{4,3,2,1,0:T(8,128)(2,1)S(1)} %bitcast.19, ...), custom_call_target="tpu_custom_call" | custom-call | flops 503316480 | bytes 4194304 | tf_op jit(solution)/shard_map/pallas_call | solution.py:147
  120.4 3.4 %collective-permute-start.7 = (bf16[2,2,128,256]{3,2,1,0:T(8,128)(2,1)S(1)}, bf16[2,2,128,256]{3,2,1,0:T(8,128)(2,1)S(1)}, u32[]{:S(2)}, u32[]{:S(2)}) collective-permute-start(bf16[2,2,128,256]{3,2,1,0:T(8,128)(2,1)S(1)} %get-tuple-element.30), channel_id=1, source_target_pairs={{0,1},{1,2},{2,3},{3,4},{4,5},{5,6},{6,7},{8,9},{9,10},{10,11},{11... | collective-permute-start | bytes 786440 | tf_op jit(solution)/shard_map/ppermute | solution.py:221
  123.9 6.2 %collective-permute-done.7.refs_6_ = bf16[2,2,128,256]{3,2,1,0:T(8,128)(2,1)S(1)} collective-permute-done((bf16[2,2,128,256]{3,2,1,0:T(8,128)(2,1)S(1)}, bf16[2,2,128,256]{3,2,1,0:T(8,128)(2,1)S(1)}, u32[]{:S(2)}, u32[]{:S(2)}) %collective-permute-start.7) | collective-permute-done | bytes 262176 | tf_op jit(solution)/shard_map/ppermute | solution.py:221
  130.1 3.2 %shard_map.67 = (bf16[2,128,256]{2,1,0:T(8,128)(2,1)S(1)}, bf16[4,128,256]{2,1,0:T(8,128)(2,1)S(1)}, bf16[2,128,128]{2,1,0:T(8,128)(2,1)S(1)}, bf16[1,2,128,256]{3,2,1,0:T(8,128)(2,1)S(1)}) custom-call(s32[2]{0:T(128)S(1)} %pad_add_fusion.refs_0_, f32[6]{0:T(128)S(1)} %pad_maximum_fusion.2.refs_1_, bf16[8,3,3,128,128]{4,3,2,1,0:T(8,128)(2,1)S(1)} %bitcast.20, ...), custom_call_target="tpu_custom_call" | custom-call | flops 503316480 | bytes 4194304 | tf_op jit(solution)/shard_map/pallas_call | solution.py:147
  133.3 2.0 %collective-permute-start.8 = (bf16[1,2,128,256]{3,2,1,0:T(8,128)(2,1)S(1)}, bf16[1,2,128,256]{3,2,1,0:T(8,128)(2,1)S(1)}, u32[]{:S(2)}, u32[]{:S(2)}) collective-permute-start(bf16[1,2,128,256]{3,2,1,0:T(8,128)(2,1)S(1)} %get-tuple-element.33), channel_id=1, source_target_pairs={{0,1},{1,2},{2,3},{3,4},{4,5},{5,6},{6,7},{8,9},{9,10},{10,11},{11... | collective-permute-start | bytes 393224 | tf_op jit(solution)/shard_map/ppermute | solution.py:254
  135.4 4.8 %collective-permute-done.8.refs_5_ = bf16[1,2,128,256]{3,2,1,0:T(8,128)(2,1)S(1)} collective-permute-done((bf16[1,2,128,256]{3,2,1,0:T(8,128)(2,1)S(1)}, bf16[1,2,128,256]{3,2,1,0:T(8,128)(2,1)S(1)}, u32[]{:S(2)}, u32[]{:S(2)}) %collective-permute-start.8) | collective-permute-done | bytes 131104 | tf_op jit(solution)/shard_map/ppermute | solution.py:254
  140.2 1.2 shard_map.68
  141.5 4.6 %all_to_all.15 = bf16[2,4,8,64,128]{4,3,2,1,0:T(8,128)(2,1)S(1)} all-to-all(bf16[2,4,8,64,128]{4,3,2,1,0:T(8,128)(2,1)S(1)} %bitcast.22), channel_id=1, replica_groups=mesh['zhi'=4,'core'=2,'x'=4,'zlo'=2,'y'=8] {'core'}, dimensions={0} | all-to-all | bytes 2097152 | tf_op jit(solution)/shard_map/all_to_all | solution.py:273
  146.3 12.6 %all_to_all.16 = bf16[8,4,64,128]{3,2,1,0:T(8,128)(2,1)S(1)} all-to-all(bf16[8,4,64,128]{3,2,1,0:T(8,128)(2,1)S(1)} %copy.11), channel_id=1, replica_groups=mesh['zhi'=4,'core'=2,'x'=4,'zlo'=2,'y'=8] {'x','zlo'}, dimensions={0} | all-to-all | bytes 1048576 | tf_op jit(solution)/shard_map/all_to_all | solution.py:276
  159.0 22.6 %all_to_all.17 = bf16[4,64,128]{2,1,0:T(8,128)(2,1)S(1)} all-to-all(bf16[4,64,128]{2,1,0:T(8,128)(2,1)S(1)} %reduce_sum.37), channel_id=1, replica_groups=mesh['zhi'=4,'core'=2,'x'=4,'zlo'=2,'y'=8] {'zhi'}, dimensions={0} | all-to-all | bytes 131072 | tf_op jit(solution)/shard_map/all_to_all | solution.py:278
  181.7 5.0 %collective-permute-start.9 = (bf16[64,128]{1,0:T(8,128)(2,1)S(1)}, bf16[64,128]{1,0:T(8,128)(2,1)S(1)}, u32[]{:S(2)}, u32[]{:S(2)}) collective-permute-start(bf16[64,128]{1,0:T(8,128)(2,1)S(1)} %reduce_sum.38), channel_id=1, source_target_pairs={{0,0},{8,1},{16,2},{24,3},{32,4},{40,5},{48,6},{56,7},{1,8},{9,9},... | collective-permute-start | bytes 49160 | tf_op jit(solution)/shard_map/ppermute | solution.py:280
  186.7 7.1 %collective-permute-done.9 = bf16[64,128]{1,0:T(8,128)(2,1)S(1)} collective-permute-done((bf16[64,128]{1,0:T(8,128)(2,1)S(1)}, bf16[64,128]{1,0:T(8,128)(2,1)S(1)}, u32[]{:S(2)}, u32[]{:S(2)}) %collective-permute-start.9) | collective-permute-done | bytes 16416 | tf_op jit(solution)/shard_map/ppermute | solution.py:280
  193.8 0.6 copy.29
  (33 shorter events, 2.4 us)
Async XLA Ops:
  6.5 52.6 %all-gather.3.cloned.1.call-start = ((), (), s32[]{:S(2)}) async-start(), calls=%async_computation.3 | async-start | bytes 2654208 | tf_op jit(solution)/shard_map/all_gather | solution.py:170
  59.1 24.6 %collective-permute-start.1 = (bf16[8,3,3,128,128]{4,3,2,1,0:T(8,128)(2,1)}, bf16[8,3,3,128,128]{4,3,2,1,0:T(8,128)(2,1)S(1)}, u32[]{:S(2)}, u32[]{:S(2)}) collective-permute-start(bf16[8,3,3,128,128]{4,3,2,1,0:T(8,128)(2,1)} %bitcast.16), channel_id=1, source_target_pairs={{0,64},{64,0},{1,65},{65,1},{2,66},{66,2},{3,67},{67,3},{4,68},{68... | collective-permute-start | bytes 7077896 | tf_op jit(solution)/shard_map/ppermute | solution.py:171
  61.0 19.3 %collective-permute-start.4 = (bf16[64,128]{1,0:T(8,128)(2,1)}, bf16[64,128]{1,0:T(8,128)(2,1)S(1)}, u32[]{:S(2)}, u32[]{:S(2)}) collective-permute-start(bf16[64,128]{1,0:T(8,128)(2,1)} %param.8), channel_id=1, source_target_pairs={{0,0},{1,8},{2,16},{3,24},{4,32},{5,40},{6,48},{7,56},{8,1},{9,9},... | collective-permute-start | bytes 49160 | tf_op jit(solution)/shard_map/ppermute | solution.py:183
  67.8 12.3 %collective-permute-start.3 = (bf16[64,128]{1,0:T(8,128)(2,1)}, bf16[64,128]{1,0:T(8,128)(2,1)S(1)}, u32[]{:S(2)}, u32[]{:S(2)}) collective-permute-start(bf16[64,128]{1,0:T(8,128)(2,1)} %param.8), channel_id=1, source_target_pairs={{4,33},{5,41},{6,49},{7,57},{12,34},{13,42},{14,50},{15,58},{20,35... | collective-permute-start | bytes 49160 | tf_op jit(solution)/shard_map/ppermute | solution.py:184
  70.5 7.6 %collective-permute-start = (f32[8]{0:T(128)S(1)}, f32[8]{0:T(128)S(1)}, u32[]{:S(2)}, u32[]{:S(2)}) collective-permute-start(f32[8]{0:T(128)S(1)} %pad_maximum_fusion.1), channel_id=1, source_target_pairs={{0,0},{1,64},{2,128},{3,192},{4,256},{5,320},{6,384},{7,448},{8,8}... | collective-permute-start | bytes 104 | tf_op jit(solution)/shard_map/ppermute | solution.py:176
  74.4 9.3 %collective-permute-start.2 = (bf16[6,128,128]{2,1,0:T(8,128)(2,1)S(1)}, bf16[6,128,128]{2,1,0:T(8,128)(2,1)S(1)}, u32[]{:S(2)}, u32[]{:S(2)}) collective-permute-start(bf16[6,128,128]{2,1,0:T(8,128)(2,1)S(1)} %select_select_fusion.1), channel_id=1, source_target_pairs={{0,0},{1,64},{2,128},{3,192},{4,256},{5,320},{6,384},{7,448},{8,8}... | collective-permute-start | bytes 589832 | tf_op jit(solution)/shard_map/ppermute | solution.py:174
  83.7 1.7 copy-start
  88.0 16.4 %collective-permute-start.5 = (bf16[2,2,128,256]{3,2,1,0:T(8,128)(2,1)S(1)}, bf16[2,2,128,256]{3,2,1,0:T(8,128)(2,1)S(1)}, u32[]{:S(2)}, u32[]{:S(2)}) collective-permute-start(bf16[2,2,128,256]{3,2,1,0:T(8,128)(2,1)S(1)} %get-tuple-element.22), channel_id=1, source_target_pairs={{0,1},{1,2},{2,3},{3,4},{4,5},{5,6},{6,7},{8,9},{9,10},{10,11},{11... | collective-permute-start | bytes 786440 | tf_op jit(solution)/shard_map/ppermute | solution.py:221
  107.8 9.2 %collective-permute-start.6 = (bf16[2,2,128,256]{3,2,1,0:T(8,128)(2,1)S(1)}, bf16[2,2,128,256]{3,2,1,0:T(8,128)(2,1)S(1)}, u32[]{:S(2)}, u32[]{:S(2)}) collective-permute-start(bf16[2,2,128,256]{3,2,1,0:T(8,128)(2,1)S(1)} %get-tuple-element.26), channel_id=1, source_target_pairs={{0,1},{1,2},{2,3},{3,4},{4,5},{5,6},{6,7},{8,9},{9,10},{10,11},{11... | collective-permute-start | bytes 786440 | tf_op jit(solution)/shard_map/ppermute | solution.py:221
  120.4 9.7 %collective-permute-start.7 = (bf16[2,2,128,256]{3,2,1,0:T(8,128)(2,1)S(1)}, bf16[2,2,128,256]{3,2,1,0:T(8,128)(2,1)S(1)}, u32[]{:S(2)}, u32[]{:S(2)}) collective-permute-start(bf16[2,2,128,256]{3,2,1,0:T(8,128)(2,1)S(1)} %get-tuple-element.30), channel_id=1, source_target_pairs={{0,1},{1,2},{2,3},{3,4},{4,5},{5,6},{6,7},{8,9},{9,10},{10,11},{11... | collective-permute-start | bytes 786440 | tf_op jit(solution)/shard_map/ppermute | solution.py:221
  133.3 6.9 %collective-permute-start.8 = (bf16[1,2,128,256]{3,2,1,0:T(8,128)(2,1)S(1)}, bf16[1,2,128,256]{3,2,1,0:T(8,128)(2,1)S(1)}, u32[]{:S(2)}, u32[]{:S(2)}) collective-permute-start(bf16[1,2,128,256]{3,2,1,0:T(8,128)(2,1)S(1)} %get-tuple-element.33), channel_id=1, source_target_pairs={{0,1},{1,2},{2,3},{3,4},{4,5},{5,6},{6,7},{8,9},{9,10},{10,11},{11... | collective-permute-start | bytes 393224 | tf_op jit(solution)/shard_map/ppermute | solution.py:254
  181.7 12.1 %collective-permute-start.9 = (bf16[64,128]{1,0:T(8,128)(2,1)S(1)}, bf16[64,128]{1,0:T(8,128)(2,1)S(1)}, u32[]{:S(2)}, u32[]{:S(2)}) collective-permute-start(bf16[64,128]{1,0:T(8,128)(2,1)S(1)} %reduce_sum.38), channel_id=1, source_target_pairs={{0,0},{8,1},{16,2},{24,3},{32,4},{40,5},{48,6},{56,7},{1,8},{9,9},... | collective-permute-start | bytes 49160 | tf_op jit(solution)/shard_map/ppermute | solution.py:280
Sparse Core Ops, SparseCore 0:
  9.4 49.6 all-gather.2

commit v2 on v1

--- a/solution.py
+++ b/solution.py
@@ -51,14 +51,8 @@
     return pairs
 
 
-def site_piece(site_blocks, slice_at, half):
-    sectors = site_blocks.shape[1]
-    first = OWN * slice_at - 1 + 3 * half
-    taken = lax.dynamic_slice_in_dim(site_blocks, jnp.clip(first, 0, sectors - 3), 3, 1)
-    zero = jnp.zeros_like(taken[:, :1])
-    low = jnp.concatenate([zero, taken[:, :2]], 1)
-    high = jnp.concatenate([taken[:, 1:], zero], 1)
-    return jnp.where(first < 0, low, jnp.where(first > sectors - 3, high, taken))
+def site_start(sectors, slice_at, half):
+    return jnp.clip(OWN * slice_at - 1 + 3 * half, 0, sectors - 3)
 
 
 def ops_piece(ops_blocks, shift, slice_at):
@@ -84,11 +78,19 @@
         return [
             pltpu.make_async_copy(
                 source.at[(site // 2) * 2 + half],
-                site_at.at[slot, :, pl.ds(3 * half, 3)],
+                site_at.at[slot, :, pl.ds(whole[2 + half], 3)],
                 sems.at[slot, half],
             )
             for half in range(2)
         ]
+
+    @pl.when(whole[2] != 0)
+    def _():
+        site_at[:, :, 0] = jnp.zeros((len(sites), STATES, BLOCK, BLOCK), BF16)
+
+    @pl.when(whole[3] != 3)
+    def _():
+        site_at[:, :, WINDOW - 1] = jnp.zeros((len(sites), STATES, BLOCK, BLOCK), BF16)
 
     for slot, site in enumerate(sites):
         @pl.when(core == site % 2)
@@ -167,8 +169,9 @@
     at_x, at_zlo, at_y = (lax.axis_index(name) for name in ("x", "zlo", "y"))
 
     site_blocks = site_tensor[0].reshape(STATES, sectors, BLOCK, BLOCK)
-    mine = lax.all_gather(site_piece(site_blocks, at_y, at_zlo), ("zhi", "zlo"))
-    other = lax.ppermute(mine, "core", [(0, 1), (1, 0)])
+    piece = lax.dynamic_slice_in_dim(site_blocks, site_start(sectors, at_y, at_zlo), 3, 1)
+    mine = lax.all_gather(piece, ("zhi", "zlo"))
+    spots = [site_start(sectors, at_y, half) - (OWN * at_y - 1) for half in range(2)]
 
     own_ops = ops_piece(term_ops[0].reshape(sectors, BLOCK, BLOCK), term_shift[0], seg)
     ops_now = lax.ppermute(own_ops, AXES, to_slices())
@@ -178,7 +181,7 @@
     partner = jnp.arange(STATES, dtype=jnp.int32) - shift
     factors = jnp.where((partner >= 0) & (partner <= 2), figures[3:6], 0.0)
     part = jnp.concatenate([figures[:3], factors])
-    whole = jnp.stack([core.astype(jnp.int32), shift])
+    whole = jnp.stack([core, shift] + spots).astype(jnp.int32)
 
     piece = lax.ppermute(env_rows, AXES, rows_to_slices(False))
     halo = lax.ppermute(env_rows, AXES, rows_to_slices(False, True))
@@ -187,6 +190,9 @@
     env_now = lax.dynamic_update_slice_in_dim(env_now, halo, jnp.maximum(spot - 2 * BLOCK, 0), 0)
     env_now = lax.dynamic_update_slice_in_dim(env_now, piece, spot + 2 * BLOCK, 0)
     window = jnp.concatenate([ops_now, env_now.reshape(WINDOW, BLOCK, BLOCK)], 2)
+
+    mine, window, whole, part = lax.optimization_barrier((mine, window, whole, part))
+    other = lax.ppermute(mine, "core", [(0, 1), (1, 0)])
 
     wide = (BLOCK, 2 * BLOCK)
     onward = [(i, i + 1) for i in range(7)]
@@ -272,10 +278,8 @@
     partial = jnp.concatenate(bonds, 0).reshape(4, 2, 8, BLOCK // 2, BLOCK).transpose(1, 0, 2, 3, 4)
     over = lax.all_to_all(partial, "core", 0, 0)
     summed = over.astype(F32).sum(0).astype(BF16)
-    summed = summed.transpose(1, 0, 2, 3)
-    over = lax.all_to_all(summed, ("x", "zlo"), 0, 0)
-    summed = over.astype(F32).sum(0).astype(BF16)
-    over = lax.all_to_all(summed, "zhi", 0, 0)
+    summed = summed.reshape(32, BLOCK // 2, BLOCK)
+    over = lax.all_to_all(summed, ("zhi", "x", "zlo"), 0, 0)
     summed = over.astype(F32).sum(0).astype(BF16)
     return lax.ppermute(summed, AXES, rows_to_slices(True))[None]
 

time: 202 us -> 187 us (0.926)
  the two profiles are of different devices: /device:TPU:12 before, /device:TPU:32 now
where the time goes in v2:
time: 187 us; the launch traced here: 186 us
  waiting for transfers between devices  72.2 us (39%)
  starting transfers between devices  40 us (21%)
  blocking collectives  29.9 us (16%)
  between operations  14.9 us (8%)
  Pallas kernels  13.9 us (7%)
  local copies, waits for them, and re-layouts  8.36 us (4%)
  other arithmetic  6.65 us (4%)
    ppermute x4, waiting for transfers between devices, body(): tails = lax.ppermute(tails, 'y', onward)  31.5 us
    all_to_all x1, blocking collectives, body(): over = lax.all_to_all(summed, ('zhi', 'x', 'zlo'), 0, 0)  24.5 us
    all_gather x1, waiting for transfers between devices, body(): mine = lax.all_gather(piece, ('zhi', 'zlo'))  22.5 us
    pallas_call x5, Pallas kernels, run_phase(): pl.pallas_call(functools.partial(phase_kernel, sites, steps, len(ins), so...  13.9 us
    ppermute x1, starting transfers between devices, body(): ops_now = lax.ppermute(own_ops, AXES, to_slices())  12.6 us
    ppermute x1, waiting for transfers between devices, body(): return lax.ppermute(summed, AXES, rows_to_slices(True))[None]  10 us
    ppermute x1, starting transfers between devices, body(): halo = lax.ppermute(env_rows, AXES, rows_to_slices(False, True))  9.18 us
    ppermute x4, starting transfers between devices, body(): tails = lax.ppermute(tails, 'y', onward)  8.02 us
  transfers between devices with their start and end apart: 11, of which 8 were waited for; matrix products, arithmetic and copies ran while one was open for 3% of the time, Pallas kernels for 0%

profile of v2, /device:TPU:32, one launch (start us, length us, event | category | flops | bytes accessed | tf_op | source)
XLA Modules:
  0.0 185.9 jit_solution(11978990787912159413)
XLA Ops:
  6.5 1.9 %copy-done = bf16[1,3,4096,128]{3,2,1,0:T(8,128)(2,1)S(1)} copy-done((bf16[1,3,4096,128]{3,2,1,0:T(8,128)(2,1)S(1)}, bf16[1,3,4096,128]{3,2,1,0:T(8,128)(2,1)}, u32[]{:S(2)}) %copy-start) | copy-done | bytes 3145752
  9.2 4.5 %collective-permute-start.2 = (bf16[64,128]{1,0:T(8,128)(2,1)}, bf16[64,128]{1,0:T(8,128)(2,1)}, u32[]{:S(2)}, u32[]{:S(2)}) collective-permute-start(bf16[64,128]{1,0:T(8,128)(2,1)} %param.8), channel_id=1, source_target_pairs={{0,0},{1,8},{2,16},{3,24},{4,32},{5,40},{6,48},{7,56},{8,1},{9,9},... | collective-permute-start | bytes 49160 | tf_op jit(solution)/shard_map/ppermute | solution.py:186
  13.7 9.2 %collective-permute-start.1 = (bf16[64,128]{1,0:T(8,128)(2,1)}, bf16[64,128]{1,0:T(8,128)(2,1)}, u32[]{:S(2)}, u32[]{:S(2)}) collective-permute-start(bf16[64,128]{1,0:T(8,128)(2,1)} %param.8), channel_id=1, source_target_pairs={{4,33},{5,41},{6,49},{7,57},{12,34},{13,42},{14,50},{15,58},{20,35... | collective-permute-start | bytes 49160 | tf_op jit(solution)/shard_map/ppermute | solution.py:187
  24.3 1.9 %collective-permute-start.3 = (f32[8]{0:T(128)S(1)}, f32[8]{0:T(128)S(1)}, u32[]{:S(2)}, u32[]{:S(2)}) collective-permute-start(f32[8]{0:T(128)S(1)} %pad_maximum_fusion.1), channel_id=1, source_target_pairs={{0,0},{1,64},{2,128},{3,192},{4,256},{5,320},{6,384},{7,448},{8,8}... | collective-permute-start | bytes 104 | tf_op jit(solution)/shard_map/ppermute | solution.py:179
  26.2 0.9 constant_dynamic-slice_fusion
  27.1 1.1 select_select_fusion
  28.2 12.6 %collective-permute-start = (bf16[6,128,128]{2,1,0:T(8,128)(2,1)S(1)}, bf16[6,128,128]{2,1,0:T(8,128)(2,1)}, u32[]{:S(2)}, u32[]{:S(2)}) collective-permute-start(bf16[6,128,128]{2,1,0:T(8,128)(2,1)S(1)} %select_select_fusion), channel_id=1, source_target_pairs={{0,0},{1,64},{2,128},{3,192},{4,256},{5,320},{6,384},{7,448},{8,8}... | collective-permute-start | bytes 589832 | tf_op jit(solution)/shard_map/ppermute | solution.py:177
  43.9 3.5 %collective-permute-done = bf16[6,128,128]{2,1,0:T(8,128)(2,1)} collective-permute-done((bf16[6,128,128]{2,1,0:T(8,128)(2,1)S(1)}, bf16[6,128,128]{2,1,0:T(8,128)(2,1)}, u32[]{:S(2)}, u32[]{:S(2)}) %collective-permute-start) | collective-permute-done | bytes 196640 | tf_op jit(solution)/shard_map/ppermute | solution.py:177
  47.4 1.1 pad_maximum_fusion.refs_4_
  48.4 22.5 %all-gather.3.cloned.1.call-done = bf16[24,3,128,128]{3,2,1,0:T(8,128)(2,1)} async-done(((bf16[3,3,128,128]{3,2,1,0:T(8,128)(2,1)}), bf16[24,3,128,128]{3,2,1,0:T(8,128)(2,1)}) %all-gather.3.cloned.1.call-update) | async-done | bytes 2359312 | tf_op jit(solution)/shard_map/all_gather | solution.py:173
  70.9 1.9 %collective-permute-start.4 = (bf16[8,3,3,128,128]{4,3,2,1,0:T(8,128)(2,1)}, bf16[8,3,3,128,128]{4,3,2,1,0:T(8,128)(2,1)S(1)}, u32[]{:S(2)}, u32[]{:S(2)}) collective-permute-start(bf16[8,3,3,128,128]{4,3,2,1,0:T(8,128)(2,1)} %bitcast.19), channel_id=1, source_target_pairs={{0,64},{64,0},{1,65},{65,1},{2,66},{66,2},{3,67},{67,3},{4,68},{68... | collective-permute-start | bytes 7077896 | tf_op jit(solution)/shard_map/ppermute | solution.py:195
  72.8 4.7 %collective-permute-done.4.refs_3_ = bf16[8,3,3,128,128]{4,3,2,1,0:T(8,128)(2,1)S(1)} collective-permute-done((bf16[8,3,3,128,128]{4,3,2,1,0:T(8,128)(2,1)}, bf16[8,3,3,128,128]{4,3,2,1,0:T(8,128)(2,1)S(1)}, u32[]{:S(2)}, u32[]{:S(2)}) %collective-permute-start.4) | collective-permute-done | bytes 2359328 | tf_op jit(solution)/shard_map/ppermute | solution.py:195
  77.5 1.7 copy-done.1
  79.2 2.6 %shard_map.64 = (bf16[4,128,256]{2,1,0:T(8,128)(2,1)S(1)}, bf16[2,128,256]{2,1,0:T(8,128)(2,1)S(1)}, bf16[2,2,128,256]{3,2,1,0:T(8,128)(2,1)S(1)}) custom-call(s32[4]{0:T(128)S(1)} %pad_add_fusion.refs_0_, f32[6]{0:T(128)S(1)} %pad_maximum_fusion.2.refs_1_, bf16[8,3,3,128,128]{4,3,2,1,0:T(8,128)(2,1)S(1)} %bitcast.20, ...), custom_call_target="tpu_custom_call" | custom-call | flops 377487360 | bytes 4194304 | tf_op jit(solution)/shard_map/pallas_call | solution.py:149
  81.8 2.3 %collective-permute-start.5 = (bf16[2,2,128,256]{3,2,1,0:T(8,128)(2,1)S(1)}, bf16[2,2,128,256]{3,2,1,0:T(8,128)(2,1)S(1)}, u32[]{:S(2)}, u32[]{:S(2)}) collective-permute-start(bf16[2,2,128,256]{3,2,1,0:T(8,128)(2,1)S(1)} %get-tuple-element.30), channel_id=1, source_target_pairs={{0,1},{1,2},{2,3},{3,4},{4,5},{5,6},{6,7},{8,9},{9,10},{10,11},{11... | collective-permute-start | bytes 786440 | tf_op jit(solution)/shard_map/ppermute | solution.py:227
  84.1 9.2 %collective-permute-done.5.refs_6_ = bf16[2,2,128,256]{3,2,1,0:T(8,128)(2,1)S(1)} collective-permute-done((bf16[2,2,128,256]{3,2,1,0:T(8,128)(2,1)S(1)}, bf16[2,2,128,256]{3,2,1,0:T(8,128)(2,1)S(1)}, u32[]{:S(2)}, u32[]{:S(2)}) %collective-permute-start.5) | collective-permute-done | bytes 262176 | tf_op jit(solution)/shard_map/ppermute | solution.py:227
  93.3 3.4 %shard_map.65 = (bf16[2,128,256]{2,1,0:T(8,128)(2,1)S(1)}, bf16[4,128,256]{2,1,0:T(8,128)(2,1)S(1)}, bf16[2,128,256]{2,1,0:T(8,128)(2,1)S(1)}, bf16[2,2,128,256]{3,2,1,0:T(8,128)(2,1)S(1)}) custom-call(s32[4]{0:T(128)S(1)} %pad_add_fusion.refs_0_, f32[6]{0:T(128)S(1)} %pad_maximum_fusion.2.refs_1_, bf16[8,3,3,128,128]{4,3,2,1,0:T(8,128)(2,1)S(1)} %bitcast.21, ...), custom_call_target="tpu_custom_call" | custom-call | flops 503316480 | bytes 4194304 | tf_op jit(solution)/shard_map/pallas_call | solution.py:149
  96.7 1.9 %collective-permute-start.6 = (bf16[2,2,128,256]{3,2,1,0:T(8,128)(2,1)S(1)}, bf16[2,2,128,256]{3,2,1,0:T(8,128)(2,1)S(1)}, u32[]{:S(2)}, u32[]{:S(2)}) collective-permute-start(bf16[2,2,128,256]{3,2,1,0:T(8,128)(2,1)S(1)} %get-tuple-element.34), channel_id=1, source_target_pairs={{0,1},{1,2},{2,3},{3,4},{4,5},{5,6},{6,7},{8,9},{9,10},{10,11},{11... | collective-permute-start | bytes 786440 | tf_op jit(solution)/shard_map/ppermute | solution.py:227
  98.7 8.6 %collective-permute-done.6.refs_6_ = bf16[2,2,128,256]{3,2,1,0:T(8,128)(2,1)S(1)} collective-permute-done((bf16[2,2,128,256]{3,2,1,0:T(8,128)(2,1)S(1)}, bf16[2,2,128,256]{3,2,1,0:T(8,128)(2,1)S(1)}, u32[]{:S(2)}, u32[]{:S(2)}) %collective-permute-start.6) | collective-permute-done | bytes 262176 | tf_op jit(solution)/shard_map/ppermute | solution.py:227
  107.3 3.4 %shard_map.66 = (bf16[2,128,256]{2,1,0:T(8,128)(2,1)S(1)}, bf16[4,128,256]{2,1,0:T(8,128)(2,1)S(1)}, bf16[2,128,256]{2,1,0:T(8,128)(2,1)S(1)}, bf16[2,2,128,256]{3,2,1,0:T(8,128)(2,1)S(1)}) custom-call(s32[4]{0:T(128)S(1)} %pad_add_fusion.refs_0_, f32[6]{0:T(128)S(1)} %pad_maximum_fusion.2.refs_1_, bf16[8,3,3,128,128]{4,3,2,1,0:T(8,128)(2,1)S(1)} %bitcast.22, ...), custom_call_target="tpu_custom_call" | custom-call | flops 503316480 | bytes 4194304 | tf_op jit(solution)/shard_map/pallas_call | solution.py:149
  110.7 1.9 %collective-permute-start.7 = (bf16[2,2,128,256]{3,2,1,0:T(8,128)(2,1)S(1)}, bf16[2,2,128,256]{3,2,1,0:T(8,128)(2,1)S(1)}, u32[]{:S(2)}, u32[]{:S(2)}) collective-permute-start(bf16[2,2,128,256]{3,2,1,0:T(8,128)(2,1)S(1)} %get-tuple-element.38), channel_id=1, source_target_pairs={{0,1},{1,2},{2,3},{3,4},{4,5},{5,6},{6,7},{8,9},{9,10},{10,11},{11... | collective-permute-start | bytes 786440 | tf_op jit(solution)/shard_map/ppermute | solution.py:227
  112.7 7.7 %collective-permute-done.7.refs_6_ = bf16[2,2,128,256]{3,2,1,0:T(8,128)(2,1)S(1)} collective-permute-done((bf16[2,2,128,256]{3,2,1,0:T(8,128)(2,1)S(1)}, bf16[2,2,128,256]{3,2,1,0:T(8,128)(2,1)S(1)}, u32[]{:S(2)}, u32[]{:S(2)}) %collective-permute-start.7) | collective-permute-done | bytes 262176 | tf_op jit(solution)/shard_map/ppermute | solution.py:227
  120.4 3.3 %shard_map.67 = (bf16[2,128,256]{2,1,0:T(8,128)(2,1)S(1)}, bf16[4,128,256]{2,1,0:T(8,128)(2,1)S(1)}, bf16[2,128,128]{2,1,0:T(8,128)(2,1)S(1)}, bf16[1,2,128,256]{3,2,1,0:T(8,128)(2,1)S(1)}) custom-call(s32[4]{0:T(128)S(1)} %pad_add_fusion.refs_0_, f32[6]{0:T(128)S(1)} %pad_maximum_fusion.2.refs_1_, bf16[8,3,3,128,128]{4,3,2,1,0:T(8,128)(2,1)S(1)} %bitcast.23, ...), custom_call_target="tpu_custom_call" | custom-call | flops 503316480 | bytes 4194304 | tf_op jit(solution)/shard_map/pallas_call | solution.py:149
  123.7 1.9 %collective-permute-start.8 = (bf16[1,2,128,256]{3,2,1,0:T(8,128)(2,1)S(1)}, bf16[1,2,128,256]{3,2,1,0:T(8,128)(2,1)S(1)}, u32[]{:S(2)}, u32[]{:S(2)}) collective-permute-start(bf16[1,2,128,256]{3,2,1,0:T(8,128)(2,1)S(1)} %get-tuple-element.41), channel_id=1, source_target_pairs={{0,1},{1,2},{2,3},{3,4},{4,5},{5,6},{6,7},{8,9},{9,10},{10,11},{11... | collective-permute-start | bytes 393224 | tf_op jit(solution)/shard_map/ppermute | solution.py:260
  125.7 6.1 %collective-permute-done.8.refs_5_ = bf16[1,2,128,256]{3,2,1,0:T(8,128)(2,1)S(1)} collective-permute-done((bf16[1,2,128,256]{3,2,1,0:T(8,128)(2,1)S(1)}, bf16[1,2,128,256]{3,2,1,0:T(8,128)(2,1)S(1)}, u32[]{:S(2)}, u32[]{:S(2)}) %collective-permute-start.8) | collective-permute-done | bytes 131104 | tf_op jit(solution)/shard_map/ppermute | solution.py:260
  131.8 1.2 shard_map.68
  133.1 5.4 %all_to_all.10 = bf16[2,4,8,64,128]{4,3,2,1,0:T(8,128)(2,1)} all-to-all(bf16[2,4,8,64,128]{4,3,2,1,0:T(8,128)(2,1)S(1)} %bitcast.25), channel_id=1, replica_groups=mesh['zhi'=4,'core'=2,'x'=4,'zlo'=2,'y'=8] {'core'}, dimensions={0} | all-to-all | bytes 2097152 | tf_op jit(solution)/shard_map/all_to_all | solution.py:279
  138.5 2.4 %reduce_sum.24 = bf16[4,8,64,128]{3,2,1,0:T(8,128)(2,1)} reduce(bf16[2,4,8,64,128]{4,3,2,1,0:T(8,128)(2,1)} %all_to_all.10, bf16[]{:T(256)} %constant.58.clone.1), dimensions={0}, to_apply=%region_0.1 | reduce | flops 262144 | bytes 1572866 | tf_op jit(solution)/shard_map/reduce_sum | solution.py:280
  140.9 24.5 %all_to_all.11 = bf16[32,64,128]{2,1,0:T(8,128)(2,1)} all-to-all(bf16[32,64,128]{2,1,0:T(8,128)(2,1)} %bitcast.26), channel_id=1, replica_groups=mesh['zhi'=4,'core'=2,'x'=4,'zlo'=2,'y'=8] {'zhi','x','zlo'}, dimensions={0} | all-to-all | bytes 1048576 | tf_op jit(solution)/shard_map/all_to_all | solution.py:282
  165.4 1.1 reduce_sum.25
  166.5 1.9 %collective-permute-start.9 = (bf16[64,128]{1,0:T(8,128)(2,1)S(1)}, bf16[64,128]{1,0:T(8,128)(2,1)S(1)}, u32[]{:S(2)}, u32[]{:S(2)}) collective-permute-start(bf16[64,128]{1,0:T(8,128)(2,1)S(1)} %reduce_sum.25), channel_id=1, source_target_pairs={{0,0},{8,1},{16,2},{24,3},{32,4},{40,5},{48,6},{56,7},{1,8},{9,9},... | collective-permute-start | bytes 49160 | tf_op jit(solution)/shard_map/ppermute | solution.py:284
  168.5 10.0 %collective-permute-done.9 = bf16[64,128]{1,0:T(8,128)(2,1)S(1)} collective-permute-done((bf16[64,128]{1,0:T(8,128)(2,1)S(1)}, bf16[64,128]{1,0:T(8,128)(2,1)S(1)}, u32[]{:S(2)}, u32[]{:S(2)}) %collective-permute-start.9) | collective-permute-done | bytes 16416 | tf_op jit(solution)/shard_map/ppermute | solution.py:284
  (33 shorter events, 4.9 us)
Async XLA Ops:
  6.5 1.9 %copy-start = (bf16[1,3,4096,128]{3,2,1,0:T(8,128)(2,1)S(1)}, bf16[1,3,4096,128]{3,2,1,0:T(8,128)(2,1)}, u32[]{:S(2)}) copy-start(bf16[1,3,4096,128]{3,2,1,0:T(8,128)(2,1)} %param.6) | copy-start | bytes 9437188
  6.5 64.4 %all-gather.3.cloned.1.call-start = ((), (), s32[]{:S(2)}) async-start(), calls=%async_computation.2 | async-start | bytes 2654208 | tf_op jit(solution)/shard_map/all_gather | solution.py:173
  9.2 33.9 %collective-permute-start.2 = (bf16[64,128]{1,0:T(8,128)(2,1)}, bf16[64,128]{1,0:T(8,128)(2,1)}, u32[]{:S(2)}, u32[]{:S(2)}) collective-permute-start(bf16[64,128]{1,0:T(8,128)(2,1)} %param.8), channel_id=1, source_target_pairs={{0,0},{1,8},{2,16},{3,24},{4,32},{5,40},{6,48},{7,56},{8,1},{9,9},... | collective-permute-start | bytes 49160 | tf_op jit(solution)/shard_map/ppermute | solution.py:186
  13.7 28.6 %collective-permute-start.1 = (bf16[64,128]{1,0:T(8,128)(2,1)}, bf16[64,128]{1,0:T(8,128)(2,1)}, u32[]{:S(2)}, u32[]{:S(2)}) collective-permute-start(bf16[64,128]{1,0:T(8,128)(2,1)} %param.8), channel_id=1, source_target_pairs={{4,33},{5,41},{6,49},{7,57},{12,34},{13,42},{14,50},{15,58},{20,35... | collective-permute-start | bytes 49160 | tf_op jit(solution)/shard_map/ppermute | solution.py:187
  24.3 16.6 %collective-permute-start.3 = (f32[8]{0:T(128)S(1)}, f32[8]{0:T(128)S(1)}, u32[]{:S(2)}, u32[]{:S(2)}) collective-permute-start(f32[8]{0:T(128)S(1)} %pad_maximum_fusion.1), channel_id=1, source_target_pairs={{0,0},{1,64},{2,128},{3,192},{4,256},{5,320},{6,384},{7,448},{8,8}... | collective-permute-start | bytes 104 | tf_op jit(solution)/shard_map/ppermute | solution.py:179
  28.2 19.2 %collective-permute-start = (bf16[6,128,128]{2,1,0:T(8,128)(2,1)S(1)}, bf16[6,128,128]{2,1,0:T(8,128)(2,1)}, u32[]{:S(2)}, u32[]{:S(2)}) collective-permute-start(bf16[6,128,128]{2,1,0:T(8,128)(2,1)S(1)} %select_select_fusion), channel_id=1, source_target_pairs={{0,0},{1,64},{2,128},{3,192},{4,256},{5,320},{6,384},{7,448},{8,8}... | collective-permute-start | bytes 589832 | tf_op jit(solution)/shard_map/ppermute | solution.py:177
  43.9 3.5 %copy-start.2 = (bf16[768,128]{1,0:T(8,128)(2,1)}, bf16[768,128]{1,0:T(8,128)(2,1)S(1)}, u32[]{:S(2)}) copy-start(bf16[768,128]{1,0:T(8,128)(2,1)S(1)} %constant_dynamic-update-slice_fusion.2) | copy-start | bytes 589828
  70.9 6.6 %collective-permute-start.4 = (bf16[8,3,3,128,128]{4,3,2,1,0:T(8,128)(2,1)}, bf16[8,3,3,128,128]{4,3,2,1,0:T(8,128)(2,1)S(1)}, u32[]{:S(2)}, u32[]{:S(2)}) collective-permute-start(bf16[8,3,3,128,128]{4,3,2,1,0:T(8,128)(2,1)} %bitcast.19), channel_id=1, source_target_pairs={{0,64},{64,0},{1,65},{65,1},{2,66},{66,2},{3,67},{67,3},{4,68},{68... | collective-permute-start | bytes 7077896 | tf_op jit(solution)/shard_map/ppermute | solution.py:195
  77.5 1.7 copy-start.1
  81.8 11.4 %collective-permute-start.5 = (bf16[2,2,128,256]{3,2,1,0:T(8,128)(2,1)S(1)}, bf16[2,2,128,256]{3,2,1,0:T(8,128)(2,1)S(1)}, u32[]{:S(2)}, u32[]{:S(2)}) collective-permute-start(bf16[2,2,128,256]{3,2,1,0:T(8,128)(2,1)S(1)} %get-tuple-element.30), channel_id=1, source_target_pairs={{0,1},{1,2},{2,3},{3,4},{4,5},{5,6},{6,7},{8,9},{9,10},{10,11},{11... | collective-permute-start | bytes 786440 | tf_op jit(solution)/shard_map/ppermute | solution.py:227
  96.7 10.6 %collective-permute-start.6 = (bf16[2,2,128,256]{3,2,1,0:T(8,128)(2,1)S(1)}, bf16[2,2,128,256]{3,2,1,0:T(8,128)(2,1)S(1)}, u32[]{:S(2)}, u32[]{:S(2)}) collective-permute-start(bf16[2,2,128,256]{3,2,1,0:T(8,128)(2,1)S(1)} %get-tuple-element.34), channel_id=1, source_target_pairs={{0,1},{1,2},{2,3},{3,4},{4,5},{5,6},{6,7},{8,9},{9,10},{10,11},{11... | collective-permute-start | bytes 786440 | tf_op jit(solution)/shard_map/ppermute | solution.py:227
  110.7 9.7 %collective-permute-start.7 = (bf16[2,2,128,256]{3,2,1,0:T(8,128)(2,1)S(1)}, bf16[2,2,128,256]{3,2,1,0:T(8,128)(2,1)S(1)}, u32[]{:S(2)}, u32[]{:S(2)}) collective-permute-start(bf16[2,2,128,256]{3,2,1,0:T(8,128)(2,1)S(1)} %get-tuple-element.38), channel_id=1, source_target_pairs={{0,1},{1,2},{2,3},{3,4},{4,5},{5,6},{6,7},{8,9},{9,10},{10,11},{11... | collective-permute-start | bytes 786440 | tf_op jit(solution)/shard_map/ppermute | solution.py:227
  123.7 8.1 %collective-permute-start.8 = (bf16[1,2,128,256]{3,2,1,0:T(8,128)(2,1)S(1)}, bf16[1,2,128,256]{3,2,1,0:T(8,128)(2,1)S(1)}, u32[]{:S(2)}, u32[]{:S(2)}) collective-permute-start(bf16[1,2,128,256]{3,2,1,0:T(8,128)(2,1)S(1)} %get-tuple-element.41), channel_id=1, source_target_pairs={{0,1},{1,2},{2,3},{3,4},{4,5},{5,6},{6,7},{8,9},{9,10},{10,11},{11... | collective-permute-start | bytes 393224 | tf_op jit(solution)/shard_map/ppermute | solution.py:260
  166.5 11.9 %collective-permute-start.9 = (bf16[64,128]{1,0:T(8,128)(2,1)S(1)}, bf16[64,128]{1,0:T(8,128)(2,1)S(1)}, u32[]{:S(2)}, u32[]{:S(2)}) collective-permute-start(bf16[64,128]{1,0:T(8,128)(2,1)S(1)} %reduce_sum.25), channel_id=1, source_target_pairs={{0,0},{8,1},{16,2},{24,3},{32,4},{40,5},{48,6},{56,7},{1,8},{9,9},... | collective-permute-start | bytes 49160 | tf_op jit(solution)/shard_map/ppermute | solution.py:284
Sparse Core Ops, SparseCore 0:
  9.4 61.4 all-gather.2

commit v3 on v2

--- a/solution.py
+++ b/solution.py
@@ -1,4 +1,5 @@
 import functools
+import itertools
 
 import jax
 import jax.numpy as jnp
@@ -11,43 +12,33 @@
 OWN = 4
 WINDOW = OWN + 2
 STATES = 3
-AXES = ("zhi", "core", "x", "zlo", "y")
+AXES = ("zhi", "core", "x", "zlo", "yl", "y0")
 BF16 = jnp.bfloat16
 F32 = jnp.float32
 
 
-def device_number(zhi, core, x, zlo, y):
-    return (((zhi * 2 + core) * 4 + x) * 2 + zlo) * 8 + y
+def device_number(zhi, core, x, zlo, yl, y0):
+    return ((((zhi * 2 + core) * 4 + x) * 2 + zlo) * 4 + yl) * 2 + y0
 
 
 def all_places():
+    return itertools.product(range(4), range(2), range(4), range(2), range(4), range(2))
+
+
+def to_groups():
     return [
-        (zhi, core, x, zlo, y)
-        for zhi in range(4)
-        for core in range(2)
-        for x in range(4)
-        for zlo in range(2)
-        for y in range(8)
+        (device_number(zhi, core, x, zlo, yl, y0), device_number(x, y0, zhi, zlo, yl, core))
+        for zhi, core, x, zlo, yl, y0 in all_places()
     ]
 
 
-def to_slices():
-    return [
-        (device_number(*place), device_number(place[4] // 2, place[4] % 2, place[2], place[3], place[0] * 2 + place[1]))
-        for place in all_places()
-    ]
-
-
-def rows_to_slices(back, halo=False):
+def rows_to_groups(halo):
     pairs = []
-    for zhi, core, x, zlo, y in all_places():
-        if not back and (zhi or core):
-            continue
-        if halo and (y < 4 or 2 * x + zlo == 7):
-            continue
-        outer = device_number(zhi, core, x, zlo, y)
-        inner = device_number(zhi, core, y // 2, y % 2, 2 * x + zlo + (1 if halo else 0))
-        pairs.append((inner, outer) if back else (outer, inner))
+    for zhi, core, x, zlo, yl, y0 in all_places():
+        group = 2 * x + zlo + halo
+        if zhi == core == 0 and group < 8 and not (halo and yl < 2):
+            target = device_number(0, 0, group // 2, y0, yl, group % 2)
+            pairs.append((device_number(0, 0, x, zlo, yl, y0), target))
     return pairs
 
 
@@ -162,31 +153,82 @@
     )(whole, part, mine, other, *ins)
 
 
+def take_piece(start, site, piece, taken, sems):
+    rows = 3 * BLOCK
+    first = pl.multiple_of(start[0] * BLOCK, BLOCK)
+    inward = [
+        pltpu.make_async_copy(site.at[0, s, pl.ds(first, rows)], taken.at[s], sems.at[0, s]) for s in range(STATES)
+    ]
+    outward = [pltpu.make_async_copy(taken.at[s], piece.at[s], sems.at[1, s]) for s in range(STATES)]
+    for copy in inward:
+        copy.start()
+    for before, after in zip(inward, outward):
+        before.wait()
+        after.start()
+    for copy in outward:
+        copy.wait()
+
+
+def add_cores(over, summed):
+    for site in range(4):
+        summed[site] = (over[0, site].astype(F32) + over[1, site].astype(F32)).astype(BF16)
+
+
+def add_columns(place, over, summed):
+    total = over[0].astype(F32)
+    for source in range(1, 16):
+        total += over[source].astype(F32)
+    total = total.astype(BF16)
+    for zlo in range(2):
+        summed[zlo] = jnp.where(place[0] == zlo, total, jnp.zeros_like(total))
+
+
+def add_up(kernel, ins, out):
+    spaces = [pltpu.SMEM if array.ndim == 1 else pltpu.VMEM for array in ins]
+    return pl.pallas_call(
+        kernel,
+        out_shape=jax.ShapeDtypeStruct(out, BF16),
+        in_specs=[pl.BlockSpec(memory_space=space) for space in spaces],
+        out_specs=pl.BlockSpec(memory_space=pltpu.VMEM),
+        compiler_params=pltpu.CompilerParams(vmem_limit_bytes=16 << 20),
+        cost_estimate=pl.CostEstimate(flops=1 << 19, bytes_accessed=2 << 20, transcendentals=0),
+    )(*ins)
+
+
 def body(site_tensor, term_ops, env_rows, term_shift, keep_weight, env_weight):
     sectors = site_tensor.shape[2] // BLOCK
     core = lax.axis_index("core")
     seg = lax.axis_index("zhi") * 2 + core
-    at_x, at_zlo, at_y = (lax.axis_index(name) for name in ("x", "zlo", "y"))
-
-    site_blocks = site_tensor[0].reshape(STATES, sectors, BLOCK, BLOCK)
-    piece = lax.dynamic_slice_in_dim(site_blocks, site_start(sectors, at_y, at_zlo), 3, 1)
+    at_zlo, at_yl, at_y0 = (lax.axis_index(name) for name in ("zlo", "yl", "y0"))
+    group = lax.axis_index("x") * 2 + at_y0
+
+    start = site_start(sectors, group, at_zlo).astype(jnp.int32).reshape(1)
+    piece = pl.pallas_call(
+        take_piece,
+        out_shape=jax.ShapeDtypeStruct((STATES, 3 * BLOCK, BLOCK), BF16),
+        in_specs=[pl.BlockSpec(memory_space=pltpu.SMEM), pl.BlockSpec(memory_space=pltpu.HBM)],
+        out_specs=pl.BlockSpec(memory_space=pltpu.HBM),
+        scratch_shapes=[pltpu.VMEM((STATES, 3 * BLOCK, BLOCK), BF16), pltpu.SemaphoreType.DMA((2, STATES))],
+        compiler_params=pltpu.CompilerParams(vmem_limit_bytes=60 << 20),
+        cost_estimate=pl.CostEstimate(flops=0, bytes_accessed=600_000, transcendentals=0),
+    )(start, site_tensor).reshape(STATES, 3, BLOCK, BLOCK)
     mine = lax.all_gather(piece, ("zhi", "zlo"))
-    spots = [site_start(sectors, at_y, half) - (OWN * at_y - 1) for half in range(2)]
+    spots = [site_start(sectors, group, half) - (OWN * group - 1) for half in range(2)]
 
     own_ops = ops_piece(term_ops[0].reshape(sectors, BLOCK, BLOCK), term_shift[0], seg)
-    ops_now = lax.ppermute(own_ops, AXES, to_slices())
+    ops_now = lax.ppermute(own_ops, AXES, to_groups())
     figures = jnp.concatenate([keep_weight[0], env_weight[0], term_shift.astype(F32), jnp.zeros((1,), F32)])
-    figures = lax.ppermute(figures, AXES, to_slices())
+    figures = lax.ppermute(figures, AXES, to_groups())
     shift = figures[6].astype(jnp.int32)
     partner = jnp.arange(STATES, dtype=jnp.int32) - shift
     factors = jnp.where((partner >= 0) & (partner <= 2), figures[3:6], 0.0)
     part = jnp.concatenate([figures[:3], factors])
     whole = jnp.stack([core, shift] + spots).astype(jnp.int32)
 
-    piece = lax.ppermute(env_rows, AXES, rows_to_slices(False))
-    halo = lax.ppermute(env_rows, AXES, rows_to_slices(False, True))
+    piece = lax.ppermute(env_rows, AXES, rows_to_groups(0))
+    halo = lax.ppermute(env_rows, AXES, rows_to_groups(1))
     env_now = jnp.zeros((WINDOW * BLOCK, BLOCK), BF16)
-    spot = at_x * BLOCK + at_zlo * (BLOCK // 2)
+    spot = at_yl * BLOCK + at_zlo * (BLOCK // 2)
     env_now = lax.dynamic_update_slice_in_dim(env_now, halo, jnp.maximum(spot - 2 * BLOCK, 0), 0)
     env_now = lax.dynamic_update_slice_in_dim(env_now, piece, spot + 2 * BLOCK, 0)
     window = jnp.concatenate([ops_now, env_now.reshape(WINDOW, BLOCK, BLOCK)], 2)
@@ -224,7 +266,7 @@
     )
     bonds = [full[:, :, BLOCK:]]
     for site in (1, 3, 5):
-        tails = lax.ppermute(tails, "y", onward)
+        tails = lax.ppermute(tails, ("x", "y0"), onward)
         last = site == 5
         sources = {}
         for sector in (-2, -1):
@@ -257,7 +299,7 @@
             other,
         )
         bonds += [lower[:, :, BLOCK:], old_upper[:, :, BLOCK:], full[:, :, BLOCK:]]
-    tails = lax.ppermute(tails, "y", onward)
+    tails = lax.ppermute(tails, ("x", "y0"), onward)
     sources = {(7, sector): (1, (0, sector + 2)) for sector in (-2, -1)}
     sources.update({(7, sector): (0, sector) for sector in range(2)})
     (lower,) = run_phase(
@@ -277,15 +319,16 @@
 
     partial = jnp.concatenate(bonds, 0).reshape(4, 2, 8, BLOCK // 2, BLOCK).transpose(1, 0, 2, 3, 4)
     over = lax.all_to_all(partial, "core", 0, 0)
-    summed = over.astype(F32).sum(0).astype(BF16)
-    summed = summed.reshape(32, BLOCK // 2, BLOCK)
-    over = lax.all_to_all(summed, ("zhi", "x", "zlo"), 0, 0)
-    summed = over.astype(F32).sum(0).astype(BF16)
-    return lax.ppermute(summed, AXES, rows_to_slices(True))[None]
+    summed = add_up(add_cores, [over], (4, 8, BLOCK // 2, BLOCK)).reshape(16, 2, BLOCK // 2, BLOCK)
+    over = lax.all_to_all(summed, ("zhi", "yl"), 0, 0)
+    place = at_y0.astype(jnp.int32).reshape(1)
+    summed = add_up(add_columns, [place, over], (2, 2, BLOCK // 2, BLOCK)).reshape(4, BLOCK // 2, BLOCK)
+    over = lax.all_to_all(summed, ("zlo", "y0"), 0, 0)
+    return over.astype(F32).sum(0).astype(BF16)[None]
 
 
 def solution(mesh):
-    parts = Mesh(mesh.devices.reshape(4, 2, 4, 2, 8), AXES)
-    seg, op = ("zhi", "core"), ("x", "zlo", "y")
+    parts = Mesh(mesh.devices.reshape(4, 2, 4, 2, 4, 2), AXES)
+    seg, op = ("zhi", "core"), ("x", "zlo", "yl", "y0")
     placed = (P(seg, None, None, None), P(op, None, None), P(op, None), P(op), P(op, None), P(op, None))
     return jax.shard_map(body, mesh=parts, in_specs=placed, out_specs=P(seg, op, None), check_vma=False)

time: 187 us -> 179 us (0.957)
  the two profiles are of different devices: /device:TPU:32 before, /device:TPU:2 now
where the time goes in v3:
time: 179 us; the launch traced here: 178 us
  waiting for transfers between devices  82.2 us (46%)
  blocking collectives  40.7 us (23%)
  starting transfers between devices  19 us (11%)
  Pallas kernels  15.8 us (9%)
  between operations  15 us (8%)
  local copies, waits for them, and re-layouts  3.74 us (2%)
  other arithmetic  2 us (1%)
    all_gather x1, waiting for transfers between devices, body(): mine = lax.all_gather(piece, ('zhi', 'zlo'))  33.5 us
    ppermute x4, waiting for transfers between devices, body(): tails = lax.ppermute(tails, ('x', 'y0'), onward)  31.5 us
    all_to_all x1, blocking collectives, body(): over = lax.all_to_all(summed, ('zhi', 'yl'), 0, 0)  28.9 us
    pallas_call x5, Pallas kernels, run_phase(): pl.pallas_call(functools.partial(phase_kernel, sites, steps, len(ins), so...  13.9 us
    ppermute x1, waiting for transfers between devices, body(): ops_now = lax.ppermute(own_ops, AXES, to_groups())  12.5 us
    ppermute x4, starting transfers between devices, body(): tails = lax.ppermute(tails, ('x', 'y0'), onward)  7.84 us
    all_to_all x1, blocking collectives, body(): over = lax.all_to_all(summed, ('zlo', 'y0'), 0, 0)  7.21 us
    ppermute x1, starting transfers between devices, body(): figures = lax.ppermute(figures, AXES, to_groups())  6.05 us
  transfers between devices with their start and end apart: 10, of which 7 were waited for; matrix products, arithmetic and copies ran while one was open for 2% of the time, Pallas kernels for 0%

profile of v3, /device:TPU:2, one launch (start us, length us, event | category | flops | bytes accessed | tf_op | source)
XLA Modules:
  0.0 178.4 jit_solution(15142311398918216511)
XLA Ops:
  6.5 1.7 shard_map.64
  8.3 0.7 collective-permute-start.2
  9.0 0.7 collective-permute-start.1
  10.4 6.1 %collective-permute-start.3 = (f32[8]{0:T(128)S(1)}, f32[8]{0:T(128)S(1)}, u32[]{:S(2)}, u32[]{:S(2)}) collective-permute-start(f32[8]{0:T(128)S(1)} %pad_maximum_fusion.1), channel_id=1, source_target_pairs={{0,0},{1,64},{2,2},{3,66},{4,4},{5,68},{6,6},{7,70},{8,8},{9,72},{... | collective-permute-start | bytes 104 | tf_op jit(solution)/shard_map/ppermute | solution.py:221
  16.5 0.9 constant_dynamic-slice_fusion
  17.4 1.0 select_select_fusion
  18.4 1.9 %collective-permute-start = (bf16[6,128,128]{2,1,0:T(8,128)(2,1)S(1)}, bf16[6,128,128]{2,1,0:T(8,128)(2,1)S(1)}, u32[]{:S(2)}, u32[]{:S(2)}) collective-permute-start(bf16[6,128,128]{2,1,0:T(8,128)(2,1)S(1)} %select_select_fusion), channel_id=1, source_target_pairs={{0,0},{1,64},{2,2},{3,66},{4,4},{5,68},{6,6},{7,70},{8,8},{9,72},{... | collective-permute-start | bytes 589832 | tf_op jit(solution)/shard_map/ppermute | solution.py:219
  20.4 0.6 slice.43
  21.9 0.2 dynamic_update_slice.6
  22.1 12.5 %collective-permute-done = bf16[6,128,128]{2,1,0:T(8,128)(2,1)S(1)} collective-permute-done((bf16[6,128,128]{2,1,0:T(8,128)(2,1)S(1)}, bf16[6,128,128]{2,1,0:T(8,128)(2,1)S(1)}, u32[]{:S(2)}, u32[]{:S(2)}) %collective-permute-start) | collective-permute-done | bytes 196640 | tf_op jit(solution)/shard_map/ppermute | solution.py:219
  34.6 33.5 %all-gather.2.cloned.1.call-done.refs_2_ = bf16[8,3,3,128,128]{4,3,2,1,0:T(8,128)(2,1)} async-done(((bf16[1,3,3,128,128]{4,3,2,1,0:T(8,128)(2,1)}), bf16[8,3,3,128,128]{4,3,2,1,0:T(8,128)(2,1)}) %all-gather.2.cloned.1.call-update) | async-done | bytes 2359312 | tf_op jit(solution)/shard_map/all_gather | solution.py:215
  68.1 1.9 %collective-permute-start.4 = (bf16[8,3,3,128,128]{4,3,2,1,0:T(8,128)(2,1)}, bf16[8,3,3,128,128]{4,3,2,1,0:T(8,128)(2,1)S(1)}, u32[]{:S(2)}, u32[]{:S(2)}) collective-permute-start(bf16[8,3,3,128,128]{4,3,2,1,0:T(8,128)(2,1)} %all-gather.2.cloned.1.call-done.refs_2_), channel_id=1, source_target_pairs={{0,64},{64,0},{1,65},{65,1},{2,66},{66,2},{3,67},{67,3},{4,68},{68... | collective-permute-start | bytes 7077896 | tf_op jit(solution)/shard_map/ppermute | solution.py:237
  70.1 4.7 %collective-permute-done.4.refs_3_ = bf16[8,3,3,128,128]{4,3,2,1,0:T(8,128)(2,1)S(1)} collective-permute-done((bf16[8,3,3,128,128]{4,3,2,1,0:T(8,128)(2,1)}, bf16[8,3,3,128,128]{4,3,2,1,0:T(8,128)(2,1)S(1)}, u32[]{:S(2)}, u32[]{:S(2)}) %collective-permute-start.4) | collective-permute-done | bytes 2359328 | tf_op jit(solution)/shard_map/ppermute | solution.py:237
  74.8 1.7 copy-done
  76.4 2.6 %shard_map.65 = (bf16[4,128,256]{2,1,0:T(8,128)(2,1)S(1)}, bf16[2,128,256]{2,1,0:T(8,128)(2,1)S(1)}, bf16[2,2,128,256]{3,2,1,0:T(8,128)(2,1)S(1)}) custom-call(s32[4]{0:T(128)S(1)} %pad_add_fusion.refs_0_, f32[6]{0:T(128)S(1)} %pad_maximum_fusion.2.refs_1_, bf16[8,3,3,128,128]{4,3,2,1,0:T(8,128)(2,1)S(1)} %copy-done, ...), custom_call_target="tpu_custom_call" | custom-call | flops 377487360 | bytes 4194304 | tf_op jit(solution)/shard_map/pallas_call | solution.py:140
  79.1 2.1 %collective-permute-start.5 = (bf16[2,2,128,256]{3,2,1,0:T(8,128)(2,1)S(1)}, bf16[2,2,128,256]{3,2,1,0:T(8,128)(2,1)S(1)}, u32[]{:S(2)}, u32[]{:S(2)}) collective-permute-start(bf16[2,2,128,256]{3,2,1,0:T(8,128)(2,1)S(1)} %get-tuple-element.30), channel_id=1, source_target_pairs={{0,1},{1,16},{16,17},{17,32},{32,33},{33,48},{48,49},{2,3},{3,18},... | collective-permute-start | bytes 786440 | tf_op jit(solution)/shard_map/ppermute | solution.py:269
  81.2 9.4 %collective-permute-done.5.refs_6_ = bf16[2,2,128,256]{3,2,1,0:T(8,128)(2,1)S(1)} collective-permute-done((bf16[2,2,128,256]{3,2,1,0:T(8,128)(2,1)S(1)}, bf16[2,2,128,256]{3,2,1,0:T(8,128)(2,1)S(1)}, u32[]{:S(2)}, u32[]{:S(2)}) %collective-permute-start.5) | collective-permute-done | bytes 262176 | tf_op jit(solution)/shard_map/ppermute | solution.py:269
  90.6 3.4 %shard_map.66 = (bf16[2,128,256]{2,1,0:T(8,128)(2,1)S(1)}, bf16[4,128,256]{2,1,0:T(8,128)(2,1)S(1)}, bf16[2,128,256]{2,1,0:T(8,128)(2,1)S(1)}, bf16[2,2,128,256]{3,2,1,0:T(8,128)(2,1)S(1)}) custom-call(s32[4]{0:T(128)S(1)} %pad_add_fusion.refs_0_, f32[6]{0:T(128)S(1)} %pad_maximum_fusion.2.refs_1_, bf16[8,3,3,128,128]{4,3,2,1,0:T(8,128)(2,1)S(1)} %copy-done, ...), custom_call_target="tpu_custom_call" | custom-call | flops 503316480 | bytes 4194304 | tf_op jit(solution)/shard_map/pallas_call | solution.py:140
  94.0 1.9 %collective-permute-start.6 = (bf16[2,2,128,256]{3,2,1,0:T(8,128)(2,1)S(1)}, bf16[2,2,128,256]{3,2,1,0:T(8,128)(2,1)S(1)}, u32[]{:S(2)}, u32[]{:S(2)}) collective-permute-start(bf16[2,2,128,256]{3,2,1,0:T(8,128)(2,1)S(1)} %get-tuple-element.34), channel_id=1, source_target_pairs={{0,1},{1,16},{16,17},{17,32},{32,33},{33,48},{48,49},{2,3},{3,18},... | collective-permute-start | bytes 786440 | tf_op jit(solution)/shard_map/ppermute | solution.py:269
  96.0 8.6 %collective-permute-done.6.refs_6_ = bf16[2,2,128,256]{3,2,1,0:T(8,128)(2,1)S(1)} collective-permute-done((bf16[2,2,128,256]{3,2,1,0:T(8,128)(2,1)S(1)}, bf16[2,2,128,256]{3,2,1,0:T(8,128)(2,1)S(1)}, u32[]{:S(2)}, u32[]{:S(2)}) %collective-permute-start.6) | collective-permute-done | bytes 262176 | tf_op jit(solution)/shard_map/ppermute | solution.py:269
  104.6 3.4 %shard_map.67 = (bf16[2,128,256]{2,1,0:T(8,128)(2,1)S(1)}, bf16[4,128,256]{2,1,0:T(8,128)(2,1)S(1)}, bf16[2,128,256]{2,1,0:T(8,128)(2,1)S(1)}, bf16[2,2,128,256]{3,2,1,0:T(8,128)(2,1)S(1)}) custom-call(s32[4]{0:T(128)S(1)} %pad_add_fusion.refs_0_, f32[6]{0:T(128)S(1)} %pad_maximum_fusion.2.refs_1_, bf16[8,3,3,128,128]{4,3,2,1,0:T(8,128)(2,1)S(1)} %copy-done, ...), custom_call_target="tpu_custom_call" | custom-call | flops 503316480 | bytes 4194304 | tf_op jit(solution)/shard_map/pallas_call | solution.py:140
  108.0 1.9 %collective-permute-start.7 = (bf16[2,2,128,256]{3,2,1,0:T(8,128)(2,1)S(1)}, bf16[2,2,128,256]{3,2,1,0:T(8,128)(2,1)S(1)}, u32[]{:S(2)}, u32[]{:S(2)}) collective-permute-start(bf16[2,2,128,256]{3,2,1,0:T(8,128)(2,1)S(1)} %get-tuple-element.38), channel_id=1, source_target_pairs={{0,1},{1,16},{16,17},{17,32},{32,33},{33,48},{48,49},{2,3},{3,18},... | collective-permute-start | bytes 786440 | tf_op jit(solution)/shard_map/ppermute | solution.py:269
  110.0 7.7 %collective-permute-done.7.refs_6_ = bf16[2,2,128,256]{3,2,1,0:T(8,128)(2,1)S(1)} collective-permute-done((bf16[2,2,128,256]{3,2,1,0:T(8,128)(2,1)S(1)}, bf16[2,2,128,256]{3,2,1,0:T(8,128)(2,1)S(1)}, u32[]{:S(2)}, u32[]{:S(2)}) %collective-permute-start.7) | collective-permute-done | bytes 262176 | tf_op jit(solution)/shard_map/ppermute | solution.py:269
  117.7 3.3 %shard_map.68 = (bf16[2,128,256]{2,1,0:T(8,128)(2,1)S(1)}, bf16[4,128,256]{2,1,0:T(8,128)(2,1)S(1)}, bf16[2,128,128]{2,1,0:T(8,128)(2,1)S(1)}, bf16[1,2,128,256]{3,2,1,0:T(8,128)(2,1)S(1)}) custom-call(s32[4]{0:T(128)S(1)} %pad_add_fusion.refs_0_, f32[6]{0:T(128)S(1)} %pad_maximum_fusion.2.refs_1_, bf16[8,3,3,128,128]{4,3,2,1,0:T(8,128)(2,1)S(1)} %copy-done, ...), custom_call_target="tpu_custom_call" | custom-call | flops 503316480 | bytes 4194304 | tf_op jit(solution)/shard_map/pallas_call | solution.py:140
  121.0 1.9 %collective-permute-start.8 = (bf16[1,2,128,256]{3,2,1,0:T(8,128)(2,1)S(1)}, bf16[1,2,128,256]{3,2,1,0:T(8,128)(2,1)S(1)}, u32[]{:S(2)}, u32[]{:S(2)}) collective-permute-start(bf16[1,2,128,256]{3,2,1,0:T(8,128)(2,1)S(1)} %get-tuple-element.41), channel_id=1, source_target_pairs={{0,1},{1,16},{16,17},{17,32},{32,33},{33,48},{48,49},{2,3},{3,18},... | collective-permute-start | bytes 393224 | tf_op jit(solution)/shard_map/ppermute | solution.py:302
  123.0 5.8 %collective-permute-done.8.refs_5_ = bf16[1,2,128,256]{3,2,1,0:T(8,128)(2,1)S(1)} collective-permute-done((bf16[1,2,128,256]{3,2,1,0:T(8,128)(2,1)S(1)}, bf16[1,2,128,256]{3,2,1,0:T(8,128)(2,1)S(1)}, u32[]{:S(2)}, u32[]{:S(2)}) %collective-permute-start.8) | collective-permute-done | bytes 131104 | tf_op jit(solution)/shard_map/ppermute | solution.py:302
  128.7 1.2 shard_map.69
  130.1 4.6 %all_to_all.15.over = bf16[2,4,8,64,128]{4,3,2,1,0:T(8,128)(2,1)S(1)} all-to-all(bf16[2,4,8,64,128]{4,3,2,1,0:T(8,128)(2,1)S(1)} %bitcast.22), channel_id=1, replica_groups=mesh['zhi'=4,'core'=2,'x'=4,'zlo'=2,'yl'=4,'y0'=2] {'core'}, dimensions={0} | all-to-all | bytes 2097152 | tf_op jit(solution)/shard_map/all_to_all | solution.py:321
  134.6 0.1 shard_map.70
  134.8 28.9 %all_to_all.16.over = bf16[16,2,64,128]{3,2,1,0:T(8,128)(2,1)S(1)} all-to-all(bf16[16,2,64,128]{3,2,1,0:T(8,128)(2,1)S(1)} %bitcast.20), channel_id=1, replica_groups=mesh['zhi'=4,'core'=2,'x'=4,'zlo'=2,'yl'=4,'y0'=2] {'zhi','yl'}, dimensions={0} | all-to-all | bytes 1048576 | tf_op jit(solution)/shard_map/all_to_all | solution.py:323
  163.7 7.2 %all_to_all.17 = bf16[4,64,128]{2,1,0:T(8,128)(2,1)S(1)} all-to-all(bf16[4,64,128]{2,1,0:T(8,128)(2,1)S(1)} %bitcast.21), channel_id=1, replica_groups=mesh['zhi'=4,'core'=2,'x'=4,'zlo'=2,'yl'=4,'y0'=2] {'zlo','y0'}, dimensions={0} | all-to-all | bytes 131072 | tf_op jit(solution)/shard_map/all_to_all | solution.py:326
  170.9 0.6 reduce_sum.12
  (34 shorter events, 0.8 us)
Async XLA Ops:
  6.5 1.7 copy-start.3
  6.5 3.7 %copy-start.1 = (f32[1,3]{1,0:T(1,128)S(1)}, f32[1,3]{1,0:T(1,128)}, u32[]{:S(2)}) copy-start(f32[1,3]{1,0:T(1,128)} %param.11) | copy-start | bytes 40
  6.5 3.8 %copy-start.2 = (f32[1,3]{1,0:T(1,128)S(1)}, f32[1,3]{1,0:T(1,128)}, u32[]{:S(2)}) copy-start(f32[1,3]{1,0:T(1,128)} %param.10) | copy-start | bytes 40
  6.5 61.6 %all-gather.2.cloned.1.call-start = ((), (), s32[]{:S(2)}) async-start(), calls=%async_computation.3 | async-start | bytes 2654208 | tf_op jit(solution)/shard_map/all_gather | solution.py:215
  8.3 13.8 %collective-permute-start.2 = (bf16[64,128]{1,0:T(8,128)(2,1)S(1)}, bf16[64,128]{1,0:T(8,128)(2,1)S(1)}, u32[]{:S(2)}, u32[]{:S(2)}) collective-permute-start(bf16[64,128]{1,0:T(8,128)(2,1)S(1)} %copy-done.3), channel_id=1, source_target_pairs={{0,0},{1,8},{2,2},{3,10},{4,4},{5,12},{6,6},{7,14},{8,1},{9,9},{10... | collective-permute-start | bytes 49160 | tf_op jit(solution)/shard_map/ppermute | solution.py:228
  9.0 12.9 %collective-permute-start.1 = (bf16[64,128]{1,0:T(8,128)(2,1)S(1)}, bf16[64,128]{1,0:T(8,128)(2,1)S(1)}, u32[]{:S(2)}, u32[]{:S(2)}) collective-permute-start(bf16[64,128]{1,0:T(8,128)(2,1)S(1)} %copy-done.3), channel_id=1, source_target_pairs={{4,5},{5,13},{6,7},{7,15},{12,20},{13,28},{14,22},{15,30},{20,21},... | collective-permute-start | bytes 49160 | tf_op jit(solution)/shard_map/ppermute | solution.py:229
  10.4 10.0 %collective-permute-start.3 = (f32[8]{0:T(128)S(1)}, f32[8]{0:T(128)S(1)}, u32[]{:S(2)}, u32[]{:S(2)}) collective-permute-start(f32[8]{0:T(128)S(1)} %pad_maximum_fusion.1), channel_id=1, source_target_pairs={{0,0},{1,64},{2,2},{3,66},{4,4},{5,68},{6,6},{7,70},{8,8},{9,72},{... | collective-permute-start | bytes 104 | tf_op jit(solution)/shard_map/ppermute | solution.py:221
  18.4 16.2 %collective-permute-start = (bf16[6,128,128]{2,1,0:T(8,128)(2,1)S(1)}, bf16[6,128,128]{2,1,0:T(8,128)(2,1)S(1)}, u32[]{:S(2)}, u32[]{:S(2)}) collective-permute-start(bf16[6,128,128]{2,1,0:T(8,128)(2,1)S(1)} %select_select_fusion), channel_id=1, source_target_pairs={{0,0},{1,64},{2,2},{3,66},{4,4},{5,68},{6,6},{7,70},{8,8},{9,72},{... | collective-permute-start | bytes 589832 | tf_op jit(solution)/shard_map/ppermute | solution.py:219
  68.1 6.6 %collective-permute-start.4 = (bf16[8,3,3,128,128]{4,3,2,1,0:T(8,128)(2,1)}, bf16[8,3,3,128,128]{4,3,2,1,0:T(8,128)(2,1)S(1)}, u32[]{:S(2)}, u32[]{:S(2)}) collective-permute-start(bf16[8,3,3,128,128]{4,3,2,1,0:T(8,128)(2,1)} %all-gather.2.cloned.1.call-done.refs_2_), channel_id=1, source_target_pairs={{0,64},{64,0},{1,65},{65,1},{2,66},{66,2},{3,67},{67,3},{4,68},{68... | collective-permute-start | bytes 7077896 | tf_op jit(solution)/shard_map/ppermute | solution.py:237
  74.8 1.7 copy-start
  79.1 11.5 %collective-permute-start.5 = (bf16[2,2,128,256]{3,2,1,0:T(8,128)(2,1)S(1)}, bf16[2,2,128,256]{3,2,1,0:T(8,128)(2,1)S(1)}, u32[]{:S(2)}, u32[]{:S(2)}) collective-permute-start(bf16[2,2,128,256]{3,2,1,0:T(8,128)(2,1)S(1)} %get-tuple-element.30), channel_id=1, source_target_pairs={{0,1},{1,16},{16,17},{17,32},{32,33},{33,48},{48,49},{2,3},{3,18},... | collective-permute-start | bytes 786440 | tf_op jit(solution)/shard_map/ppermute | solution.py:269
  94.0 10.6 %collective-permute-start.6 = (bf16[2,2,128,256]{3,2,1,0:T(8,128)(2,1)S(1)}, bf16[2,2,128,256]{3,2,1,0:T(8,128)(2,1)S(1)}, u32[]{:S(2)}, u32[]{:S(2)}) collective-permute-start(bf16[2,2,128,256]{3,2,1,0:T(8,128)(2,1)S(1)} %get-tuple-element.34), channel_id=1, source_target_pairs={{0,1},{1,16},{16,17},{17,32},{32,33},{33,48},{48,49},{2,3},{3,18},... | collective-permute-start | bytes 786440 | tf_op jit(solution)/shard_map/ppermute | solution.py:269
  108.0 9.7 %collective-permute-start.7 = (bf16[2,2,128,256]{3,2,1,0:T(8,128)(2,1)S(1)}, bf16[2,2,128,256]{3,2,1,0:T(8,128)(2,1)S(1)}, u32[]{:S(2)}, u32[]{:S(2)}) collective-permute-start(bf16[2,2,128,256]{3,2,1,0:T(8,128)(2,1)S(1)} %get-tuple-element.38), channel_id=1, source_target_pairs={{0,1},{1,16},{16,17},{17,32},{32,33},{33,48},{48,49},{2,3},{3,18},... | collective-permute-start | bytes 786440 | tf_op jit(solution)/shard_map/ppermute | solution.py:269
  121.0 7.8 %collective-permute-start.8 = (bf16[1,2,128,256]{3,2,1,0:T(8,128)(2,1)S(1)}, bf16[1,2,128,256]{3,2,1,0:T(8,128)(2,1)S(1)}, u32[]{:S(2)}, u32[]{:S(2)}) collective-permute-start(bf16[1,2,128,256]{3,2,1,0:T(8,128)(2,1)S(1)} %get-tuple-element.41), channel_id=1, source_target_pairs={{0,1},{1,16},{16,17},{17,32},{32,33},{33,48},{48,49},{2,3},{3,18},... | collective-permute-start | bytes 393224 | tf_op jit(solution)/shard_map/ppermute | solution.py:302
Sparse Core Ops, SparseCore 0:
  9.4 58.6 all-gather.1

commit v4 on v3

v4 whole, which is shorter than its diff:
```python
import functools
import itertools

import jax
import jax.numpy as jnp
from jax import lax
from jax.experimental import pallas as pl
from jax.experimental.pallas import tpu as pltpu
from jax.sharding import Mesh, PartitionSpec as P

BLOCK = 128
OWN = 4
HALF = 4
WINDOW = 2 * HALF
BEFORE = 3
STATES = 3
AXES = ("zhi", "core", "x", "zlo", "yl", "y0")
BF16 = jnp.bfloat16
F32 = jnp.float32


def device_number(zhi, core, x, zlo, yl, y0):
    return ((((zhi * 2 + core) * 4 + x) * 2 + zlo) * 4 + yl) * 2 + y0


def all_places():
    return itertools.product(range(4), range(2), range(4), range(2), range(4), range(2))


def to_groups():
    return [
        (device_number(zhi, core, x, zlo, yl, y0), device_number(x, y0, zhi, zlo, yl, core))
        for zhi, core, x, zlo, yl, y0 in all_places()
    ]


def rows_to_groups(halo):
    pairs = []
    for zhi, core, x, zlo, yl, y0 in all_places():
        group = 2 * x + zlo + halo
        if zhi == 0 and core == y0 and group < 8:
            target = device_number(0, core, group // 2, zlo, yl, group % 2)
            pairs.append((device_number(0, core, x, zlo, yl, y0), target))
    return pairs


SWAP = [(1, 2), (2, 1)]


def site_start(sectors, slice_at, half):
    return jnp.clip(OWN * slice_at - BEFORE + HALF * half, 0, sectors - HALF)


def ops_pieces(ops_blocks, shift, core):
    sectors = ops_blocks.shape[0]
    target = jnp.arange(sectors, dtype=jnp.int32) + shift
    inside = (target >= 0) & (target < sectors)
    masked = jnp.where(inside[:, None, None], ops_blocks, jnp.zeros((), BF16))
    lower = jnp.concatenate([jnp.zeros_like(masked[:OWN]), masked[:-OWN]], 0)
    return jnp.where(core == 0, lower, masked).reshape(4, 2 * OWN, BLOCK, BLOCK)


def phase_kernel(sites, steps, n_in, sources, targets, with_ops, *refs):
    whole, part, mine, other = refs[:4]
    ins = refs[4 : 4 + n_in]
    outs = refs[4 + n_in : -2]
    site_at, sems = refs[-2:]
    core = whole[0]
    shift = whole[1]

    def copies(slot, site, source):
        return [
            pltpu.make_async_copy(
                source.at[(site // 2) * 2 + half],
                site_at.at[slot, :, pl.ds(whole[2 + half], HALF)],
                sems.at[slot, half],
            )
            for half in range(2)
        ]

    @pl.when(whole[2] != 0)
    def _():
        site_at[:, :, :BEFORE] = jnp.zeros((len(sites), STATES, BEFORE, BLOCK, BLOCK), BF16)

    @pl.when(whole[3] != HALF)
    def _():
        site_at[:, :, WINDOW - 1] = jnp.zeros((len(sites), STATES, BLOCK, BLOCK), BF16)

    for slot, site in enumerate(sites):
        @pl.when(core == site % 2)
        def _():
            for copy in copies(slot, site, mine):
                copy.start()

        @pl.when(core != site % 2)
        def _():
            for copy in copies(slot, site, other):
                copy.start()

    done_sites = set()
    state = {}

    def get(site, sector):
        if (site, sector) in state:
            return state[site, sector]
        where, index = sources[site, sector]
        return ins[where][index]

    for site, first in steps:
        slot = sites.index(site)
        if site not in done_sites:
            done_sites.add(site)
            for copy in copies(slot, site, mine):
                copy.wait()
        for sector in (first, first + 1):
            total = None
            for s in range(STATES):
                block = get(site, sector - s)
                ops, env = block[:, :BLOCK], block[:, BLOCK:]
                left = site_at[slot, s, sector + BEFORE]
                cross = site_at[slot, jnp.clip(s - shift, 0, 2), sector + BEFORE]
                half_env = jnp.dot(env, left, preferred_element_type=F32)
                if with_ops(site):
                    right = site_at[slot, s, sector + BEFORE + shift]
                    both = jnp.dot(ops, jnp.concatenate([right, cross], 1), preferred_element_type=F32)
                    image = jnp.concatenate(
                        [part[s] * both[:, :BLOCK], half_env + part[3 + s] * both[:, BLOCK:]], 1
                    )
                else:
                    image = half_env + part[3 + s] * jnp.dot(ops, cross, preferred_element_type=F32)
                product = lax.dot_general(
                    left, image.astype(BF16), (((0,), (0,)), ((), ())), preferred_element_type=F32
                )
                total = product if total is None else total + product
            total = total.astype(BF16)
            state[site + 1, sector] = total
            for which, index in targets[site + 1, sector]:
                outs[which][index] = total


def run_phase(sites, steps, ins, sources, outs, targets, with_ops, whole, part, mine, other):
    blocks = 2 * len(steps) * (15 if with_ops(sites[0]) else 9)
    return pl.pallas_call(
        functools.partial(phase_kernel, sites, steps, len(ins), sources, targets, with_ops),
        out_shape=[jax.ShapeDtypeStruct(shape, BF16) for shape in outs],
        in_specs=[pl.BlockSpec(memory_space=pltpu.SMEM)] * 2
        + [pl.BlockSpec(memory_space=pl.ANY)] * 2
        + [pl.BlockSpec(memory_space=pltpu.VMEM)] * len(ins),
        out_specs=[pl.BlockSpec(memory_space=pltpu.VMEM)] * len(outs),
        scratch_shapes=[
            pltpu.VMEM((len(sites), STATES, WINDOW, BLOCK, BLOCK), BF16),
            pltpu.SemaphoreType.DMA((len(sites), 2)),
        ],
        compiler_params=pltpu.CompilerParams(vmem_limit_bytes=32 * 1024 * 1024),
        cost_estimate=pl.CostEstimate(flops=blocks * 2 * BLOCK**3, bytes_accessed=4 << 20, transcendentals=0),
    )(whole, part, mine, other, *ins)


def take_piece(start, site, piece, taken, sems):
    rows = HALF * BLOCK
    first = pl.multiple_of(start[0] * BLOCK, BLOCK)
    inward = [
        pltpu.make_async_copy(site.at[0, s, pl.ds(first, rows)], taken.at[s], sems.at[0, s]) for s in range(STATES)
    ]
    outward = [pltpu.make_async_copy(taken.at[s], piece.at[s], sems.at[1, s]) for s in range(STATES)]
    for copy in inward:
        copy.start()
    for before, after in zip(inward, outward):
        before.wait()
        after.start()
    for copy in outward:
        copy.wait()


def add_cores(over, summed):
    for site in range(4):
        both = (over[0, site].astype(F32) + over[1, site].astype(F32)).astype(BF16)
        for piece in range(8):
            summed[site, piece % 2, piece // 2] = both[piece]


def add_columns(over, summed):
    total = over[0].astype(F32)
    for source in range(1, 32):
        total += over[source].astype(F32)
    summed[...] = total.astype(BF16)


def add_up(kernel, array, out):
    return pl.pallas_call(
        kernel,
        out_shape=jax.ShapeDtypeStruct(out, BF16),
        in_specs=[pl.BlockSpec(memory_space=pltpu.VMEM)],
        out_specs=pl.BlockSpec(memory_space=pltpu.VMEM),
        compiler_params=pltpu.CompilerParams(vmem_limit_bytes=16 << 20),
        cost_estimate=pl.CostEstimate(flops=1 << 19, bytes_accessed=2 << 20, transcendentals=0),
    )(array)


def body(site_tensor, term_ops, env_rows, term_shift, keep_weight, env_weight):
    sectors = site_tensor.shape[2] // BLOCK
    core = lax.axis_index("core")
    at_zlo, at_yl, at_y0 = (lax.axis_index(name) for name in ("zlo", "yl", "y0"))
    group = lax.axis_index("x") * 2 + at_y0

    start = site_start(sectors, group, at_zlo).astype(jnp.int32).reshape(1)
    piece = pl.pallas_call(
        take_piece,
        out_shape=jax.ShapeDtypeStruct((STATES, HALF * BLOCK, BLOCK), BF16),
        in_specs=[pl.BlockSpec(memory_space=pltpu.SMEM), pl.BlockSpec(memory_space=pltpu.HBM)],
        out_specs=pl.BlockSpec(memory_space=pltpu.HBM),
        scratch_shapes=[pltpu.VMEM((STATES, HALF * BLOCK, BLOCK), BF16), pltpu.SemaphoreType.DMA((2, STATES))],
        compiler_params=pltpu.CompilerParams(vmem_limit_bytes=60 << 20),
        cost_estimate=pl.CostEstimate(flops=0, bytes_accessed=800_000, transcendentals=0),
    )(start, site_tensor).reshape(STATES, HALF, BLOCK, BLOCK)
    mine = lax.all_gather(piece, ("zhi", "zlo"))
    spots = [site_start(sectors, group, half) - (OWN * group - BEFORE) for half in range(2)]

    pieces = ops_pieces(term_ops[0].reshape(sectors, BLOCK, BLOCK), term_shift[0], core)
    over = lax.all_to_all(pieces, "x", 0, 0)
    ops_now = lax.dynamic_index_in_dim(over, lax.axis_index("zhi"), 0, keepdims=False)
    ops_now = lax.ppermute(ops_now, ("core", "y0"), [(0, 0), (1, 2), (2, 1), (3, 3)])
    figures = jnp.concatenate([keep_weight[0], env_weight[0], term_shift.astype(F32), jnp.zeros((1,), F32)])
    figures = lax.ppermute(figures, AXES, to_groups())
    shift = figures[6].astype(jnp.int32)
    partner = jnp.arange(STATES, dtype=jnp.int32) - shift
    factors = jnp.where((partner >= 0) & (partner <= 2), figures[3:6], 0.0)
    part = jnp.concatenate([figures[:3], factors])
    whole = jnp.stack([core, shift] + spots).astype(jnp.int32)

    piece = lax.ppermute(env_rows, AXES, rows_to_groups(0))
    halo = lax.ppermute(env_rows, AXES, rows_to_groups(1))
    env_now = jnp.zeros((2 * OWN * BLOCK, BLOCK), BF16)
    spot = at_yl * BLOCK + core * (BLOCK // 2)
    env_now = lax.dynamic_update_slice_in_dim(env_now, halo, spot, 0)
    env_now = lax.dynamic_update_slice_in_dim(env_now, piece, spot + OWN * BLOCK, 0)
    window = jnp.concatenate([ops_now, env_now.reshape(2 * OWN, BLOCK, BLOCK)], 2)

    mine, window, whole, part = lax.optimization_barrier((mine, window, whole, part))
    other = lax.ppermute(mine, "core", [(0, 1), (1, 0)])

    wide = (BLOCK, 2 * BLOCK)
    onward = [(i, i + 1) for i in range(7)]

    def before_last(site):
        return site < 7

    sources = {(0, sector): (0, sector + OWN) for sector in range(-OWN, OWN)}
    targets = {(1, -2): [], (1, -1): []}
    for sector in range(OWN):
        targets[1, sector] = [(0, sector)]
        targets[2, sector] = [(1, sector)] + ([(3, (0, sector - 2))] if sector >= 2 else [])
    for sector in (2, 3):
        targets[3, sector] = [(2, sector - 2), (3, (1, sector - 2))]
    first, full, upper, tails = run_phase(
        [0, 1, 2],
        [(0, 0), (0, 2), (0, -2), (1, 2), (1, 0), (2, 2)],
        [window],
        sources,
        [(OWN,) + wide, (OWN,) + wide, (2,) + wide, (2, 2) + wide],
        targets,
        before_last,
        whole,
        part,
        mine,
        other,
    )
    bonds = [first[:, :, BLOCK:], full[:, :, BLOCK:]]
    for site in (2, 4, 6):
        tails = lax.ppermute(tails, ("x", "y0"), onward)
        last = site == 6
        sources = {}
        for sector in (-2, -1):
            sources[site, sector] = (2, (0, sector + 2))
            sources[site + 1, sector] = (2, (1, sector + 2))
        for sector in range(OWN):
            sources[site, sector] = (0, sector)
        for sector in (2, 3):
            sources[site + 1, sector] = (1, sector - 2)
        targets = {}
        for sector in (0, 1):
            targets[site + 1, sector] = [(0, sector)]
        for sector in range(OWN):
            targets[site + 2, sector] = [(1, sector)]
        steps = [(site, 0), (site + 1, 2), (site + 1, 0)]
        outs = [(2,) + wide, (OWN,) + ((BLOCK, BLOCK) if last else wide)]
        if not last:
            for sector in (2, 3):
                targets[site + 2, sector].append((3, (0, sector - 2)))
                targets[site + 3, sector] = [(2, sector - 2), (3, (1, sector - 2))]
            steps.append((site + 2, 2))
            outs += [(2,) + wide, (2, 2) + wide]
        old_upper = upper
        lower, full, *rest = run_phase(
            [site, site + 1] + ([] if last else [site + 2]),
            steps,
            [full, upper, tails],
            sources,
            outs,
            targets,
            before_last,
            whole,
            part,
            mine,
            other,
        )
        bonds += [lower[:, :, BLOCK:], old_upper[:, :, BLOCK:], full if last else full[:, :, BLOCK:]]
        if not last:
            upper, tails = rest

    partial = jnp.concatenate(bonds, 0).reshape(4, 2, 8, BLOCK // 2, BLOCK).transpose(1, 0, 2, 3, 4)
    over = lax.all_to_all(partial, "core", 0, 0)
    summed = add_up(add_cores, over, (4, 2, 4, BLOCK // 2, BLOCK)).reshape(32, BLOCK // 2, BLOCK)
    over = lax.all_to_all(summed, ("zhi", "zlo", "yl"), 0, 0)
    summed = add_up(add_columns, over, (BLOCK // 2, BLOCK))
    swapped = lax.ppermute(summed, ("zlo", "y0"), SWAP)
    return jnp.where(at_zlo == at_y0, summed, swapped)[None]


def solution(mesh):
    parts = Mesh(mesh.devices.reshape(4, 2, 4, 2, 4, 2), AXES)
    seg, op = ("zhi", "core"), ("x", "zlo", "yl", "y0")
    placed = (P(seg, None, None, None), P(op, None, None), P(op, None), P(op), P(op, None), P(op, None))
    return jax.shard_map(body, mesh=parts, in_specs=placed, out_specs=P(seg, op, None), check_vma=False)
```

time: 179 us -> 165 us (0.922)
  the two profiles are of different devices: /device:TPU:2 before, /device:TPU:66 now
where the time goes in v4:
time: 165 us; the launch traced here: 164 us
  waiting for transfers between devices  67.9 us (41%)
  blocking collectives  33.9 us (21%)
  starting transfers between devices  25.9 us (16%)
  Pallas kernels  16.6 us (10%)
  between operations  15 us (9%)
  local copies, waits for them, and re-layouts  2.93 us (2%)
  other arithmetic  2.3 us (1%)
    all_gather x1, waiting for transfers between devices, body(): mine = lax.all_gather(piece, ('zhi', 'zlo'))  29.3 us
    all_to_all x1, blocking collectives, body(): over = lax.all_to_all(summed, ('zhi', 'zlo', 'yl'), 0, 0)  29.3 us
    ppermute x3, waiting for transfers between devices, body(): tails = lax.ppermute(tails, ('x', 'y0'), onward)  22.8 us
    pallas_call x4, Pallas kernels, run_phase(): pl.pallas_call(functools.partial(phase_kernel, sites, steps, len(ins), so...  14.5 us
    ppermute x3, starting transfers between devices, body(): tails = lax.ppermute(tails, ('x', 'y0'), onward)  7.81 us
    ppermute x1, waiting for transfers between devices, body(): other = lax.ppermute(mine, 'core', [(0, 1), (1, 0)])  5.84 us
    ppermute x1, waiting for transfers between devices, body(): figures = lax.ppermute(figures, AXES, to_groups())  5.28 us
    all_to_all x1, starting transfers between devices, body(): over = lax.all_to_all(pieces, 'x', 0, 0)  4.82 us
  transfers between devices with their start and end apart: 11, of which 7 were waited for; matrix products, arithmetic and copies ran while one was open for 2% of the time, Pallas kernels for 0%

profile of v4, /device:TPU:66, one launch (start us, length us, event | category | flops | bytes accessed | tf_op | source)
XLA Modules:
  0.0 164.4 jit_solution(4502041318166100769)
XLA Ops:
  6.5 1.8 %shard_map.64 = bf16[3,512,128]{2,1,0:T(8,128)(2,1)} custom-call(s32[1]{0:T(128)} %bitcast.start, bf16[1,3,4096,128]{3,2,1,0:T(8,128)(2,1)} %site.1), custom_call_target="tpu_custom_call" | custom-call | bytes 800000 | tf_op jit(solution)/shard_map/pallas_call | solution.py:207
  9.1 0.1 broadcast_select_fusion
  9.3 1.2 pad_select_fusion
  10.5 4.8 %all-to-all-start = ((bf16[4,8,128,128]{3,2,1,0:T(8,128)(2,1)}), bf16[4,8,128,128]{3,2,1,0:T(8,128)(2,1)S(1)}, u32[]{:S(2)}, u32[]{:S(2)}) async-start(bf16[4,8,128,128]{3,2,1,0:T(8,128)(2,1)} %bitcast.4), calls=%async_computation | async-start | bytes 2097152 | tf_op jit(solution)/shard_map/all_to_all | solution.py:220
  15.3 3.5 %collective-permute-start.2 = (bf16[64,128]{1,0:T(8,128)(2,1)S(1)}, bf16[64,128]{1,0:T(8,128)(2,1)S(1)}, u32[]{:S(2)}, u32[]{:S(2)}) collective-permute-start(bf16[64,128]{1,0:T(8,128)(2,1)S(1)} %copy-done.4), channel_id=1, source_target_pairs={{0,0},{2,2},{4,4},{6,6},{8,9},{10,11},{12,13},{14,15},{16,16},{18,... | collective-permute-start | bytes 49160 | tf_op jit(solution)/shard_map/ppermute | solution.py:231
  18.8 3.4 %collective-permute-start.1 = (bf16[64,128]{1,0:T(8,128)(2,1)S(1)}, bf16[64,128]{1,0:T(8,128)(2,1)S(1)}, u32[]{:S(2)}, u32[]{:S(2)}) collective-permute-start(bf16[64,128]{1,0:T(8,128)(2,1)S(1)} %copy-done.4), channel_id=1, source_target_pairs={{0,1},{2,3},{4,5},{6,7},{8,24},{10,26},{12,28},{14,30},{16,17},{18... | collective-permute-start | bytes 49160 | tf_op jit(solution)/shard_map/ppermute | solution.py:232
  22.3 1.9 %collective-permute-start.3 = (f32[8]{0:T(128)S(1)}, f32[8]{0:T(128)S(1)}, u32[]{:S(2)}, u32[]{:S(2)}) collective-permute-start(f32[8]{0:T(128)S(1)} %pad_maximum_fusion.1), channel_id=1, source_target_pairs={{0,0},{1,64},{2,2},{3,66},{4,4},{5,68},{6,6},{7,70},{8,8},{9,72},{... | collective-permute-start | bytes 104 | tf_op jit(solution)/shard_map/ppermute | solution.py:224
  24.2 5.3 %collective-permute-done.3 = f32[8]{0:T(128)S(1)} collective-permute-done((f32[8]{0:T(128)S(1)}, f32[8]{0:T(128)S(1)}, u32[]{:S(2)}, u32[]{:S(2)}) %collective-permute-start.3) | collective-permute-done | bytes 64 | tf_op jit(solution)/shard_map/ppermute | solution.py:224
  29.5 0.6 slice.43
  30.8 0.7 collective-permute-start
  31.5 0.1 pad_add_fusion.refs_0_
  31.8 29.3 %all-gather.2.cloned.1.call-done.refs_2_ = bf16[8,3,4,128,128]{4,3,2,1,0:T(8,128)(2,1)} async-done(((bf16[1,3,4,128,128]{4,3,2,1,0:T(8,128)(2,1)}), bf16[8,3,4,128,128]{4,3,2,1,0:T(8,128)(2,1)}) %all-gather.2.cloned.1.call-update) | async-done | bytes 3145744 | tf_op jit(solution)/shard_map/all_gather | solution.py:216
  61.1 1.9 %collective-permute-start.4 = (bf16[8,3,4,128,128]{4,3,2,1,0:T(8,128)(2,1)}, bf16[8,3,4,128,128]{4,3,2,1,0:T(8,128)(2,1)S(1)}, u32[]{:S(2)}, u32[]{:S(2)}) collective-permute-start(bf16[8,3,4,128,128]{4,3,2,1,0:T(8,128)(2,1)} %all-gather.2.cloned.1.call-done.refs_2_), channel_id=1, source_target_pairs={{0,64},{64,0},{1,65},{65,1},{2,66},{66,2},{3,67},{67,3},{4,68},{68... | collective-permute-start | bytes 9437192 | tf_op jit(solution)/shard_map/ppermute | solution.py:240
  63.0 5.8 %collective-permute-done.4.refs_3_ = bf16[8,3,4,128,128]{4,3,2,1,0:T(8,128)(2,1)S(1)} collective-permute-done((bf16[8,3,4,128,128]{4,3,2,1,0:T(8,128)(2,1)}, bf16[8,3,4,128,128]{4,3,2,1,0:T(8,128)(2,1)S(1)}, u32[]{:S(2)}, u32[]{:S(2)}) %collective-permute-start.4) | collective-permute-done | bytes 3145760 | tf_op jit(solution)/shard_map/ppermute | solution.py:240
  68.8 1.9 %copy-done = bf16[8,3,4,128,128]{4,3,2,1,0:T(8,128)(2,1)S(1)} copy-done((bf16[8,3,4,128,128]{4,3,2,1,0:T(8,128)(2,1)S(1)}, bf16[8,3,4,128,128]{4,3,2,1,0:T(8,128)(2,1)}, u32[]{:S(2)}) %copy-start) | copy-done | bytes 3145752
  70.7 4.7 %shard_map.65 = (bf16[4,128,256]{2,1,0:T(8,128)(2,1)S(1)}, bf16[4,128,256]{2,1,0:T(8,128)(2,1)S(1)}, bf16[2,128,256]{2,1,0:T(8,128)(2,1)S(1)}, bf16[2,2,128,256]{3,2,1,0:T(8,128)(2,1)S(1)}) custom-call(s32[4]{0:T(128)S(1)} %pad_add_fusion.refs_0_, f32[6]{0:T(128)S(1)} %pad_maximum_fusion.2.refs_1_, bf16[8,3,4,128,128]{4,3,2,1,0:T(8,128)(2,1)S(1)} %copy-done, ...), custom_call_target="tpu_custom_call" | custom-call | flops 754974720 | bytes 4194304 | tf_op jit(solution)/shard_map/pallas_call | solution.py:143
  75.4 3.4 %collective-permute-start.5 = (bf16[2,2,128,256]{3,2,1,0:T(8,128)(2,1)S(1)}, bf16[2,2,128,256]{3,2,1,0:T(8,128)(2,1)S(1)}, u32[]{:S(2)}, u32[]{:S(2)}) collective-permute-start(bf16[2,2,128,256]{3,2,1,0:T(8,128)(2,1)S(1)} %get-tuple-element.30), channel_id=1, source_target_pairs={{0,1},{1,16},{16,17},{17,32},{32,33},{33,48},{48,49},{2,3},{3,18},... | collective-permute-start | bytes 786440 | tf_op jit(solution)/shard_map/ppermute | solution.py:270
  78.9 7.7 %collective-permute-done.5.refs_6_ = bf16[2,2,128,256]{3,2,1,0:T(8,128)(2,1)S(1)} collective-permute-done((bf16[2,2,128,256]{3,2,1,0:T(8,128)(2,1)S(1)}, bf16[2,2,128,256]{3,2,1,0:T(8,128)(2,1)S(1)}, u32[]{:S(2)}, u32[]{:S(2)}) %collective-permute-start.5) | collective-permute-done | bytes 262176 | tf_op jit(solution)/shard_map/ppermute | solution.py:270
  86.6 3.7 %shard_map.66 = (bf16[2,128,256]{2,1,0:T(8,128)(2,1)S(1)}, bf16[4,128,256]{2,1,0:T(8,128)(2,1)S(1)}, bf16[2,128,256]{2,1,0:T(8,128)(2,1)S(1)}, bf16[2,2,128,256]{3,2,1,0:T(8,128)(2,1)S(1)}) custom-call(s32[4]{0:T(128)S(1)} %pad_add_fusion.refs_0_, f32[6]{0:T(128)S(1)} %pad_maximum_fusion.2.refs_1_, bf16[8,3,4,128,128]{4,3,2,1,0:T(8,128)(2,1)S(1)} %copy-done, ...), custom_call_target="tpu_custom_call" | custom-call | flops 503316480 | bytes 4194304 | tf_op jit(solution)/shard_map/pallas_call | solution.py:143
  90.2 2.5 %collective-permute-start.6 = (bf16[2,2,128,256]{3,2,1,0:T(8,128)(2,1)S(1)}, bf16[2,2,128,256]{3,2,1,0:T(8,128)(2,1)S(1)}, u32[]{:S(2)}, u32[]{:S(2)}) collective-permute-start(bf16[2,2,128,256]{3,2,1,0:T(8,128)(2,1)S(1)} %get-tuple-element.34), channel_id=1, source_target_pairs={{0,1},{1,16},{16,17},{17,32},{32,33},{33,48},{48,49},{2,3},{3,18},... | collective-permute-start | bytes 786440 | tf_op jit(solution)/shard_map/ppermute | solution.py:270
  92.8 7.7 %collective-permute-done.6.refs_6_ = bf16[2,2,128,256]{3,2,1,0:T(8,128)(2,1)S(1)} collective-permute-done((bf16[2,2,128,256]{3,2,1,0:T(8,128)(2,1)S(1)}, bf16[2,2,128,256]{3,2,1,0:T(8,128)(2,1)S(1)}, u32[]{:S(2)}, u32[]{:S(2)}) %collective-permute-start.6) | collective-permute-done | bytes 262176 | tf_op jit(solution)/shard_map/ppermute | solution.py:270
  100.6 3.7 %shard_map.67 = (bf16[2,128,256]{2,1,0:T(8,128)(2,1)S(1)}, bf16[4,128,256]{2,1,0:T(8,128)(2,1)S(1)}, bf16[2,128,256]{2,1,0:T(8,128)(2,1)S(1)}, bf16[2,2,128,256]{3,2,1,0:T(8,128)(2,1)S(1)}) custom-call(s32[4]{0:T(128)S(1)} %pad_add_fusion.refs_0_, f32[6]{0:T(128)S(1)} %pad_maximum_fusion.2.refs_1_, bf16[8,3,4,128,128]{4,3,2,1,0:T(8,128)(2,1)S(1)} %copy-done, ...), custom_call_target="tpu_custom_call" | custom-call | flops 503316480 | bytes 4194304 | tf_op jit(solution)/shard_map/pallas_call | solution.py:143
  104.2 1.9 %collective-permute-start.7 = (bf16[2,2,128,256]{3,2,1,0:T(8,128)(2,1)S(1)}, bf16[2,2,128,256]{3,2,1,0:T(8,128)(2,1)S(1)}, u32[]{:S(2)}, u32[]{:S(2)}) collective-permute-start(bf16[2,2,128,256]{3,2,1,0:T(8,128)(2,1)S(1)} %get-tuple-element.38), channel_id=1, source_target_pairs={{0,1},{1,16},{16,17},{17,32},{32,33},{33,48},{48,49},{2,3},{3,18},... | collective-permute-start | bytes 786440 | tf_op jit(solution)/shard_map/ppermute | solution.py:270
  106.2 7.4 %collective-permute-done.7.refs_6_ = bf16[2,2,128,256]{3,2,1,0:T(8,128)(2,1)S(1)} collective-permute-done((bf16[2,2,128,256]{3,2,1,0:T(8,128)(2,1)S(1)}, bf16[2,2,128,256]{3,2,1,0:T(8,128)(2,1)S(1)}, u32[]{:S(2)}, u32[]{:S(2)}) %collective-permute-start.7) | collective-permute-done | bytes 262176 | tf_op jit(solution)/shard_map/ppermute | solution.py:270
  113.6 2.5 %shard_map.68 = (bf16[2,128,256]{2,1,0:T(8,128)(2,1)S(1)}, bf16[4,128,128]{2,1,0:T(8,128)(2,1)S(1)}) custom-call(s32[4]{0:T(128)S(1)} %pad_add_fusion.refs_0_, f32[6]{0:T(128)S(1)} %pad_maximum_fusion.2.refs_1_, bf16[8,3,4,128,128]{4,3,2,1,0:T(8,128)(2,1)S(1)} %copy-done, bf16[8,3,4,128,128]{4,3,2,1,0:T(8,128)(2,1)S(1)} %collective-permute-done.4.refs_3_, ...), custom_call_target="tpu_custom_call" | custom-call | flops 377487360 | bytes 4194304 | tf_op jit(solution)/shard_map/pallas_call | solution.py:143
  116.3 4.6 %all_to_all.15.over = bf16[2,4,8,64,128]{4,3,2,1,0:T(8,128)(2,1)S(1)} all-to-all(bf16[2,4,8,64,128]{4,3,2,1,0:T(8,128)(2,1)S(1)} %bitcast.25), channel_id=1, replica_groups=mesh['zhi'=4,'core'=2,'x'=4,'zlo'=2,'yl'=4,'y0'=2] {'core'}, dimensions={0} | all-to-all | bytes 2097152 | tf_op jit(solution)/shard_map/all_to_all | solution.py:312
  120.9 0.1 shard_map.69
  121.0 29.3 %all_to_all.16.over = bf16[32,64,128]{2,1,0:T(8,128)(2,1)S(1)} all-to-all(bf16[32,64,128]{2,1,0:T(8,128)(2,1)S(1)} %bitcast.22), channel_id=1, replica_groups=mesh['zhi'=4,'core'=2,'x'=4,'zlo'=2,'yl'=4,'y0'=2] {'zhi','zlo','yl'}, dimensions={0} | all-to-all | bytes 1048576 | tf_op jit(solution)/shard_map/all_to_all | solution.py:314
  150.3 0.1 shard_map.70
  150.4 1.9 %collective-permute-start.8 = (bf16[64,128]{1,0:T(8,128)(2,1)S(1)}, bf16[64,128]{1,0:T(8,128)(2,1)S(1)}, u32[]{:S(2)}, u32[]{:S(2)}) collective-permute-start(bf16[64,128]{1,0:T(8,128)(2,1)S(1)} %shard_map.70), channel_id=1, source_target_pairs={{1,8},{8,1},{3,10},{10,3},{5,12},{12,5},{7,14},{14,7},{17,24},{24,... | collective-permute-start | bytes 49160 | tf_op jit(solution)/shard_map/ppermute | solution.py:316
  152.3 4.6 %collective-permute-done.8 = bf16[64,128]{1,0:T(8,128)(2,1)S(1)} collective-permute-done((bf16[64,128]{1,0:T(8,128)(2,1)S(1)}, bf16[64,128]{1,0:T(8,128)(2,1)S(1)}, u32[]{:S(2)}, u32[]{:S(2)}) %collective-permute-start.8) | collective-permute-done | bytes 16416 | tf_op jit(solution)/shard_map/ppermute | solution.py:316
  156.9 0.6 select_bitcast_fusion
  (37 shorter events, 0.8 us)
Async XLA Ops:
  6.5 2.5 %copy-start.1 = (bf16[1,4096,128]{2,1,0:T(8,128)(2,1)S(1)}, bf16[1,4096,128]{2,1,0:T(8,128)(2,1)}, u32[]{:S(2)}) copy-start(bf16[1,4096,128]{2,1,0:T(8,128)(2,1)} %param.7) | copy-start | bytes 3145732
  6.5 54.6 %all-gather.2.cloned.1.call-start = ((), (), s32[]{:S(2)}) async-start(), calls=%async_computation.3 | async-start | bytes 3538944 | tf_op jit(solution)/shard_map/all_gather | solution.py:216
  9.2 6.1 %copy-start.4 = (bf16[64,128]{1,0:T(8,128)(2,1)S(1)}, bf16[64,128]{1,0:T(8,128)(2,1)}, u32[]{:S(2)}) copy-start(bf16[64,128]{1,0:T(8,128)(2,1)} %param.8) | copy-start | bytes 49156
  9.2 12.9 %copy-start.2 = (f32[1,3]{1,0:T(1,128)S(1)}, f32[1,3]{1,0:T(1,128)}, u32[]{:S(2)}) copy-start(f32[1,3]{1,0:T(1,128)} %param.11) | copy-start | bytes 40
  9.2 12.9 %copy-start.3 = (f32[1,3]{1,0:T(1,128)S(1)}, f32[1,3]{1,0:T(1,128)}, u32[]{:S(2)}) copy-start(f32[1,3]{1,0:T(1,128)} %param.10) | copy-start | bytes 40
  10.5 20.3 %all-to-all-start = ((bf16[4,8,128,128]{3,2,1,0:T(8,128)(2,1)}), bf16[4,8,128,128]{3,2,1,0:T(8,128)(2,1)S(1)}, u32[]{:S(2)}, u32[]{:S(2)}) async-start(bf16[4,8,128,128]{3,2,1,0:T(8,128)(2,1)} %bitcast.4), calls=%async_computation | async-start | bytes 2097152 | tf_op jit(solution)/shard_map/all_to_all | solution.py:220
  15.3 16.3 %collective-permute-start.2 = (bf16[64,128]{1,0:T(8,128)(2,1)S(1)}, bf16[64,128]{1,0:T(8,128)(2,1)S(1)}, u32[]{:S(2)}, u32[]{:S(2)}) collective-permute-start(bf16[64,128]{1,0:T(8,128)(2,1)S(1)} %copy-done.4), channel_id=1, source_target_pairs={{0,0},{2,2},{4,4},{6,6},{8,9},{10,11},{12,13},{14,15},{16,16},{18,... | collective-permute-start | bytes 49160 | tf_op jit(solution)/shard_map/ppermute | solution.py:231
  18.8 12.8 %collective-permute-start.1 = (bf16[64,128]{1,0:T(8,128)(2,1)S(1)}, bf16[64,128]{1,0:T(8,128)(2,1)S(1)}, u32[]{:S(2)}, u32[]{:S(2)}) collective-permute-start(bf16[64,128]{1,0:T(8,128)(2,1)S(1)} %copy-done.4), channel_id=1, source_target_pairs={{0,1},{2,3},{4,5},{6,7},{8,24},{10,26},{12,28},{14,30},{16,17},{18... | collective-permute-start | bytes 49160 | tf_op jit(solution)/shard_map/ppermute | solution.py:232
  22.3 7.2 %collective-permute-start.3 = (f32[8]{0:T(128)S(1)}, f32[8]{0:T(128)S(1)}, u32[]{:S(2)}, u32[]{:S(2)}) collective-permute-start(f32[8]{0:T(128)S(1)} %pad_maximum_fusion.1), channel_id=1, source_target_pairs={{0,0},{1,64},{2,2},{3,66},{4,4},{5,68},{6,6},{7,70},{8,8},{9,72},{... | collective-permute-start | bytes 104 | tf_op jit(solution)/shard_map/ppermute | solution.py:224
  30.8 0.9 collective-permute-start
  61.1 7.8 %collective-permute-start.4 = (bf16[8,3,4,128,128]{4,3,2,1,0:T(8,128)(2,1)}, bf16[8,3,4,128,128]{4,3,2,1,0:T(8,128)(2,1)S(1)}, u32[]{:S(2)}, u32[]{:S(2)}) collective-permute-start(bf16[8,3,4,128,128]{4,3,2,1,0:T(8,128)(2,1)} %all-gather.2.cloned.1.call-done.refs_2_), channel_id=1, source_target_pairs={{0,64},{64,0},{1,65},{65,1},{2,66},{66,2},{3,67},{67,3},{4,68},{68... | collective-permute-start | bytes 9437192 | tf_op jit(solution)/shard_map/ppermute | solution.py:240
  68.8 1.9 %copy-start = (bf16[8,3,4,128,128]{4,3,2,1,0:T(8,128)(2,1)S(1)}, bf16[8,3,4,128,128]{4,3,2,1,0:T(8,128)(2,1)}, u32[]{:S(2)}) copy-start(bf16[8,3,4,128,128]{4,3,2,1,0:T(8,128)(2,1)} %all-gather.2.cloned.1.call-done.refs_2_) | copy-start | bytes 9437188
  75.4 11.1 %collective-permute-start.5 = (bf16[2,2,128,256]{3,2,1,0:T(8,128)(2,1)S(1)}, bf16[2,2,128,256]{3,2,1,0:T(8,128)(2,1)S(1)}, u32[]{:S(2)}, u32[]{:S(2)}) collective-permute-start(bf16[2,2,128,256]{3,2,1,0:T(8,128)(2,1)S(1)} %get-tuple-element.30), channel_id=1, source_target_pairs={{0,1},{1,16},{16,17},{17,32},{32,33},{33,48},{48,49},{2,3},{3,18},... | collective-permute-start | bytes 786440 | tf_op jit(solution)/shard_map/ppermute | solution.py:270
  90.2 10.3 %collective-permute-start.6 = (bf16[2,2,128,256]{3,2,1,0:T(8,128)(2,1)S(1)}, bf16[2,2,128,256]{3,2,1,0:T(8,128)(2,1)S(1)}, u32[]{:S(2)}, u32[]{:S(2)}) collective-permute-start(bf16[2,2,128,256]{3,2,1,0:T(8,128)(2,1)S(1)} %get-tuple-element.34), channel_id=1, source_target_pairs={{0,1},{1,16},{16,17},{17,32},{32,33},{33,48},{48,49},{2,3},{3,18},... | collective-permute-start | bytes 786440 | tf_op jit(solution)/shard_map/ppermute | solution.py:270
  104.2 9.4 %collective-permute-start.7 = (bf16[2,2,128,256]{3,2,1,0:T(8,128)(2,1)S(1)}, bf16[2,2,128,256]{3,2,1,0:T(8,128)(2,1)S(1)}, u32[]{:S(2)}, u32[]{:S(2)}) collective-permute-start(bf16[2,2,128,256]{3,2,1,0:T(8,128)(2,1)S(1)} %get-tuple-element.38), channel_id=1, source_target_pairs={{0,1},{1,16},{16,17},{17,32},{32,33},{33,48},{48,49},{2,3},{3,18},... | collective-permute-start | bytes 786440 | tf_op jit(solution)/shard_map/ppermute | solution.py:270
  150.4 6.5 %collective-permute-start.8 = (bf16[64,128]{1,0:T(8,128)(2,1)S(1)}, bf16[64,128]{1,0:T(8,128)(2,1)S(1)}, u32[]{:S(2)}, u32[]{:S(2)}) collective-permute-start(bf16[64,128]{1,0:T(8,128)(2,1)S(1)} %shard_map.70), channel_id=1, source_target_pairs={{1,8},{8,1},{3,10},{10,3},{5,12},{12,5},{7,14},{14,7},{17,24},{24,... | collective-permute-start | bytes 49160 | tf_op jit(solution)/shard_map/ppermute | solution.py:316
Sparse Core Ops, SparseCore 0:
  9.4 51.6 all-gather.1

commit v5 on v4

--- a/solution.py
+++ b/solution.py
@@ -44,9 +44,6 @@
     return pairs
 
 
-SWAP = [(1, 2), (2, 1)]
-
-
 def site_start(sectors, slice_at, half):
     return jnp.clip(OWN * slice_at - BEFORE + HALF * half, 0, sectors - HALF)
 
@@ -60,18 +57,21 @@
     return jnp.where(core == 0, lower, masked).reshape(4, 2 * OWN, BLOCK, BLOCK)
 
 
-def phase_kernel(sites, steps, n_in, sources, targets, with_ops, *refs):
-    whole, part, mine, other = refs[:4]
-    ins = refs[4 : 4 + n_in]
-    outs = refs[4 + n_in : -2]
+def phase_kernel(sites, steps, halves, n_in, sources, targets, with_ops, *refs):
+    whole, part = refs[:2]
+    blocks = dict(zip(halves, zip(refs[2::2], refs[3::2])))
+    refs = refs[2 + 2 * len(halves) :]
+    ins = refs[:n_in]
+    outs = refs[n_in:-2]
     site_at, sems = refs[-2:]
     core = whole[0]
     shift = whole[1]
 
-    def copies(slot, site, source):
+    def copies(slot, site, which):
+        source = blocks[site // 4][which]
         return [
             pltpu.make_async_copy(
-                source.at[(site // 2) * 2 + half],
+                source.at[(site % 4 // 2) * 2 + half],
                 site_at.at[slot, :, pl.ds(whole[2 + half], HALF)],
                 sems.at[slot, half],
             )
@@ -89,12 +89,12 @@
     for slot, site in enumerate(sites):
         @pl.when(core == site % 2)
         def _():
-            for copy in copies(slot, site, mine):
+            for copy in copies(slot, site, 0):
                 copy.start()
 
         @pl.when(core != site % 2)
         def _():
-            for copy in copies(slot, site, other):
+            for copy in copies(slot, site, 1):
                 copy.start()
 
     done_sites = set()
@@ -110,24 +110,25 @@
         slot = sites.index(site)
         if site not in done_sites:
             done_sites.add(site)
-            for copy in copies(slot, site, mine):
+            for copy in copies(slot, site, 0):
                 copy.wait()
         for sector in (first, first + 1):
             total = None
             for s in range(STATES):
-                block = get(site, sector - s)
-                ops, env = block[:, :BLOCK], block[:, BLOCK:]
                 left = site_at[slot, s, sector + BEFORE]
                 cross = site_at[slot, jnp.clip(s - shift, 0, 2), sector + BEFORE]
-                half_env = jnp.dot(env, left, preferred_element_type=F32)
+                cross = (part[3 + s] * cross.astype(F32)).astype(BF16)
                 if with_ops(site):
                     right = site_at[slot, s, sector + BEFORE + shift]
-                    both = jnp.dot(ops, jnp.concatenate([right, cross], 1), preferred_element_type=F32)
-                    image = jnp.concatenate(
-                        [part[s] * both[:, :BLOCK], half_env + part[3 + s] * both[:, BLOCK:]], 1
-                    )
+                    upper = jnp.concatenate([right, cross], 1)
+                    lower = jnp.concatenate([jnp.zeros_like(left), left], 1)
                 else:
-                    image = half_env + part[3 + s] * jnp.dot(ops, cross, preferred_element_type=F32)
+                    upper, lower = cross, left
+                image = jnp.dot(
+                    get(site, sector - s), jnp.concatenate([upper, lower], 0), preferred_element_type=F32
+                )
+                if with_ops(site):
+                    image = jnp.concatenate([part[s] * image[:, :BLOCK], image[:, BLOCK:]], 1)
                 product = lax.dot_general(
                     left, image.astype(BF16), (((0,), (0,)), ((), ())), preferred_element_type=F32
                 )
@@ -138,13 +139,14 @@
                 outs[which][index] = total
 
 
-def run_phase(sites, steps, ins, sources, outs, targets, with_ops, whole, part, mine, other):
+def run_phase(sites, steps, ins, sources, outs, targets, with_ops, whole, part, pairs):
+    halves = sorted({site // 4 for site in sites})
     blocks = 2 * len(steps) * (15 if with_ops(sites[0]) else 9)
     return pl.pallas_call(
-        functools.partial(phase_kernel, sites, steps, len(ins), sources, targets, with_ops),
+        functools.partial(phase_kernel, sites, steps, halves, len(ins), sources, targets, with_ops),
         out_shape=[jax.ShapeDtypeStruct(shape, BF16) for shape in outs],
         in_specs=[pl.BlockSpec(memory_space=pltpu.SMEM)] * 2
-        + [pl.BlockSpec(memory_space=pl.ANY)] * 2
+        + [pl.BlockSpec(memory_space=pl.ANY)] * (2 * len(halves))
         + [pl.BlockSpec(memory_space=pltpu.VMEM)] * len(ins),
         out_specs=[pl.BlockSpec(memory_space=pltpu.VMEM)] * len(outs),
         scratch_shapes=[
@@ -153,7 +155,7 @@
         ],
         compiler_params=pltpu.CompilerParams(vmem_limit_bytes=32 * 1024 * 1024),
         cost_estimate=pl.CostEstimate(flops=blocks * 2 * BLOCK**3, bytes_accessed=4 << 20, transcendentals=0),
-    )(whole, part, mine, other, *ins)
+    )(whole, part, *(array for half in halves for array in pairs[half]), *ins)
 
 
 def take_piece(start, site, piece, taken, sems):
@@ -172,29 +174,30 @@
         copy.wait()
 
 
-def add_cores(over, summed):
+def add_cores(place, over, summed):
     for site in range(4):
         both = (over[0, site].astype(F32) + over[1, site].astype(F32)).astype(BF16)
-        for piece in range(8):
-            summed[site, piece % 2, piece // 2] = both[piece]
+        for zlo in range(2):
+            summed[site, zlo] = jnp.where(place[0] == zlo, both, jnp.zeros_like(both))
 
 
 def add_columns(over, summed):
     total = over[0].astype(F32)
-    for source in range(1, 32):
+    for source in range(1, 64):
         total += over[source].astype(F32)
     summed[...] = total.astype(BF16)
 
 
-def add_up(kernel, array, out):
+def add_up(kernel, ins, out):
+    spaces = [pltpu.SMEM if array.ndim == 1 else pltpu.VMEM for array in ins]
     return pl.pallas_call(
         kernel,
         out_shape=jax.ShapeDtypeStruct(out, BF16),
-        in_specs=[pl.BlockSpec(memory_space=pltpu.VMEM)],
+        in_specs=[pl.BlockSpec(memory_space=space) for space in spaces],
         out_specs=pl.BlockSpec(memory_space=pltpu.VMEM),
         compiler_params=pltpu.CompilerParams(vmem_limit_bytes=16 << 20),
         cost_estimate=pl.CostEstimate(flops=1 << 19, bytes_accessed=2 << 20, transcendentals=0),
-    )(array)
+    )(*ins)
 
 
 def body(site_tensor, term_ops, env_rows, term_shift, keep_weight, env_weight):
@@ -237,7 +240,8 @@
     window = jnp.concatenate([ops_now, env_now.reshape(2 * OWN, BLOCK, BLOCK)], 2)
 
     mine, window, whole, part = lax.optimization_barrier((mine, window, whole, part))
-    other = lax.ppermute(mine, "core", [(0, 1), (1, 0)])
+    mine_low, mine_high = mine[:4], mine[4:]
+    pairs = [(mine_low, lax.ppermute(mine_low, "core", [(0, 1), (1, 0)]))]
 
     wide = (BLOCK, 2 * BLOCK)
     onward = [(i, i + 1) for i in range(7)]
@@ -262,9 +266,10 @@
         before_last,
         whole,
         part,
-        mine,
-        other,
+        pairs,
     )
+    mine_high, tails = lax.optimization_barrier((mine_high, tails))
+    pairs.append((mine_high, lax.ppermute(mine_high, "core", [(0, 1), (1, 0)])))
     bonds = [first[:, :, BLOCK:], full[:, :, BLOCK:]]
     for site in (2, 4, 6):
         tails = lax.ppermute(tails, ("x", "y0"), onward)
@@ -301,8 +306,7 @@
             before_last,
             whole,
             part,
-            mine,
-            other,
+            pairs,
         )
         bonds += [lower[:, :, BLOCK:], old_upper[:, :, BLOCK:], full if last else full[:, :, BLOCK:]]
         if not last:
@@ -310,11 +314,10 @@
 
     partial = jnp.concatenate(bonds, 0).reshape(4, 2, 8, BLOCK // 2, BLOCK).transpose(1, 0, 2, 3, 4)
     over = lax.all_to_all(partial, "core", 0, 0)
-    summed = add_up(add_cores, over, (4, 2, 4, BLOCK // 2, BLOCK)).reshape(32, BLOCK // 2, BLOCK)
-    over = lax.all_to_all(summed, ("zhi", "zlo", "yl"), 0, 0)
-    summed = add_up(add_columns, over, (BLOCK // 2, BLOCK))
-    swapped = lax.ppermute(summed, ("zlo", "y0"), SWAP)
-    return jnp.where(at_zlo == at_y0, summed, swapped)[None]
+    place = at_y0.astype(jnp.int32).reshape(1)
+    summed = add_up(add_cores, [place, over], (4, 2, 8, BLOCK // 2, BLOCK)).reshape(64, BLOCK // 2, BLOCK)
+    over = lax.all_to_all(summed, ("zhi", "zlo", "yl", "y0"), 0, 0)
+    return add_up(add_columns, [over], (BLOCK // 2, BLOCK))[None]
 
 
 def solution(mesh):

time: 165 us -> 168 us (1.018)
  the two profiles are of different devices: /device:TPU:66 before, /device:TPU:2 now
where the time goes in v5:
time: 168 us
  waiting for transfers between devices  63 us (38%)
  blocking collectives  44.3 us (26%)
  starting transfers between devices  25.8 us (15%)
  between operations  15.1 us (9%)
  Pallas kernels  14.2 us (8%)
  local copies, waits for them, and re-layouts  3.4 us (2%)
  other arithmetic  1.68 us (1%)
    all_to_all x1, blocking collectives, body(): over = lax.all_to_all(summed, ('zhi', 'zlo', 'yl', 'y0'), 0, 0)  39.7 us
    all_gather x1, waiting for transfers between devices, body(): mine = lax.all_gather(piece, ('zhi', 'zlo'))  30.8 us
    ppermute x3, waiting for transfers between devices, body(): tails = lax.ppermute(tails, ('x', 'y0'), onward)  23.5 us
    pallas_call x4, Pallas kernels, run_phase(): pl.pallas_call(functools.partial(phase_kernel, sites, steps, halves, len(...  11.4 us
    all_to_all x1, starting transfers between devices, body(): over = lax.all_to_all(pieces, 'x', 0, 0)  9.52 us
    ppermute x3, starting transfers between devices, body(): tails = lax.ppermute(tails, ('x', 'y0'), onward)  7.82 us
    ppermute x1, waiting for transfers between devices, body(): figures = lax.ppermute(figures, AXES, to_groups())  5.28 us
    all_to_all x1, blocking collectives, body(): over = lax.all_to_all(partial, 'core', 0, 0)  4.58 us
  transfers between devices with their start and end apart: 11, of which 6 were waited for; matrix products, arithmetic and copies ran while one was open for 2% of the time, Pallas kernels for 0%

profile of v5, /device:TPU:2, one launch (start us, length us, event | category | flops | bytes accessed | tf_op | source)
XLA Modules:
  0.0 167.5 jit_solution(1447573320422964303)
XLA Ops:
  6.5 1.8 %shard_map.64 = bf16[3,512,128]{2,1,0:T(8,128)(2,1)} custom-call(s32[1]{0:T(128)} %bitcast.1.start, bf16[1,3,4096,128]{3,2,1,0:T(8,128)(2,1)} %site.1), custom_call_target="tpu_custom_call" | custom-call | bytes 800000 | tf_op jit(solution)/shard_map/pallas_call | solution.py:210
  9.1 0.1 broadcast_select_fusion
  9.3 1.2 pad_select_fusion
  10.5 9.5 %all-to-all-start = ((bf16[4,8,128,128]{3,2,1,0:T(8,128)(2,1)}), bf16[4,8,128,128]{3,2,1,0:T(8,128)(2,1)S(1)}, u32[]{:S(2)}, u32[]{:S(2)}) async-start(bf16[4,8,128,128]{3,2,1,0:T(8,128)(2,1)} %bitcast.5), calls=%async_computation | async-start | bytes 2097152 | tf_op jit(solution)/shard_map/all_to_all | solution.py:223
  20.0 1.3 collective-permute-start.1
  21.3 0.7 collective-permute-start.2
  22.0 0.1 pad_maximum_fusion.1
  22.0 1.9 %collective-permute-start.3 = (f32[8]{0:T(128)S(1)}, f32[8]{0:T(128)S(1)}, u32[]{:S(2)}, u32[]{:S(2)}) collective-permute-start(f32[8]{0:T(128)S(1)} %pad_maximum_fusion.1), channel_id=1, source_target_pairs={{0,0},{1,64},{2,2},{3,66},{4,4},{5,68},{6,6},{7,70},{8,8},{9,72},{... | collective-permute-start | bytes 104 | tf_op jit(solution)/shard_map/ppermute | solution.py:227
  24.0 5.3 %collective-permute-done.3 = f32[8]{0:T(128)S(1)} collective-permute-done((f32[8]{0:T(128)S(1)}, f32[8]{0:T(128)S(1)}, u32[]{:S(2)}, u32[]{:S(2)}) %collective-permute-start.3) | collective-permute-done | bytes 64 | tf_op jit(solution)/shard_map/ppermute | solution.py:227
  29.3 0.7 slice.49
  30.7 0.1 pad_maximum_fusion.2.refs_1_
  30.8 0.7 collective-permute-start
  31.5 0.1 pad_add_fusion.refs_0_
  31.7 30.8 %all-gather.2.cloned.1.call-done = bf16[8,3,4,128,128]{4,3,2,1,0:T(8,128)(2,1)} async-done(((bf16[1,3,4,128,128]{4,3,2,1,0:T(8,128)(2,1)}), bf16[8,3,4,128,128]{4,3,2,1,0:T(8,128)(2,1)}) %all-gather.2.cloned.1.call-update) | async-done | bytes 3145744 | tf_op jit(solution)/shard_map/all_gather | solution.py:219
  62.5 2.3 %fusion = (bf16[4,3,4,128,128]{4,3,2,1,0:T(8,128)(2,1)S(1)}, bf16[4,3,4,128,128]{4,3,2,1,0:T(8,128)(2,1)S(1)}) fusion(bf16[8,3,4,128,128]{4,3,2,1,0:T(8,128)(2,1)} %all-gather.2.cloned.1.call-done), kind=kLoop, calls=%fused_computation.23 | loop fusion | bytes 6291456 | tf_op jit(solution)/shard_map/slice | solution.py:243
  64.8 1.9 %collective-permute-start.4 = (bf16[4,3,4,128,128]{4,3,2,1,0:T(8,128)(2,1)S(1)}, bf16[4,3,4,128,128]{4,3,2,1,0:T(8,128)(2,1)S(1)}, u32[]{:S(2)}, u32[]{:S(2)}) collective-permute-start(bf16[4,3,4,128,128]{4,3,2,1,0:T(8,128)(2,1)S(1)} %get-tuple-element.46.refs_2_), channel_id=1, source_target_pairs={{0,64},{64,0},{1,65},{65,1},{2,66},{66,2},{3,67},{67,3},{4,68},{68... | collective-permute-start | bytes 4718600 | tf_op jit(solution)/shard_map/ppermute | solution.py:244
  66.7 3.4 %collective-permute-done.4.refs_3_ = bf16[4,3,4,128,128]{4,3,2,1,0:T(8,128)(2,1)S(1)} collective-permute-done((bf16[4,3,4,128,128]{4,3,2,1,0:T(8,128)(2,1)S(1)}, bf16[4,3,4,128,128]{4,3,2,1,0:T(8,128)(2,1)S(1)}, u32[]{:S(2)}, u32[]{:S(2)}) %collective-permute-start.4) | collective-permute-done | bytes 1572896 | tf_op jit(solution)/shard_map/ppermute | solution.py:244
  70.1 3.3 %shard_map.65 = (bf16[4,128,256]{2,1,0:T(8,128)(2,1)S(1)}, bf16[4,128,256]{2,1,0:T(8,128)(2,1)S(1)}, bf16[2,128,256]{2,1,0:T(8,128)(2,1)S(1)}, bf16[2,2,128,256]{3,2,1,0:T(8,128)(2,1)S(1)}) custom-call(s32[4]{0:T(128)S(1)} %pad_add_fusion.refs_0_, f32[6]{0:T(128)S(1)} %pad_maximum_fusion.2.refs_1_, ...), custom_call_target="tpu_custom_call" | custom-call | flops 754974720 | bytes 4194304 | tf_op jit(solution)/shard_map/pallas_call | solution.py:145
  73.4 2.0 %collective-permute-start.5 = (bf16[4,3,4,128,128]{4,3,2,1,0:T(8,128)(2,1)S(1)}, bf16[4,3,4,128,128]{4,3,2,1,0:T(8,128)(2,1)S(1)}, u32[]{:S(2)}, u32[]{:S(2)}) collective-permute-start(bf16[4,3,4,128,128]{4,3,2,1,0:T(8,128)(2,1)S(1)} %get-tuple-element.32.refs_4_.refs_2_), channel_id=1, source_target_pairs={{0,64},{64,0},{1,65},{65,1},{2,66},{66,2},{3,67},{67,3},{4,68},{68... | collective-permute-start | bytes 4718600 | tf_op jit(solution)/shard_map/ppermute | solution.py:272
  75.5 3.4 %collective-permute-start.6 = (bf16[2,2,128,256]{3,2,1,0:T(8,128)(2,1)S(1)}, bf16[2,2,128,256]{3,2,1,0:T(8,128)(2,1)S(1)}, u32[]{:S(2)}, u32[]{:S(2)}) collective-permute-start(bf16[2,2,128,256]{3,2,1,0:T(8,128)(2,1)S(1)} %get-tuple-element.34), channel_id=1, source_target_pairs={{0,1},{1,16},{16,17},{17,32},{32,33},{33,48},{48,49},{2,3},{3,18},... | collective-permute-start | bytes 786440 | tf_op jit(solution)/shard_map/ppermute | solution.py:275
  79.0 7.9 %collective-permute-done.6.refs_8_ = bf16[2,2,128,256]{3,2,1,0:T(8,128)(2,1)S(1)} collective-permute-done((bf16[2,2,128,256]{3,2,1,0:T(8,128)(2,1)S(1)}, bf16[2,2,128,256]{3,2,1,0:T(8,128)(2,1)S(1)}, u32[]{:S(2)}, u32[]{:S(2)}) %collective-permute-start.6) | collective-permute-done | bytes 262176 | tf_op jit(solution)/shard_map/ppermute | solution.py:275
  86.9 2.9 %shard_map.66 = (bf16[2,128,256]{2,1,0:T(8,128)(2,1)S(1)}, bf16[4,128,256]{2,1,0:T(8,128)(2,1)S(1)}, bf16[2,128,256]{2,1,0:T(8,128)(2,1)S(1)}, bf16[2,2,128,256]{3,2,1,0:T(8,128)(2,1)S(1)}) custom-call(s32[4]{0:T(128)S(1)} %pad_add_fusion.refs_0_, f32[6]{0:T(128)S(1)} %pad_maximum_fusion.2.refs_1_, ...), custom_call_target="tpu_custom_call" | custom-call | flops 503316480 | bytes 4194304 | tf_op jit(solution)/shard_map/pallas_call | solution.py:145
  89.7 2.5 %collective-permute-start.7 = (bf16[2,2,128,256]{3,2,1,0:T(8,128)(2,1)S(1)}, bf16[2,2,128,256]{3,2,1,0:T(8,128)(2,1)S(1)}, u32[]{:S(2)}, u32[]{:S(2)}) collective-permute-start(bf16[2,2,128,256]{3,2,1,0:T(8,128)(2,1)S(1)} %get-tuple-element.38), channel_id=1, source_target_pairs={{0,1},{1,16},{16,17},{17,32},{32,33},{33,48},{48,49},{2,3},{3,18},... | collective-permute-start | bytes 786440 | tf_op jit(solution)/shard_map/ppermute | solution.py:275
  92.3 8.0 %collective-permute-done.7.refs_6_ = bf16[2,2,128,256]{3,2,1,0:T(8,128)(2,1)S(1)} collective-permute-done((bf16[2,2,128,256]{3,2,1,0:T(8,128)(2,1)S(1)}, bf16[2,2,128,256]{3,2,1,0:T(8,128)(2,1)S(1)}, u32[]{:S(2)}, u32[]{:S(2)}) %collective-permute-start.7) | collective-permute-done | bytes 262176 | tf_op jit(solution)/shard_map/ppermute | solution.py:275
  100.3 2.9 %shard_map.67 = (bf16[2,128,256]{2,1,0:T(8,128)(2,1)S(1)}, bf16[4,128,256]{2,1,0:T(8,128)(2,1)S(1)}, bf16[2,128,256]{2,1,0:T(8,128)(2,1)S(1)}, bf16[2,2,128,256]{3,2,1,0:T(8,128)(2,1)S(1)}) custom-call(s32[4]{0:T(128)S(1)} %pad_add_fusion.refs_0_, f32[6]{0:T(128)S(1)} %pad_maximum_fusion.2.refs_1_, ...), custom_call_target="tpu_custom_call" | custom-call | flops 503316480 | bytes 4194304 | tf_op jit(solution)/shard_map/pallas_call | solution.py:145
  103.2 1.9 %collective-permute-start.8 = (bf16[2,2,128,256]{3,2,1,0:T(8,128)(2,1)S(1)}, bf16[2,2,128,256]{3,2,1,0:T(8,128)(2,1)S(1)}, u32[]{:S(2)}, u32[]{:S(2)}) collective-permute-start(bf16[2,2,128,256]{3,2,1,0:T(8,128)(2,1)S(1)} %get-tuple-element.42), channel_id=1, source_target_pairs={{0,1},{1,16},{16,17},{17,32},{32,33},{33,48},{48,49},{2,3},{3,18},... | collective-permute-start | bytes 786440 | tf_op jit(solution)/shard_map/ppermute | solution.py:275
  105.2 7.6 %collective-permute-done.8.refs_6_ = bf16[2,2,128,256]{3,2,1,0:T(8,128)(2,1)S(1)} collective-permute-done((bf16[2,2,128,256]{3,2,1,0:T(8,128)(2,1)S(1)}, bf16[2,2,128,256]{3,2,1,0:T(8,128)(2,1)S(1)}, u32[]{:S(2)}, u32[]{:S(2)}) %collective-permute-start.8) | collective-permute-done | bytes 262176 | tf_op jit(solution)/shard_map/ppermute | solution.py:275
  112.8 2.4 %shard_map.68 = (bf16[2,128,256]{2,1,0:T(8,128)(2,1)S(1)}, bf16[4,128,128]{2,1,0:T(8,128)(2,1)S(1)}) custom-call(s32[4]{0:T(128)S(1)} %pad_add_fusion.refs_0_, f32[6]{0:T(128)S(1)} %pad_maximum_fusion.2.refs_1_, bf16[4,3,4,128,128]{4,3,2,1,0:T(8,128)(2,1)S(1)} %get-tuple-element.32.refs_4_.refs_2_, ...), custom_call_target="tpu_custom_call" | custom-call | flops 377487360 | bytes 4194304 | tf_op jit(solution)/shard_map/pallas_call | solution.py:145
  115.4 4.6 %all_to_all.15.over = bf16[2,4,8,64,128]{4,3,2,1,0:T(8,128)(2,1)S(1)} all-to-all(bf16[2,4,8,64,128]{4,3,2,1,0:T(8,128)(2,1)S(1)} %bitcast.25), channel_id=1, replica_groups=mesh['zhi'=4,'core'=2,'x'=4,'zlo'=2,'yl'=4,'y0'=2] {'core'}, dimensions={0} | all-to-all | bytes 2097152 | tf_op jit(solution)/shard_map/all_to_all | solution.py:316
  120.0 0.2 shard_map.69
  120.2 39.7 %all_to_all.16.over = bf16[64,64,128]{2,1,0:T(8,128)(2,1)S(1)} all-to-all(bf16[64,64,128]{2,1,0:T(8,128)(2,1)S(1)} %bitcast.22), channel_id=1, replica_groups=mesh['zhi'=4,'core'=2,'x'=4,'zlo'=2,'yl'=4,'y0'=2] {'zhi','zlo','yl','y0'}, dimensions={0} | all-to-all | bytes 2097152 | tf_op jit(solution)/shard_map/all_to_all | solution.py:319
  159.9 0.8 shard_map.70
  (35 shorter events, 0.6 us)
Async XLA Ops:
  6.5 56.0 %all-gather.2.cloned.1.call-start = ((), (), s32[]{:S(2)}) async-start(), calls=%async_computation.3 | async-start | bytes 3538944 | tf_op jit(solution)/shard_map/all_gather | solution.py:219
  6.5 2.5 %copy-start = (bf16[1,4096,128]{2,1,0:T(8,128)(2,1)S(1)}, bf16[1,4096,128]{2,1,0:T(8,128)(2,1)}, u32[]{:S(2)}) copy-start(bf16[1,4096,128]{2,1,0:T(8,128)(2,1)} %param.7) | copy-start | bytes 3145732
  10.4 9.5 %copy-start.3 = (bf16[64,128]{1,0:T(8,128)(2,1)S(1)}, bf16[64,128]{1,0:T(8,128)(2,1)}, u32[]{:S(2)}) copy-start(bf16[64,128]{1,0:T(8,128)(2,1)} %param.8) | copy-start | bytes 49156
  10.5 11.5 %copy-start.1 = (f32[1,3]{1,0:T(1,128)S(1)}, f32[1,3]{1,0:T(1,128)}, u32[]{:S(2)}) copy-start(f32[1,3]{1,0:T(1,128)} %param.11) | copy-start | bytes 40
  10.5 11.5 %copy-start.2 = (f32[1,3]{1,0:T(1,128)S(1)}, f32[1,3]{1,0:T(1,128)}, u32[]{:S(2)}) copy-start(f32[1,3]{1,0:T(1,128)} %param.10) | copy-start | bytes 40
  10.5 20.3 %all-to-all-start = ((bf16[4,8,128,128]{3,2,1,0:T(8,128)(2,1)}), bf16[4,8,128,128]{3,2,1,0:T(8,128)(2,1)S(1)}, u32[]{:S(2)}, u32[]{:S(2)}) async-start(bf16[4,8,128,128]{3,2,1,0:T(8,128)(2,1)} %bitcast.5), calls=%async_computation | async-start | bytes 2097152 | tf_op jit(solution)/shard_map/all_to_all | solution.py:223
  20.0 11.6 %collective-permute-start.1 = (bf16[64,128]{1,0:T(8,128)(2,1)S(1)}, bf16[64,128]{1,0:T(8,128)(2,1)S(1)}, u32[]{:S(2)}, u32[]{:S(2)}) collective-permute-start(bf16[64,128]{1,0:T(8,128)(2,1)S(1)} %copy-done.3), channel_id=1, source_target_pairs={{0,1},{2,3},{4,5},{6,7},{8,24},{10,26},{12,28},{14,30},{16,17},{18... | collective-permute-start | bytes 49160 | tf_op jit(solution)/shard_map/ppermute | solution.py:235
  21.3 10.4 %collective-permute-start.2 = (bf16[64,128]{1,0:T(8,128)(2,1)S(1)}, bf16[64,128]{1,0:T(8,128)(2,1)S(1)}, u32[]{:S(2)}, u32[]{:S(2)}) collective-permute-start(bf16[64,128]{1,0:T(8,128)(2,1)S(1)} %copy-done.3), channel_id=1, source_target_pairs={{0,0},{2,2},{4,4},{6,6},{8,9},{10,11},{12,13},{14,15},{16,16},{18,... | collective-permute-start | bytes 49160 | tf_op jit(solution)/shard_map/ppermute | solution.py:234
  22.0 7.2 %collective-permute-start.3 = (f32[8]{0:T(128)S(1)}, f32[8]{0:T(128)S(1)}, u32[]{:S(2)}, u32[]{:S(2)}) collective-permute-start(f32[8]{0:T(128)S(1)} %pad_maximum_fusion.1), channel_id=1, source_target_pairs={{0,0},{1,64},{2,2},{3,66},{4,4},{5,68},{6,6},{7,70},{8,8},{9,72},{... | collective-permute-start | bytes 104 | tf_op jit(solution)/shard_map/ppermute | solution.py:227
  30.8 0.9 collective-permute-start
  64.8 5.3 %collective-permute-start.4 = (bf16[4,3,4,128,128]{4,3,2,1,0:T(8,128)(2,1)S(1)}, bf16[4,3,4,128,128]{4,3,2,1,0:T(8,128)(2,1)S(1)}, u32[]{:S(2)}, u32[]{:S(2)}) collective-permute-start(bf16[4,3,4,128,128]{4,3,2,1,0:T(8,128)(2,1)S(1)} %get-tuple-element.46.refs_2_), channel_id=1, source_target_pairs={{0,64},{64,0},{1,65},{65,1},{2,66},{66,2},{3,67},{67,3},{4,68},{68... | collective-permute-start | bytes 4718600 | tf_op jit(solution)/shard_map/ppermute | solution.py:244
  73.4 13.4 %collective-permute-start.5 = (bf16[4,3,4,128,128]{4,3,2,1,0:T(8,128)(2,1)S(1)}, bf16[4,3,4,128,128]{4,3,2,1,0:T(8,128)(2,1)S(1)}, u32[]{:S(2)}, u32[]{:S(2)}) collective-permute-start(bf16[4,3,4,128,128]{4,3,2,1,0:T(8,128)(2,1)S(1)} %get-tuple-element.32.refs_4_.refs_2_), channel_id=1, source_target_pairs={{0,64},{64,0},{1,65},{65,1},{2,66},{66,2},{3,67},{67,3},{4,68},{68... | collective-permute-start | bytes 4718600 | tf_op jit(solution)/shard_map/ppermute | solution.py:272
  75.5 11.4 %collective-permute-start.6 = (bf16[2,2,128,256]{3,2,1,0:T(8,128)(2,1)S(1)}, bf16[2,2,128,256]{3,2,1,0:T(8,128)(2,1)S(1)}, u32[]{:S(2)}, u32[]{:S(2)}) collective-permute-start(bf16[2,2,128,256]{3,2,1,0:T(8,128)(2,1)S(1)} %get-tuple-element.34), channel_id=1, source_target_pairs={{0,1},{1,16},{16,17},{17,32},{32,33},{33,48},{48,49},{2,3},{3,18},... | collective-permute-start | bytes 786440 | tf_op jit(solution)/shard_map/ppermute | solution.py:275
  89.7 10.6 %collective-permute-start.7 = (bf16[2,2,128,256]{3,2,1,0:T(8,128)(2,1)S(1)}, bf16[2,2,128,256]{3,2,1,0:T(8,128)(2,1)S(1)}, u32[]{:S(2)}, u32[]{:S(2)}) collective-permute-start(bf16[2,2,128,256]{3,2,1,0:T(8,128)(2,1)S(1)} %get-tuple-element.38), channel_id=1, source_target_pairs={{0,1},{1,16},{16,17},{17,32},{32,33},{33,48},{48,49},{2,3},{3,18},... | collective-permute-start | bytes 786440 | tf_op jit(solution)/shard_map/ppermute | solution.py:275
  103.2 9.7 %collective-permute-start.8 = (bf16[2,2,128,256]{3,2,1,0:T(8,128)(2,1)S(1)}, bf16[2,2,128,256]{3,2,1,0:T(8,128)(2,1)S(1)}, u32[]{:S(2)}, u32[]{:S(2)}) collective-permute-start(bf16[2,2,128,256]{3,2,1,0:T(8,128)(2,1)S(1)} %get-tuple-element.42), channel_id=1, source_target_pairs={{0,1},{1,16},{16,17},{17,32},{32,33},{33,48},{48,49},{2,3},{3,18},... | collective-permute-start | bytes 786440 | tf_op jit(solution)/shard_map/ppermute | solution.py:275
Sparse Core Ops, SparseCore 0:
  9.4 53.0 all-gather.1

commit v6 on v4

--- a/solution.py
+++ b/solution.py
@@ -115,19 +115,20 @@
         for sector in (first, first + 1):
             total = None
             for s in range(STATES):
-                block = get(site, sector - s)
-                ops, env = block[:, :BLOCK], block[:, BLOCK:]
                 left = site_at[slot, s, sector + BEFORE]
                 cross = site_at[slot, jnp.clip(s - shift, 0, 2), sector + BEFORE]
-                half_env = jnp.dot(env, left, preferred_element_type=F32)
+                cross = (part[3 + s] * cross.astype(F32)).astype(BF16)
                 if with_ops(site):
                     right = site_at[slot, s, sector + BEFORE + shift]
-                    both = jnp.dot(ops, jnp.concatenate([right, cross], 1), preferred_element_type=F32)
-                    image = jnp.concatenate(
-                        [part[s] * both[:, :BLOCK], half_env + part[3 + s] * both[:, BLOCK:]], 1
-                    )
+                    upper = jnp.concatenate([right, cross], 1)
+                    lower = jnp.concatenate([jnp.zeros_like(left), left], 1)
                 else:
-                    image = half_env + part[3 + s] * jnp.dot(ops, cross, preferred_element_type=F32)
+                    upper, lower = cross, left
+                image = jnp.dot(
+                    get(site, sector - s), jnp.concatenate([upper, lower], 0), preferred_element_type=F32
+                )
+                if with_ops(site):
+                    image = jnp.concatenate([part[s] * image[:, :BLOCK], image[:, BLOCK:]], 1)
                 product = lax.dot_general(
                     left, image.astype(BF16), (((0,), (0,)), ((), ())), preferred_element_type=F32
                 )
@@ -172,6 +173,12 @@
         copy.wait()
 
 
+def bring(blocks, held, sem):
+    copy = pltpu.make_async_copy(blocks, held, sem)
+    copy.start()
+    copy.wait()
+
+
 def add_cores(over, summed):
     for site in range(4):
         both = (over[0, site].astype(F32) + over[1, site].astype(F32)).astype(BF16)
@@ -238,6 +245,15 @@
 
     mine, window, whole, part = lax.optimization_barrier((mine, window, whole, part))
     other = lax.ppermute(mine, "core", [(0, 1), (1, 0)])
+    mine = pl.pallas_call(
+        bring,
+        out_shape=jax.ShapeDtypeStruct(mine.shape, BF16),
+        in_specs=[pl.BlockSpec(memory_space=pl.ANY)],
+        out_specs=pl.BlockSpec(memory_space=pltpu.VMEM),
+        scratch_shapes=[pltpu.SemaphoreType.DMA],
+        compiler_params=pltpu.CompilerParams(vmem_limit_bytes=16 << 20),
+        cost_estimate=pl.CostEstimate(flops=0, bytes_accessed=6 << 20, transcendentals=0),
+    )(mine)
 
     wide = (BLOCK, 2 * BLOCK)
     onward = [(i, i + 1) for i in range(7)]

time: 165 us -> 160 us (0.970)
  Pallas kernels: 16.6 us -> 13.7 us
  starting transfers between devices: 25.9 us -> 24 us
    pallas_call x4, Pallas kernels: 14.5 us -> 11.4 us  [run_phase(): pl.pallas_call(functools.partial(phase_kernel, sites, steps, len(ins), so...]
    ppermute x1, starting transfers between devices: 3.47 us -> 1.29 us  [body(): piece = lax.ppermute(env_rows, AXES, rows_to_groups(0))]
    ppermute x1, waiting for transfers between devices: 5.84 us -> 3.72 us  [body(): other = lax.ppermute(mine, 'core', [(0, 1), (1, 0)])]
    all_gather x1, waiting for transfers between devices: 29.3 us -> 31.2 us  [body(): mine = lax.all_gather(piece, ('zhi', 'zlo'))]
  transfers between devices with their start and end apart: 11 -> 11, of which waited for: 7 -> 8; matrix products, arithmetic and copies ran while one was open for 2% -> 2% of each run, Pallas kernels for 0% -> 0%
where the time goes in v6:
time: 160 us; the launch traced here: 159 us
  waiting for transfers between devices  67.7 us (42%)
  blocking collectives  33.9 us (21%)
  starting transfers between devices  24 us (15%)
  between operations  15 us (9%)
  Pallas kernels  13.7 us (9%)
  local copies, waits for them, and re-layouts  2.92 us (2%)
  other arithmetic  2.3 us (1%)
    all_gather x1, waiting for transfers between devices, body(): mine = lax.all_gather(piece, ('zhi', 'zlo'))  31.2 us
    all_to_all x1, blocking collectives, body(): over = lax.all_to_all(summed, ('zhi', 'zlo', 'yl'), 0, 0)  29.3 us
    ppermute x3, waiting for transfers between devices, body(): tails = lax.ppermute(tails, ('x', 'y0'), onward)  22.8 us
    pallas_call x4, Pallas kernels, run_phase(): pl.pallas_call(functools.partial(phase_kernel, sites, steps, len(ins), so...  11.4 us
    ppermute x3, starting transfers between devices, body(): tails = lax.ppermute(tails, ('x', 'y0'), onward)  7.81 us
    ppermute x1, waiting for transfers between devices, body(): figures = lax.ppermute(figures, AXES, to_groups())  5.01 us
    all_to_all x1, starting transfers between devices, body(): over = lax.all_to_all(pieces, 'x', 0, 0)  4.82 us
    ppermute x1, waiting for transfers between devices, body(): swapped = lax.ppermute(summed, ('zlo', 'y0'), SWAP)  4.6 us
  transfers between devices with their start and end apart: 11, of which 8 were waited for; matrix products, arithmetic and copies ran while one was open for 2% of the time, Pallas kernels for 0%

profile of v6, /device:TPU:66, one launch (start us, length us, event | category | flops | bytes accessed | tf_op | source)
XLA Modules:
  0.0 159.4 jit_solution(8983453317375644604)
XLA Ops:
  6.5 1.8 %shard_map.64 = bf16[3,512,128]{2,1,0:T(8,128)(2,1)} custom-call(s32[1]{0:T(128)} %bitcast.start, bf16[1,3,4096,128]{3,2,1,0:T(8,128)(2,1)} %site.1), custom_call_target="tpu_custom_call" | custom-call | bytes 800000 | tf_op jit(solution)/shard_map/pallas_call | solution.py:214
  9.1 0.1 broadcast_select_fusion
  9.3 1.2 pad_select_fusion
  10.5 4.8 %all-to-all-start = ((bf16[4,8,128,128]{3,2,1,0:T(8,128)(2,1)}), bf16[4,8,128,128]{3,2,1,0:T(8,128)(2,1)S(1)}, u32[]{:S(2)}, u32[]{:S(2)}) async-start(bf16[4,8,128,128]{3,2,1,0:T(8,128)(2,1)} %bitcast.4), calls=%async_computation | async-start | bytes 2097152 | tf_op jit(solution)/shard_map/all_to_all | solution.py:227
  15.3 3.4 %collective-permute-start.1 = (bf16[64,128]{1,0:T(8,128)(2,1)S(1)}, bf16[64,128]{1,0:T(8,128)(2,1)S(1)}, u32[]{:S(2)}, u32[]{:S(2)}) collective-permute-start(bf16[64,128]{1,0:T(8,128)(2,1)S(1)} %copy-done.4), channel_id=1, source_target_pairs={{0,1},{2,3},{4,5},{6,7},{8,24},{10,26},{12,28},{14,30},{16,17},{18... | collective-permute-start | bytes 49160 | tf_op jit(solution)/shard_map/ppermute | solution.py:239
  18.7 1.3 collective-permute-start.2
  20.1 2.2 %collective-permute-start.3 = (f32[8]{0:T(128)S(1)}, f32[8]{0:T(128)S(1)}, u32[]{:S(2)}, u32[]{:S(2)}) collective-permute-start(f32[8]{0:T(128)S(1)} %pad_maximum_fusion.1), channel_id=1, source_target_pairs={{0,0},{1,64},{2,2},{3,66},{4,4},{5,68},{6,6},{7,70},{8,8},{9,72},{... | collective-permute-start | bytes 104 | tf_op jit(solution)/shard_map/ppermute | solution.py:231
  22.3 5.0 %collective-permute-done.3 = f32[8]{0:T(128)S(1)} collective-permute-done((f32[8]{0:T(128)S(1)}, f32[8]{0:T(128)S(1)}, u32[]{:S(2)}, u32[]{:S(2)}) %collective-permute-start.3) | collective-permute-done | bytes 64 | tf_op jit(solution)/shard_map/ppermute | solution.py:231
  27.3 0.6 slice.43
  28.6 0.3 all-to-all-done
  29.0 0.7 collective-permute-start
  29.9 31.2 %all-gather.2.cloned.1.call-done.blocks = bf16[8,3,4,128,128]{4,3,2,1,0:T(8,128)(2,1)} async-done(((bf16[1,3,4,128,128]{4,3,2,1,0:T(8,128)(2,1)}), bf16[8,3,4,128,128]{4,3,2,1,0:T(8,128)(2,1)}) %all-gather.2.cloned.1.call-update) | async-done | bytes 3145744 | tf_op jit(solution)/shard_map/all_gather | solution.py:223
  61.1 1.9 %collective-permute-start.4 = (bf16[8,3,4,128,128]{4,3,2,1,0:T(8,128)(2,1)}, bf16[8,3,4,128,128]{4,3,2,1,0:T(8,128)(2,1)S(1)}, u32[]{:S(2)}, u32[]{:S(2)}) collective-permute-start(bf16[8,3,4,128,128]{4,3,2,1,0:T(8,128)(2,1)} %all-gather.2.cloned.1.call-done.blocks), channel_id=1, source_target_pairs={{0,64},{64,0},{1,65},{65,1},{2,66},{66,2},{3,67},{67,3},{4,68},{68... | collective-permute-start | bytes 9437192 | tf_op jit(solution)/shard_map/ppermute | solution.py:247
  63.0 1.9 %copy-done = bf16[8,3,4,128,128]{4,3,2,1,0:T(8,128)(2,1)S(1)} copy-done((bf16[8,3,4,128,128]{4,3,2,1,0:T(8,128)(2,1)S(1)}, bf16[8,3,4,128,128]{4,3,2,1,0:T(8,128)(2,1)}, u32[]{:S(2)}) %copy-start) | copy-done | bytes 3145752
  64.9 0.2 shard_map.65.refs_2_
  65.1 3.7 %collective-permute-done.4.refs_3_ = bf16[8,3,4,128,128]{4,3,2,1,0:T(8,128)(2,1)S(1)} collective-permute-done((bf16[8,3,4,128,128]{4,3,2,1,0:T(8,128)(2,1)}, bf16[8,3,4,128,128]{4,3,2,1,0:T(8,128)(2,1)S(1)}, u32[]{:S(2)}, u32[]{:S(2)}) %collective-permute-start.4) | collective-permute-done | bytes 3145760 | tf_op jit(solution)/shard_map/ppermute | solution.py:247
  68.8 3.3 %shard_map.66 = (bf16[4,128,256]{2,1,0:T(8,128)(2,1)S(1)}, bf16[4,128,256]{2,1,0:T(8,128)(2,1)S(1)}, bf16[2,128,256]{2,1,0:T(8,128)(2,1)S(1)}, bf16[2,2,128,256]{3,2,1,0:T(8,128)(2,1)S(1)}) custom-call(s32[4]{0:T(128)S(1)} %pad_add_fusion.refs_0_, f32[6]{0:T(128)S(1)} %pad_maximum_fusion.2.refs_1_, bf16[8,3,4,128,128]{4,3,2,1,0:T(8,128)(2,1)S(1)} %shard_map.65.refs_2_, ...), custom_call_target="tpu_custom_call" | custom-call | flops 754974720 | bytes 4194304 | tf_op jit(solution)/shard_map/pallas_call | solution.py:144
  72.1 3.4 %collective-permute-start.5 = (bf16[2,2,128,256]{3,2,1,0:T(8,128)(2,1)S(1)}, bf16[2,2,128,256]{3,2,1,0:T(8,128)(2,1)S(1)}, u32[]{:S(2)}, u32[]{:S(2)}) collective-permute-start(bf16[2,2,128,256]{3,2,1,0:T(8,128)(2,1)S(1)} %get-tuple-element.30), channel_id=1, source_target_pairs={{0,1},{1,16},{16,17},{17,32},{32,33},{33,48},{48,49},{2,3},{3,18},... | collective-permute-start | bytes 786440 | tf_op jit(solution)/shard_map/ppermute | solution.py:286
  75.6 7.7 %collective-permute-done.5.refs_6_ = bf16[2,2,128,256]{3,2,1,0:T(8,128)(2,1)S(1)} collective-permute-done((bf16[2,2,128,256]{3,2,1,0:T(8,128)(2,1)S(1)}, bf16[2,2,128,256]{3,2,1,0:T(8,128)(2,1)S(1)}, u32[]{:S(2)}, u32[]{:S(2)}) %collective-permute-start.5) | collective-permute-done | bytes 262176 | tf_op jit(solution)/shard_map/ppermute | solution.py:286
  83.3 2.9 %shard_map.67 = (bf16[2,128,256]{2,1,0:T(8,128)(2,1)S(1)}, bf16[4,128,256]{2,1,0:T(8,128)(2,1)S(1)}, bf16[2,128,256]{2,1,0:T(8,128)(2,1)S(1)}, bf16[2,2,128,256]{3,2,1,0:T(8,128)(2,1)S(1)}) custom-call(s32[4]{0:T(128)S(1)} %pad_add_fusion.refs_0_, f32[6]{0:T(128)S(1)} %pad_maximum_fusion.2.refs_1_, bf16[8,3,4,128,128]{4,3,2,1,0:T(8,128)(2,1)S(1)} %shard_map.65.refs_2_, ...), custom_call_target="tpu_custom_call" | custom-call | flops 503316480 | bytes 4194304 | tf_op jit(solution)/shard_map/pallas_call | solution.py:144
  86.1 2.5 %collective-permute-start.6 = (bf16[2,2,128,256]{3,2,1,0:T(8,128)(2,1)S(1)}, bf16[2,2,128,256]{3,2,1,0:T(8,128)(2,1)S(1)}, u32[]{:S(2)}, u32[]{:S(2)}) collective-permute-start(bf16[2,2,128,256]{3,2,1,0:T(8,128)(2,1)S(1)} %get-tuple-element.34), channel_id=1, source_target_pairs={{0,1},{1,16},{16,17},{17,32},{32,33},{33,48},{48,49},{2,3},{3,18},... | collective-permute-start | bytes 786440 | tf_op jit(solution)/shard_map/ppermute | solution.py:286
  88.7 7.7 %collective-permute-done.6.refs_6_ = bf16[2,2,128,256]{3,2,1,0:T(8,128)(2,1)S(1)} collective-permute-done((bf16[2,2,128,256]{3,2,1,0:T(8,128)(2,1)S(1)}, bf16[2,2,128,256]{3,2,1,0:T(8,128)(2,1)S(1)}, u32[]{:S(2)}, u32[]{:S(2)}) %collective-permute-start.6) | collective-permute-done | bytes 262176 | tf_op jit(solution)/shard_map/ppermute | solution.py:286
  96.5 2.9 %shard_map.68 = (bf16[2,128,256]{2,1,0:T(8,128)(2,1)S(1)}, bf16[4,128,256]{2,1,0:T(8,128)(2,1)S(1)}, bf16[2,128,256]{2,1,0:T(8,128)(2,1)S(1)}, bf16[2,2,128,256]{3,2,1,0:T(8,128)(2,1)S(1)}) custom-call(s32[4]{0:T(128)S(1)} %pad_add_fusion.refs_0_, f32[6]{0:T(128)S(1)} %pad_maximum_fusion.2.refs_1_, bf16[8,3,4,128,128]{4,3,2,1,0:T(8,128)(2,1)S(1)} %shard_map.65.refs_2_, ...), custom_call_target="tpu_custom_call" | custom-call | flops 503316480 | bytes 4194304 | tf_op jit(solution)/shard_map/pallas_call | solution.py:144
  99.3 1.9 %collective-permute-start.7 = (bf16[2,2,128,256]{3,2,1,0:T(8,128)(2,1)S(1)}, bf16[2,2,128,256]{3,2,1,0:T(8,128)(2,1)S(1)}, u32[]{:S(2)}, u32[]{:S(2)}) collective-permute-start(bf16[2,2,128,256]{3,2,1,0:T(8,128)(2,1)S(1)} %get-tuple-element.38), channel_id=1, source_target_pairs={{0,1},{1,16},{16,17},{17,32},{32,33},{33,48},{48,49},{2,3},{3,18},... | collective-permute-start | bytes 786440 | tf_op jit(solution)/shard_map/ppermute | solution.py:286
  101.3 7.4 %collective-permute-done.7.refs_6_ = bf16[2,2,128,256]{3,2,1,0:T(8,128)(2,1)S(1)} collective-permute-done((bf16[2,2,128,256]{3,2,1,0:T(8,128)(2,1)S(1)}, bf16[2,2,128,256]{3,2,1,0:T(8,128)(2,1)S(1)}, u32[]{:S(2)}, u32[]{:S(2)}) %collective-permute-start.7) | collective-permute-done | bytes 262176 | tf_op jit(solution)/shard_map/ppermute | solution.py:286
  108.7 2.4 %shard_map.69 = (bf16[2,128,256]{2,1,0:T(8,128)(2,1)S(1)}, bf16[4,128,128]{2,1,0:T(8,128)(2,1)S(1)}) custom-call(s32[4]{0:T(128)S(1)} %pad_add_fusion.refs_0_, f32[6]{0:T(128)S(1)} %pad_maximum_fusion.2.refs_1_, bf16[8,3,4,128,128]{4,3,2,1,0:T(8,128)(2,1)S(1)} %shard_map.65.refs_2_, bf16[8,3,4,128,128]{4,3,2,1,0:T(8,128)(2,1)S(1)} %collective-permute-done.4.refs_3_, ...), custom_call_target="tpu_custom_call" | custom-call | flops 377487360 | bytes 4194304 | tf_op jit(solution)/shard_map/pallas_call | solution.py:144
  111.3 4.6 %all_to_all.15.over = bf16[2,4,8,64,128]{4,3,2,1,0:T(8,128)(2,1)S(1)} all-to-all(bf16[2,4,8,64,128]{4,3,2,1,0:T(8,128)(2,1)S(1)} %bitcast.25), channel_id=1, replica_groups=mesh['zhi'=4,'core'=2,'x'=4,'zlo'=2,'yl'=4,'y0'=2] {'core'}, dimensions={0} | all-to-all | bytes 2097152 | tf_op jit(solution)/shard_map/all_to_all | solution.py:328
  115.9 0.1 shard_map.70
  116.0 29.3 %all_to_all.16.over = bf16[32,64,128]{2,1,0:T(8,128)(2,1)S(1)} all-to-all(bf16[32,64,128]{2,1,0:T(8,128)(2,1)S(1)} %bitcast.22), channel_id=1, replica_groups=mesh['zhi'=4,'core'=2,'x'=4,'zlo'=2,'yl'=4,'y0'=2] {'zhi','zlo','yl'}, dimensions={0} | all-to-all | bytes 1048576 | tf_op jit(solution)/shard_map/all_to_all | solution.py:330
  145.4 1.9 %collective-permute-start.8 = (bf16[64,128]{1,0:T(8,128)(2,1)S(1)}, bf16[64,128]{1,0:T(8,128)(2,1)S(1)}, u32[]{:S(2)}, u32[]{:S(2)}) collective-permute-start(bf16[64,128]{1,0:T(8,128)(2,1)S(1)} %shard_map.71), channel_id=1, source_target_pairs={{1,8},{8,1},{3,10},{10,3},{5,12},{12,5},{7,14},{14,7},{17,24},{24,... | collective-permute-start | bytes 49160 | tf_op jit(solution)/shard_map/ppermute | solution.py:332
  147.3 4.6 %collective-permute-done.8 = bf16[64,128]{1,0:T(8,128)(2,1)S(1)} collective-permute-done((bf16[64,128]{1,0:T(8,128)(2,1)S(1)}, bf16[64,128]{1,0:T(8,128)(2,1)S(1)}, u32[]{:S(2)}, u32[]{:S(2)}) %collective-permute-start.8) | collective-permute-done | bytes 16416 | tf_op jit(solution)/shard_map/ppermute | solution.py:332
  151.9 0.6 select_bitcast_fusion
  (38 shorter events, 1.0 us)
Async XLA Ops:
  6.5 2.5 %copy-start.1 = (bf16[1,4096,128]{2,1,0:T(8,128)(2,1)S(1)}, bf16[1,4096,128]{2,1,0:T(8,128)(2,1)}, u32[]{:S(2)}) copy-start(bf16[1,4096,128]{2,1,0:T(8,128)(2,1)} %param.7) | copy-start | bytes 3145732
  6.5 54.6 %all-gather.2.cloned.1.call-start = ((), (), s32[]{:S(2)}) async-start(), calls=%async_computation.3 | async-start | bytes 3538944 | tf_op jit(solution)/shard_map/all_gather | solution.py:223
  9.2 6.1 %copy-start.4 = (bf16[64,128]{1,0:T(8,128)(2,1)S(1)}, bf16[64,128]{1,0:T(8,128)(2,1)}, u32[]{:S(2)}) copy-start(bf16[64,128]{1,0:T(8,128)(2,1)} %param.8) | copy-start | bytes 49156
  9.2 10.8 %copy-start.2 = (f32[1,3]{1,0:T(1,128)S(1)}, f32[1,3]{1,0:T(1,128)}, u32[]{:S(2)}) copy-start(f32[1,3]{1,0:T(1,128)} %param.11) | copy-start | bytes 40
  9.2 10.8 %copy-start.3 = (f32[1,3]{1,0:T(1,128)S(1)}, f32[1,3]{1,0:T(1,128)}, u32[]{:S(2)}) copy-start(f32[1,3]{1,0:T(1,128)} %param.10) | copy-start | bytes 40
  10.5 18.5 %all-to-all-start = ((bf16[4,8,128,128]{3,2,1,0:T(8,128)(2,1)}), bf16[4,8,128,128]{3,2,1,0:T(8,128)(2,1)S(1)}, u32[]{:S(2)}, u32[]{:S(2)}) async-start(bf16[4,8,128,128]{3,2,1,0:T(8,128)(2,1)} %bitcast.4), calls=%async_computation | async-start | bytes 2097152 | tf_op jit(solution)/shard_map/all_to_all | solution.py:227
  15.3 14.4 %collective-permute-start.1 = (bf16[64,128]{1,0:T(8,128)(2,1)S(1)}, bf16[64,128]{1,0:T(8,128)(2,1)S(1)}, u32[]{:S(2)}, u32[]{:S(2)}) collective-permute-start(bf16[64,128]{1,0:T(8,128)(2,1)S(1)} %copy-done.4), channel_id=1, source_target_pairs={{0,1},{2,3},{4,5},{6,7},{8,24},{10,26},{12,28},{14,30},{16,17},{18... | collective-permute-start | bytes 49160 | tf_op jit(solution)/shard_map/ppermute | solution.py:239
  18.7 11.1 %collective-permute-start.2 = (bf16[64,128]{1,0:T(8,128)(2,1)S(1)}, bf16[64,128]{1,0:T(8,128)(2,1)S(1)}, u32[]{:S(2)}, u32[]{:S(2)}) collective-permute-start(bf16[64,128]{1,0:T(8,128)(2,1)S(1)} %copy-done.4), channel_id=1, source_target_pairs={{0,0},{2,2},{4,4},{6,6},{8,9},{10,11},{12,13},{14,15},{16,16},{18,... | collective-permute-start | bytes 49160 | tf_op jit(solution)/shard_map/ppermute | solution.py:238
  20.1 7.2 %collective-permute-start.3 = (f32[8]{0:T(128)S(1)}, f32[8]{0:T(128)S(1)}, u32[]{:S(2)}, u32[]{:S(2)}) collective-permute-start(f32[8]{0:T(128)S(1)} %pad_maximum_fusion.1), channel_id=1, source_target_pairs={{0,0},{1,64},{2,2},{3,66},{4,4},{5,68},{6,6},{7,70},{8,8},{9,72},{... | collective-permute-start | bytes 104 | tf_op jit(solution)/shard_map/ppermute | solution.py:231
  29.0 0.9 collective-permute-start
  61.1 7.8 %collective-permute-start.4 = (bf16[8,3,4,128,128]{4,3,2,1,0:T(8,128)(2,1)}, bf16[8,3,4,128,128]{4,3,2,1,0:T(8,128)(2,1)S(1)}, u32[]{:S(2)}, u32[]{:S(2)}) collective-permute-start(bf16[8,3,4,128,128]{4,3,2,1,0:T(8,128)(2,1)} %all-gather.2.cloned.1.call-done.blocks), channel_id=1, source_target_pairs={{0,64},{64,0},{1,65},{65,1},{2,66},{66,2},{3,67},{67,3},{4,68},{68... | collective-permute-start | bytes 9437192 | tf_op jit(solution)/shard_map/ppermute | solution.py:247
  63.0 1.9 %copy-start = (bf16[8,3,4,128,128]{4,3,2,1,0:T(8,128)(2,1)S(1)}, bf16[8,3,4,128,128]{4,3,2,1,0:T(8,128)(2,1)}, u32[]{:S(2)}) copy-start(bf16[8,3,4,128,128]{4,3,2,1,0:T(8,128)(2,1)} %all-gather.2.cloned.1.call-done.blocks) | copy-start | bytes 9437188
  72.1 11.1 %collective-permute-start.5 = (bf16[2,2,128,256]{3,2,1,0:T(8,128)(2,1)S(1)}, bf16[2,2,128,256]{3,2,1,0:T(8,128)(2,1)S(1)}, u32[]{:S(2)}, u32[]{:S(2)}) collective-permute-start(bf16[2,2,128,256]{3,2,1,0:T(8,128)(2,1)S(1)} %get-tuple-element.30), channel_id=1, source_target_pairs={{0,1},{1,16},{16,17},{17,32},{32,33},{33,48},{48,49},{2,3},{3,18},... | collective-permute-start | bytes 786440 | tf_op jit(solution)/shard_map/ppermute | solution.py:286
  86.1 10.3 %collective-permute-start.6 = (bf16[2,2,128,256]{3,2,1,0:T(8,128)(2,1)S(1)}, bf16[2,2,128,256]{3,2,1,0:T(8,128)(2,1)S(1)}, u32[]{:S(2)}, u32[]{:S(2)}) collective-permute-start(bf16[2,2,128,256]{3,2,1,0:T(8,128)(2,1)S(1)} %get-tuple-element.34), channel_id=1, source_target_pairs={{0,1},{1,16},{16,17},{17,32},{32,33},{33,48},{48,49},{2,3},{3,18},... | collective-permute-start | bytes 786440 | tf_op jit(solution)/shard_map/ppermute | solution.py:286
  99.3 9.4 %collective-permute-start.7 = (bf16[2,2,128,256]{3,2,1,0:T(8,128)(2,1)S(1)}, bf16[2,2,128,256]{3,2,1,0:T(8,128)(2,1)S(1)}, u32[]{:S(2)}, u32[]{:S(2)}) collective-permute-start(bf16[2,2,128,256]{3,2,1,0:T(8,128)(2,1)S(1)} %get-tuple-element.38), channel_id=1, source_target_pairs={{0,1},{1,16},{16,17},{17,32},{32,33},{33,48},{48,49},{2,3},{3,18},... | collective-permute-start | bytes 786440 | tf_op jit(solution)/shard_map/ppermute | solution.py:286
  145.4 6.5 %collective-permute-start.8 = (bf16[64,128]{1,0:T(8,128)(2,1)S(1)}, bf16[64,128]{1,0:T(8,128)(2,1)S(1)}, u32[]{:S(2)}, u32[]{:S(2)}) collective-permute-start(bf16[64,128]{1,0:T(8,128)(2,1)S(1)} %shard_map.71), channel_id=1, source_target_pairs={{1,8},{8,1},{3,10},{10,3},{5,12},{12,5},{7,14},{14,7},{17,24},{24,... | collective-permute-start | bytes 49160 | tf_op jit(solution)/shard_map/ppermute | solution.py:332
Sparse Core Ops, SparseCore 0:
  9.4 51.6 all-gather.1

commit v7 on v6

--- a/solution.py
+++ b/solution.py
@@ -97,7 +97,6 @@
             for copy in copies(slot, site, other):
                 copy.start()
 
-    done_sites = set()
     state = {}
 
     def get(site, sector):
@@ -106,14 +105,12 @@
         where, index = sources[site, sector]
         return ins[where][index]
 
-    for site, first in steps:
+    for site, sectors in steps:
         slot = sites.index(site)
-        if site not in done_sites:
-            done_sites.add(site)
-            for copy in copies(slot, site, mine):
-                copy.wait()
-        for sector in (first, first + 1):
-            total = None
+        for copy in copies(slot, site, mine):
+            copy.wait()
+        lefts, images = {}, {}
+        for sector in sectors:
             for s in range(STATES):
                 left = site_at[slot, s, sector + BEFORE]
                 cross = site_at[slot, jnp.clip(s - shift, 0, 2), sector + BEFORE]
@@ -129,18 +126,21 @@
                 )
                 if with_ops(site):
                     image = jnp.concatenate([part[s] * image[:, :BLOCK], image[:, BLOCK:]], 1)
-                product = lax.dot_general(
-                    left, image.astype(BF16), (((0,), (0,)), ((), ())), preferred_element_type=F32
-                )
-                total = product if total is None else total + product
-            total = total.astype(BF16)
+                lefts[sector, s], images[sector, s] = left, image.astype(BF16)
+        for sector in sectors:
+            total = lax.dot_general(
+                jnp.concatenate([lefts[sector, s] for s in range(STATES)], 0),
+                jnp.concatenate([images[sector, s] for s in range(STATES)], 0),
+                (((0,), (0,)), ((), ())),
+                preferred_element_type=F32,
+            ).astype(BF16)
             state[site + 1, sector] = total
             for which, index in targets[site + 1, sector]:
                 outs[which][index] = total
 
 
 def run_phase(sites, steps, ins, sources, outs, targets, with_ops, whole, part, mine, other):
-    blocks = 2 * len(steps) * (15 if with_ops(sites[0]) else 9)
+    blocks = 15 * sum(len(sectors) for _, sectors in steps)
     return pl.pallas_call(
         functools.partial(phase_kernel, sites, steps, len(ins), sources, targets, with_ops),
         out_shape=[jax.ShapeDtypeStruct(shape, BF16) for shape in outs],
@@ -158,12 +158,20 @@
 
 
 def take_piece(start, site, piece, taken, sems):
-    rows = HALF * BLOCK
     first = pl.multiple_of(start[0] * BLOCK, BLOCK)
+    spots = [(s, sector * BLOCK) for s in range(STATES) for sector in range(HALF)]
     inward = [
-        pltpu.make_async_copy(site.at[0, s, pl.ds(first, rows)], taken.at[s], sems.at[0, s]) for s in range(STATES)
+        pltpu.make_async_copy(
+            site.at[0, s, pl.ds(first + row, BLOCK)], taken.at[s, pl.ds(row, BLOCK)], sems.at[0, number]
+        )
+        for number, (s, row) in enumerate(spots)
     ]
-    outward = [pltpu.make_async_copy(taken.at[s], piece.at[s], sems.at[1, s]) for s in range(STATES)]
+    outward = [
+        pltpu.make_async_copy(
+            taken.at[s, pl.ds(row, BLOCK)], piece.at[s, pl.ds(row, BLOCK)], sems.at[1, number]
+        )
+        for number, (s, row) in enumerate(spots)
+    ]
     for copy in inward:
         copy.start()
     for before, after in zip(inward, outward):
@@ -216,7 +224,7 @@
         out_shape=jax.ShapeDtypeStruct((STATES, HALF * BLOCK, BLOCK), BF16),
         in_specs=[pl.BlockSpec(memory_space=pltpu.SMEM), pl.BlockSpec(memory_space=pltpu.HBM)],
         out_specs=pl.BlockSpec(memory_space=pltpu.HBM),
-        scratch_shapes=[pltpu.VMEM((STATES, HALF * BLOCK, BLOCK), BF16), pltpu.SemaphoreType.DMA((2, STATES))],
+        scratch_shapes=[pltpu.VMEM((STATES, HALF * BLOCK, BLOCK), BF16), pltpu.SemaphoreType.DMA((2, STATES * HALF))],
         compiler_params=pltpu.CompilerParams(vmem_limit_bytes=60 << 20),
         cost_estimate=pl.CostEstimate(flops=0, bytes_accessed=800_000, transcendentals=0),
     )(start, site_tensor).reshape(STATES, HALF, BLOCK, BLOCK)
@@ -270,7 +278,7 @@
         targets[3, sector] = [(2, sector - 2), (3, (1, sector - 2))]
     first, full, upper, tails = run_phase(
         [0, 1, 2],
-        [(0, 0), (0, 2), (0, -2), (1, 2), (1, 0), (2, 2)],
+        [(0, range(-2, OWN)), (1, range(OWN)), (2, (2, 3))],
         [window],
         sources,
         [(OWN,) + wide, (OWN,) + wide, (2,) + wide, (2, 2) + wide],
@@ -298,13 +306,13 @@
             targets[site + 1, sector] = [(0, sector)]
         for sector in range(OWN):
             targets[site + 2, sector] = [(1, sector)]
-        steps = [(site, 0), (site + 1, 2), (site + 1, 0)]
+        steps = [(site, (0, 1)), (site + 1, range(OWN))]
         outs = [(2,) + wide, (OWN,) + ((BLOCK, BLOCK) if last else wide)]
         if not last:
             for sector in (2, 3):
                 targets[site + 2, sector].append((3, (0, sector - 2)))
                 targets[site + 3, sector] = [(2, sector - 2), (3, (1, sector - 2))]
-            steps.append((site + 2, 2))
+            steps.append((site + 2, (2, 3)))
             outs += [(2,) + wide, (2, 2) + wide]
         old_upper = upper
         lower, full, *rest = run_phase(

time: 160 us -> 158 us (0.988)
  Pallas kernels: 13.7 us -> 12 us
    pallas_call x4, Pallas kernels: 11.4 us -> 9.7 us  [run_phase(): pl.pallas_call(functools.partial(phase_kernel, sites, steps, len(ins), so...]
where the time goes in v7:
time: 158 us
  waiting for transfers between devices  67.6 us (43%)
  blocking collectives  34 us (22%)
  starting transfers between devices  24 us (15%)
  between operations  15 us (9%)
  Pallas kernels  12 us (8%)
  local copies, waits for them, and re-layouts  2.92 us (2%)
  other arithmetic  2.3 us (1%)
    all_gather x1, waiting for transfers between devices, body(): mine = lax.all_gather(piece, ('zhi', 'zlo'))  31.2 us
    all_to_all x1, blocking collectives, body(): over = lax.all_to_all(summed, ('zhi', 'zlo', 'yl'), 0, 0)  29.4 us
    ppermute x3, waiting for transfers between devices, body(): tails = lax.ppermute(tails, ('x', 'y0'), onward)  22.7 us
    pallas_call x4, Pallas kernels, run_phase(): pl.pallas_call(functools.partial(phase_kernel, sites, steps, len(ins), so...  9.7 us
    ppermute x3, starting transfers between devices, body(): tails = lax.ppermute(tails, ('x', 'y0'), onward)  7.82 us
    ppermute x1, waiting for transfers between devices, body(): figures = lax.ppermute(figures, AXES, to_groups())  5.01 us
    all_to_all x1, starting transfers between devices, body(): over = lax.all_to_all(pieces, 'x', 0, 0)  4.82 us
    ppermute x1, waiting for transfers between devices, body(): swapped = lax.ppermute(summed, ('zlo', 'y0'), SWAP)  4.6 us
  transfers between devices with their start and end apart: 11, of which 8 were waited for; matrix products, arithmetic and copies ran while one was open for 2% of the time, Pallas kernels for 0%

profile of v7, /device:TPU:66, one launch (start us, length us, event | category | flops | bytes accessed | tf_op | source)
XLA Modules:
  0.0 157.7 jit_solution(13804970454324442594)
XLA Ops:
  6.5 1.8 %shard_map.64 = bf16[3,512,128]{2,1,0:T(8,128)(2,1)} custom-call(s32[1]{0:T(128)} %bitcast.start, bf16[1,3,4096,128]{3,2,1,0:T(8,128)(2,1)} %site.1), custom_call_target="tpu_custom_call" | custom-call | bytes 800000 | tf_op jit(solution)/shard_map/pallas_call | solution.py:222
  9.1 0.1 broadcast_select_fusion
  9.3 1.2 pad_select_fusion
  10.5 4.8 %all-to-all-start = ((bf16[4,8,128,128]{3,2,1,0:T(8,128)(2,1)}), bf16[4,8,128,128]{3,2,1,0:T(8,128)(2,1)S(1)}, u32[]{:S(2)}, u32[]{:S(2)}) async-start(bf16[4,8,128,128]{3,2,1,0:T(8,128)(2,1)} %bitcast.4), calls=%async_computation | async-start | bytes 2097152 | tf_op jit(solution)/shard_map/all_to_all | solution.py:235
  15.3 3.4 %collective-permute-start.1 = (bf16[64,128]{1,0:T(8,128)(2,1)S(1)}, bf16[64,128]{1,0:T(8,128)(2,1)S(1)}, u32[]{:S(2)}, u32[]{:S(2)}) collective-permute-start(bf16[64,128]{1,0:T(8,128)(2,1)S(1)} %copy-done.4), channel_id=1, source_target_pairs={{0,1},{2,3},{4,5},{6,7},{8,24},{10,26},{12,28},{14,30},{16,17},{18... | collective-permute-start | bytes 49160 | tf_op jit(solution)/shard_map/ppermute | solution.py:247
  18.7 1.3 collective-permute-start.2
  20.1 2.2 %collective-permute-start.3 = (f32[8]{0:T(128)S(1)}, f32[8]{0:T(128)S(1)}, u32[]{:S(2)}, u32[]{:S(2)}) collective-permute-start(f32[8]{0:T(128)S(1)} %pad_maximum_fusion.1), channel_id=1, source_target_pairs={{0,0},{1,64},{2,2},{3,66},{4,4},{5,68},{6,6},{7,70},{8,8},{9,72},{... | collective-permute-start | bytes 104 | tf_op jit(solution)/shard_map/ppermute | solution.py:239
  22.3 5.0 %collective-permute-done.3 = f32[8]{0:T(128)S(1)} collective-permute-done((f32[8]{0:T(128)S(1)}, f32[8]{0:T(128)S(1)}, u32[]{:S(2)}, u32[]{:S(2)}) %collective-permute-start.3) | collective-permute-done | bytes 64 | tf_op jit(solution)/shard_map/ppermute | solution.py:239
  27.3 0.6 slice.43
  28.6 0.3 all-to-all-done
  29.0 0.7 collective-permute-start
  29.9 31.2 %all-gather.2.cloned.1.call-done.blocks = bf16[8,3,4,128,128]{4,3,2,1,0:T(8,128)(2,1)} async-done(((bf16[1,3,4,128,128]{4,3,2,1,0:T(8,128)(2,1)}), bf16[8,3,4,128,128]{4,3,2,1,0:T(8,128)(2,1)}) %all-gather.2.cloned.1.call-update) | async-done | bytes 3145744 | tf_op jit(solution)/shard_map/all_gather | solution.py:231
  61.1 1.9 %collective-permute-start.4 = (bf16[8,3,4,128,128]{4,3,2,1,0:T(8,128)(2,1)}, bf16[8,3,4,128,128]{4,3,2,1,0:T(8,128)(2,1)S(1)}, u32[]{:S(2)}, u32[]{:S(2)}) collective-permute-start(bf16[8,3,4,128,128]{4,3,2,1,0:T(8,128)(2,1)} %all-gather.2.cloned.1.call-done.blocks), channel_id=1, source_target_pairs={{0,64},{64,0},{1,65},{65,1},{2,66},{66,2},{3,67},{67,3},{4,68},{68... | collective-permute-start | bytes 9437192 | tf_op jit(solution)/shard_map/ppermute | solution.py:255
  63.0 1.9 %copy-done = bf16[8,3,4,128,128]{4,3,2,1,0:T(8,128)(2,1)S(1)} copy-done((bf16[8,3,4,128,128]{4,3,2,1,0:T(8,128)(2,1)S(1)}, bf16[8,3,4,128,128]{4,3,2,1,0:T(8,128)(2,1)}, u32[]{:S(2)}) %copy-start) | copy-done | bytes 3145752
  64.9 0.2 shard_map.65.refs_2_
  65.1 3.7 %collective-permute-done.4.refs_3_ = bf16[8,3,4,128,128]{4,3,2,1,0:T(8,128)(2,1)S(1)} collective-permute-done((bf16[8,3,4,128,128]{4,3,2,1,0:T(8,128)(2,1)}, bf16[8,3,4,128,128]{4,3,2,1,0:T(8,128)(2,1)S(1)}, u32[]{:S(2)}, u32[]{:S(2)}) %collective-permute-start.4) | collective-permute-done | bytes 3145760 | tf_op jit(solution)/shard_map/ppermute | solution.py:255
  68.8 2.8 %shard_map.66 = (bf16[4,128,256]{2,1,0:T(8,128)(2,1)S(1)}, bf16[4,128,256]{2,1,0:T(8,128)(2,1)S(1)}, bf16[2,128,256]{2,1,0:T(8,128)(2,1)S(1)}, bf16[2,2,128,256]{3,2,1,0:T(8,128)(2,1)S(1)}) custom-call(s32[4]{0:T(128)S(1)} %pad_add_fusion.refs_0_, f32[6]{0:T(128)S(1)} %pad_maximum_fusion.2.refs_1_, bf16[8,3,4,128,128]{4,3,2,1,0:T(8,128)(2,1)S(1)} %shard_map.65.refs_2_, ...), custom_call_target="tpu_custom_call" | custom-call | flops 754974720 | bytes 4194304 | tf_op jit(solution)/shard_map/pallas_call | solution.py:144
  71.6 3.4 %collective-permute-start.5 = (bf16[2,2,128,256]{3,2,1,0:T(8,128)(2,1)S(1)}, bf16[2,2,128,256]{3,2,1,0:T(8,128)(2,1)S(1)}, u32[]{:S(2)}, u32[]{:S(2)}) collective-permute-start(bf16[2,2,128,256]{3,2,1,0:T(8,128)(2,1)S(1)} %get-tuple-element.30), channel_id=1, source_target_pairs={{0,1},{1,16},{16,17},{17,32},{32,33},{33,48},{48,49},{2,3},{3,18},... | collective-permute-start | bytes 786440 | tf_op jit(solution)/shard_map/ppermute | solution.py:294
  75.1 7.7 %collective-permute-done.5.refs_6_ = bf16[2,2,128,256]{3,2,1,0:T(8,128)(2,1)S(1)} collective-permute-done((bf16[2,2,128,256]{3,2,1,0:T(8,128)(2,1)S(1)}, bf16[2,2,128,256]{3,2,1,0:T(8,128)(2,1)S(1)}, u32[]{:S(2)}, u32[]{:S(2)}) %collective-permute-start.5) | collective-permute-done | bytes 262176 | tf_op jit(solution)/shard_map/ppermute | solution.py:294
  82.7 2.5 %shard_map.67 = (bf16[2,128,256]{2,1,0:T(8,128)(2,1)S(1)}, bf16[4,128,256]{2,1,0:T(8,128)(2,1)S(1)}, bf16[2,128,256]{2,1,0:T(8,128)(2,1)S(1)}, bf16[2,2,128,256]{3,2,1,0:T(8,128)(2,1)S(1)}) custom-call(s32[4]{0:T(128)S(1)} %pad_add_fusion.refs_0_, f32[6]{0:T(128)S(1)} %pad_maximum_fusion.2.refs_1_, bf16[8,3,4,128,128]{4,3,2,1,0:T(8,128)(2,1)S(1)} %shard_map.65.refs_2_, ...), custom_call_target="tpu_custom_call" | custom-call | flops 503316480 | bytes 4194304 | tf_op jit(solution)/shard_map/pallas_call | solution.py:144
  85.3 2.5 %collective-permute-start.6 = (bf16[2,2,128,256]{3,2,1,0:T(8,128)(2,1)S(1)}, bf16[2,2,128,256]{3,2,1,0:T(8,128)(2,1)S(1)}, u32[]{:S(2)}, u32[]{:S(2)}) collective-permute-start(bf16[2,2,128,256]{3,2,1,0:T(8,128)(2,1)S(1)} %get-tuple-element.34), channel_id=1, source_target_pairs={{0,1},{1,16},{16,17},{17,32},{32,33},{33,48},{48,49},{2,3},{3,18},... | collective-permute-start | bytes 786440 | tf_op jit(solution)/shard_map/ppermute | solution.py:294
  87.9 7.7 %collective-permute-done.6.refs_6_ = bf16[2,2,128,256]{3,2,1,0:T(8,128)(2,1)S(1)} collective-permute-done((bf16[2,2,128,256]{3,2,1,0:T(8,128)(2,1)S(1)}, bf16[2,2,128,256]{3,2,1,0:T(8,128)(2,1)S(1)}, u32[]{:S(2)}, u32[]{:S(2)}) %collective-permute-start.6) | collective-permute-done | bytes 262176 | tf_op jit(solution)/shard_map/ppermute | solution.py:294
  95.6 2.5 %shard_map.68 = (bf16[2,128,256]{2,1,0:T(8,128)(2,1)S(1)}, bf16[4,128,256]{2,1,0:T(8,128)(2,1)S(1)}, bf16[2,128,256]{2,1,0:T(8,128)(2,1)S(1)}, bf16[2,2,128,256]{3,2,1,0:T(8,128)(2,1)S(1)}) custom-call(s32[4]{0:T(128)S(1)} %pad_add_fusion.refs_0_, f32[6]{0:T(128)S(1)} %pad_maximum_fusion.2.refs_1_, bf16[8,3,4,128,128]{4,3,2,1,0:T(8,128)(2,1)S(1)} %shard_map.65.refs_2_, ...), custom_call_target="tpu_custom_call" | custom-call | flops 503316480 | bytes 4194304 | tf_op jit(solution)/shard_map/pallas_call | solution.py:144
  98.1 1.9 %collective-permute-start.7 = (bf16[2,2,128,256]{3,2,1,0:T(8,128)(2,1)S(1)}, bf16[2,2,128,256]{3,2,1,0:T(8,128)(2,1)S(1)}, u32[]{:S(2)}, u32[]{:S(2)}) collective-permute-start(bf16[2,2,128,256]{3,2,1,0:T(8,128)(2,1)S(1)} %get-tuple-element.38), channel_id=1, source_target_pairs={{0,1},{1,16},{16,17},{17,32},{32,33},{33,48},{48,49},{2,3},{3,18},... | collective-permute-start | bytes 786440 | tf_op jit(solution)/shard_map/ppermute | solution.py:294
  100.1 7.4 %collective-permute-done.7.refs_6_ = bf16[2,2,128,256]{3,2,1,0:T(8,128)(2,1)S(1)} collective-permute-done((bf16[2,2,128,256]{3,2,1,0:T(8,128)(2,1)S(1)}, bf16[2,2,128,256]{3,2,1,0:T(8,128)(2,1)S(1)}, u32[]{:S(2)}, u32[]{:S(2)}) %collective-permute-start.7) | collective-permute-done | bytes 262176 | tf_op jit(solution)/shard_map/ppermute | solution.py:294
  107.5 1.9 %shard_map.69 = (bf16[2,128,256]{2,1,0:T(8,128)(2,1)S(1)}, bf16[4,128,128]{2,1,0:T(8,128)(2,1)S(1)}) custom-call(s32[4]{0:T(128)S(1)} %pad_add_fusion.refs_0_, f32[6]{0:T(128)S(1)} %pad_maximum_fusion.2.refs_1_, bf16[8,3,4,128,128]{4,3,2,1,0:T(8,128)(2,1)S(1)} %shard_map.65.refs_2_, bf16[8,3,4,128,128]{4,3,2,1,0:T(8,128)(2,1)S(1)} %collective-permute-done.4.refs_3_, ...), custom_call_target="tpu_custom_call" | custom-call | flops 377487360 | bytes 4194304 | tf_op jit(solution)/shard_map/pallas_call | solution.py:144
  109.5 4.6 %all_to_all.15.over = bf16[2,4,8,64,128]{4,3,2,1,0:T(8,128)(2,1)S(1)} all-to-all(bf16[2,4,8,64,128]{4,3,2,1,0:T(8,128)(2,1)S(1)} %bitcast.25), channel_id=1, replica_groups=mesh['zhi'=4,'core'=2,'x'=4,'zlo'=2,'yl'=4,'y0'=2] {'core'}, dimensions={0} | all-to-all | bytes 2097152 | tf_op jit(solution)/shard_map/all_to_all | solution.py:336
  114.1 0.1 shard_map.70
  114.2 29.4 %all_to_all.16.over = bf16[32,64,128]{2,1,0:T(8,128)(2,1)S(1)} all-to-all(bf16[32,64,128]{2,1,0:T(8,128)(2,1)S(1)} %bitcast.22), channel_id=1, replica_groups=mesh['zhi'=4,'core'=2,'x'=4,'zlo'=2,'yl'=4,'y0'=2] {'zhi','zlo','yl'}, dimensions={0} | all-to-all | bytes 1048576 | tf_op jit(solution)/shard_map/all_to_all | solution.py:338
  143.7 1.9 %collective-permute-start.8 = (bf16[64,128]{1,0:T(8,128)(2,1)S(1)}, bf16[64,128]{1,0:T(8,128)(2,1)S(1)}, u32[]{:S(2)}, u32[]{:S(2)}) collective-permute-start(bf16[64,128]{1,0:T(8,128)(2,1)S(1)} %shard_map.71), channel_id=1, source_target_pairs={{1,8},{8,1},{3,10},{10,3},{5,12},{12,5},{7,14},{14,7},{17,24},{24,... | collective-permute-start | bytes 49160 | tf_op jit(solution)/shard_map/ppermute | solution.py:340
  145.6 4.6 %collective-permute-done.8 = bf16[64,128]{1,0:T(8,128)(2,1)S(1)} collective-permute-done((bf16[64,128]{1,0:T(8,128)(2,1)S(1)}, bf16[64,128]{1,0:T(8,128)(2,1)S(1)}, u32[]{:S(2)}, u32[]{:S(2)}) %collective-permute-start.8) | collective-permute-done | bytes 16416 | tf_op jit(solution)/shard_map/ppermute | solution.py:340
  150.2 0.6 select_bitcast_fusion
  (38 shorter events, 1.0 us)
Async XLA Ops:
  6.5 2.5 %copy-start.1 = (bf16[1,4096,128]{2,1,0:T(8,128)(2,1)S(1)}, bf16[1,4096,128]{2,1,0:T(8,128)(2,1)}, u32[]{:S(2)}) copy-start(bf16[1,4096,128]{2,1,0:T(8,128)(2,1)} %param.7) | copy-start | bytes 3145732
  6.5 54.6 %all-gather.2.cloned.1.call-start = ((), (), s32[]{:S(2)}) async-start(), calls=%async_computation.3 | async-start | bytes 3538944 | tf_op jit(solution)/shard_map/all_gather | solution.py:231
  9.2 6.1 %copy-start.4 = (bf16[64,128]{1,0:T(8,128)(2,1)S(1)}, bf16[64,128]{1,0:T(8,128)(2,1)}, u32[]{:S(2)}) copy-start(bf16[64,128]{1,0:T(8,128)(2,1)} %param.8) | copy-start | bytes 49156
  9.2 10.8 %copy-start.2 = (f32[1,3]{1,0:T(1,128)S(1)}, f32[1,3]{1,0:T(1,128)}, u32[]{:S(2)}) copy-start(f32[1,3]{1,0:T(1,128)} %param.11) | copy-start | bytes 40
  9.3 10.8 %copy-start.3 = (f32[1,3]{1,0:T(1,128)S(1)}, f32[1,3]{1,0:T(1,128)}, u32[]{:S(2)}) copy-start(f32[1,3]{1,0:T(1,128)} %param.10) | copy-start | bytes 40
  10.5 18.5 %all-to-all-start = ((bf16[4,8,128,128]{3,2,1,0:T(8,128)(2,1)}), bf16[4,8,128,128]{3,2,1,0:T(8,128)(2,1)S(1)}, u32[]{:S(2)}, u32[]{:S(2)}) async-start(bf16[4,8,128,128]{3,2,1,0:T(8,128)(2,1)} %bitcast.4), calls=%async_computation | async-start | bytes 2097152 | tf_op jit(solution)/shard_map/all_to_all | solution.py:235
  15.3 14.4 %collective-permute-start.1 = (bf16[64,128]{1,0:T(8,128)(2,1)S(1)}, bf16[64,128]{1,0:T(8,128)(2,1)S(1)}, u32[]{:S(2)}, u32[]{:S(2)}) collective-permute-start(bf16[64,128]{1,0:T(8,128)(2,1)S(1)} %copy-done.4), channel_id=1, source_target_pairs={{0,1},{2,3},{4,5},{6,7},{8,24},{10,26},{12,28},{14,30},{16,17},{18... | collective-permute-start | bytes 49160 | tf_op jit(solution)/shard_map/ppermute | solution.py:247
  18.7 11.1 %collective-permute-start.2 = (bf16[64,128]{1,0:T(8,128)(2,1)S(1)}, bf16[64,128]{1,0:T(8,128)(2,1)S(1)}, u32[]{:S(2)}, u32[]{:S(2)}) collective-permute-start(bf16[64,128]{1,0:T(8,128)(2,1)S(1)} %copy-done.4), channel_id=1, source_target_pairs={{0,0},{2,2},{4,4},{6,6},{8,9},{10,11},{12,13},{14,15},{16,16},{18,... | collective-permute-start | bytes 49160 | tf_op jit(solution)/shard_map/ppermute | solution.py:246
  20.1 7.2 %collective-permute-start.3 = (f32[8]{0:T(128)S(1)}, f32[8]{0:T(128)S(1)}, u32[]{:S(2)}, u32[]{:S(2)}) collective-permute-start(f32[8]{0:T(128)S(1)} %pad_maximum_fusion.1), channel_id=1, source_target_pairs={{0,0},{1,64},{2,2},{3,66},{4,4},{5,68},{6,6},{7,70},{8,8},{9,72},{... | collective-permute-start | bytes 104 | tf_op jit(solution)/shard_map/ppermute | solution.py:239
  29.0 0.9 collective-permute-start
  61.1 7.8 %collective-permute-start.4 = (bf16[8,3,4,128,128]{4,3,2,1,0:T(8,128)(2,1)}, bf16[8,3,4,128,128]{4,3,2,1,0:T(8,128)(2,1)S(1)}, u32[]{:S(2)}, u32[]{:S(2)}) collective-permute-start(bf16[8,3,4,128,128]{4,3,2,1,0:T(8,128)(2,1)} %all-gather.2.cloned.1.call-done.blocks), channel_id=1, source_target_pairs={{0,64},{64,0},{1,65},{65,1},{2,66},{66,2},{3,67},{67,3},{4,68},{68... | collective-permute-start | bytes 9437192 | tf_op jit(solution)/shard_map/ppermute | solution.py:255
  63.0 1.9 %copy-start = (bf16[8,3,4,128,128]{4,3,2,1,0:T(8,128)(2,1)S(1)}, bf16[8,3,4,128,128]{4,3,2,1,0:T(8,128)(2,1)}, u32[]{:S(2)}) copy-start(bf16[8,3,4,128,128]{4,3,2,1,0:T(8,128)(2,1)} %all-gather.2.cloned.1.call-done.blocks) | copy-start | bytes 9437188
  71.6 11.1 %collective-permute-start.5 = (bf16[2,2,128,256]{3,2,1,0:T(8,128)(2,1)S(1)}, bf16[2,2,128,256]{3,2,1,0:T(8,128)(2,1)S(1)}, u32[]{:S(2)}, u32[]{:S(2)}) collective-permute-start(bf16[2,2,128,256]{3,2,1,0:T(8,128)(2,1)S(1)} %get-tuple-element.30), channel_id=1, source_target_pairs={{0,1},{1,16},{16,17},{17,32},{32,33},{33,48},{48,49},{2,3},{3,18},... | collective-permute-start | bytes 786440 | tf_op jit(solution)/shard_map/ppermute | solution.py:294
  85.3 10.3 %collective-permute-start.6 = (bf16[2,2,128,256]{3,2,1,0:T(8,128)(2,1)S(1)}, bf16[2,2,128,256]{3,2,1,0:T(8,128)(2,1)S(1)}, u32[]{:S(2)}, u32[]{:S(2)}) collective-permute-start(bf16[2,2,128,256]{3,2,1,0:T(8,128)(2,1)S(1)} %get-tuple-element.34), channel_id=1, source_target_pairs={{0,1},{1,16},{16,17},{17,32},{32,33},{33,48},{48,49},{2,3},{3,18},... | collective-permute-start | bytes 786440 | tf_op jit(solution)/shard_map/ppermute | solution.py:294
  98.1 9.4 %collective-permute-start.7 = (bf16[2,2,128,256]{3,2,1,0:T(8,128)(2,1)S(1)}, bf16[2,2,128,256]{3,2,1,0:T(8,128)(2,1)S(1)}, u32[]{:S(2)}, u32[]{:S(2)}) collective-permute-start(bf16[2,2,128,256]{3,2,1,0:T(8,128)(2,1)S(1)} %get-tuple-element.38), channel_id=1, source_target_pairs={{0,1},{1,16},{16,17},{17,32},{32,33},{33,48},{48,49},{2,3},{3,18},... | collective-permute-start | bytes 786440 | tf_op jit(solution)/shard_map/ppermute | solution.py:294
  143.7 6.5 %collective-permute-start.8 = (bf16[64,128]{1,0:T(8,128)(2,1)S(1)}, bf16[64,128]{1,0:T(8,128)(2,1)S(1)}, u32[]{:S(2)}, u32[]{:S(2)}) collective-permute-start(bf16[64,128]{1,0:T(8,128)(2,1)S(1)} %shard_map.71), channel_id=1, source_target_pairs={{1,8},{8,1},{3,10},{10,3},{5,12},{12,5},{7,14},{14,7},{17,24},{24,... | collective-permute-start | bytes 49160 | tf_op jit(solution)/shard_map/ppermute | solution.py:340
Sparse Core Ops, SparseCore 0:
  9.4 51.6 all-gather.1

commit v8 on v7

--- a/solution.py
+++ b/solution.py
@@ -13,6 +13,7 @@
 HALF = 4
 WINDOW = 2 * HALF
 BEFORE = 3
+RING = 8
 STATES = 3
 AXES = ("zhi", "core", "x", "zlo", "yl", "y0")
 BF16 = jnp.bfloat16
@@ -157,34 +158,47 @@
     )(whole, part, mine, other, *ins)
 
 
-def take_piece(start, site, piece, taken, sems):
+def take_piece(start, site, piece, sems):
     first = pl.multiple_of(start[0] * BLOCK, BLOCK)
-    spots = [(s, sector * BLOCK) for s in range(STATES) for sector in range(HALF)]
-    inward = [
-        pltpu.make_async_copy(
-            site.at[0, s, pl.ds(first + row, BLOCK)], taken.at[s, pl.ds(row, BLOCK)], sems.at[0, number]
-        )
-        for number, (s, row) in enumerate(spots)
+    taken = [
+        pltpu.make_async_copy(site.at[0, s, pl.ds(first, HALF * BLOCK)], piece.at[s], sems.at[s])
+        for s in range(STATES)
     ]
-    outward = [
-        pltpu.make_async_copy(
-            taken.at[s, pl.ds(row, BLOCK)], piece.at[s, pl.ds(row, BLOCK)], sems.at[1, number]
-        )
-        for number, (s, row) in enumerate(spots)
+    for copy in taken:
+        copy.start()
+    for copy in taken:
+        copy.wait()
+
+
+def in_order(steps, place, *refs):
+    pieces, held, sems = refs[:-2], refs[-2], refs[-1]
+    brought = [
+        pltpu.make_async_copy(piece, held.at[lax.rem(place[0] + step + RING, RING)], sems.at[number])
+        for number, (step, piece) in enumerate(zip(steps, pieces))
     ]
-    for copy in inward:
+    for copy in brought:
         copy.start()
-    for before, after in zip(inward, outward):
-        before.wait()
-        after.start()
-    for copy in outward:
+    for copy in brought:
         copy.wait()
 
 
-def bring(blocks, held, sem):
-    copy = pltpu.make_async_copy(blocks, held, sem)
-    copy.start()
-    copy.wait()
+def gather_along_z(piece, place):
+    upward = [(i, (i + 1) % RING) for i in range(RING)]
+    downward = [(i, (i - 1) % RING) for i in range(RING)]
+    arrived = {0: piece}
+    for step in range(1, RING // 2 + 1):
+        arrived[-step] = lax.ppermute(arrived[1 - step], ("zhi", "zlo"), upward)
+        if step < RING // 2:
+            arrived[step] = lax.ppermute(arrived[step - 1], ("zhi", "zlo"), downward)
+    return pl.pallas_call(
+        functools.partial(in_order, tuple(arrived)),
+        out_shape=jax.ShapeDtypeStruct((RING,) + piece.shape, BF16),
+        in_specs=[pl.BlockSpec(memory_space=pltpu.SMEM)] + [pl.BlockSpec(memory_space=pl.ANY)] * RING,
+        out_specs=pl.BlockSpec(memory_space=pltpu.VMEM),
+        scratch_shapes=[pltpu.SemaphoreType.DMA((RING,))],
+        compiler_params=pltpu.CompilerParams(vmem_limit_bytes=16 << 20),
+        cost_estimate=pl.CostEstimate(flops=0, bytes_accessed=6 << 20, transcendentals=0),
+    )(place, *arrived.values())
 
 
 def add_cores(over, summed):
@@ -222,13 +236,14 @@
     piece = pl.pallas_call(
         take_piece,
         out_shape=jax.ShapeDtypeStruct((STATES, HALF * BLOCK, BLOCK), BF16),
-        in_specs=[pl.BlockSpec(memory_space=pltpu.SMEM), pl.BlockSpec(memory_space=pltpu.HBM)],
-        out_specs=pl.BlockSpec(memory_space=pltpu.HBM),
-        scratch_shapes=[pltpu.VMEM((STATES, HALF * BLOCK, BLOCK), BF16), pltpu.SemaphoreType.DMA((2, STATES * HALF))],
+        in_specs=[pl.BlockSpec(memory_space=pltpu.SMEM), pl.BlockSpec(memory_space=pl.ANY)],
+        out_specs=pl.BlockSpec(memory_space=pltpu.VMEM),
+        scratch_shapes=[pltpu.SemaphoreType.DMA((STATES,))],
         compiler_params=pltpu.CompilerParams(vmem_limit_bytes=60 << 20),
         cost_estimate=pl.CostEstimate(flops=0, bytes_accessed=800_000, transcendentals=0),
     )(start, site_tensor).reshape(STATES, HALF, BLOCK, BLOCK)
-    mine = lax.all_gather(piece, ("zhi", "zlo"))
+    place = (lax.axis_index("zhi") * 2 + at_zlo).astype(jnp.int32).reshape(1)
+    mine = gather_along_z(piece, place)
     spots = [site_start(sectors, group, half) - (OWN * group - BEFORE) for half in range(2)]
 
     pieces = ops_pieces(term_ops[0].reshape(sectors, BLOCK, BLOCK), term_shift[0], core)
@@ -253,15 +268,6 @@
 
     mine, window, whole, part = lax.optimization_barrier((mine, window, whole, part))
     other = lax.ppermute(mine, "core", [(0, 1), (1, 0)])
-    mine = pl.pallas_call(
-        bring,
-        out_shape=jax.ShapeDtypeStruct(mine.shape, BF16),
-        in_specs=[pl.BlockSpec(memory_space=pl.ANY)],
-        out_specs=pl.BlockSpec(memory_space=pltpu.VMEM),
-        scratch_shapes=[pltpu.SemaphoreType.DMA],
-        compiler_params=pltpu.CompilerParams(vmem_limit_bytes=16 << 20),
-        cost_estimate=pl.CostEstimate(flops=0, bytes_accessed=6 << 20, transcendentals=0),
-    )(mine)
 
     wide = (BLOCK, 2 * BLOCK)
     onward = [(i, i + 1) for i in range(7)]

time: 158 us -> 159 us (level)
  the two profiles are of different devices: /device:TPU:66 before, /device:TPU:70 now
where the time goes in v8:
time: 159 us
  starting transfers between devices  50.7 us (32%)
  waiting for transfers between devices  50.7 us (32%)
  blocking collectives  38.8 us (24%)
  Pallas kernels  13.5 us (8%)
  other arithmetic  2.36 us (1%)
  between operations  1.68 us (1%)
    all_to_all x1, blocking collectives, body(): over = lax.all_to_all(summed, ('zhi', 'zlo', 'yl'), 0, 0)  34.2 us
    ppermute x3, waiting for transfers between devices, body(): tails = lax.ppermute(tails, ('x', 'y0'), onward)  25.1 us
    ppermute x3, starting transfers between devices, gather_along_z(): arrived[step] = lax.ppermute(arrived[step - 1], ('zhi', 'zlo'), downward)  12.3 us
    ppermute x4, starting transfers between devices, gather_along_z(): arrived[-step] = lax.ppermute(arrived[1 - step], ('zhi', 'zlo'), upward)  12.2 us
    pallas_call x4, Pallas kernels, run_phase(): pl.pallas_call(functools.partial(phase_kernel, sites, steps, len(ins), so...  9.76 us
    ppermute x3, waiting for transfers between devices, gather_along_z(): arrived[step] = lax.ppermute(arrived[step - 1], ('zhi', 'zlo'), downward)  9.41 us
    ppermute x3, starting transfers between devices, body(): tails = lax.ppermute(tails, ('x', 'y0'), onward)  6.64 us
    ppermute x1, waiting for transfers between devices, body(): other = lax.ppermute(mine, 'core', [(0, 1), (1, 0)])  5.63 us
  transfers between devices with their start and end apart: 17, of which 9 were waited for; matrix products, arithmetic and copies ran while one was open for 2% of the time, Pallas kernels for 0%

profile of v8, /device:TPU:70, one launch (start us, length us, event | category | flops | bytes accessed | tf_op | source)
XLA Modules:
  0.0 158.8 jit_solution(6569319250288607991)
XLA Ops:
  0.0 1.9 %shard_map.64 = bf16[3,512,128]{2,1,0:T(8,128)(2,1)} custom-call(s32[1]{0:T(128)} %bitcast.1.start, bf16[1,3,4096,128]{3,2,1,0:T(8,128)(2,1)} %site.1), custom_call_target="tpu_custom_call" | custom-call | bytes 800000 | tf_op jit(solution)/shard_map/pallas_call | solution.py:236
  1.9 4.3 %collective-permute-start = (bf16[3,4,128,128]{3,2,1,0:T(8,128)(2,1)}, bf16[3,4,128,128]{3,2,1,0:T(8,128)(2,1)S(1)}, u32[]{:S(2)}, u32[]{:S(2)}) collective-permute-start(bf16[3,4,128,128]{3,2,1,0:T(8,128)(2,1)} %bitcast.24), channel_id=1, source_target_pairs={{0,8},{8,128},{128,136},{136,256},{256,264},{264,384},{384,392},{3... | collective-permute-start | bytes 1179656 | tf_op jit(solution)/shard_map/ppermute | solution.py:190
  8.4 4.8 %all-to-all-start = ((bf16[4,8,128,128]{3,2,1,0:T(8,128)(2,1)}), bf16[4,8,128,128]{3,2,1,0:T(8,128)(2,1)S(1)}, u32[]{:S(2)}, u32[]{:S(2)}) async-start(bf16[4,8,128,128]{3,2,1,0:T(8,128)(2,1)} %bitcast.5), calls=%async_computation | async-start | bytes 2097152 | tf_op jit(solution)/shard_map/all_to_all | solution.py:250
  13.1 3.8 %collective-permute-start.1 = (bf16[3,4,128,128]{3,2,1,0:T(8,128)(2,1)S(1)}, bf16[3,4,128,128]{3,2,1,0:T(8,128)(2,1)S(1)}, u32[]{:S(2)}, u32[]{:S(2)}) collective-permute-start(bf16[3,4,128,128]{3,2,1,0:T(8,128)(2,1)S(1)} %bitcast.25), channel_id=1, source_target_pairs={{0,392},{8,0},{128,8},{136,128},{256,136},{264,256},{384,264},{392... | collective-permute-start | bytes 1179656 | tf_op jit(solution)/shard_map/ppermute | solution.py:192
  16.9 2.4 %collective-permute-start.2 = (bf16[3,4,128,128]{3,2,1,0:T(8,128)(2,1)S(1)}, bf16[3,4,128,128]{3,2,1,0:T(8,128)(2,1)S(1)}, u32[]{:S(2)}, u32[]{:S(2)}) collective-permute-start(bf16[3,4,128,128]{3,2,1,0:T(8,128)(2,1)S(1)} %collective-permute-done.refs_1_), channel_id=1, source_target_pairs={{0,8},{8,128},{128,136},{136,256},{256,264},{264,384},{384,392},{3... | collective-permute-start | bytes 1179656 | tf_op jit(solution)/shard_map/ppermute | solution.py:190
  19.4 3.5 %collective-permute-start.9 = (bf16[64,128]{1,0:T(8,128)(2,1)S(1)}, bf16[64,128]{1,0:T(8,128)(2,1)S(1)}, u32[]{:S(2)}, u32[]{:S(2)}) collective-permute-start(bf16[64,128]{1,0:T(8,128)(2,1)S(1)} %copy-done.4), channel_id=1, source_target_pairs={{0,0},{2,2},{4,4},{6,6},{8,9},{10,11},{12,13},{14,15},{16,16},{18,... | collective-permute-start | bytes 49160 | tf_op jit(solution)/shard_map/ppermute | solution.py:261
  22.8 1.3 collective-permute-start.8
  24.3 5.4 %collective-permute-start.10 = (f32[8]{0:T(128)S(1)}, f32[8]{0:T(128)S(1)}, u32[]{:S(2)}, u32[]{:S(2)}) collective-permute-start(f32[8]{0:T(128)S(1)} %pad_maximum_fusion.1), channel_id=1, source_target_pairs={{0,0},{1,64},{2,2},{3,66},{4,4},{5,68},{6,6},{7,70},{8,8},{9,72},{... | collective-permute-start | bytes 104 | tf_op jit(solution)/shard_map/ppermute | solution.py:254
  29.7 4.8 %collective-permute-done.10 = f32[8]{0:T(128)S(1)} collective-permute-done((f32[8]{0:T(128)S(1)}, f32[8]{0:T(128)S(1)}, u32[]{:S(2)}, u32[]{:S(2)}) %collective-permute-start.10) | collective-permute-done | bytes 64 | tf_op jit(solution)/shard_map/ppermute | solution.py:254
  35.7 5.0 %collective-permute-start.3 = (bf16[3,4,128,128]{3,2,1,0:T(8,128)(2,1)S(1)}, bf16[3,4,128,128]{3,2,1,0:T(8,128)(2,1)S(1)}, u32[]{:S(2)}, u32[]{:S(2)}) collective-permute-start(bf16[3,4,128,128]{3,2,1,0:T(8,128)(2,1)S(1)} %collective-permute-done.1.refs_2_), channel_id=1, source_target_pairs={{0,392},{8,0},{128,8},{136,128},{256,136},{264,256},{384,264},{392... | collective-permute-start | bytes 1179656 | tf_op jit(solution)/shard_map/ppermute | solution.py:192
  40.7 1.9 %collective-permute-start.4 = (bf16[3,4,128,128]{3,2,1,0:T(8,128)(2,1)S(1)}, bf16[3,4,128,128]{3,2,1,0:T(8,128)(2,1)S(1)}, u32[]{:S(2)}, u32[]{:S(2)}) collective-permute-start(bf16[3,4,128,128]{3,2,1,0:T(8,128)(2,1)S(1)} %collective-permute-done.2.refs_3_), channel_id=1, source_target_pairs={{0,8},{8,128},{128,136},{136,256},{256,264},{264,384},{384,392},{3... | collective-permute-start | bytes 1179656 | tf_op jit(solution)/shard_map/ppermute | solution.py:190
  43.5 4.0 %collective-permute-done.3.refs_4_ = bf16[3,4,128,128]{3,2,1,0:T(8,128)(2,1)S(1)} collective-permute-done((bf16[3,4,128,128]{3,2,1,0:T(8,128)(2,1)S(1)}, bf16[3,4,128,128]{3,2,1,0:T(8,128)(2,1)S(1)}, u32[]{:S(2)}, u32[]{:S(2)}) %collective-permute-start.3) | collective-permute-done | bytes 393248 | tf_op jit(solution)/shard_map/ppermute | solution.py:192
  47.5 3.5 %collective-permute-start.5 = (bf16[3,4,128,128]{3,2,1,0:T(8,128)(2,1)S(1)}, bf16[3,4,128,128]{3,2,1,0:T(8,128)(2,1)S(1)}, u32[]{:S(2)}, u32[]{:S(2)}) collective-permute-start(bf16[3,4,128,128]{3,2,1,0:T(8,128)(2,1)S(1)} %collective-permute-done.3.refs_4_), channel_id=1, source_target_pairs={{0,392},{8,0},{128,8},{136,128},{256,136},{264,256},{384,264},{392... | collective-permute-start | bytes 1179656 | tf_op jit(solution)/shard_map/ppermute | solution.py:192
  51.0 3.6 %collective-permute-start.6 = (bf16[3,4,128,128]{3,2,1,0:T(8,128)(2,1)S(1)}, bf16[3,4,128,128]{3,2,1,0:T(8,128)(2,1)S(1)}, u32[]{:S(2)}, u32[]{:S(2)}) collective-permute-start(bf16[3,4,128,128]{3,2,1,0:T(8,128)(2,1)S(1)} %collective-permute-done.4.refs_5_), channel_id=1, source_target_pairs={{0,8},{8,128},{128,136},{136,256},{256,264},{264,384},{384,392},{3... | collective-permute-start | bytes 1179656 | tf_op jit(solution)/shard_map/ppermute | solution.py:190
  54.9 5.4 %collective-permute-done.5.refs_6_ = bf16[3,4,128,128]{3,2,1,0:T(8,128)(2,1)S(1)} collective-permute-done((bf16[3,4,128,128]{3,2,1,0:T(8,128)(2,1)S(1)}, bf16[3,4,128,128]{3,2,1,0:T(8,128)(2,1)S(1)}, u32[]{:S(2)}, u32[]{:S(2)}) %collective-permute-start.5) | collective-permute-done | bytes 393248 | tf_op jit(solution)/shard_map/ppermute | solution.py:192
  61.6 1.6 %shard_map.65.refs_2_ = bf16[8,3,4,128,128]{4,3,2,1,0:T(8,128)(2,1)S(1)} custom-call(s32[1]{0:T(128)} %bitcast.place, bf16[3,4,128,128]{3,2,1,0:T(8,128)(2,1)S(1)} %bitcast.26, bf16[3,4,128,128]{3,2,1,0:T(8,128)(2,1)S(1)} %collective-permute-done.refs_1_, bf16[3,4,128,128]{3,2,1,0:T(8,128)(2,1)S(1)} %collective-permute-done.1.refs_2_, ...), custom_call_target="tpu_custom_call" | custom-call | bytes 6291456 | tf_op jit(solution)/shard_map/pallas_call | solution.py:193
  63.2 1.9 %collective-permute-start.11 = (bf16[8,3,4,128,128]{4,3,2,1,0:T(8,128)(2,1)S(1)}, bf16[8,3,4,128,128]{4,3,2,1,0:T(8,128)(2,1)S(1)}, u32[]{:S(2)}, u32[]{:S(2)}) collective-permute-start(bf16[8,3,4,128,128]{4,3,2,1,0:T(8,128)(2,1)S(1)} %shard_map.65.refs_2_), channel_id=1, source_target_pairs={{0,64},{64,0},{1,65},{65,1},{2,66},{66,2},{3,67},{67,3},{4,68},{68... | collective-permute-start | bytes 9437192 | tf_op jit(solution)/shard_map/ppermute | solution.py:270
  65.1 5.6 %collective-permute-done.11.refs_3_ = bf16[8,3,4,128,128]{4,3,2,1,0:T(8,128)(2,1)S(1)} collective-permute-done((bf16[8,3,4,128,128]{4,3,2,1,0:T(8,128)(2,1)S(1)}, bf16[8,3,4,128,128]{4,3,2,1,0:T(8,128)(2,1)S(1)}, u32[]{:S(2)}, u32[]{:S(2)}) %collective-permute-start.11) | collective-permute-done | bytes 3145760 | tf_op jit(solution)/shard_map/ppermute | solution.py:270
  70.7 2.8 %shard_map.66 = (bf16[4,128,256]{2,1,0:T(8,128)(2,1)S(1)}, bf16[4,128,256]{2,1,0:T(8,128)(2,1)S(1)}, bf16[2,128,256]{2,1,0:T(8,128)(2,1)S(1)}, bf16[2,2,128,256]{3,2,1,0:T(8,128)(2,1)S(1)}) custom-call(s32[4]{0:T(128)S(1)} %pad_add_fusion.refs_0_, f32[6]{0:T(128)S(1)} %pad_maximum_fusion.2.refs_1_, bf16[8,3,4,128,128]{4,3,2,1,0:T(8,128)(2,1)S(1)} %shard_map.65.refs_2_, ...), custom_call_target="tpu_custom_call" | custom-call | flops 754974720 | bytes 4194304 | tf_op jit(solution)/shard_map/pallas_call | solution.py:145
  73.5 2.8 %collective-permute-start.12 = (bf16[2,2,128,256]{3,2,1,0:T(8,128)(2,1)S(1)}, bf16[2,2,128,256]{3,2,1,0:T(8,128)(2,1)S(1)}, u32[]{:S(2)}, u32[]{:S(2)}) collective-permute-start(bf16[2,2,128,256]{3,2,1,0:T(8,128)(2,1)S(1)} %get-tuple-element.30), channel_id=1, source_target_pairs={{0,1},{1,16},{16,17},{17,32},{32,33},{33,48},{48,49},{2,3},{3,18},... | collective-permute-start | bytes 786440 | tf_op jit(solution)/shard_map/ppermute | solution.py:300
  76.4 8.7 %collective-permute-done.12.refs_6_ = bf16[2,2,128,256]{3,2,1,0:T(8,128)(2,1)S(1)} collective-permute-done((bf16[2,2,128,256]{3,2,1,0:T(8,128)(2,1)S(1)}, bf16[2,2,128,256]{3,2,1,0:T(8,128)(2,1)S(1)}, u32[]{:S(2)}, u32[]{:S(2)}) %collective-permute-start.12) | collective-permute-done | bytes 262176 | tf_op jit(solution)/shard_map/ppermute | solution.py:300
  85.1 2.5 %shard_map.67 = (bf16[2,128,256]{2,1,0:T(8,128)(2,1)S(1)}, bf16[4,128,256]{2,1,0:T(8,128)(2,1)S(1)}, bf16[2,128,256]{2,1,0:T(8,128)(2,1)S(1)}, bf16[2,2,128,256]{3,2,1,0:T(8,128)(2,1)S(1)}) custom-call(s32[4]{0:T(128)S(1)} %pad_add_fusion.refs_0_, f32[6]{0:T(128)S(1)} %pad_maximum_fusion.2.refs_1_, bf16[8,3,4,128,128]{4,3,2,1,0:T(8,128)(2,1)S(1)} %shard_map.65.refs_2_, ...), custom_call_target="tpu_custom_call" | custom-call | flops 503316480 | bytes 4194304 | tf_op jit(solution)/shard_map/pallas_call | solution.py:145
  87.7 1.9 %collective-permute-start.13 = (bf16[2,2,128,256]{3,2,1,0:T(8,128)(2,1)S(1)}, bf16[2,2,128,256]{3,2,1,0:T(8,128)(2,1)S(1)}, u32[]{:S(2)}, u32[]{:S(2)}) collective-permute-start(bf16[2,2,128,256]{3,2,1,0:T(8,128)(2,1)S(1)} %get-tuple-element.34), channel_id=1, source_target_pairs={{0,1},{1,16},{16,17},{17,32},{32,33},{33,48},{48,49},{2,3},{3,18},... | collective-permute-start | bytes 786440 | tf_op jit(solution)/shard_map/ppermute | solution.py:300
  89.7 8.6 %collective-permute-done.13.refs_6_ = bf16[2,2,128,256]{3,2,1,0:T(8,128)(2,1)S(1)} collective-permute-done((bf16[2,2,128,256]{3,2,1,0:T(8,128)(2,1)S(1)}, bf16[2,2,128,256]{3,2,1,0:T(8,128)(2,1)S(1)}, u32[]{:S(2)}, u32[]{:S(2)}) %collective-permute-start.13) | collective-permute-done | bytes 262176 | tf_op jit(solution)/shard_map/ppermute | solution.py:300
  98.3 2.5 %shard_map.68 = (bf16[2,128,256]{2,1,0:T(8,128)(2,1)S(1)}, bf16[4,128,256]{2,1,0:T(8,128)(2,1)S(1)}, bf16[2,128,256]{2,1,0:T(8,128)(2,1)S(1)}, bf16[2,2,128,256]{3,2,1,0:T(8,128)(2,1)S(1)}) custom-call(s32[4]{0:T(128)S(1)} %pad_add_fusion.refs_0_, f32[6]{0:T(128)S(1)} %pad_maximum_fusion.2.refs_1_, bf16[8,3,4,128,128]{4,3,2,1,0:T(8,128)(2,1)S(1)} %shard_map.65.refs_2_, ...), custom_call_target="tpu_custom_call" | custom-call | flops 503316480 | bytes 4194304 | tf_op jit(solution)/shard_map/pallas_call | solution.py:145
  100.9 1.9 %collective-permute-start.14 = (bf16[2,2,128,256]{3,2,1,0:T(8,128)(2,1)S(1)}, bf16[2,2,128,256]{3,2,1,0:T(8,128)(2,1)S(1)}, u32[]{:S(2)}, u32[]{:S(2)}) collective-permute-start(bf16[2,2,128,256]{3,2,1,0:T(8,128)(2,1)S(1)} %get-tuple-element.38), channel_id=1, source_target_pairs={{0,1},{1,16},{16,17},{17,32},{32,33},{33,48},{48,49},{2,3},{3,18},... | collective-permute-start | bytes 786440 | tf_op jit(solution)/shard_map/ppermute | solution.py:300
  102.9 7.7 %collective-permute-done.14.refs_6_ = bf16[2,2,128,256]{3,2,1,0:T(8,128)(2,1)S(1)} collective-permute-done((bf16[2,2,128,256]{3,2,1,0:T(8,128)(2,1)S(1)}, bf16[2,2,128,256]{3,2,1,0:T(8,128)(2,1)S(1)}, u32[]{:S(2)}, u32[]{:S(2)}) %collective-permute-start.14) | collective-permute-done | bytes 262176 | tf_op jit(solution)/shard_map/ppermute | solution.py:300
  110.6 1.9 %shard_map.69 = (bf16[2,128,256]{2,1,0:T(8,128)(2,1)S(1)}, bf16[4,128,128]{2,1,0:T(8,128)(2,1)S(1)}) custom-call(s32[4]{0:T(128)S(1)} %pad_add_fusion.refs_0_, f32[6]{0:T(128)S(1)} %pad_maximum_fusion.2.refs_1_, bf16[8,3,4,128,128]{4,3,2,1,0:T(8,128)(2,1)S(1)} %shard_map.65.refs_2_, bf16[8,3,4,128,128]{4,3,2,1,0:T(8,128)(2,1)S(1)} %collective-permute-done.11.refs_3_, ...), custom_call_target="tpu_custom_call" | custom-call | flops 377487360 | bytes 4194304 | tf_op jit(solution)/shard_map/pallas_call | solution.py:145
  112.6 4.6 %all_to_all.15.over = bf16[2,4,8,64,128]{4,3,2,1,0:T(8,128)(2,1)S(1)} all-to-all(bf16[2,4,8,64,128]{4,3,2,1,0:T(8,128)(2,1)S(1)} %bitcast.29), channel_id=1, replica_groups=mesh['zhi'=4,'core'=2,'x'=4,'zlo'=2,'yl'=4,'y0'=2] {'core'}, dimensions={0} | all-to-all | bytes 2097152 | tf_op jit(solution)/shard_map/all_to_all | solution.py:342
  117.3 34.2 %all_to_all.16.over = bf16[32,64,128]{2,1,0:T(8,128)(2,1)S(1)} all-to-all(bf16[32,64,128]{2,1,0:T(8,128)(2,1)S(1)} %bitcast.23), channel_id=1, replica_groups=mesh['zhi'=4,'core'=2,'x'=4,'zlo'=2,'yl'=4,'y0'=2] {'zhi','zlo','yl'}, dimensions={0} | all-to-all | bytes 1048576 | tf_op jit(solution)/shard_map/all_to_all | solution.py:344
  151.6 1.9 %collective-permute-start.15 = (bf16[64,128]{1,0:T(8,128)(2,1)S(1)}, bf16[64,128]{1,0:T(8,128)(2,1)S(1)}, u32[]{:S(2)}, u32[]{:S(2)}) collective-permute-start(bf16[64,128]{1,0:T(8,128)(2,1)S(1)} %shard_map.71), channel_id=1, source_target_pairs={{1,8},{8,1},{3,10},{10,3},{5,12},{12,5},{7,14},{14,7},{17,24},{24,... | collective-permute-start | bytes 49160 | tf_op jit(solution)/shard_map/ppermute | solution.py:346
  153.5 4.6 %collective-permute-done.15 = bf16[64,128]{1,0:T(8,128)(2,1)S(1)} collective-permute-done((bf16[64,128]{1,0:T(8,128)(2,1)S(1)}, bf16[64,128]{1,0:T(8,128)(2,1)S(1)}, u32[]{:S(2)}, u32[]{:S(2)}) %collective-permute-start.15) | collective-permute-done | bytes 16416 | tf_op jit(solution)/shard_map/ppermute | solution.py:346
  (49 shorter events, 5.6 us)
Async XLA Ops:
  0.0 6.8 %copy-start.1 = (bf16[1,4096,128]{2,1,0:T(8,128)(2,1)S(1)}, bf16[1,4096,128]{2,1,0:T(8,128)(2,1)}, u32[]{:S(2)}) copy-start(bf16[1,4096,128]{2,1,0:T(8,128)(2,1)} %param.7) | copy-start | bytes 3145732
  1.9 15.0 %collective-permute-start = (bf16[3,4,128,128]{3,2,1,0:T(8,128)(2,1)}, bf16[3,4,128,128]{3,2,1,0:T(8,128)(2,1)S(1)}, u32[]{:S(2)}, u32[]{:S(2)}) collective-permute-start(bf16[3,4,128,128]{3,2,1,0:T(8,128)(2,1)} %bitcast.24), channel_id=1, source_target_pairs={{0,8},{8,128},{128,136},{136,256},{256,264},{264,384},{384,392},{3... | collective-permute-start | bytes 1179656 | tf_op jit(solution)/shard_map/ppermute | solution.py:190
  7.0 6.1 %copy-start = (bf16[3,512,128]{2,1,0:T(8,128)(2,1)S(1)}, bf16[3,512,128]{2,1,0:T(8,128)(2,1)}, u32[]{:S(2)}) copy-start(bf16[3,512,128]{2,1,0:T(8,128)(2,1)} %shard_map.64) | copy-start | bytes 1179652
  7.0 12.3 %copy-start.4 = (bf16[64,128]{1,0:T(8,128)(2,1)S(1)}, bf16[64,128]{1,0:T(8,128)(2,1)}, u32[]{:S(2)}) copy-start(bf16[64,128]{1,0:T(8,128)(2,1)} %param.8) | copy-start | bytes 49156
  7.0 17.1 %copy-start.2 = (f32[1,3]{1,0:T(1,128)S(1)}, f32[1,3]{1,0:T(1,128)}, u32[]{:S(2)}) copy-start(f32[1,3]{1,0:T(1,128)} %param.11) | copy-start | bytes 40
  7.0 17.1 %copy-start.3 = (f32[1,3]{1,0:T(1,128)S(1)}, f32[1,3]{1,0:T(1,128)}, u32[]{:S(2)}) copy-start(f32[1,3]{1,0:T(1,128)} %param.10) | copy-start | bytes 40
  8.4 34.5 %all-to-all-start = ((bf16[4,8,128,128]{3,2,1,0:T(8,128)(2,1)}), bf16[4,8,128,128]{3,2,1,0:T(8,128)(2,1)S(1)}, u32[]{:S(2)}, u32[]{:S(2)}) async-start(bf16[4,8,128,128]{3,2,1,0:T(8,128)(2,1)} %bitcast.5), calls=%async_computation | async-start | bytes 2097152 | tf_op jit(solution)/shard_map/all_to_all | solution.py:250
  13.1 22.6 %collective-permute-start.1 = (bf16[3,4,128,128]{3,2,1,0:T(8,128)(2,1)S(1)}, bf16[3,4,128,128]{3,2,1,0:T(8,128)(2,1)S(1)}, u32[]{:S(2)}, u32[]{:S(2)}) collective-permute-start(bf16[3,4,128,128]{3,2,1,0:T(8,128)(2,1)S(1)} %bitcast.25), channel_id=1, source_target_pairs={{0,392},{8,0},{128,8},{136,128},{256,136},{264,256},{384,264},{392... | collective-permute-start | bytes 1179656 | tf_op jit(solution)/shard_map/ppermute | solution.py:192
  16.9 23.8 %collective-permute-start.2 = (bf16[3,4,128,128]{3,2,1,0:T(8,128)(2,1)S(1)}, bf16[3,4,128,128]{3,2,1,0:T(8,128)(2,1)S(1)}, u32[]{:S(2)}, u32[]{:S(2)}) collective-permute-start(bf16[3,4,128,128]{3,2,1,0:T(8,128)(2,1)S(1)} %collective-permute-done.refs_1_), channel_id=1, source_target_pairs={{0,8},{8,128},{128,136},{136,256},{256,264},{264,384},{384,392},{3... | collective-permute-start | bytes 1179656 | tf_op jit(solution)/shard_map/ppermute | solution.py:190
  19.4 35.5 %collective-permute-start.9 = (bf16[64,128]{1,0:T(8,128)(2,1)S(1)}, bf16[64,128]{1,0:T(8,128)(2,1)S(1)}, u32[]{:S(2)}, u32[]{:S(2)}) collective-permute-start(bf16[64,128]{1,0:T(8,128)(2,1)S(1)} %copy-done.4), channel_id=1, source_target_pairs={{0,0},{2,2},{4,4},{6,6},{8,9},{10,11},{12,13},{14,15},{16,16},{18,... | collective-permute-start | bytes 49160 | tf_op jit(solution)/shard_map/ppermute | solution.py:261
  22.8 31.9 %collective-permute-start.8 = (bf16[64,128]{1,0:T(8,128)(2,1)S(1)}, bf16[64,128]{1,0:T(8,128)(2,1)S(1)}, u32[]{:S(2)}, u32[]{:S(2)}) collective-permute-start(bf16[64,128]{1,0:T(8,128)(2,1)S(1)} %copy-done.4), channel_id=1, source_target_pairs={{0,1},{2,3},{4,5},{6,7},{8,24},{10,26},{12,28},{14,30},{16,17},{18... | collective-permute-start | bytes 49160 | tf_op jit(solution)/shard_map/ppermute | solution.py:262
  24.3 10.3 %collective-permute-start.10 = (f32[8]{0:T(128)S(1)}, f32[8]{0:T(128)S(1)}, u32[]{:S(2)}, u32[]{:S(2)}) collective-permute-start(f32[8]{0:T(128)S(1)} %pad_maximum_fusion.1), channel_id=1, source_target_pairs={{0,0},{1,64},{2,2},{3,66},{4,4},{5,68},{6,6},{7,70},{8,8},{9,72},{... | collective-permute-start | bytes 104 | tf_op jit(solution)/shard_map/ppermute | solution.py:254
  35.7 11.8 %collective-permute-start.3 = (bf16[3,4,128,128]{3,2,1,0:T(8,128)(2,1)S(1)}, bf16[3,4,128,128]{3,2,1,0:T(8,128)(2,1)S(1)}, u32[]{:S(2)}, u32[]{:S(2)}) collective-permute-start(bf16[3,4,128,128]{3,2,1,0:T(8,128)(2,1)S(1)} %collective-permute-done.1.refs_2_), channel_id=1, source_target_pairs={{0,392},{8,0},{128,8},{136,128},{256,136},{264,256},{384,264},{392... | collective-permute-start | bytes 1179656 | tf_op jit(solution)/shard_map/ppermute | solution.py:192
  40.7 10.3 %collective-permute-start.4 = (bf16[3,4,128,128]{3,2,1,0:T(8,128)(2,1)S(1)}, bf16[3,4,128,128]{3,2,1,0:T(8,128)(2,1)S(1)}, u32[]{:S(2)}, u32[]{:S(2)}) collective-permute-start(bf16[3,4,128,128]{3,2,1,0:T(8,128)(2,1)S(1)} %collective-permute-done.2.refs_3_), channel_id=1, source_target_pairs={{0,8},{8,128},{128,136},{136,256},{256,264},{264,384},{384,392},{3... | collective-permute-start | bytes 1179656 | tf_op jit(solution)/shard_map/ppermute | solution.py:190
  42.8 12.0 %collective-permute-start.7 = (bf16[8,128,128]{2,1,0:T(8,128)(2,1)S(1)}, bf16[8,128,128]{2,1,0:T(8,128)(2,1)S(1)}, u32[]{:S(2)}, u32[]{:S(2)}) collective-permute-start(bf16[8,128,128]{2,1,0:T(8,128)(2,1)S(1)} %dynamic-slice_bitcast_fusion), channel_id=1, source_target_pairs={{0,0},{1,64},{64,1},{65,65},{2,2},{3,66},{66,3},{67,67},{4,4},{5,6... | collective-permute-start | bytes 786440 | tf_op jit(solution)/shard_map/ppermute | solution.py:252
  47.5 12.9 %collective-permute-start.5 = (bf16[3,4,128,128]{3,2,1,0:T(8,128)(2,1)S(1)}, bf16[3,4,128,128]{3,2,1,0:T(8,128)(2,1)S(1)}, u32[]{:S(2)}, u32[]{:S(2)}) collective-permute-start(bf16[3,4,128,128]{3,2,1,0:T(8,128)(2,1)S(1)} %collective-permute-done.3.refs_4_), channel_id=1, source_target_pairs={{0,392},{8,0},{128,8},{136,128},{256,136},{264,256},{384,264},{392... | collective-permute-start | bytes 1179656 | tf_op jit(solution)/shard_map/ppermute | solution.py:192
  51.0 10.5 %collective-permute-start.6 = (bf16[3,4,128,128]{3,2,1,0:T(8,128)(2,1)S(1)}, bf16[3,4,128,128]{3,2,1,0:T(8,128)(2,1)S(1)}, u32[]{:S(2)}, u32[]{:S(2)}) collective-permute-start(bf16[3,4,128,128]{3,2,1,0:T(8,128)(2,1)S(1)} %collective-permute-done.4.refs_5_), channel_id=1, source_target_pairs={{0,8},{8,128},{128,136},{136,256},{256,264},{264,384},{384,392},{3... | collective-permute-start | bytes 1179656 | tf_op jit(solution)/shard_map/ppermute | solution.py:190
  63.2 7.6 %collective-permute-start.11 = (bf16[8,3,4,128,128]{4,3,2,1,0:T(8,128)(2,1)S(1)}, bf16[8,3,4,128,128]{4,3,2,1,0:T(8,128)(2,1)S(1)}, u32[]{:S(2)}, u32[]{:S(2)}) collective-permute-start(bf16[8,3,4,128,128]{4,3,2,1,0:T(8,128)(2,1)S(1)} %shard_map.65.refs_2_), channel_id=1, source_target_pairs={{0,64},{64,0},{1,65},{65,1},{2,66},{66,2},{3,67},{67,3},{4,68},{68... | collective-permute-start | bytes 9437192 | tf_op jit(solution)/shard_map/ppermute | solution.py:270
  73.5 11.6 %collective-permute-start.12 = (bf16[2,2,128,256]{3,2,1,0:T(8,128)(2,1)S(1)}, bf16[2,2,128,256]{3,2,1,0:T(8,128)(2,1)S(1)}, u32[]{:S(2)}, u32[]{:S(2)}) collective-permute-start(bf16[2,2,128,256]{3,2,1,0:T(8,128)(2,1)S(1)} %get-tuple-element.30), channel_id=1, source_target_pairs={{0,1},{1,16},{16,17},{17,32},{32,33},{33,48},{48,49},{2,3},{3,18},... | collective-permute-start | bytes 786440 | tf_op jit(solution)/shard_map/ppermute | solution.py:300
  87.7 10.6 %collective-permute-start.13 = (bf16[2,2,128,256]{3,2,1,0:T(8,128)(2,1)S(1)}, bf16[2,2,128,256]{3,2,1,0:T(8,128)(2,1)S(1)}, u32[]{:S(2)}, u32[]{:S(2)}) collective-permute-start(bf16[2,2,128,256]{3,2,1,0:T(8,128)(2,1)S(1)} %get-tuple-element.34), channel_id=1, source_target_pairs={{0,1},{1,16},{16,17},{17,32},{32,33},{33,48},{48,49},{2,3},{3,18},... | collective-permute-start | bytes 786440 | tf_op jit(solution)/shard_map/ppermute | solution.py:300
  100.9 9.7 %collective-permute-start.14 = (bf16[2,2,128,256]{3,2,1,0:T(8,128)(2,1)S(1)}, bf16[2,2,128,256]{3,2,1,0:T(8,128)(2,1)S(1)}, u32[]{:S(2)}, u32[]{:S(2)}) collective-permute-start(bf16[2,2,128,256]{3,2,1,0:T(8,128)(2,1)S(1)} %get-tuple-element.38), channel_id=1, source_target_pairs={{0,1},{1,16},{16,17},{17,32},{32,33},{33,48},{48,49},{2,3},{3,18},... | collective-permute-start | bytes 786440 | tf_op jit(solution)/shard_map/ppermute | solution.py:300
  151.6 6.5 %collective-permute-start.15 = (bf16[64,128]{1,0:T(8,128)(2,1)S(1)}, bf16[64,128]{1,0:T(8,128)(2,1)S(1)}, u32[]{:S(2)}, u32[]{:S(2)}) collective-permute-start(bf16[64,128]{1,0:T(8,128)(2,1)S(1)} %shard_map.71), channel_id=1, source_target_pairs={{1,8},{8,1},{3,10},{10,3},{5,12},{12,5},{7,14},{14,7},{17,24},{24,... | collective-permute-start | bytes 49160 | tf_op jit(solution)/shard_map/ppermute | solution.py:346

commit v9 on v8

--- a/solution.py
+++ b/solution.py
@@ -182,23 +182,57 @@
         copy.wait()
 
 
-def gather_along_z(piece, place):
+def fill_in(place, last_mine, last_other, mine_in, other_in, mine, other, sems):
+    brought = []
+    for step in range(1 - RING // 2, RING // 2 + 1):
+        spot = lax.rem(place[0] + step + RING, RING)
+        for number, (last, most, held) in enumerate(((last_mine, mine_in, mine), (last_other, other_in, other))):
+            source = last if step == RING // 2 else most.at[spot]
+            brought.append(pltpu.make_async_copy(source, held.at[spot], sems.at[number, step + RING // 2 - 1]))
+    for copy in brought:
+        copy.start()
+    for copy in brought:
+        copy.wait()
+
+
+def gather_along_z(piece, place, between):
     upward = [(i, (i + 1) % RING) for i in range(RING)]
     downward = [(i, (i - 1) % RING) for i in range(RING)]
+    swap = [(0, 1), (1, 0)]
     arrived = {0: piece}
-    for step in range(1, RING // 2 + 1):
-        arrived[-step] = lax.ppermute(arrived[1 - step], ("zhi", "zlo"), upward)
-        if step < RING // 2:
-            arrived[step] = lax.ppermute(arrived[step - 1], ("zhi", "zlo"), downward)
-    return pl.pallas_call(
+    rest = None
+    for step in range(1, RING // 2):
+        up, down = arrived[1 - step], arrived[step - 1]
+        if step > 1:
+            rest = between[step - 2](rest)
+        up = lax.ppermute(up, ("zhi", "zlo"), upward)
+        down = lax.ppermute(down, ("zhi", "zlo"), downward)
+        arrived[-step], arrived[step], rest = lax.optimization_barrier((up, down, rest))
+    last_mine = lax.ppermute(arrived[1 - RING // 2], ("zhi", "zlo"), upward)
+    held = jax.ShapeDtypeStruct((RING,) + piece.shape, BF16)
+    params = pltpu.CompilerParams(vmem_limit_bytes=16 << 20)
+    scalars, vmem = pl.BlockSpec(memory_space=pltpu.SMEM), pl.BlockSpec(memory_space=pltpu.VMEM)
+    mine = pl.pallas_call(
         functools.partial(in_order, tuple(arrived)),
-        out_shape=jax.ShapeDtypeStruct((RING,) + piece.shape, BF16),
-        in_specs=[pl.BlockSpec(memory_space=pltpu.SMEM)] + [pl.BlockSpec(memory_space=pl.ANY)] * RING,
-        out_specs=pl.BlockSpec(memory_space=pltpu.VMEM),
-        scratch_shapes=[pltpu.SemaphoreType.DMA((RING,))],
-        compiler_params=pltpu.CompilerParams(vmem_limit_bytes=16 << 20),
+        out_shape=held,
+        in_specs=[scalars] + [pl.BlockSpec(memory_space=pl.ANY)] * len(arrived),
+        out_specs=vmem,
+        scratch_shapes=[pltpu.SemaphoreType.DMA((len(arrived),))],
+        compiler_params=params,
         cost_estimate=pl.CostEstimate(flops=0, bytes_accessed=6 << 20, transcendentals=0),
     )(place, *arrived.values())
+    other = lax.ppermute(mine, "core", swap)
+    last_other = lax.ppermute(last_mine, "core", swap)
+    mine, other = pl.pallas_call(
+        fill_in,
+        out_shape=[held, held],
+        in_specs=[scalars] + [pl.BlockSpec(memory_space=pl.ANY)] * 4,
+        out_specs=[vmem, vmem],
+        scratch_shapes=[pltpu.SemaphoreType.DMA((2, RING))],
+        compiler_params=params,
+        cost_estimate=pl.CostEstimate(flops=0, bytes_accessed=2 << 20, transcendentals=0),
+    )(place, last_mine, last_other, mine, other)
+    return mine, other, rest
 
 
 def add_cores(over, summed):
@@ -243,31 +277,33 @@
         cost_estimate=pl.CostEstimate(flops=0, bytes_accessed=800_000, transcendentals=0),
     )(start, site_tensor).reshape(STATES, HALF, BLOCK, BLOCK)
     place = (lax.axis_index("zhi") * 2 + at_zlo).astype(jnp.int32).reshape(1)
-    mine = gather_along_z(piece, place)
     spots = [site_start(sectors, group, half) - (OWN * group - BEFORE) for half in range(2)]
 
-    pieces = ops_pieces(term_ops[0].reshape(sectors, BLOCK, BLOCK), term_shift[0], core)
-    over = lax.all_to_all(pieces, "x", 0, 0)
-    ops_now = lax.dynamic_index_in_dim(over, lax.axis_index("zhi"), 0, keepdims=False)
-    ops_now = lax.ppermute(ops_now, ("core", "y0"), [(0, 0), (1, 2), (2, 1), (3, 3)])
-    figures = jnp.concatenate([keep_weight[0], env_weight[0], term_shift.astype(F32), jnp.zeros((1,), F32)])
-    figures = lax.ppermute(figures, AXES, to_groups())
+    def cross_x(_):
+        pieces = ops_pieces(term_ops[0].reshape(sectors, BLOCK, BLOCK), term_shift[0], core)
+        return lax.all_to_all(pieces, "x", 0, 0)
+
+    def cross_y(over):
+        ops_now = lax.dynamic_index_in_dim(over, lax.axis_index("zhi"), 0, keepdims=False)
+        ops_now = lax.ppermute(ops_now, ("core", "y0"), [(0, 0), (1, 2), (2, 1), (3, 3)])
+        figures = [keep_weight[0], env_weight[0], term_shift.astype(F32), jnp.zeros((1,), F32)]
+        figures = lax.ppermute(jnp.concatenate(figures), AXES, to_groups())
+        piece = lax.ppermute(env_rows, AXES, rows_to_groups(0))
+        halo = lax.ppermute(env_rows, AXES, rows_to_groups(1))
+        return ops_now, figures, piece, halo
+
+    mine, other, (ops_now, figures, piece, halo) = gather_along_z(piece, place, [cross_x, cross_y])
     shift = figures[6].astype(jnp.int32)
     partner = jnp.arange(STATES, dtype=jnp.int32) - shift
     factors = jnp.where((partner >= 0) & (partner <= 2), figures[3:6], 0.0)
     part = jnp.concatenate([figures[:3], factors])
     whole = jnp.stack([core, shift] + spots).astype(jnp.int32)
 
-    piece = lax.ppermute(env_rows, AXES, rows_to_groups(0))
-    halo = lax.ppermute(env_rows, AXES, rows_to_groups(1))
     env_now = jnp.zeros((2 * OWN * BLOCK, BLOCK), BF16)
     spot = at_yl * BLOCK + core * (BLOCK // 2)
     env_now = lax.dynamic_update_slice_in_dim(env_now, halo, spot, 0)
     env_now = lax.dynamic_update_slice_in_dim(env_now, piece, spot + OWN * BLOCK, 0)
     window = jnp.concatenate([ops_now, env_now.reshape(2 * OWN, BLOCK, BLOCK)], 2)
-
-    mine, window, whole, part = lax.optimization_barrier((mine, window, whole, part))
-    other = lax.ppermute(mine, "core", [(0, 1), (1, 0)])
 
     wide = (BLOCK, 2 * BLOCK)
     onward = [(i, i + 1) for i in range(7)]

time: 159 us -> 178 us (1.12)
  local copies, waits for them, and re-layouts: 1.1 us -> 11 us
  blocking collectives: 38.8 us -> 32.9 us
  waiting for transfers between devices: 50.7 us -> 56.2 us
  starting transfers between devices: 50.7 us -> 55.2 us
  Pallas kernels: 13.5 us -> 16.5 us
    unnamed x20 -> x44, local copies, waits for them, and re-layouts: 0.24 us -> 8.86 us
    all_to_all x1, blocking collectives: 34.2 us -> 28.3 us  [body(): over = lax.all_to_all(summed, ('zhi', 'zlo', 'yl'), 0, 0)]
    ppermute x12 -> x13, waiting for transfers between devices: 21.1 us -> 25.4 us  [the longest x1 8.48 us: gather_along_z(): last_mine = lax.ppermute(arrived[1 - RING // 2], ('zhi', 'zlo'), upward)]
    pallas_call x1 -> x2, Pallas kernels: 1.61 us -> 4.6 us  [the longest x1 2.61 us: gather_along_z(): pl.pallas_call(fill_in, out_shape=[held, held], in_specs=[scalars] + [pl....]
    ppermute x12 -> x13, starting transfers between devices: 37.3 us -> 39.7 us  [the longest x3 13.4 us: gather_along_z(): up = lax.ppermute(up, ('zhi', 'zlo'), upward)]
    all_to_all x1, starting transfers between devices: 4.77 us -> 6.62 us  [cross_x(): return lax.all_to_all(pieces, 'x', 0, 0)]
  transfers between devices with their start and end apart: 17 -> 18, of which waited for: 9 -> 10; matrix products, arithmetic and copies ran while one was open for 2% -> 3% of each run, Pallas kernels for 0% -> 0%
where the time goes in v9:
time: 178 us; the launch traced here: 177 us
  waiting for transfers between devices  56.2 us (32%)
  starting transfers between devices  55.2 us (31%)
  blocking collectives  32.9 us (18%)
  Pallas kernels  16.5 us (9%)
  local copies, waits for them, and re-layouts  11 us (6%)
  other arithmetic  4 us (2%)
    all_to_all x1, blocking collectives, body(): over = lax.all_to_all(summed, ('zhi', 'zlo', 'yl'), 0, 0)  28.3 us
    ppermute x3, waiting for transfers between devices, body(): tails = lax.ppermute(tails, ('x', 'y0'), onward)  26.2 us
    ppermute x3, starting transfers between devices, gather_along_z(): up = lax.ppermute(up, ('zhi', 'zlo'), upward)  13.4 us
    pallas_call x4, Pallas kernels, run_phase(): pl.pallas_call(functools.partial(phase_kernel, sites, steps, len(ins), so...  9.77 us
    unnamed x44, local copies, waits for them, and re-layouts  8.86 us
    ppermute x1, waiting for transfers between devices, gather_along_z(): last_mine = lax.ppermute(arrived[1 - RING // 2], ('zhi', 'zlo'), upward)  8.48 us
    ppermute x3, waiting for transfers between devices, gather_along_z(): down = lax.ppermute(down, ('zhi', 'zlo'), downward)  6.9 us
    ppermute x3, starting transfers between devices, body(): tails = lax.ppermute(tails, ('x', 'y0'), onward)  6.88 us
  transfers between devices with their start and end apart: 18, of which 10 were waited for; matrix products, arithmetic and copies ran while one was open for 3% of the time, Pallas kernels for 0%

profile of v9, /device:TPU:70, one launch (start us, length us, event | category | flops | bytes accessed | tf_op | source)
XLA Modules:
  0.0 177.4 jit_solution(8615799861460069718)
XLA Ops:
  1.9 4.3 %collective-permute-start = (bf16[3,4,128,128]{3,2,1,0:T(8,128)(2,1)}, bf16[3,4,128,128]{3,2,1,0:T(8,128)(2,1)S(1)}, u32[]{:S(2)}, u32[]{:S(2)}) collective-permute-start(bf16[3,4,128,128]{3,2,1,0:T(8,128)(2,1)} %bitcast.24), channel_id=1, source_target_pairs={{0,8},{8,128},{128,136},{136,256},{256,264},{264,384},{384,392},{3... | collective-permute-start | bytes 1179656 | tf_op jit(solution)/shard_map/ppermute | solution.py:208
  6.2 1.9 %collective-permute-start.1 = (bf16[3,4,128,128]{3,2,1,0:T(8,128)(2,1)}, bf16[3,4,128,128]{3,2,1,0:T(8,128)(2,1)S(1)}, u32[]{:S(2)}, u32[]{:S(2)}) collective-permute-start(bf16[3,4,128,128]{3,2,1,0:T(8,128)(2,1)} %bitcast.25), channel_id=1, source_target_pairs={{0,392},{8,0},{128,8},{136,128},{256,136},{264,256},{384,264},{392... | collective-permute-start | bytes 1179656 | tf_op jit(solution)/shard_map/ppermute | solution.py:209
  10.2 6.6 %all-to-all-start = ((bf16[4,8,128,128]{3,2,1,0:T(8,128)(2,1)}), bf16[4,8,128,128]{3,2,1,0:T(8,128)(2,1)S(1)}, u32[]{:S(2)}, u32[]{:S(2)}) async-start(bf16[4,8,128,128]{3,2,1,0:T(8,128)(2,1)} %bitcast.5), calls=%async_computation | async-start | bytes 2097152 | tf_op jit(solution)/shard_map/all_to_all | solution.py:284
  16.9 2.7 %collective-permute-done.1.refs_2_ = bf16[3,4,128,128]{3,2,1,0:T(8,128)(2,1)S(1)} collective-permute-done((bf16[3,4,128,128]{3,2,1,0:T(8,128)(2,1)}, bf16[3,4,128,128]{3,2,1,0:T(8,128)(2,1)S(1)}, u32[]{:S(2)}, u32[]{:S(2)}) %collective-permute-start.1) | collective-permute-done | bytes 393248 | tf_op jit(solution)/shard_map/ppermute | solution.py:209
  19.5 5.5 %collective-permute-start.2 = (bf16[3,4,128,128]{3,2,1,0:T(8,128)(2,1)S(1)}, bf16[3,4,128,128]{3,2,1,0:T(8,128)(2,1)S(1)}, u32[]{:S(2)}, u32[]{:S(2)}) collective-permute-start(bf16[3,4,128,128]{3,2,1,0:T(8,128)(2,1)S(1)} %collective-permute-done.refs_1_), channel_id=1, source_target_pairs={{0,8},{8,128},{128,136},{136,256},{256,264},{264,384},{384,392},{3... | collective-permute-start | bytes 1179656 | tf_op jit(solution)/shard_map/ppermute | solution.py:208
  25.0 1.9 %collective-permute-start.3 = (bf16[3,4,128,128]{3,2,1,0:T(8,128)(2,1)S(1)}, bf16[3,4,128,128]{3,2,1,0:T(8,128)(2,1)S(1)}, u32[]{:S(2)}, u32[]{:S(2)}) collective-permute-start(bf16[3,4,128,128]{3,2,1,0:T(8,128)(2,1)S(1)} %collective-permute-done.1.refs_2_), channel_id=1, source_target_pairs={{0,392},{8,0},{128,8},{136,128},{256,136},{264,256},{384,264},{392... | collective-permute-start | bytes 1179656 | tf_op jit(solution)/shard_map/ppermute | solution.py:209
  27.7 5.5 %collective-permute-done.2.refs_3_ = bf16[3,4,128,128]{3,2,1,0:T(8,128)(2,1)S(1)} collective-permute-done((bf16[3,4,128,128]{3,2,1,0:T(8,128)(2,1)S(1)}, bf16[3,4,128,128]{3,2,1,0:T(8,128)(2,1)S(1)}, u32[]{:S(2)}, u32[]{:S(2)}) %collective-permute-start.2) | collective-permute-done | bytes 393248 | tf_op jit(solution)/shard_map/ppermute | solution.py:208
  33.2 4.2 %collective-permute-done.3.refs_4_ = bf16[3,4,128,128]{3,2,1,0:T(8,128)(2,1)S(1)} collective-permute-done((bf16[3,4,128,128]{3,2,1,0:T(8,128)(2,1)S(1)}, bf16[3,4,128,128]{3,2,1,0:T(8,128)(2,1)S(1)}, u32[]{:S(2)}, u32[]{:S(2)}) %collective-permute-start.3) | collective-permute-done | bytes 393248 | tf_op jit(solution)/shard_map/ppermute | solution.py:209
  37.5 3.6 %collective-permute-start.4 = (bf16[3,4,128,128]{3,2,1,0:T(8,128)(2,1)S(1)}, bf16[3,4,128,128]{3,2,1,0:T(8,128)(2,1)}, u32[]{:S(2)}, u32[]{:S(2)}) collective-permute-start(bf16[3,4,128,128]{3,2,1,0:T(8,128)(2,1)S(1)} %collective-permute-done.2.refs_3_), channel_id=1, source_target_pairs={{0,8},{8,128},{128,136},{136,256},{256,264},{264,384},{384,392},{3... | collective-permute-start | bytes 1179656 | tf_op jit(solution)/shard_map/ppermute | solution.py:208
  41.9 2.2 %collective-permute-start.5 = (bf16[3,4,128,128]{3,2,1,0:T(8,128)(2,1)S(1)}, bf16[3,4,128,128]{3,2,1,0:T(8,128)(2,1)S(1)}, u32[]{:S(2)}, u32[]{:S(2)}) collective-permute-start(bf16[3,4,128,128]{3,2,1,0:T(8,128)(2,1)S(1)} %collective-permute-done.3.refs_4_), channel_id=1, source_target_pairs={{0,392},{8,0},{128,8},{136,128},{256,136},{264,256},{384,264},{392... | collective-permute-start | bytes 1179656 | tf_op jit(solution)/shard_map/ppermute | solution.py:209
  45.6 5.5 %collective-permute-start.7 = (f32[8]{0:T(128)S(1)}, f32[8]{0:T(128)S(1)}, u32[]{:S(2)}, u32[]{:S(2)}) collective-permute-start(f32[8]{0:T(128)S(1)} %pad_maximum_fusion.1), channel_id=1, source_target_pairs={{0,0},{1,64},{2,2},{3,66},{4,4},{5,68},{6,6},{7,70},{8,8},{9,72},{... | collective-permute-start | bytes 104 | tf_op jit(solution)/shard_map/ppermute | solution.py:290
  51.1 5.9 %collective-permute-start.8 = (bf16[64,128]{1,0:T(8,128)(2,1)S(1)}, bf16[64,128]{1,0:T(8,128)(2,1)S(1)}, u32[]{:S(2)}, u32[]{:S(2)}) collective-permute-start(bf16[64,128]{1,0:T(8,128)(2,1)S(1)} %copy-done.16), channel_id=1, source_target_pairs={{0,0},{2,2},{4,4},{6,6},{8,9},{10,11},{12,13},{14,15},{16,16},{18,... | collective-permute-start | bytes 49160 | tf_op jit(solution)/shard_map/ppermute | solution.py:291
  58.4 4.3 %collective-permute-done.9 = bf16[64,128]{1,0:T(8,128)(2,1)} collective-permute-done((bf16[64,128]{1,0:T(8,128)(2,1)S(1)}, bf16[64,128]{1,0:T(8,128)(2,1)}, u32[]{:S(2)}, u32[]{:S(2)}) %collective-permute-start.9) | collective-permute-done | bytes 16416 | tf_op jit(solution)/shard_map/ppermute | solution.py:292
  69.2 2.0 %shard_map.65.mine_in = bf16[8,3,4,128,128]{4,3,2,1,0:T(8,128)(2,1)S(1)} custom-call(s32[1]{0:T(128)} %bitcast.12.place, bf16[3,4,128,128]{3,2,1,0:T(8,128)(2,1)S(1)} %bitcast.26, bf16[3,4,128,128]{3,2,1,0:T(8,128)(2,1)S(1)} %copy-done.2, bf16[3,4,128,128]{3,2,1,0:T(8,128)(2,1)S(1)} %copy-done.4, bf16[3,4,128,128]{3,2,1,0:T(8,128)(2,1)S(1)} %copy-done.6, ...), custom_call_target="tpu_custom_call" | custom-call | bytes 6291456 | tf_op jit(solution)/shard_map/pallas_call | solution.py:215
  71.2 3.1 %collective-permute-start.12 = (bf16[8,3,4,128,128]{4,3,2,1,0:T(8,128)(2,1)S(1)}, bf16[8,3,4,128,128]{4,3,2,1,0:T(8,128)(2,1)}, u32[]{:S(2)}, u32[]{:S(2)}) collective-permute-start(bf16[8,3,4,128,128]{4,3,2,1,0:T(8,128)(2,1)S(1)} %shard_map.65.mine_in), channel_id=1, source_target_pairs={{0,64},{64,0},{1,65},{65,1},{2,66},{66,2},{3,67},{67,3},{4,68},{68... | collective-permute-start | bytes 9437192 | tf_op jit(solution)/shard_map/ppermute | solution.py:224
  74.4 1.9 %collective-permute-start.10 = (bf16[3,4,128,128]{3,2,1,0:T(8,128)(2,1)}, bf16[3,4,128,128]{3,2,1,0:T(8,128)(2,1)S(1)}, u32[]{:S(2)}, u32[]{:S(2)}) collective-permute-start(bf16[3,4,128,128]{3,2,1,0:T(8,128)(2,1)} %collective-permute-done.4.refs_5_), channel_id=1, source_target_pairs={{0,8},{8,128},{128,136},{136,256},{256,264},{264,384},{384,392},{3... | collective-permute-start | bytes 1179656 | tf_op jit(solution)/shard_map/ppermute | solution.py:211
  79.0 8.5 %collective-permute-done.10.last_mine = bf16[3,4,128,128]{3,2,1,0:T(8,128)(2,1)S(1)} collective-permute-done((bf16[3,4,128,128]{3,2,1,0:T(8,128)(2,1)}, bf16[3,4,128,128]{3,2,1,0:T(8,128)(2,1)S(1)}, u32[]{:S(2)}, u32[]{:S(2)}) %collective-permute-start.10) | collective-permute-done | bytes 393248 | tf_op jit(solution)/shard_map/ppermute | solution.py:211
  87.5 1.9 %collective-permute-start.11 = (bf16[3,4,128,128]{3,2,1,0:T(8,128)(2,1)S(1)}, bf16[3,4,128,128]{3,2,1,0:T(8,128)(2,1)S(1)}, u32[]{:S(2)}, u32[]{:S(2)}) collective-permute-start(bf16[3,4,128,128]{3,2,1,0:T(8,128)(2,1)S(1)} %collective-permute-done.10.last_mine), channel_id=1, source_target_pairs={{0,64},{64,0},{1,65},{65,1},{2,66},{66,2},{3,67},{67,3},{4,68},{68... | collective-permute-start | bytes 1179656 | tf_op jit(solution)/shard_map/ppermute | solution.py:225
  91.3 2.6 %shard_map.66 = (bf16[8,3,4,128,128]{4,3,2,1,0:T(8,128)(2,1)S(1)}, bf16[8,3,4,128,128]{4,3,2,1,0:T(8,128)(2,1)S(1)}) custom-call(s32[1]{0:T(128)} %bitcast.12.place, bf16[3,4,128,128]{3,2,1,0:T(8,128)(2,1)S(1)} %collective-permute-done.10.last_mine, bf16[3,4,128,128]{3,2,1,0:T(8,128)(2,1)S(1)} %collective-permute-done.11.last_other, ...), custom_call_target="tpu_custom_call" | custom-call | bytes 2097152 | tf_op jit(solution)/shard_map/pallas_call | solution.py:226
  93.9 2.8 %shard_map.67 = (bf16[4,128,256]{2,1,0:T(8,128)(2,1)S(1)}, bf16[4,128,256]{2,1,0:T(8,128)(2,1)S(1)}, bf16[2,128,256]{2,1,0:T(8,128)(2,1)S(1)}, bf16[2,2,128,256]{3,2,1,0:T(8,128)(2,1)S(1)}) custom-call(s32[4]{0:T(128)S(1)} %pad_add_fusion.refs_0_, f32[6]{0:T(128)S(1)} %pad_maximum_fusion.2.refs_1_, ...), custom_call_target="tpu_custom_call" | custom-call | flops 754974720 | bytes 4194304 | tf_op jit(solution)/shard_map/pallas_call | solution.py:145
  96.8 3.0 %collective-permute-start.13 = (bf16[2,2,128,256]{3,2,1,0:T(8,128)(2,1)S(1)}, bf16[2,2,128,256]{3,2,1,0:T(8,128)(2,1)S(1)}, u32[]{:S(2)}, u32[]{:S(2)}) collective-permute-start(bf16[2,2,128,256]{3,2,1,0:T(8,128)(2,1)S(1)} %get-tuple-element.48), channel_id=1, source_target_pairs={{0,1},{1,16},{16,17},{17,32},{32,33},{33,48},{48,49},{2,3},{3,18},... | collective-permute-start | bytes 786440 | tf_op jit(solution)/shard_map/ppermute | solution.py:336
  99.9 9.2 %collective-permute-done.13.refs_6_ = bf16[2,2,128,256]{3,2,1,0:T(8,128)(2,1)S(1)} collective-permute-done((bf16[2,2,128,256]{3,2,1,0:T(8,128)(2,1)S(1)}, bf16[2,2,128,256]{3,2,1,0:T(8,128)(2,1)S(1)}, u32[]{:S(2)}, u32[]{:S(2)}) %collective-permute-start.13) | collective-permute-done | bytes 262176 | tf_op jit(solution)/shard_map/ppermute | solution.py:336
  109.1 2.5 %shard_map.68 = (bf16[2,128,256]{2,1,0:T(8,128)(2,1)S(1)}, bf16[4,128,256]{2,1,0:T(8,128)(2,1)S(1)}, bf16[2,128,256]{2,1,0:T(8,128)(2,1)S(1)}, bf16[2,2,128,256]{3,2,1,0:T(8,128)(2,1)S(1)}) custom-call(s32[4]{0:T(128)S(1)} %pad_add_fusion.refs_0_, f32[6]{0:T(128)S(1)} %pad_maximum_fusion.2.refs_1_, ...), custom_call_target="tpu_custom_call" | custom-call | flops 503316480 | bytes 4194304 | tf_op jit(solution)/shard_map/pallas_call | solution.py:145
  111.6 1.9 %collective-permute-start.14 = (bf16[2,2,128,256]{3,2,1,0:T(8,128)(2,1)S(1)}, bf16[2,2,128,256]{3,2,1,0:T(8,128)(2,1)S(1)}, u32[]{:S(2)}, u32[]{:S(2)}) collective-permute-start(bf16[2,2,128,256]{3,2,1,0:T(8,128)(2,1)S(1)} %get-tuple-element.52), channel_id=1, source_target_pairs={{0,1},{1,16},{16,17},{17,32},{32,33},{33,48},{48,49},{2,3},{3,18},... | collective-permute-start | bytes 786440 | tf_op jit(solution)/shard_map/ppermute | solution.py:336
  113.6 8.9 %collective-permute-done.14.refs_6_ = bf16[2,2,128,256]{3,2,1,0:T(8,128)(2,1)S(1)} collective-permute-done((bf16[2,2,128,256]{3,2,1,0:T(8,128)(2,1)S(1)}, bf16[2,2,128,256]{3,2,1,0:T(8,128)(2,1)S(1)}, u32[]{:S(2)}, u32[]{:S(2)}) %collective-permute-start.14) | collective-permute-done | bytes 262176 | tf_op jit(solution)/shard_map/ppermute | solution.py:336
  122.5 2.5 %shard_map.69 = (bf16[2,128,256]{2,1,0:T(8,128)(2,1)S(1)}, bf16[4,128,256]{2,1,0:T(8,128)(2,1)S(1)}, bf16[2,128,256]{2,1,0:T(8,128)(2,1)S(1)}, bf16[2,2,128,256]{3,2,1,0:T(8,128)(2,1)S(1)}) custom-call(s32[4]{0:T(128)S(1)} %pad_add_fusion.refs_0_, f32[6]{0:T(128)S(1)} %pad_maximum_fusion.2.refs_1_, ...), custom_call_target="tpu_custom_call" | custom-call | flops 503316480 | bytes 4194304 | tf_op jit(solution)/shard_map/pallas_call | solution.py:145
  125.1 1.9 %collective-permute-start.15 = (bf16[2,2,128,256]{3,2,1,0:T(8,128)(2,1)S(1)}, bf16[2,2,128,256]{3,2,1,0:T(8,128)(2,1)S(1)}, u32[]{:S(2)}, u32[]{:S(2)}) collective-permute-start(bf16[2,2,128,256]{3,2,1,0:T(8,128)(2,1)S(1)} %get-tuple-element.56), channel_id=1, source_target_pairs={{0,1},{1,16},{16,17},{17,32},{32,33},{33,48},{48,49},{2,3},{3,18},... | collective-permute-start | bytes 786440 | tf_op jit(solution)/shard_map/ppermute | solution.py:336
  127.1 8.1 %collective-permute-done.15.refs_6_ = bf16[2,2,128,256]{3,2,1,0:T(8,128)(2,1)S(1)} collective-permute-done((bf16[2,2,128,256]{3,2,1,0:T(8,128)(2,1)S(1)}, bf16[2,2,128,256]{3,2,1,0:T(8,128)(2,1)S(1)}, u32[]{:S(2)}, u32[]{:S(2)}) %collective-permute-start.15) | collective-permute-done | bytes 262176 | tf_op jit(solution)/shard_map/ppermute | solution.py:336
  137.2 4.6 %all_to_all.15.over = bf16[2,4,8,64,128]{4,3,2,1,0:T(8,128)(2,1)S(1)} all-to-all(bf16[2,4,8,64,128]{4,3,2,1,0:T(8,128)(2,1)S(1)} %bitcast.29), channel_id=1, replica_groups=mesh['zhi'=4,'core'=2,'x'=4,'zlo'=2,'yl'=4,'y0'=2] {'core'}, dimensions={0} | all-to-all | bytes 2097152 | tf_op jit(solution)/shard_map/all_to_all | solution.py:378
  141.9 28.3 %all_to_all.16.over = bf16[32,64,128]{2,1,0:T(8,128)(2,1)S(1)} all-to-all(bf16[32,64,128]{2,1,0:T(8,128)(2,1)S(1)} %bitcast.23), channel_id=1, replica_groups=mesh['zhi'=4,'core'=2,'x'=4,'zlo'=2,'yl'=4,'y0'=2] {'zhi','zlo','yl'}, dimensions={0} | all-to-all | bytes 1048576 | tf_op jit(solution)/shard_map/all_to_all | solution.py:380
  170.3 1.9 %collective-permute-start.16 = (bf16[64,128]{1,0:T(8,128)(2,1)S(1)}, bf16[64,128]{1,0:T(8,128)(2,1)S(1)}, u32[]{:S(2)}, u32[]{:S(2)}) collective-permute-start(bf16[64,128]{1,0:T(8,128)(2,1)S(1)} %shard_map.72), channel_id=1, source_target_pairs={{1,8},{8,1},{3,10},{10,3},{5,12},{12,5},{7,14},{14,7},{17,24},{24,... | collective-permute-start | bytes 49160 | tf_op jit(solution)/shard_map/ppermute | solution.py:382
  172.2 4.6 %collective-permute-done.16 = bf16[64,128]{1,0:T(8,128)(2,1)S(1)} collective-permute-done((bf16[64,128]{1,0:T(8,128)(2,1)S(1)}, bf16[64,128]{1,0:T(8,128)(2,1)S(1)}, u32[]{:S(2)}, u32[]{:S(2)}) %collective-permute-start.16) | collective-permute-done | bytes 16416 | tf_op jit(solution)/shard_map/ppermute | solution.py:382
  (76 shorter events, 21.1 us)
Async XLA Ops:
  0.0 8.8 %copy-start.11 = (bf16[1,4096,128]{2,1,0:T(8,128)(2,1)S(1)}, bf16[1,4096,128]{2,1,0:T(8,128)(2,1)}, u32[]{:S(2)}) copy-start(bf16[1,4096,128]{2,1,0:T(8,128)(2,1)} %param.7) | copy-start | bytes 3145732
  1.9 14.9 %collective-permute-start = (bf16[3,4,128,128]{3,2,1,0:T(8,128)(2,1)}, bf16[3,4,128,128]{3,2,1,0:T(8,128)(2,1)S(1)}, u32[]{:S(2)}, u32[]{:S(2)}) collective-permute-start(bf16[3,4,128,128]{3,2,1,0:T(8,128)(2,1)} %bitcast.24), channel_id=1, source_target_pairs={{0,8},{8,128},{128,136},{136,256},{256,264},{264,384},{384,392},{3... | collective-permute-start | bytes 1179656 | tf_op jit(solution)/shard_map/ppermute | solution.py:208
  6.2 13.3 %collective-permute-start.1 = (bf16[3,4,128,128]{3,2,1,0:T(8,128)(2,1)}, bf16[3,4,128,128]{3,2,1,0:T(8,128)(2,1)S(1)}, u32[]{:S(2)}, u32[]{:S(2)}) collective-permute-start(bf16[3,4,128,128]{3,2,1,0:T(8,128)(2,1)} %bitcast.25), channel_id=1, source_target_pairs={{0,392},{8,0},{128,8},{136,128},{256,136},{264,256},{384,264},{392... | collective-permute-start | bytes 1179656 | tf_op jit(solution)/shard_map/ppermute | solution.py:209
  9.0 36.5 %copy-start.14 = (f32[1,3]{1,0:T(1,128)S(1)}, f32[1,3]{1,0:T(1,128)}, u32[]{:S(2)}) copy-start(f32[1,3]{1,0:T(1,128)} %param.11) | copy-start | bytes 40
  9.0 36.5 %copy-start.15 = (f32[1,3]{1,0:T(1,128)S(1)}, f32[1,3]{1,0:T(1,128)}, u32[]{:S(2)}) copy-start(f32[1,3]{1,0:T(1,128)} %param.10) | copy-start | bytes 40
  9.0 42.1 %copy-start.16 = (bf16[64,128]{1,0:T(8,128)(2,1)S(1)}, bf16[64,128]{1,0:T(8,128)(2,1)}, u32[]{:S(2)}) copy-start(bf16[64,128]{1,0:T(8,128)(2,1)} %param.8) | copy-start | bytes 49156
  9.0 55.2 %copy-start = (bf16[3,512,128]{2,1,0:T(8,128)(2,1)S(1)}, bf16[3,512,128]{2,1,0:T(8,128)(2,1)}, u32[]{:S(2)}) copy-start(bf16[3,512,128]{2,1,0:T(8,128)(2,1)} %shard_map.64) | copy-start | bytes 1179652
  10.2 27.3 %all-to-all-start = ((bf16[4,8,128,128]{3,2,1,0:T(8,128)(2,1)}), bf16[4,8,128,128]{3,2,1,0:T(8,128)(2,1)S(1)}, u32[]{:S(2)}, u32[]{:S(2)}) async-start(bf16[4,8,128,128]{3,2,1,0:T(8,128)(2,1)} %bitcast.5), calls=%async_computation | async-start | bytes 2097152 | tf_op jit(solution)/shard_map/all_to_all | solution.py:284
  16.8 46.0 %copy-start.1 = (bf16[3,4,128,128]{3,2,1,0:T(8,128)(2,1)}, bf16[3,4,128,128]{3,2,1,0:T(8,128)(2,1)S(1)}, u32[]{:S(2)}) copy-start(bf16[3,4,128,128]{3,2,1,0:T(8,128)(2,1)S(1)} %collective-permute-done.refs_1_) | copy-start | bytes 1179652
  19.5 13.7 %collective-permute-start.2 = (bf16[3,4,128,128]{3,2,1,0:T(8,128)(2,1)S(1)}, bf16[3,4,128,128]{3,2,1,0:T(8,128)(2,1)S(1)}, u32[]{:S(2)}, u32[]{:S(2)}) collective-permute-start(bf16[3,4,128,128]{3,2,1,0:T(8,128)(2,1)S(1)} %collective-permute-done.refs_1_), channel_id=1, source_target_pairs={{0,8},{8,128},{128,136},{136,256},{256,264},{264,384},{384,392},{3... | collective-permute-start | bytes 1179656 | tf_op jit(solution)/shard_map/ppermute | solution.py:208
  25.0 12.5 %collective-permute-start.3 = (bf16[3,4,128,128]{3,2,1,0:T(8,128)(2,1)S(1)}, bf16[3,4,128,128]{3,2,1,0:T(8,128)(2,1)S(1)}, u32[]{:S(2)}, u32[]{:S(2)}) collective-permute-start(bf16[3,4,128,128]{3,2,1,0:T(8,128)(2,1)S(1)} %collective-permute-done.1.refs_2_), channel_id=1, source_target_pairs={{0,392},{8,0},{128,8},{136,128},{256,136},{264,256},{384,264},{392... | collective-permute-start | bytes 1179656 | tf_op jit(solution)/shard_map/ppermute | solution.py:209
  26.9 0.8 copy-start.3
  37.5 25.3 %collective-permute-start.4 = (bf16[3,4,128,128]{3,2,1,0:T(8,128)(2,1)S(1)}, bf16[3,4,128,128]{3,2,1,0:T(8,128)(2,1)}, u32[]{:S(2)}, u32[]{:S(2)}) collective-permute-start(bf16[3,4,128,128]{3,2,1,0:T(8,128)(2,1)S(1)} %collective-permute-done.2.refs_3_), channel_id=1, source_target_pairs={{0,8},{8,128},{128,136},{136,256},{256,264},{264,384},{384,392},{3... | collective-permute-start | bytes 1179656 | tf_op jit(solution)/shard_map/ppermute | solution.py:208
  41.1 0.8 copy-start.5
  41.9 20.9 %collective-permute-start.5 = (bf16[3,4,128,128]{3,2,1,0:T(8,128)(2,1)S(1)}, bf16[3,4,128,128]{3,2,1,0:T(8,128)(2,1)S(1)}, u32[]{:S(2)}, u32[]{:S(2)}) collective-permute-start(bf16[3,4,128,128]{3,2,1,0:T(8,128)(2,1)S(1)} %collective-permute-done.3.refs_4_), channel_id=1, source_target_pairs={{0,392},{8,0},{128,8},{136,128},{256,136},{264,256},{384,264},{392... | collective-permute-start | bytes 1179656 | tf_op jit(solution)/shard_map/ppermute | solution.py:209
  44.8 17.9 %collective-permute-start.6 = (bf16[8,128,128]{2,1,0:T(8,128)(2,1)S(1)}, bf16[8,128,128]{2,1,0:T(8,128)(2,1)S(1)}, u32[]{:S(2)}, u32[]{:S(2)}) collective-permute-start(bf16[8,128,128]{2,1,0:T(8,128)(2,1)S(1)} %dynamic-slice_bitcast_fusion), channel_id=1, source_target_pairs={{0,0},{1,64},{64,1},{65,65},{2,2},{3,66},{66,3},{67,67},{4,4},{5,6... | collective-permute-start | bytes 786440 | tf_op jit(solution)/shard_map/ppermute | solution.py:288
  45.6 11.4 %collective-permute-start.7 = (f32[8]{0:T(128)S(1)}, f32[8]{0:T(128)S(1)}, u32[]{:S(2)}, u32[]{:S(2)}) collective-permute-start(f32[8]{0:T(128)S(1)} %pad_maximum_fusion.1), channel_id=1, source_target_pairs={{0,0},{1,64},{2,2},{3,66},{4,4},{5,68},{6,6},{7,70},{8,8},{9,72},{... | collective-permute-start | bytes 104 | tf_op jit(solution)/shard_map/ppermute | solution.py:290
  51.1 7.3 %collective-permute-start.8 = (bf16[64,128]{1,0:T(8,128)(2,1)S(1)}, bf16[64,128]{1,0:T(8,128)(2,1)S(1)}, u32[]{:S(2)}, u32[]{:S(2)}) collective-permute-start(bf16[64,128]{1,0:T(8,128)(2,1)S(1)} %copy-done.16), channel_id=1, source_target_pairs={{0,0},{2,2},{4,4},{6,6},{8,9},{10,11},{12,13},{14,15},{16,16},{18,... | collective-permute-start | bytes 49160 | tf_op jit(solution)/shard_map/ppermute | solution.py:291
  57.0 5.8 %copy-start.13 = (f32[8]{0:T(128)}, f32[8]{0:T(128)S(1)}, u32[]{:S(2)}) copy-start(f32[8]{0:T(128)S(1)} %collective-permute-done.7) | copy-start | bytes 100
  57.0 5.7 %collective-permute-start.9 = (bf16[64,128]{1,0:T(8,128)(2,1)S(1)}, bf16[64,128]{1,0:T(8,128)(2,1)}, u32[]{:S(2)}, u32[]{:S(2)}) collective-permute-start(bf16[64,128]{1,0:T(8,128)(2,1)S(1)} %copy-done.16), channel_id=1, source_target_pairs={{0,1},{2,3},{4,5},{6,7},{8,24},{10,26},{12,28},{14,30},{16,17},{18... | collective-permute-start | bytes 49160 | tf_op jit(solution)/shard_map/ppermute | solution.py:292
  64.2 1.0 copy-start.2
  65.2 1.0 copy-start.4
  66.2 1.0 copy-start.6
  67.2 1.0 copy-start.8
  68.2 1.0 copy-start.10
  71.2 20.1 %collective-permute-start.12 = (bf16[8,3,4,128,128]{4,3,2,1,0:T(8,128)(2,1)S(1)}, bf16[8,3,4,128,128]{4,3,2,1,0:T(8,128)(2,1)}, u32[]{:S(2)}, u32[]{:S(2)}) collective-permute-start(bf16[8,3,4,128,128]{4,3,2,1,0:T(8,128)(2,1)S(1)} %shard_map.65.mine_in), channel_id=1, source_target_pairs={{0,64},{64,0},{1,65},{65,1},{2,66},{66,2},{3,67},{67,3},{4,68},{68... | collective-permute-start | bytes 9437192 | tf_op jit(solution)/shard_map/ppermute | solution.py:224
  74.4 13.1 %collective-permute-start.10 = (bf16[3,4,128,128]{3,2,1,0:T(8,128)(2,1)}, bf16[3,4,128,128]{3,2,1,0:T(8,128)(2,1)S(1)}, u32[]{:S(2)}, u32[]{:S(2)}) collective-permute-start(bf16[3,4,128,128]{3,2,1,0:T(8,128)(2,1)} %collective-permute-done.4.refs_5_), channel_id=1, source_target_pairs={{0,8},{8,128},{128,136},{136,256},{256,264},{264,384},{384,392},{3... | collective-permute-start | bytes 1179656 | tf_op jit(solution)/shard_map/ppermute | solution.py:211
  87.5 3.8 %collective-permute-start.11 = (bf16[3,4,128,128]{3,2,1,0:T(8,128)(2,1)S(1)}, bf16[3,4,128,128]{3,2,1,0:T(8,128)(2,1)S(1)}, u32[]{:S(2)}, u32[]{:S(2)}) collective-permute-start(bf16[3,4,128,128]{3,2,1,0:T(8,128)(2,1)S(1)} %collective-permute-done.10.last_mine), channel_id=1, source_target_pairs={{0,64},{64,0},{1,65},{65,1},{2,66},{66,2},{3,67},{67,3},{4,68},{68... | collective-permute-start | bytes 1179656 | tf_op jit(solution)/shard_map/ppermute | solution.py:225
  96.8 12.3 %collective-permute-start.13 = (bf16[2,2,128,256]{3,2,1,0:T(8,128)(2,1)S(1)}, bf16[2,2,128,256]{3,2,1,0:T(8,128)(2,1)S(1)}, u32[]{:S(2)}, u32[]{:S(2)}) collective-permute-start(bf16[2,2,128,256]{3,2,1,0:T(8,128)(2,1)S(1)} %get-tuple-element.48), channel_id=1, source_target_pairs={{0,1},{1,16},{16,17},{17,32},{32,33},{33,48},{48,49},{2,3},{3,18},... | collective-permute-start | bytes 786440 | tf_op jit(solution)/shard_map/ppermute | solution.py:336
  111.6 10.9 %collective-permute-start.14 = (bf16[2,2,128,256]{3,2,1,0:T(8,128)(2,1)S(1)}, bf16[2,2,128,256]{3,2,1,0:T(8,128)(2,1)S(1)}, u32[]{:S(2)}, u32[]{:S(2)}) collective-permute-start(bf16[2,2,128,256]{3,2,1,0:T(8,128)(2,1)S(1)} %get-tuple-element.52), channel_id=1, source_target_pairs={{0,1},{1,16},{16,17},{17,32},{32,33},{33,48},{48,49},{2,3},{3,18},... | collective-permute-start | bytes 786440 | tf_op jit(solution)/shard_map/ppermute | solution.py:336
  125.1 10.1 %collective-permute-start.15 = (bf16[2,2,128,256]{3,2,1,0:T(8,128)(2,1)S(1)}, bf16[2,2,128,256]{3,2,1,0:T(8,128)(2,1)S(1)}, u32[]{:S(2)}, u32[]{:S(2)}) collective-permute-start(bf16[2,2,128,256]{3,2,1,0:T(8,128)(2,1)S(1)} %get-tuple-element.56), channel_id=1, source_target_pairs={{0,1},{1,16},{16,17},{17,32},{32,33},{33,48},{48,49},{2,3},{3,18},... | collective-permute-start | bytes 786440 | tf_op jit(solution)/shard_map/ppermute | solution.py:336
  170.3 6.5 %collective-permute-start.16 = (bf16[64,128]{1,0:T(8,128)(2,1)S(1)}, bf16[64,128]{1,0:T(8,128)(2,1)S(1)}, u32[]{:S(2)}, u32[]{:S(2)}) collective-permute-start(bf16[64,128]{1,0:T(8,128)(2,1)S(1)} %shard_map.72), channel_id=1, source_target_pairs={{1,8},{8,1},{3,10},{10,3},{5,12},{12,5},{7,14},{14,7},{17,24},{24,... | collective-permute-start | bytes 49160 | tf_op jit(solution)/shard_map/ppermute | solution.py:382
  (3 other events, 2.2 us)

commit v10 on v8

--- a/solution.py
+++ b/solution.py
@@ -62,22 +62,16 @@
 
 
 def phase_kernel(sites, steps, n_in, sources, targets, with_ops, *refs):
-    whole, part, mine, other = refs[:4]
-    ins = refs[4 : 4 + n_in]
-    outs = refs[4 + n_in : -2]
+    whole, part, mine, other, last_mine, last_other = refs[:6]
+    ins = refs[6 : 6 + n_in]
+    outs = refs[6 + n_in : -2]
     site_at, sems = refs[-2:]
-    core = whole[0]
-    shift = whole[1]
-
-    def copies(slot, site, source):
-        return [
-            pltpu.make_async_copy(
-                source.at[(site // 2) * 2 + half],
-                site_at.at[slot, :, pl.ds(whole[2 + half], HALF)],
-                sems.at[slot, half],
-            )
-            for half in range(2)
-        ]
+    core, shift, opposite = whole[0], whole[1], whole[4]
+
+    def copy(slot, half, source):
+        return pltpu.make_async_copy(
+            source, site_at.at[slot, :, pl.ds(whole[2 + half], HALF)], sems.at[slot, half]
+        )
 
     @pl.when(whole[2] != 0)
     def _():
@@ -88,15 +82,18 @@
         site_at[:, :, WINDOW - 1] = jnp.zeros((len(sites), STATES, BLOCK, BLOCK), BF16)
 
     for slot, site in enumerate(sites):
-        @pl.when(core == site % 2)
-        def _():
-            for copy in copies(slot, site, mine):
-                copy.start()
-
-        @pl.when(core != site % 2)
-        def _():
-            for copy in copies(slot, site, other):
-                copy.start()
+        for half in range(2):
+            spot = site // 2 * 2 + half
+            for own, held, last in ((True, mine, last_mine), (False, other, last_other)):
+                here = (core == site % 2) == own
+
+                @pl.when(here & (opposite != spot))
+                def _():
+                    copy(slot, half, held.at[spot]).start()
+
+                @pl.when(here & (opposite == spot))
+                def _():
+                    copy(slot, half, last).start()
 
     state = {}
 
@@ -108,8 +105,8 @@
 
     for site, sectors in steps:
         slot = sites.index(site)
-        for copy in copies(slot, site, mine):
-            copy.wait()
+        for half in range(2):
+            copy(slot, half, last_mine).wait()
         lefts, images = {}, {}
         for sector in sectors:
             for s in range(STATES):
@@ -140,13 +137,13 @@
                 outs[which][index] = total
 
 
-def run_phase(sites, steps, ins, sources, outs, targets, with_ops, whole, part, mine, other):
-    blocks = 15 * sum(len(sectors) for _, sectors in steps)
+def run_phase(sites, steps, ins, sources, outs, targets, with_ops, whole, part, blocks):
+    products = 15 * sum(len(sectors) for _, sectors in steps)
     return pl.pallas_call(
         functools.partial(phase_kernel, sites, steps, len(ins), sources, targets, with_ops),
         out_shape=[jax.ShapeDtypeStruct(shape, BF16) for shape in outs],
         in_specs=[pl.BlockSpec(memory_space=pltpu.SMEM)] * 2
-        + [pl.BlockSpec(memory_space=pl.ANY)] * 2
+        + [pl.BlockSpec(memory_space=pl.ANY)] * 4
         + [pl.BlockSpec(memory_space=pltpu.VMEM)] * len(ins),
         out_specs=[pl.BlockSpec(memory_space=pltpu.VMEM)] * len(outs),
         scratch_shapes=[
@@ -154,8 +151,8 @@
             pltpu.SemaphoreType.DMA((len(sites), 2)),
         ],
         compiler_params=pltpu.CompilerParams(vmem_limit_bytes=32 * 1024 * 1024),
-        cost_estimate=pl.CostEstimate(flops=blocks * 2 * BLOCK**3, bytes_accessed=4 << 20, transcendentals=0),
-    )(whole, part, mine, other, *ins)
+        cost_estimate=pl.CostEstimate(flops=products * 2 * BLOCK**3, bytes_accessed=4 << 20, transcendentals=0),
+    )(whole, part, *blocks, *ins)
 
 
 def take_piece(start, site, piece, sems):
@@ -190,15 +187,17 @@
         arrived[-step] = lax.ppermute(arrived[1 - step], ("zhi", "zlo"), upward)
         if step < RING // 2:
             arrived[step] = lax.ppermute(arrived[step - 1], ("zhi", "zlo"), downward)
-    return pl.pallas_call(
+    last = arrived.pop(-RING // 2)
+    mine = pl.pallas_call(
         functools.partial(in_order, tuple(arrived)),
         out_shape=jax.ShapeDtypeStruct((RING,) + piece.shape, BF16),
-        in_specs=[pl.BlockSpec(memory_space=pltpu.SMEM)] + [pl.BlockSpec(memory_space=pl.ANY)] * RING,
+        in_specs=[pl.BlockSpec(memory_space=pltpu.SMEM)] + [pl.BlockSpec(memory_space=pl.ANY)] * len(arrived),
         out_specs=pl.BlockSpec(memory_space=pltpu.VMEM),
-        scratch_shapes=[pltpu.SemaphoreType.DMA((RING,))],
+        scratch_shapes=[pltpu.SemaphoreType.DMA((len(arrived),))],
         compiler_params=pltpu.CompilerParams(vmem_limit_bytes=16 << 20),
         cost_estimate=pl.CostEstimate(flops=0, bytes_accessed=6 << 20, transcendentals=0),
     )(place, *arrived.values())
+    return mine, last
 
 
 def add_cores(over, summed):
@@ -243,7 +242,7 @@
         cost_estimate=pl.CostEstimate(flops=0, bytes_accessed=800_000, transcendentals=0),
     )(start, site_tensor).reshape(STATES, HALF, BLOCK, BLOCK)
     place = (lax.axis_index("zhi") * 2 + at_zlo).astype(jnp.int32).reshape(1)
-    mine = gather_along_z(piece, place)
+    mine, last = gather_along_z(piece, place)
     spots = [site_start(sectors, group, half) - (OWN * group - BEFORE) for half in range(2)]
 
     pieces = ops_pieces(term_ops[0].reshape(sectors, BLOCK, BLOCK), term_shift[0], core)
@@ -256,7 +255,8 @@
     partner = jnp.arange(STATES, dtype=jnp.int32) - shift
     factors = jnp.where((partner >= 0) & (partner <= 2), figures[3:6], 0.0)
     part = jnp.concatenate([figures[:3], factors])
-    whole = jnp.stack([core, shift] + spots).astype(jnp.int32)
+    opposite = lax.rem(place[0] + RING // 2, RING)
+    whole = jnp.stack([core, shift] + spots + [opposite]).astype(jnp.int32)
 
     piece = lax.ppermute(env_rows, AXES, rows_to_groups(0))
     halo = lax.ppermute(env_rows, AXES, rows_to_groups(1))
@@ -267,7 +267,8 @@
     window = jnp.concatenate([ops_now, env_now.reshape(2 * OWN, BLOCK, BLOCK)], 2)
 
     mine, window, whole, part = lax.optimization_barrier((mine, window, whole, part))
-    other = lax.ppermute(mine, "core", [(0, 1), (1, 0)])
+    swap = [(0, 1), (1, 0)]
+    blocks = [mine, lax.ppermute(mine, "core", swap), last, lax.ppermute(last, "core", swap)]
 
     wide = (BLOCK, 2 * BLOCK)
     onward = [(i, i + 1) for i in range(7)]
@@ -292,8 +293,7 @@
         before_last,
         whole,
         part,
-        mine,
-        other,
+        blocks,
     )
     bonds = [first[:, :, BLOCK:], full[:, :, BLOCK:]]
     for site in (2, 4, 6):
@@ -331,8 +331,7 @@
             before_last,
             whole,
             part,
-            mine,
-            other,
+            blocks,
         )
         bonds += [lower[:, :, BLOCK:], old_upper[:, :, BLOCK:], full if last else full[:, :, BLOCK:]]
         if not last:

time: 159 us -> 172 us (1.082)
  the two profiles are of different devices: /device:TPU:70 before, /device:TPU:66 now
where the time goes in v10:
time: 172 us
  waiting for transfers between devices  61.9 us (36%)
  starting transfers between devices  55 us (32%)
  blocking collectives  33.8 us (20%)
  Pallas kernels  13.5 us (8%)
  other arithmetic  3.47 us (2%)
  local copies, waits for them, and re-layouts  2.15 us (1%)
  between operations  1.79 us (1%)
    all_to_all x1, blocking collectives, body(): over = lax.all_to_all(summed, ('zhi', 'zlo', 'yl'), 0, 0)  29.2 us
    ppermute x3, waiting for transfers between devices, body(): tails = lax.ppermute(tails, ('x', 'y0'), onward)  24.8 us
    ppermute x4, waiting for transfers between devices, gather_along_z(): arrived[-step] = lax.ppermute(arrived[1 - step], ('zhi', 'zlo'), upward)  23 us
    ppermute x3, starting transfers between devices, gather_along_z(): arrived[step] = lax.ppermute(arrived[step - 1], ('zhi', 'zlo'), downward)  18.8 us
    pallas_call x4, Pallas kernels, run_phase(): pl.pallas_call(functools.partial(phase_kernel, sites, steps, len(ins), so...  10.1 us
    ppermute x4, starting transfers between devices, gather_along_z(): arrived[-step] = lax.ppermute(arrived[1 - step], ('zhi', 'zlo'), upward)  7.67 us
    ppermute x3, starting transfers between devices, body(): tails = lax.ppermute(tails, ('x', 'y0'), onward)  5.76 us
    all_to_all x1, starting transfers between devices, body(): over = lax.all_to_all(pieces, 'x', 0, 0)  4.96 us
  transfers between devices with their start and end apart: 18, of which 10 were waited for; matrix products, arithmetic and copies ran while one was open for 1% of the time, Pallas kernels for 1%

profile of v10, /device:TPU:66, one launch (start us, length us, event | category | flops | bytes accessed | tf_op | source)
XLA Modules:
  0.0 171.6 jit_solution(3141731725797646455)
XLA Ops:
  3.4 5.0 %all-to-all-start = ((bf16[4,8,128,128]{3,2,1,0:T(8,128)(2,1)}), bf16[4,8,128,128]{3,2,1,0:T(8,128)(2,1)S(1)}, u32[]{:S(2)}, u32[]{:S(2)}) async-start(bf16[4,8,128,128]{3,2,1,0:T(8,128)(2,1)} %bitcast.5), calls=%async_computation | async-start | bytes 2097152 | tf_op jit(solution)/shard_map/all_to_all | solution.py:249
  8.4 1.8 %shard_map.64 = bf16[3,512,128]{2,1,0:T(8,128)(2,1)} custom-call(s32[1]{0:T(128)} %bitcast.1.start, bf16[1,3,4096,128]{3,2,1,0:T(8,128)(2,1)} %site.1), custom_call_target="tpu_custom_call" | custom-call | bytes 800000 | tf_op jit(solution)/shard_map/pallas_call | solution.py:235
  10.2 6.1 %collective-permute-start.1 = (bf16[3,4,128,128]{3,2,1,0:T(8,128)(2,1)}, bf16[3,4,128,128]{3,2,1,0:T(8,128)(2,1)S(1)}, u32[]{:S(2)}, u32[]{:S(2)}) collective-permute-start(bf16[3,4,128,128]{3,2,1,0:T(8,128)(2,1)} %bitcast.25), channel_id=1, source_target_pairs={{0,392},{8,0},{128,8},{136,128},{256,136},{264,256},{384,264},{392... | collective-permute-start | bytes 1179656 | tf_op jit(solution)/shard_map/ppermute | solution.py:189
  16.3 1.9 %collective-permute-start = (bf16[3,4,128,128]{3,2,1,0:T(8,128)(2,1)}, bf16[3,4,128,128]{3,2,1,0:T(8,128)(2,1)S(1)}, u32[]{:S(2)}, u32[]{:S(2)}) collective-permute-start(bf16[3,4,128,128]{3,2,1,0:T(8,128)(2,1)} %bitcast.26), channel_id=1, source_target_pairs={{0,8},{8,128},{128,136},{136,256},{256,264},{264,384},{384,392},{3... | collective-permute-start | bytes 1179656 | tf_op jit(solution)/shard_map/ppermute | solution.py:187
  19.9 3.4 %collective-permute-start.7 = (bf16[64,128]{1,0:T(8,128)(2,1)S(1)}, bf16[64,128]{1,0:T(8,128)(2,1)S(1)}, u32[]{:S(2)}, u32[]{:S(2)}) collective-permute-start(bf16[64,128]{1,0:T(8,128)(2,1)S(1)} %copy-done.4), channel_id=1, source_target_pairs={{0,1},{2,3},{4,5},{6,7},{8,24},{10,26},{12,28},{14,30},{16,17},{18... | collective-permute-start | bytes 49160 | tf_op jit(solution)/shard_map/ppermute | solution.py:262
  23.3 7.5 %collective-permute-start.3 = (bf16[3,4,128,128]{3,2,1,0:T(8,128)(2,1)S(1)}, bf16[3,4,128,128]{3,2,1,0:T(8,128)(2,1)S(1)}, u32[]{:S(2)}, u32[]{:S(2)}) collective-permute-start(bf16[3,4,128,128]{3,2,1,0:T(8,128)(2,1)S(1)} %collective-permute-done.1.refs_2_), channel_id=1, source_target_pairs={{0,392},{8,0},{128,8},{136,128},{256,136},{264,256},{384,264},{392... | collective-permute-start | bytes 1179656 | tf_op jit(solution)/shard_map/ppermute | solution.py:189
  31.2 1.9 %collective-permute-start.2 = (bf16[3,4,128,128]{3,2,1,0:T(8,128)(2,1)S(1)}, bf16[3,4,128,128]{3,2,1,0:T(8,128)(2,1)S(1)}, u32[]{:S(2)}, u32[]{:S(2)}) collective-permute-start(bf16[3,4,128,128]{3,2,1,0:T(8,128)(2,1)S(1)} %collective-permute-done.refs_1_), channel_id=1, source_target_pairs={{0,8},{8,128},{128,136},{136,256},{256,264},{264,384},{384,392},{3... | collective-permute-start | bytes 1179656 | tf_op jit(solution)/shard_map/ppermute | solution.py:187
  33.2 4.2 %collective-permute-start.9 = (f32[8]{0:T(128)S(1)}, f32[8]{0:T(128)S(1)}, u32[]{:S(2)}, u32[]{:S(2)}) collective-permute-start(f32[8]{0:T(128)S(1)} %pad_maximum_fusion.1), channel_id=1, source_target_pairs={{0,0},{1,64},{2,2},{3,66},{4,4},{5,68},{6,6},{7,70},{8,8},{9,72},{... | collective-permute-start | bytes 104 | tf_op jit(solution)/shard_map/ppermute | solution.py:253
  37.4 3.0 %collective-permute-done.9 = f32[8]{0:T(128)S(1)} collective-permute-done((f32[8]{0:T(128)S(1)}, f32[8]{0:T(128)S(1)}, u32[]{:S(2)}, u32[]{:S(2)}) %collective-permute-start.9) | collective-permute-done | bytes 64 | tf_op jit(solution)/shard_map/ppermute | solution.py:253
  42.4 5.1 %collective-permute-start.5 = (bf16[3,4,128,128]{3,2,1,0:T(8,128)(2,1)S(1)}, bf16[3,4,128,128]{3,2,1,0:T(8,128)(2,1)S(1)}, u32[]{:S(2)}, u32[]{:S(2)}) collective-permute-start(bf16[3,4,128,128]{3,2,1,0:T(8,128)(2,1)S(1)} %collective-permute-done.3.refs_4_), channel_id=1, source_target_pairs={{0,392},{8,0},{128,8},{136,128},{256,136},{264,256},{384,264},{392... | collective-permute-start | bytes 1179656 | tf_op jit(solution)/shard_map/ppermute | solution.py:189
  47.6 1.9 %collective-permute-start.4 = (bf16[3,4,128,128]{3,2,1,0:T(8,128)(2,1)S(1)}, bf16[3,4,128,128]{3,2,1,0:T(8,128)(2,1)S(1)}, u32[]{:S(2)}, u32[]{:S(2)}) collective-permute-start(bf16[3,4,128,128]{3,2,1,0:T(8,128)(2,1)S(1)} %collective-permute-done.2.refs_3_), channel_id=1, source_target_pairs={{0,8},{8,128},{128,136},{136,256},{256,264},{264,384},{384,392},{3... | collective-permute-start | bytes 1179656 | tf_op jit(solution)/shard_map/ppermute | solution.py:187
  49.9 4.9 %collective-permute-done.5.refs_6_ = bf16[3,4,128,128]{3,2,1,0:T(8,128)(2,1)S(1)} collective-permute-done((bf16[3,4,128,128]{3,2,1,0:T(8,128)(2,1)S(1)}, bf16[3,4,128,128]{3,2,1,0:T(8,128)(2,1)S(1)}, u32[]{:S(2)}, u32[]{:S(2)}) %collective-permute-start.5) | collective-permute-done | bytes 393248 | tf_op jit(solution)/shard_map/ppermute | solution.py:189
  54.7 10.1 %collective-permute-done.4.refs_5_ = bf16[3,4,128,128]{3,2,1,0:T(8,128)(2,1)S(1)} collective-permute-done((bf16[3,4,128,128]{3,2,1,0:T(8,128)(2,1)S(1)}, bf16[3,4,128,128]{3,2,1,0:T(8,128)(2,1)S(1)}, u32[]{:S(2)}, u32[]{:S(2)}) %collective-permute-start.4) | collective-permute-done | bytes 393248 | tf_op jit(solution)/shard_map/ppermute | solution.py:187
  67.2 4.1 %collective-permute-start.10 = (bf16[8,3,4,128,128]{4,3,2,1,0:T(8,128)(2,1)S(1)}, bf16[8,3,4,128,128]{4,3,2,1,0:T(8,128)(2,1)S(1)}, u32[]{:S(2)}, u32[]{:S(2)}) collective-permute-start(bf16[8,3,4,128,128]{4,3,2,1,0:T(8,128)(2,1)S(1)} %shard_map.65.refs_2_), channel_id=1, source_target_pairs={{0,64},{64,0},{1,65},{65,1},{2,66},{66,2},{3,67},{67,3},{4,68},{68... | collective-permute-start | bytes 9437192 | tf_op jit(solution)/shard_map/ppermute | solution.py:271
  71.3 1.9 %collective-permute-start.11 = (bf16[3,4,128,128]{3,2,1,0:T(8,128)(2,1)S(1)}, bf16[3,4,128,128]{3,2,1,0:T(8,128)(2,1)S(1)}, u32[]{:S(2)}, u32[]{:S(2)}) collective-permute-start(bf16[3,4,128,128]{3,2,1,0:T(8,128)(2,1)S(1)} %collective-permute-done.4.refs_5_), channel_id=1, source_target_pairs={{0,8},{8,128},{128,136},{136,256},{256,264},{264,384},{384,392},{3... | collective-permute-start | bytes 1179656 | tf_op jit(solution)/shard_map/ppermute | solution.py:187
  73.2 12.5 %collective-permute-done.11.refs_4_ = bf16[3,4,128,128]{3,2,1,0:T(8,128)(2,1)S(1)} collective-permute-done((bf16[3,4,128,128]{3,2,1,0:T(8,128)(2,1)S(1)}, bf16[3,4,128,128]{3,2,1,0:T(8,128)(2,1)S(1)}, u32[]{:S(2)}, u32[]{:S(2)}) %collective-permute-start.11) | collective-permute-done | bytes 393248 | tf_op jit(solution)/shard_map/ppermute | solution.py:187
  85.7 1.9 %collective-permute-start.12 = (bf16[3,4,128,128]{3,2,1,0:T(8,128)(2,1)S(1)}, bf16[3,4,128,128]{3,2,1,0:T(8,128)(2,1)S(1)}, u32[]{:S(2)}, u32[]{:S(2)}) collective-permute-start(bf16[3,4,128,128]{3,2,1,0:T(8,128)(2,1)S(1)} %collective-permute-done.11.refs_4_), channel_id=1, source_target_pairs={{0,64},{64,0},{1,65},{65,1},{2,66},{66,2},{3,67},{67,3},{4,68},{68... | collective-permute-start | bytes 1179656 | tf_op jit(solution)/shard_map/ppermute | solution.py:271
  87.7 1.7 collective-permute-done.12.refs_5_
  89.3 2.9 %shard_map.66 = (bf16[4,128,256]{2,1,0:T(8,128)(2,1)S(1)}, bf16[4,128,256]{2,1,0:T(8,128)(2,1)S(1)}, bf16[2,128,256]{2,1,0:T(8,128)(2,1)S(1)}, bf16[2,2,128,256]{3,2,1,0:T(8,128)(2,1)S(1)}) custom-call(s32[5]{0:T(128)S(1)} %stack.20.refs_0_, f32[6]{0:T(128)S(1)} %pad_maximum_fusion.2.refs_1_, bf16[8,3,4,128,128]{4,3,2,1,0:T(8,128)(2,1)S(1)} %shard_map.65.refs_2_, ...), custom_call_target="tpu_custom_call" | custom-call | flops 754974720 | bytes 4194304 | tf_op jit(solution)/shard_map/pallas_call | solution.py:142
  92.3 1.9 %collective-permute-start.13 = (bf16[2,2,128,256]{3,2,1,0:T(8,128)(2,1)S(1)}, bf16[2,2,128,256]{3,2,1,0:T(8,128)(2,1)S(1)}, u32[]{:S(2)}, u32[]{:S(2)}) collective-permute-start(bf16[2,2,128,256]{3,2,1,0:T(8,128)(2,1)S(1)} %get-tuple-element.30), channel_id=1, source_target_pairs={{0,1},{1,16},{16,17},{17,32},{32,33},{33,48},{48,49},{2,3},{3,18},... | collective-permute-start | bytes 786440 | tf_op jit(solution)/shard_map/ppermute | solution.py:300
  94.3 9.1 %collective-permute-done.13.refs_8_ = bf16[2,2,128,256]{3,2,1,0:T(8,128)(2,1)S(1)} collective-permute-done((bf16[2,2,128,256]{3,2,1,0:T(8,128)(2,1)S(1)}, bf16[2,2,128,256]{3,2,1,0:T(8,128)(2,1)S(1)}, u32[]{:S(2)}, u32[]{:S(2)}) %collective-permute-start.13) | collective-permute-done | bytes 262176 | tf_op jit(solution)/shard_map/ppermute | solution.py:300
  103.4 2.6 %shard_map.67 = (bf16[2,128,256]{2,1,0:T(8,128)(2,1)S(1)}, bf16[4,128,256]{2,1,0:T(8,128)(2,1)S(1)}, bf16[2,128,256]{2,1,0:T(8,128)(2,1)S(1)}, bf16[2,2,128,256]{3,2,1,0:T(8,128)(2,1)S(1)}) custom-call(s32[5]{0:T(128)S(1)} %stack.20.refs_0_, f32[6]{0:T(128)S(1)} %pad_maximum_fusion.2.refs_1_, bf16[8,3,4,128,128]{4,3,2,1,0:T(8,128)(2,1)S(1)} %shard_map.65.refs_2_, ...), custom_call_target="tpu_custom_call" | custom-call | flops 503316480 | bytes 4194304 | tf_op jit(solution)/shard_map/pallas_call | solution.py:142
  106.0 1.9 %collective-permute-start.14 = (bf16[2,2,128,256]{3,2,1,0:T(8,128)(2,1)S(1)}, bf16[2,2,128,256]{3,2,1,0:T(8,128)(2,1)S(1)}, u32[]{:S(2)}, u32[]{:S(2)}) collective-permute-start(bf16[2,2,128,256]{3,2,1,0:T(8,128)(2,1)S(1)} %get-tuple-element.34), channel_id=1, source_target_pairs={{0,1},{1,16},{16,17},{17,32},{32,33},{33,48},{48,49},{2,3},{3,18},... | collective-permute-start | bytes 786440 | tf_op jit(solution)/shard_map/ppermute | solution.py:300
  108.1 8.3 %collective-permute-done.14.refs_8_ = bf16[2,2,128,256]{3,2,1,0:T(8,128)(2,1)S(1)} collective-permute-done((bf16[2,2,128,256]{3,2,1,0:T(8,128)(2,1)S(1)}, bf16[2,2,128,256]{3,2,1,0:T(8,128)(2,1)S(1)}, u32[]{:S(2)}, u32[]{:S(2)}) %collective-permute-start.14) | collective-permute-done | bytes 262176 | tf_op jit(solution)/shard_map/ppermute | solution.py:300
  116.3 2.6 %shard_map.68 = (bf16[2,128,256]{2,1,0:T(8,128)(2,1)S(1)}, bf16[4,128,256]{2,1,0:T(8,128)(2,1)S(1)}, bf16[2,128,256]{2,1,0:T(8,128)(2,1)S(1)}, bf16[2,2,128,256]{3,2,1,0:T(8,128)(2,1)S(1)}) custom-call(s32[5]{0:T(128)S(1)} %stack.20.refs_0_, f32[6]{0:T(128)S(1)} %pad_maximum_fusion.2.refs_1_, bf16[8,3,4,128,128]{4,3,2,1,0:T(8,128)(2,1)S(1)} %shard_map.65.refs_2_, ...), custom_call_target="tpu_custom_call" | custom-call | flops 503316480 | bytes 4194304 | tf_op jit(solution)/shard_map/pallas_call | solution.py:142
  119.0 1.9 %collective-permute-start.15 = (bf16[2,2,128,256]{3,2,1,0:T(8,128)(2,1)S(1)}, bf16[2,2,128,256]{3,2,1,0:T(8,128)(2,1)S(1)}, u32[]{:S(2)}, u32[]{:S(2)}) collective-permute-start(bf16[2,2,128,256]{3,2,1,0:T(8,128)(2,1)S(1)} %get-tuple-element.38), channel_id=1, source_target_pairs={{0,1},{1,16},{16,17},{17,32},{32,33},{33,48},{48,49},{2,3},{3,18},... | collective-permute-start | bytes 786440 | tf_op jit(solution)/shard_map/ppermute | solution.py:300
  121.0 7.4 %collective-permute-done.15.refs_8_ = bf16[2,2,128,256]{3,2,1,0:T(8,128)(2,1)S(1)} collective-permute-done((bf16[2,2,128,256]{3,2,1,0:T(8,128)(2,1)S(1)}, bf16[2,2,128,256]{3,2,1,0:T(8,128)(2,1)S(1)}, u32[]{:S(2)}, u32[]{:S(2)}) %collective-permute-start.15) | collective-permute-done | bytes 262176 | tf_op jit(solution)/shard_map/ppermute | solution.py:300
  128.4 1.9 %shard_map.69 = (bf16[2,128,256]{2,1,0:T(8,128)(2,1)S(1)}, bf16[4,128,128]{2,1,0:T(8,128)(2,1)S(1)}) custom-call(s32[5]{0:T(128)S(1)} %stack.20.refs_0_, f32[6]{0:T(128)S(1)} %pad_maximum_fusion.2.refs_1_, bf16[8,3,4,128,128]{4,3,2,1,0:T(8,128)(2,1)S(1)} %shard_map.65.refs_2_, bf16[8,3,4,128,128]{4,3,2,1,0:T(8,128)(2,1)S(1)} %collective-permute-done.10.refs_3_, ...), custom_call_target="tpu_custom_call" | custom-call | flops 377487360 | bytes 4194304 | tf_op jit(solution)/shard_map/pallas_call | solution.py:142
  130.5 4.6 %all_to_all.15.over = bf16[2,4,8,64,128]{4,3,2,1,0:T(8,128)(2,1)S(1)} all-to-all(bf16[2,4,8,64,128]{4,3,2,1,0:T(8,128)(2,1)S(1)} %bitcast.30), channel_id=1, replica_groups=mesh['zhi'=4,'core'=2,'x'=4,'zlo'=2,'yl'=4,'y0'=2] {'core'}, dimensions={0} | all-to-all | bytes 2097152 | tf_op jit(solution)/shard_map/all_to_all | solution.py:341
  135.2 29.2 %all_to_all.16.over = bf16[32,64,128]{2,1,0:T(8,128)(2,1)S(1)} all-to-all(bf16[32,64,128]{2,1,0:T(8,128)(2,1)S(1)} %bitcast.24), channel_id=1, replica_groups=mesh['zhi'=4,'core'=2,'x'=4,'zlo'=2,'yl'=4,'y0'=2] {'zhi','zlo','yl'}, dimensions={0} | all-to-all | bytes 1048576 | tf_op jit(solution)/shard_map/all_to_all | solution.py:343
  164.4 1.9 %collective-permute-start.16 = (bf16[64,128]{1,0:T(8,128)(2,1)S(1)}, bf16[64,128]{1,0:T(8,128)(2,1)S(1)}, u32[]{:S(2)}, u32[]{:S(2)}) collective-permute-start(bf16[64,128]{1,0:T(8,128)(2,1)S(1)} %shard_map.71), channel_id=1, source_target_pairs={{1,8},{8,1},{3,10},{10,3},{5,12},{12,5},{7,14},{14,7},{17,24},{24,... | collective-permute-start | bytes 49160 | tf_op jit(solution)/shard_map/ppermute | solution.py:345
  166.4 4.6 %collective-permute-done.16 = bf16[64,128]{1,0:T(8,128)(2,1)S(1)} collective-permute-done((bf16[64,128]{1,0:T(8,128)(2,1)S(1)}, bf16[64,128]{1,0:T(8,128)(2,1)S(1)}, u32[]{:S(2)}, u32[]{:S(2)}) %collective-permute-start.16) | collective-permute-done | bytes 16416 | tf_op jit(solution)/shard_map/ppermute | solution.py:345
  (51 shorter events, 9.9 us)
Async XLA Ops:
  0.0 2.2 %copy-start.1 = (bf16[1,4096,128]{2,1,0:T(8,128)(2,1)S(1)}, bf16[1,4096,128]{2,1,0:T(8,128)(2,1)}, u32[]{:S(2)}) copy-start(bf16[1,4096,128]{2,1,0:T(8,128)(2,1)} %param.7) | copy-start | bytes 3145732
  3.4 14.8 %copy-start.4 = (bf16[64,128]{1,0:T(8,128)(2,1)S(1)}, bf16[64,128]{1,0:T(8,128)(2,1)}, u32[]{:S(2)}) copy-start(bf16[64,128]{1,0:T(8,128)(2,1)} %param.8) | copy-start | bytes 49156
  3.4 29.7 %copy-start.2 = (f32[1,3]{1,0:T(1,128)S(1)}, f32[1,3]{1,0:T(1,128)}, u32[]{:S(2)}) copy-start(f32[1,3]{1,0:T(1,128)} %param.11) | copy-start | bytes 40
  3.4 29.7 %copy-start.3 = (f32[1,3]{1,0:T(1,128)S(1)}, f32[1,3]{1,0:T(1,128)}, u32[]{:S(2)}) copy-start(f32[1,3]{1,0:T(1,128)} %param.10) | copy-start | bytes 40
  3.4 38.3 %all-to-all-start = ((bf16[4,8,128,128]{3,2,1,0:T(8,128)(2,1)}), bf16[4,8,128,128]{3,2,1,0:T(8,128)(2,1)S(1)}, u32[]{:S(2)}, u32[]{:S(2)}) async-start(bf16[4,8,128,128]{3,2,1,0:T(8,128)(2,1)} %bitcast.5), calls=%async_computation | async-start | bytes 2097152 | tf_op jit(solution)/shard_map/all_to_all | solution.py:249
  10.2 13.1 %collective-permute-start.1 = (bf16[3,4,128,128]{3,2,1,0:T(8,128)(2,1)}, bf16[3,4,128,128]{3,2,1,0:T(8,128)(2,1)S(1)}, u32[]{:S(2)}, u32[]{:S(2)}) collective-permute-start(bf16[3,4,128,128]{3,2,1,0:T(8,128)(2,1)} %bitcast.25), channel_id=1, source_target_pairs={{0,392},{8,0},{128,8},{136,128},{256,136},{264,256},{384,264},{392... | collective-permute-start | bytes 1179656 | tf_op jit(solution)/shard_map/ppermute | solution.py:189
  16.3 14.9 %collective-permute-start = (bf16[3,4,128,128]{3,2,1,0:T(8,128)(2,1)}, bf16[3,4,128,128]{3,2,1,0:T(8,128)(2,1)S(1)}, u32[]{:S(2)}, u32[]{:S(2)}) collective-permute-start(bf16[3,4,128,128]{3,2,1,0:T(8,128)(2,1)} %bitcast.26), channel_id=1, source_target_pairs={{0,8},{8,128},{128,136},{136,256},{256,264},{264,384},{384,392},{3... | collective-permute-start | bytes 1179656 | tf_op jit(solution)/shard_map/ppermute | solution.py:187
  18.2 31.5 %collective-permute-start.8 = (bf16[64,128]{1,0:T(8,128)(2,1)S(1)}, bf16[64,128]{1,0:T(8,128)(2,1)S(1)}, u32[]{:S(2)}, u32[]{:S(2)}) collective-permute-start(bf16[64,128]{1,0:T(8,128)(2,1)S(1)} %copy-done.4), channel_id=1, source_target_pairs={{0,0},{2,2},{4,4},{6,6},{8,9},{10,11},{12,13},{14,15},{16,16},{18,... | collective-permute-start | bytes 49160 | tf_op jit(solution)/shard_map/ppermute | solution.py:261
  19.9 29.8 %collective-permute-start.7 = (bf16[64,128]{1,0:T(8,128)(2,1)S(1)}, bf16[64,128]{1,0:T(8,128)(2,1)S(1)}, u32[]{:S(2)}, u32[]{:S(2)}) collective-permute-start(bf16[64,128]{1,0:T(8,128)(2,1)S(1)} %copy-done.4), channel_id=1, source_target_pairs={{0,1},{2,3},{4,5},{6,7},{8,24},{10,26},{12,28},{14,30},{16,17},{18... | collective-permute-start | bytes 49160 | tf_op jit(solution)/shard_map/ppermute | solution.py:262
  23.3 19.1 %collective-permute-start.3 = (bf16[3,4,128,128]{3,2,1,0:T(8,128)(2,1)S(1)}, bf16[3,4,128,128]{3,2,1,0:T(8,128)(2,1)S(1)}, u32[]{:S(2)}, u32[]{:S(2)}) collective-permute-start(bf16[3,4,128,128]{3,2,1,0:T(8,128)(2,1)S(1)} %collective-permute-done.1.refs_2_), channel_id=1, source_target_pairs={{0,392},{8,0},{128,8},{136,128},{256,136},{264,256},{384,264},{392... | collective-permute-start | bytes 1179656 | tf_op jit(solution)/shard_map/ppermute | solution.py:189
  31.2 16.4 %collective-permute-start.2 = (bf16[3,4,128,128]{3,2,1,0:T(8,128)(2,1)S(1)}, bf16[3,4,128,128]{3,2,1,0:T(8,128)(2,1)S(1)}, u32[]{:S(2)}, u32[]{:S(2)}) collective-permute-start(bf16[3,4,128,128]{3,2,1,0:T(8,128)(2,1)S(1)} %collective-permute-done.refs_1_), channel_id=1, source_target_pairs={{0,8},{8,128},{128,136},{136,256},{256,264},{264,384},{384,392},{3... | collective-permute-start | bytes 1179656 | tf_op jit(solution)/shard_map/ppermute | solution.py:187
  33.2 7.2 %collective-permute-start.9 = (f32[8]{0:T(128)S(1)}, f32[8]{0:T(128)S(1)}, u32[]{:S(2)}, u32[]{:S(2)}) collective-permute-start(f32[8]{0:T(128)S(1)} %pad_maximum_fusion.1), channel_id=1, source_target_pairs={{0,0},{1,64},{2,2},{3,66},{4,4},{5,68},{6,6},{7,70},{8,8},{9,72},{... | collective-permute-start | bytes 104 | tf_op jit(solution)/shard_map/ppermute | solution.py:253
  41.7 8.0 %collective-permute-start.6 = (bf16[8,128,128]{2,1,0:T(8,128)(2,1)S(1)}, bf16[8,128,128]{2,1,0:T(8,128)(2,1)S(1)}, u32[]{:S(2)}, u32[]{:S(2)}) collective-permute-start(bf16[8,128,128]{2,1,0:T(8,128)(2,1)S(1)} %dynamic-slice_bitcast_fusion), channel_id=1, source_target_pairs={{0,0},{1,64},{64,1},{65,65},{2,2},{3,66},{66,3},{67,67},{4,4},{5,6... | collective-permute-start | bytes 786440 | tf_op jit(solution)/shard_map/ppermute | solution.py:251
  42.4 12.3 %collective-permute-start.5 = (bf16[3,4,128,128]{3,2,1,0:T(8,128)(2,1)S(1)}, bf16[3,4,128,128]{3,2,1,0:T(8,128)(2,1)S(1)}, u32[]{:S(2)}, u32[]{:S(2)}) collective-permute-start(bf16[3,4,128,128]{3,2,1,0:T(8,128)(2,1)S(1)} %collective-permute-done.3.refs_4_), channel_id=1, source_target_pairs={{0,392},{8,0},{128,8},{136,128},{256,136},{264,256},{384,264},{392... | collective-permute-start | bytes 1179656 | tf_op jit(solution)/shard_map/ppermute | solution.py:189
  47.6 17.3 %collective-permute-start.4 = (bf16[3,4,128,128]{3,2,1,0:T(8,128)(2,1)S(1)}, bf16[3,4,128,128]{3,2,1,0:T(8,128)(2,1)S(1)}, u32[]{:S(2)}, u32[]{:S(2)}) collective-permute-start(bf16[3,4,128,128]{3,2,1,0:T(8,128)(2,1)S(1)} %collective-permute-done.2.refs_3_), channel_id=1, source_target_pairs={{0,8},{8,128},{128,136},{136,256},{256,264},{264,384},{384,392},{3... | collective-permute-start | bytes 1179656 | tf_op jit(solution)/shard_map/ppermute | solution.py:187
  64.9 1.0 copy-start
  67.2 22.1 %collective-permute-start.10 = (bf16[8,3,4,128,128]{4,3,2,1,0:T(8,128)(2,1)S(1)}, bf16[8,3,4,128,128]{4,3,2,1,0:T(8,128)(2,1)S(1)}, u32[]{:S(2)}, u32[]{:S(2)}) collective-permute-start(bf16[8,3,4,128,128]{4,3,2,1,0:T(8,128)(2,1)S(1)} %shard_map.65.refs_2_), channel_id=1, source_target_pairs={{0,64},{64,0},{1,65},{65,1},{2,66},{66,2},{3,67},{67,3},{4,68},{68... | collective-permute-start | bytes 9437192 | tf_op jit(solution)/shard_map/ppermute | solution.py:271
  71.3 14.4 %collective-permute-start.11 = (bf16[3,4,128,128]{3,2,1,0:T(8,128)(2,1)S(1)}, bf16[3,4,128,128]{3,2,1,0:T(8,128)(2,1)S(1)}, u32[]{:S(2)}, u32[]{:S(2)}) collective-permute-start(bf16[3,4,128,128]{3,2,1,0:T(8,128)(2,1)S(1)} %collective-permute-done.4.refs_5_), channel_id=1, source_target_pairs={{0,8},{8,128},{128,136},{136,256},{256,264},{264,384},{384,392},{3... | collective-permute-start | bytes 1179656 | tf_op jit(solution)/shard_map/ppermute | solution.py:187
  85.7 3.6 %collective-permute-start.12 = (bf16[3,4,128,128]{3,2,1,0:T(8,128)(2,1)S(1)}, bf16[3,4,128,128]{3,2,1,0:T(8,128)(2,1)S(1)}, u32[]{:S(2)}, u32[]{:S(2)}) collective-permute-start(bf16[3,4,128,128]{3,2,1,0:T(8,128)(2,1)S(1)} %collective-permute-done.11.refs_4_), channel_id=1, source_target_pairs={{0,64},{64,0},{1,65},{65,1},{2,66},{66,2},{3,67},{67,3},{4,68},{68... | collective-permute-start | bytes 1179656 | tf_op jit(solution)/shard_map/ppermute | solution.py:271
  92.3 11.1 %collective-permute-start.13 = (bf16[2,2,128,256]{3,2,1,0:T(8,128)(2,1)S(1)}, bf16[2,2,128,256]{3,2,1,0:T(8,128)(2,1)S(1)}, u32[]{:S(2)}, u32[]{:S(2)}) collective-permute-start(bf16[2,2,128,256]{3,2,1,0:T(8,128)(2,1)S(1)} %get-tuple-element.30), channel_id=1, source_target_pairs={{0,1},{1,16},{16,17},{17,32},{32,33},{33,48},{48,49},{2,3},{3,18},... | collective-permute-start | bytes 786440 | tf_op jit(solution)/shard_map/ppermute | solution.py:300
  106.0 10.3 %collective-permute-start.14 = (bf16[2,2,128,256]{3,2,1,0:T(8,128)(2,1)S(1)}, bf16[2,2,128,256]{3,2,1,0:T(8,128)(2,1)S(1)}, u32[]{:S(2)}, u32[]{:S(2)}) collective-permute-start(bf16[2,2,128,256]{3,2,1,0:T(8,128)(2,1)S(1)} %get-tuple-element.34), channel_id=1, source_target_pairs={{0,1},{1,16},{16,17},{17,32},{32,33},{33,48},{48,49},{2,3},{3,18},... | collective-permute-start | bytes 786440 | tf_op jit(solution)/shard_map/ppermute | solution.py:300
  119.0 9.4 %collective-permute-start.15 = (bf16[2,2,128,256]{3,2,1,0:T(8,128)(2,1)S(1)}, bf16[2,2,128,256]{3,2,1,0:T(8,128)(2,1)S(1)}, u32[]{:S(2)}, u32[]{:S(2)}) collective-permute-start(bf16[2,2,128,256]{3,2,1,0:T(8,128)(2,1)S(1)} %get-tuple-element.38), channel_id=1, source_target_pairs={{0,1},{1,16},{16,17},{17,32},{32,33},{33,48},{48,49},{2,3},{3,18},... | collective-permute-start | bytes 786440 | tf_op jit(solution)/shard_map/ppermute | solution.py:300
  164.4 6.5 %collective-permute-start.16 = (bf16[64,128]{1,0:T(8,128)(2,1)S(1)}, bf16[64,128]{1,0:T(8,128)(2,1)S(1)}, u32[]{:S(2)}, u32[]{:S(2)}) collective-permute-start(bf16[64,128]{1,0:T(8,128)(2,1)S(1)} %shard_map.71), channel_id=1, source_target_pairs={{1,8},{8,1},{3,10},{10,3},{5,12},{12,5},{7,14},{14,7},{17,24},{24,... | collective-permute-start | bytes 49160 | tf_op jit(solution)/shard_map/ppermute | solution.py:345

commit v11 on v7

--- a/solution.py
+++ b/solution.py
@@ -187,9 +187,15 @@
     copy.wait()
 
 
-def add_cores(over, summed):
+def core_exchange(bonds):
+    partial = jnp.concatenate(bonds, 0).reshape(-1, 2, 8, BLOCK // 2, BLOCK).swapaxes(0, 1)
+    return lax.all_to_all(partial, "core", 0, 0)
+
+
+def add_cores(early, late, summed):
     for site in range(4):
-        both = (over[0, site].astype(F32) + over[1, site].astype(F32)).astype(BF16)
+        pair = [early[core, site] if site < 3 else late[core, 0] for core in range(2)]
+        both = (pair[0].astype(F32) + pair[1].astype(F32)).astype(BF16)
         for piece in range(8):
             summed[site, piece % 2, piece // 2] = both[piece]
 
@@ -201,15 +207,15 @@
     summed[...] = total.astype(BF16)
 
 
-def add_up(kernel, array, out):
+def add_up(kernel, out, *arrays):
     return pl.pallas_call(
         kernel,
         out_shape=jax.ShapeDtypeStruct(out, BF16),
-        in_specs=[pl.BlockSpec(memory_space=pltpu.VMEM)],
+        in_specs=[pl.BlockSpec(memory_space=pltpu.VMEM)] * len(arrays),
         out_specs=pl.BlockSpec(memory_space=pltpu.VMEM),
         compiler_params=pltpu.CompilerParams(vmem_limit_bytes=16 << 20),
         cost_estimate=pl.CostEstimate(flops=1 << 19, bytes_accessed=2 << 20, transcendentals=0),
-    )(array)
+    )(*arrays)
 
 
 def body(site_tensor, term_ops, env_rows, term_shift, keep_weight, env_weight):
@@ -293,6 +299,9 @@
     for site in (2, 4, 6):
         tails = lax.ppermute(tails, ("x", "y0"), onward)
         last = site == 6
+        if last:
+            early = len(bonds)
+            over = core_exchange(bonds)
         sources = {}
         for sector in (-2, -1):
             sources[site, sector] = (2, (0, sector + 2))
@@ -332,11 +341,10 @@
         if not last:
             upper, tails = rest
 
-    partial = jnp.concatenate(bonds, 0).reshape(4, 2, 8, BLOCK // 2, BLOCK).transpose(1, 0, 2, 3, 4)
-    over = lax.all_to_all(partial, "core", 0, 0)
-    summed = add_up(add_cores, over, (4, 2, 4, BLOCK // 2, BLOCK)).reshape(32, BLOCK // 2, BLOCK)
+    late = core_exchange(bonds[early:])
+    summed = add_up(add_cores, (4, 2, 4, BLOCK // 2, BLOCK), over, late).reshape(32, BLOCK // 2, BLOCK)
     over = lax.all_to_all(summed, ("zhi", "zlo", "yl"), 0, 0)
-    summed = add_up(add_columns, over, (BLOCK // 2, BLOCK))
+    summed = add_up(add_columns, (BLOCK // 2, BLOCK), over)
     swapped = lax.ppermute(summed, ("zlo", "y0"), SWAP)
     return jnp.where(at_zlo == at_y0, summed, swapped)[None]
 

time: 158 us -> 164 us (1.038)
  the two profiles are of different devices: /device:TPU:66 before, /device:TPU:8 now
where the time goes in v11:
time: 164 us; the launch traced here: 163 us
  waiting for transfers between devices  59.4 us (36%)
  blocking collectives  33.8 us (21%)
  starting transfers between devices  31 us (19%)
  between operations  15.1 us (9%)
  Pallas kernels  14.2 us (9%)
  local copies, waits for them, and re-layouts  6.37 us (4%)
  other arithmetic  3.12 us (2%)
    all_to_all x1, blocking collectives, body(): over = lax.all_to_all(summed, ('zhi', 'zlo', 'yl'), 0, 0)  29.9 us
    all_gather x1, waiting for transfers between devices, body(): mine = lax.all_gather(piece, ('zhi', 'zlo'))  24 us
    ppermute x3, starting transfers between devices, body(): tails = lax.ppermute(tails, ('x', 'y0'), onward)  12.8 us
    ppermute x3, waiting for transfers between devices, body(): tails = lax.ppermute(tails, ('x', 'y0'), onward)  11.9 us
    pallas_call x4, Pallas kernels, run_phase(): pl.pallas_call(functools.partial(phase_kernel, sites, steps, len(ins), so...  10.8 us
    all_to_all x1, waiting for transfers between devices, body(): over = lax.all_to_all(pieces, 'x', 0, 0)  6.74 us
    ppermute x1, waiting for transfers between devices, body(): lax.ppermute(ops_now, ('core', 'y0'), [(0, 0), (1, 2), (2, 1), (3, 3)])  5.59 us
    ppermute x1, waiting for transfers between devices, body(): swapped = lax.ppermute(summed, ('zlo', 'y0'), SWAP)  4.6 us
  transfers between devices with their start and end apart: 12, of which 8 were waited for; matrix products, arithmetic and copies ran while one was open for 3% of the time, Pallas kernels for 2%

profile of v11, /device:TPU:8, one launch (start us, length us, event | category | flops | bytes accessed | tf_op | source)
XLA Modules:
  0.0 163.0 jit_solution(5884925578420336664)
XLA Ops:
  6.5 1.8 %shard_map.64 = bf16[3,512,128]{2,1,0:T(8,128)(2,1)} custom-call(s32[1]{0:T(128)} %bitcast.start, bf16[1,3,4096,128]{3,2,1,0:T(8,128)(2,1)} %site.1), custom_call_target="tpu_custom_call" | custom-call | bytes 800000 | tf_op jit(solution)/shard_map/pallas_call | solution.py:228
  9.3 1.2 pad_select_fusion
  10.5 4.3 %all-to-all-start = ((bf16[4,8,128,128]{3,2,1,0:T(8,128)(2,1)}), bf16[4,8,128,128]{3,2,1,0:T(8,128)(2,1)S(1)}, u32[]{:S(2)}, u32[]{:S(2)}) async-start(bf16[4,8,128,128]{3,2,1,0:T(8,128)(2,1)} %bitcast.4), calls=%async_computation | async-start | bytes 2097152 | tf_op jit(solution)/shard_map/all_to_all | solution.py:241
  14.8 1.3 collective-permute-start.1
  16.1 0.7 collective-permute-start.2
  16.9 1.9 %collective-permute-start.3 = (f32[8]{0:T(128)S(1)}, f32[8]{0:T(128)S(1)}, u32[]{:S(2)}, u32[]{:S(2)}) collective-permute-start(f32[8]{0:T(128)S(1)} %pad_maximum_fusion.2), channel_id=1, source_target_pairs={{0,0},{1,64},{2,2},{3,66},{4,4},{5,68},{6,6},{7,70},{8,8},{9,72},{... | collective-permute-start | bytes 104 | tf_op jit(solution)/shard_map/ppermute | solution.py:245
  18.8 2.9 %collective-permute-done.3 = f32[8]{0:T(128)S(1)} collective-permute-done((f32[8]{0:T(128)S(1)}, f32[8]{0:T(128)S(1)}, u32[]{:S(2)}, u32[]{:S(2)}) %collective-permute-start.3) | collective-permute-done | bytes 64 | tf_op jit(solution)/shard_map/ppermute | solution.py:245
  23.1 6.7 %all-to-all-done = bf16[4,8,128,128]{3,2,1,0:T(8,128)(2,1)S(1)} async-done(((bf16[4,8,128,128]{3,2,1,0:T(8,128)(2,1)}), bf16[4,8,128,128]{3,2,1,0:T(8,128)(2,1)S(1)}, u32[]{:S(2)}, u32[]{:S(2)}) %all-to-all-start) | async-done | bytes 1048608 | tf_op jit(solution)/shard_map/all_to_all | solution.py:241
  29.9 1.9 %collective-permute-start = (bf16[8,128,128]{2,1,0:T(8,128)(2,1)S(1)}, bf16[8,128,128]{2,1,0:T(8,128)(2,1)S(1)}, u32[]{:S(2)}, u32[]{:S(2)}) collective-permute-start(bf16[8,128,128]{2,1,0:T(8,128)(2,1)S(1)} %dynamic-slice_bitcast_fusion), channel_id=1, source_target_pairs={{0,0},{1,64},{64,1},{65,65},{2,2},{3,66},{66,3},{67,67},{4,4},{5,6... | collective-permute-start | bytes 786440 | tf_op jit(solution)/shard_map/ppermute | solution.py:243
  32.0 5.6 %collective-permute-done = bf16[8,128,128]{2,1,0:T(8,128)(2,1)S(1)} collective-permute-done((bf16[8,128,128]{2,1,0:T(8,128)(2,1)S(1)}, bf16[8,128,128]{2,1,0:T(8,128)(2,1)S(1)}, u32[]{:S(2)}, u32[]{:S(2)}) %collective-permute-start) | collective-permute-done | bytes 262176 | tf_op jit(solution)/shard_map/ppermute | solution.py:243
  37.6 0.9 pad_maximum_fusion.refs_4_
  38.5 24.0 %all-gather.2.cloned.1.call-done.blocks = bf16[8,3,4,128,128]{4,3,2,1,0:T(8,128)(2,1)} async-done(((bf16[1,3,4,128,128]{4,3,2,1,0:T(8,128)(2,1)}), bf16[8,3,4,128,128]{4,3,2,1,0:T(8,128)(2,1)}) %all-gather.2.cloned.1.call-update) | async-done | bytes 3145744 | tf_op jit(solution)/shard_map/all_gather | solution.py:237
  62.5 1.9 %collective-permute-start.4 = (bf16[8,3,4,128,128]{4,3,2,1,0:T(8,128)(2,1)}, bf16[8,3,4,128,128]{4,3,2,1,0:T(8,128)(2,1)S(1)}, u32[]{:S(2)}, u32[]{:S(2)}) collective-permute-start(bf16[8,3,4,128,128]{4,3,2,1,0:T(8,128)(2,1)} %all-gather.2.cloned.1.call-done.blocks), channel_id=1, source_target_pairs={{0,64},{64,0},{1,65},{65,1},{2,66},{66,2},{3,67},{67,3},{4,68},{68... | collective-permute-start | bytes 9437192 | tf_op jit(solution)/shard_map/ppermute | solution.py:261
  64.4 1.9 %copy-done.2 = bf16[8,3,4,128,128]{4,3,2,1,0:T(8,128)(2,1)S(1)} copy-done((bf16[8,3,4,128,128]{4,3,2,1,0:T(8,128)(2,1)S(1)}, bf16[8,3,4,128,128]{4,3,2,1,0:T(8,128)(2,1)}, u32[]{:S(2)}) %copy-start.2) | copy-done | bytes 3145752
  66.5 3.7 %collective-permute-done.4.refs_3_ = bf16[8,3,4,128,128]{4,3,2,1,0:T(8,128)(2,1)S(1)} collective-permute-done((bf16[8,3,4,128,128]{4,3,2,1,0:T(8,128)(2,1)}, bf16[8,3,4,128,128]{4,3,2,1,0:T(8,128)(2,1)S(1)}, u32[]{:S(2)}, u32[]{:S(2)}) %collective-permute-start.4) | collective-permute-done | bytes 3145760 | tf_op jit(solution)/shard_map/ppermute | solution.py:261
  70.2 2.8 %shard_map.66 = (bf16[4,128,256]{2,1,0:T(8,128)(2,1)S(1)}, bf16[4,128,256]{2,1,0:T(8,128)(2,1)S(1)}, bf16[2,128,256]{2,1,0:T(8,128)(2,1)S(1)}, bf16[2,2,128,256]{3,2,1,0:T(8,128)(2,1)S(1)}) custom-call(s32[4]{0:T(128)S(1)} %pad_add_fusion.refs_0_, f32[6]{0:T(128)S(1)} %pad_maximum_fusion.3.refs_1_, bf16[8,3,4,128,128]{4,3,2,1,0:T(8,128)(2,1)S(1)} %shard_map.65.refs_2_, ...), custom_call_target="tpu_custom_call" | custom-call | flops 754974720 | bytes 4194304 | tf_op jit(solution)/shard_map/pallas_call | solution.py:144
  73.0 3.3 %collective-permute-start.5 = (bf16[2,2,128,256]{3,2,1,0:T(8,128)(2,1)S(1)}, bf16[2,2,128,256]{3,2,1,0:T(8,128)(2,1)S(1)}, u32[]{:S(2)}, u32[]{:S(2)}) collective-permute-start(bf16[2,2,128,256]{3,2,1,0:T(8,128)(2,1)S(1)} %get-tuple-element.30), channel_id=1, source_target_pairs={{0,1},{1,16},{16,17},{17,32},{32,33},{33,48},{48,49},{2,3},{3,18},... | collective-permute-start | bytes 786440 | tf_op jit(solution)/shard_map/ppermute | solution.py:300
  76.4 6.8 %collective-permute-done.5.refs_6_ = bf16[2,2,128,256]{3,2,1,0:T(8,128)(2,1)S(1)} collective-permute-done((bf16[2,2,128,256]{3,2,1,0:T(8,128)(2,1)S(1)}, bf16[2,2,128,256]{3,2,1,0:T(8,128)(2,1)S(1)}, u32[]{:S(2)}, u32[]{:S(2)}) %collective-permute-start.5) | collective-permute-done | bytes 262176 | tf_op jit(solution)/shard_map/ppermute | solution.py:300
  83.2 2.5 %shard_map.67 = (bf16[2,128,256]{2,1,0:T(8,128)(2,1)S(1)}, bf16[4,128,256]{2,1,0:T(8,128)(2,1)S(1)}, bf16[2,128,256]{2,1,0:T(8,128)(2,1)S(1)}, bf16[2,2,128,256]{3,2,1,0:T(8,128)(2,1)S(1)}) custom-call(s32[4]{0:T(128)S(1)} %pad_add_fusion.refs_0_, f32[6]{0:T(128)S(1)} %pad_maximum_fusion.3.refs_1_, bf16[8,3,4,128,128]{4,3,2,1,0:T(8,128)(2,1)S(1)} %shard_map.65.refs_2_, ...), custom_call_target="tpu_custom_call" | custom-call | flops 503316480 | bytes 4194304 | tf_op jit(solution)/shard_map/pallas_call | solution.py:144
  85.8 4.3 %collective-permute-start.6 = (bf16[2,2,128,256]{3,2,1,0:T(8,128)(2,1)S(1)}, bf16[2,2,128,256]{3,2,1,0:T(8,128)(2,1)S(1)}, u32[]{:S(2)}, u32[]{:S(2)}) collective-permute-start(bf16[2,2,128,256]{3,2,1,0:T(8,128)(2,1)S(1)} %get-tuple-element.34), channel_id=1, source_target_pairs={{0,1},{1,16},{16,17},{17,32},{32,33},{33,48},{48,49},{2,3},{3,18},... | collective-permute-start | bytes 786440 | tf_op jit(solution)/shard_map/ppermute | solution.py:300
  90.1 5.1 %collective-permute-done.6.refs_6_ = bf16[2,2,128,256]{3,2,1,0:T(8,128)(2,1)S(1)} collective-permute-done((bf16[2,2,128,256]{3,2,1,0:T(8,128)(2,1)S(1)}, bf16[2,2,128,256]{3,2,1,0:T(8,128)(2,1)S(1)}, u32[]{:S(2)}, u32[]{:S(2)}) %collective-permute-start.6) | collective-permute-done | bytes 262176 | tf_op jit(solution)/shard_map/ppermute | solution.py:300
  95.2 3.2 %shard_map.68 = (bf16[2,128,256]{2,1,0:T(8,128)(2,1)S(1)}, bf16[4,128,256]{2,1,0:T(8,128)(2,1)S(1)}, bf16[2,128,256]{2,1,0:T(8,128)(2,1)S(1)}, bf16[2,2,128,256]{3,2,1,0:T(8,128)(2,1)}) custom-call(s32[4]{0:T(128)S(1)} %pad_add_fusion.refs_0_, f32[6]{0:T(128)S(1)} %pad_maximum_fusion.3.refs_1_, bf16[8,3,4,128,128]{4,3,2,1,0:T(8,128)(2,1)S(1)} %shard_map.65.refs_2_, ...), custom_call_target="tpu_custom_call" | custom-call | flops 503316480 | bytes 4194304 | tf_op jit(solution)/shard_map/pallas_call | solution.py:144
  98.4 5.2 %collective-permute-start.7 = (bf16[2,2,128,256]{3,2,1,0:T(8,128)(2,1)}, bf16[2,2,128,256]{3,2,1,0:T(8,128)(2,1)}, u32[]{:S(2)}, u32[]{:S(2)}) collective-permute-start(bf16[2,2,128,256]{3,2,1,0:T(8,128)(2,1)} %get-tuple-element.38), channel_id=1, source_target_pairs={{0,1},{1,16},{16,17},{17,32},{32,33},{33,48},{48,49},{2,3},{3,18},... | collective-permute-start | bytes 786440 | tf_op jit(solution)/shard_map/ppermute | solution.py:300
  104.3 1.0 copy.10
  105.2 4.3 %all-to-all-start.1 = ((bf16[2,3,8,64,128]{4,3,2,1,0:T(8,128)(2,1)}), bf16[2,3,8,64,128]{4,3,2,1,0:T(8,128)(2,1)}, u32[]{:S(2)}, u32[]{:S(2)}) async-start(bf16[2,3,8,64,128]{4,3,2,1,0:T(8,128)(2,1)} %bitcast.26), calls=%async_computation.1 | async-start | bytes 1572864 | tf_op jit(solution)/shard_map/all_to_all | solution.py:192
  109.6 1.9 %copy-done.1 = bf16[8,3,4,128,128]{4,3,2,1,0:T(8,128)(2,1)S(1)} copy-done((bf16[8,3,4,128,128]{4,3,2,1,0:T(8,128)(2,1)S(1)}, bf16[8,3,4,128,128]{4,3,2,1,0:T(8,128)(2,1)}, u32[]{:S(2)}) %copy-start.1) | copy-done | bytes 3145752
  111.4 2.3 %shard_map.69 = (bf16[2,128,256]{2,1,0:T(8,128)(2,1)S(1)}, bf16[4,128,128]{2,1,0:T(8,128)(2,1)S(1)}) custom-call(s32[4]{0:T(128)S(1)} %pad_add_fusion.refs_0_, f32[6]{0:T(128)S(1)} %pad_maximum_fusion.3.refs_1_, bf16[8,3,4,128,128]{4,3,2,1,0:T(8,128)(2,1)S(1)} %shard_map.65.refs_2_, bf16[8,3,4,128,128]{4,3,2,1,0:T(8,128)(2,1)S(1)} %copy-done.1, ...), custom_call_target="tpu_custom_call" | custom-call | flops 377487360 | bytes 4194304 | tf_op jit(solution)/shard_map/pallas_call | solution.py:144
  113.9 3.9 %all_to_all.20.late = bf16[2,1,8,64,128]{4,3,2,1,0:T(8,128)(2,1)S(1)} all-to-all(bf16[2,1,8,64,128]{4,3,2,1,0:T(8,128)(2,1)S(1)} %bitcast.29), channel_id=1, replica_groups=mesh['zhi'=4,'core'=2,'x'=4,'zlo'=2,'yl'=4,'y0'=2] {'core'}, dimensions={0} | all-to-all | bytes 524288 | tf_op jit(solution)/shard_map/all_to_all | solution.py:192
  117.8 1.3 shard_map.70
  119.1 29.9 %all_to_all.21.over = bf16[32,64,128]{2,1,0:T(8,128)(2,1)S(1)} all-to-all(bf16[32,64,128]{2,1,0:T(8,128)(2,1)S(1)} %bitcast.23), channel_id=1, replica_groups=mesh['zhi'=4,'core'=2,'x'=4,'zlo'=2,'yl'=4,'y0'=2] {'zhi','zlo','yl'}, dimensions={0} | all-to-all | bytes 1048576 | tf_op jit(solution)/shard_map/all_to_all | solution.py:346
  149.0 1.9 %collective-permute-start.8 = (bf16[64,128]{1,0:T(8,128)(2,1)S(1)}, bf16[64,128]{1,0:T(8,128)(2,1)S(1)}, u32[]{:S(2)}, u32[]{:S(2)}) collective-permute-start(bf16[64,128]{1,0:T(8,128)(2,1)S(1)} %shard_map.71), channel_id=1, source_target_pairs={{1,8},{8,1},{3,10},{10,3},{5,12},{12,5},{7,14},{14,7},{17,24},{24,... | collective-permute-start | bytes 49160 | tf_op jit(solution)/shard_map/ppermute | solution.py:348
  150.9 4.6 %collective-permute-done.8 = bf16[64,128]{1,0:T(8,128)(2,1)S(1)} collective-permute-done((bf16[64,128]{1,0:T(8,128)(2,1)S(1)}, bf16[64,128]{1,0:T(8,128)(2,1)S(1)}, u32[]{:S(2)}, u32[]{:S(2)}) %collective-permute-start.8) | collective-permute-done | bytes 16416 | tf_op jit(solution)/shard_map/ppermute | solution.py:348
  (48 shorter events, 3.1 us)
Async XLA Ops:
  6.5 2.5 %copy-start.4 = (bf16[1,4096,128]{2,1,0:T(8,128)(2,1)S(1)}, bf16[1,4096,128]{2,1,0:T(8,128)(2,1)}, u32[]{:S(2)}) copy-start(bf16[1,4096,128]{2,1,0:T(8,128)(2,1)} %param.7) | copy-start | bytes 3145732
  6.5 55.9 %all-gather.2.cloned.1.call-start = ((), (), s32[]{:S(2)}) async-start(), calls=%async_computation.4 | async-start | bytes 3538944 | tf_op jit(solution)/shard_map/all_gather | solution.py:237
  9.2 5.6 %copy-start.8 = (bf16[64,128]{1,0:T(8,128)(2,1)S(1)}, bf16[64,128]{1,0:T(8,128)(2,1)}, u32[]{:S(2)}) copy-start(bf16[64,128]{1,0:T(8,128)(2,1)} %param.8) | copy-start | bytes 49156
  9.3 7.5 %copy-start.6 = (f32[1,3]{1,0:T(1,128)S(1)}, f32[1,3]{1,0:T(1,128)}, u32[]{:S(2)}) copy-start(f32[1,3]{1,0:T(1,128)} %param.11) | copy-start | bytes 40
  9.3 7.5 %copy-start.7 = (f32[1,3]{1,0:T(1,128)S(1)}, f32[1,3]{1,0:T(1,128)}, u32[]{:S(2)}) copy-start(f32[1,3]{1,0:T(1,128)} %param.10) | copy-start | bytes 40
  10.5 19.4 %all-to-all-start = ((bf16[4,8,128,128]{3,2,1,0:T(8,128)(2,1)}), bf16[4,8,128,128]{3,2,1,0:T(8,128)(2,1)S(1)}, u32[]{:S(2)}, u32[]{:S(2)}) async-start(bf16[4,8,128,128]{3,2,1,0:T(8,128)(2,1)} %bitcast.4), calls=%async_computation | async-start | bytes 2097152 | tf_op jit(solution)/shard_map/all_to_all | solution.py:241
  14.8 17.1 %collective-permute-start.1 = (bf16[64,128]{1,0:T(8,128)(2,1)S(1)}, bf16[64,128]{1,0:T(8,128)(2,1)S(1)}, u32[]{:S(2)}, u32[]{:S(2)}) collective-permute-start(bf16[64,128]{1,0:T(8,128)(2,1)S(1)} %copy-done.8), channel_id=1, source_target_pairs={{0,1},{2,3},{4,5},{6,7},{8,24},{10,26},{12,28},{14,30},{16,17},{18... | collective-permute-start | bytes 49160 | tf_op jit(solution)/shard_map/ppermute | solution.py:253
  16.1 15.9 %collective-permute-start.2 = (bf16[64,128]{1,0:T(8,128)(2,1)S(1)}, bf16[64,128]{1,0:T(8,128)(2,1)S(1)}, u32[]{:S(2)}, u32[]{:S(2)}) collective-permute-start(bf16[64,128]{1,0:T(8,128)(2,1)S(1)} %copy-done.8), channel_id=1, source_target_pairs={{0,0},{2,2},{4,4},{6,6},{8,9},{10,11},{12,13},{14,15},{16,16},{18,... | collective-permute-start | bytes 49160 | tf_op jit(solution)/shard_map/ppermute | solution.py:252
  16.9 4.8 %collective-permute-start.3 = (f32[8]{0:T(128)S(1)}, f32[8]{0:T(128)S(1)}, u32[]{:S(2)}, u32[]{:S(2)}) collective-permute-start(f32[8]{0:T(128)S(1)} %pad_maximum_fusion.2), channel_id=1, source_target_pairs={{0,0},{1,64},{2,2},{3,66},{4,4},{5,68},{6,6},{7,70},{8,8},{9,72},{... | collective-permute-start | bytes 104 | tf_op jit(solution)/shard_map/ppermute | solution.py:245
  29.9 7.7 %collective-permute-start = (bf16[8,128,128]{2,1,0:T(8,128)(2,1)S(1)}, bf16[8,128,128]{2,1,0:T(8,128)(2,1)S(1)}, u32[]{:S(2)}, u32[]{:S(2)}) collective-permute-start(bf16[8,128,128]{2,1,0:T(8,128)(2,1)S(1)} %dynamic-slice_bitcast_fusion), channel_id=1, source_target_pairs={{0,0},{1,64},{64,1},{65,65},{2,2},{3,66},{66,3},{67,67},{4,4},{5,6... | collective-permute-start | bytes 786440 | tf_op jit(solution)/shard_map/ppermute | solution.py:243
  62.5 7.8 %collective-permute-start.4 = (bf16[8,3,4,128,128]{4,3,2,1,0:T(8,128)(2,1)}, bf16[8,3,4,128,128]{4,3,2,1,0:T(8,128)(2,1)S(1)}, u32[]{:S(2)}, u32[]{:S(2)}) collective-permute-start(bf16[8,3,4,128,128]{4,3,2,1,0:T(8,128)(2,1)} %all-gather.2.cloned.1.call-done.blocks), channel_id=1, source_target_pairs={{0,64},{64,0},{1,65},{65,1},{2,66},{66,2},{3,67},{67,3},{4,68},{68... | collective-permute-start | bytes 9437192 | tf_op jit(solution)/shard_map/ppermute | solution.py:261
  64.4 1.9 %copy-start.2 = (bf16[8,3,4,128,128]{4,3,2,1,0:T(8,128)(2,1)S(1)}, bf16[8,3,4,128,128]{4,3,2,1,0:T(8,128)(2,1)}, u32[]{:S(2)}) copy-start(bf16[8,3,4,128,128]{4,3,2,1,0:T(8,128)(2,1)} %all-gather.2.cloned.1.call-done.blocks) | copy-start | bytes 9437188
  66.3 3.9 %copy-start.3 = (bf16[8,128,256]{2,1,0:T(8,128)(2,1)S(1)}, bf16[8,128,256]{2,1,0:T(8,128)(2,1)}, u32[]{:S(2)}) copy-start(bf16[8,128,256]{2,1,0:T(8,128)(2,1)} %pad_maximum_fusion.refs_4_) | copy-start | bytes 1572868
  70.2 25.0 %copy-start = (bf16[8,3,4,128,128]{4,3,2,1,0:T(8,128)(2,1)}, bf16[8,3,4,128,128]{4,3,2,1,0:T(8,128)(2,1)S(1)}, u32[]{:S(2)}) copy-start(bf16[8,3,4,128,128]{4,3,2,1,0:T(8,128)(2,1)S(1)} %collective-permute-done.4.refs_3_) | copy-start | bytes 9437188
  73.0 10.2 %collective-permute-start.5 = (bf16[2,2,128,256]{3,2,1,0:T(8,128)(2,1)S(1)}, bf16[2,2,128,256]{3,2,1,0:T(8,128)(2,1)S(1)}, u32[]{:S(2)}, u32[]{:S(2)}) collective-permute-start(bf16[2,2,128,256]{3,2,1,0:T(8,128)(2,1)S(1)} %get-tuple-element.30), channel_id=1, source_target_pairs={{0,1},{1,16},{16,17},{17,32},{32,33},{33,48},{48,49},{2,3},{3,18},... | collective-permute-start | bytes 786440 | tf_op jit(solution)/shard_map/ppermute | solution.py:300
  85.8 9.4 %collective-permute-start.6 = (bf16[2,2,128,256]{3,2,1,0:T(8,128)(2,1)S(1)}, bf16[2,2,128,256]{3,2,1,0:T(8,128)(2,1)S(1)}, u32[]{:S(2)}, u32[]{:S(2)}) collective-permute-start(bf16[2,2,128,256]{3,2,1,0:T(8,128)(2,1)S(1)} %get-tuple-element.34), channel_id=1, source_target_pairs={{0,1},{1,16},{16,17},{17,32},{32,33},{33,48},{48,49},{2,3},{3,18},... | collective-permute-start | bytes 786440 | tf_op jit(solution)/shard_map/ppermute | solution.py:300
  98.4 11.1 %collective-permute-start.7 = (bf16[2,2,128,256]{3,2,1,0:T(8,128)(2,1)}, bf16[2,2,128,256]{3,2,1,0:T(8,128)(2,1)}, u32[]{:S(2)}, u32[]{:S(2)}) collective-permute-start(bf16[2,2,128,256]{3,2,1,0:T(8,128)(2,1)} %get-tuple-element.38), channel_id=1, source_target_pairs={{0,1},{1,16},{16,17},{17,32},{32,33},{33,48},{48,49},{2,3},{3,18},... | collective-permute-start | bytes 786440 | tf_op jit(solution)/shard_map/ppermute | solution.py:300
  105.2 8.6 %all-to-all-start.1 = ((bf16[2,3,8,64,128]{4,3,2,1,0:T(8,128)(2,1)}), bf16[2,3,8,64,128]{4,3,2,1,0:T(8,128)(2,1)}, u32[]{:S(2)}, u32[]{:S(2)}) async-start(bf16[2,3,8,64,128]{4,3,2,1,0:T(8,128)(2,1)} %bitcast.26), calls=%async_computation.1 | async-start | bytes 1572864 | tf_op jit(solution)/shard_map/all_to_all | solution.py:192
  109.6 1.9 %copy-start.1 = (bf16[8,3,4,128,128]{4,3,2,1,0:T(8,128)(2,1)S(1)}, bf16[8,3,4,128,128]{4,3,2,1,0:T(8,128)(2,1)}, u32[]{:S(2)}) copy-start(bf16[8,3,4,128,128]{4,3,2,1,0:T(8,128)(2,1)} %copy-done) | copy-start | bytes 9437188
  111.4 2.4 %copy-start.5 = (bf16[2,128,128]{2,1,0:T(8,128)(2,1)S(1)}, bf16[2,128,128]{2,1,0:T(8,128)(2,1)}, u32[]{:S(2)}) copy-start(bf16[2,128,128]{2,1,0:T(8,128)(2,1)} %slice.55) | copy-start | bytes 196612
  149.0 6.5 %collective-permute-start.8 = (bf16[64,128]{1,0:T(8,128)(2,1)S(1)}, bf16[64,128]{1,0:T(8,128)(2,1)S(1)}, u32[]{:S(2)}, u32[]{:S(2)}) collective-permute-start(bf16[64,128]{1,0:T(8,128)(2,1)S(1)} %shard_map.71), channel_id=1, source_target_pairs={{1,8},{8,1},{3,10},{10,3},{5,12},{12,5},{7,14},{14,7},{17,24},{24,... | collective-permute-start | bytes 49160 | tf_op jit(solution)/shard_map/ppermute | solution.py:348
Sparse Core Ops, SparseCore 0:
  9.4 52.9 all-gather.1
